TPU v7x, 32 devices: a whole 2x2x4 slice. The times are simulated.
32 devices in a mesh: cells: 4 (over y, x), sensors: 8 (over z, core).
Axes of the slice: x: 2, y: 2, z: 4, core: 2. Of those that a mesh axis runs over, the one named last changes fastest.
Arguments:
- rhs: float32 [256, 6, 128, 128], P('sensors', None, 'cells'), may hold values from -18 to 18
- forward_map: bfloat16 [2, 128, 128, 16384], P(None, None, 'sensors', 'cells'), may hold values from -0.125 to 0.125
- stiffness: float32 [128, 128], P('cells'), may hold values from 0.5 to 1.5
- reaction: float32 [128, 128], P('cells'), may hold values from 0.25 to 2
- noise_weight: float32 [128], replicated, may hold values from 0.3 to 3
- sensor_cell: int32 [128], replicated, may hold values from 0 to 16383, as said below
Outputs:
- solution: float32 [256, 6, 128, 128], P('sensors', None, 'cells')
- residual: float32 [256, 6, 128, 128], P('sensors', None, 'cells')
Inputs may be any that keep to these rules, and one draw needn't show every extreme that they name: `sensor_cell`: row-major index over the 128 x 128 grid of the cell under each sensor; several sensors may share a cell.
All inputs are finite; a program needn't handle non-finite values.
Results may differ from a plain program's by a relative error of at most 0.0073.
Values may be sent and summed in bfloat16 or wider, within the bound.
No kernel may reach another device: no remote copies, remote signals or barrier semaphores. Data moves between devices by JAX's collectives and lax.ppermute only.
A program may use at most 192 MiB of HBM per device.

v0:
```python
import math

import jax
import jax.numpy as jnp
from jax import lax
from jax.sharding import PartitionSpec as P

SWEEPS = 4
ITERS = 2


DAMPING = 0.8


def padded_2(array, sides, width):
    for axis, dim in sides:
        size, length = (lax.axis_size(axis), array.shape[dim])
        up = [(i, (i + 1) % size) for i in range(size - 1)]
        down = [(j, i) for i, j in up]
        last = lax.slice_in_dim(array, length - width, length, axis=dim)
        first = lax.slice_in_dim(array, 0, width, axis=dim)
        before = lax.ppermute(last, axis, up)
        after = lax.ppermute(first, axis, down)
        array = jnp.concatenate([before, array, after], axis=dim)
    return array


def neighbour_sum(extended):
    padded = jnp.pad(extended, [(0, 0)] * (extended.ndim - 1) + [(1, 1)])
    return (
        padded[..., 2:, 1:-1]
        + padded[..., :-2, 1:-1]
        + padded[..., 1:-1, 2:]
        + padded[..., 1:-1, :-2]
    )


def transform_table(freqs, period):
    wave = jnp.arange(freqs, dtype=jnp.int32)[:, None]
    moment = jnp.arange(period, dtype=jnp.int32)[None, :]
    phase = (wave * moment % period).astype(jnp.float32) * (2.0 * math.pi / period)
    factor = 1.0 / math.sqrt(period)
    return jnp.concatenate([jnp.cos(phase) * factor, -jnp.sin(phase) * factor], axis=0).astype(
        jnp.bfloat16
    )


def observe(map_pair, spectrum, sensor_marks):
    freqs = map_pair.shape[1]
    field_real = spectrum[:freqs]
    field_imag = spectrum[freqs:]

    def project(weights, values):
        return jnp.einsum("fsc,fbc->fbs", weights, values, preferred_element_type=jnp.float32)

    def select_cells(values):
        return jnp.einsum("fbc,cs->fbs", values, sensor_marks, preferred_element_type=jnp.float32)

    obs_real = (
        project(map_pair[0], field_real)
        - project(map_pair[1], field_imag)
        + select_cells(field_real)
    )
    obs_imag = (
        project(map_pair[0], field_imag)
        + project(map_pair[1], field_real)
        + select_cells(field_imag)
    )
    return jnp.stack([obs_real, obs_imag])


def pull_back(map_pair, weighted, sensor_marks):

    def spread_back(weights, values):
        return jnp.einsum("fsc,fbs->fbc", weights, values, preferred_element_type=jnp.float32)

    def place_cells(values):
        return jnp.einsum("fbs,cs->fbc", values, sensor_marks, preferred_element_type=jnp.float32)

    back_real = (
        spread_back(map_pair[0], weighted[0])
        + spread_back(map_pair[1], weighted[1])
        + place_cells(weighted[0])
    )
    back_imag = (
        spread_back(map_pair[0], weighted[1])
        - spread_back(map_pair[1], weighted[0])
        + place_cells(weighted[1])
    )
    return jnp.concatenate([back_real, back_imag], axis=0)


def shards(rhs, forward_map, stiffness, reaction, noise_weight, sensor_cell):
    time_here, samples, rows_here, grid_cols = rhs.shape
    freqs = forward_map.shape[1]
    period = 2 * freqs
    depth = SWEEPS - 1
    table = transform_table(freqs, period)
    table_wide = table.astype(jnp.float32)
    diagonal = reaction + 4.0 * stiffness * stiffness
    inverse = 1.0 / diagonal
    coeff_wide = padded_2(jnp.stack([stiffness, inverse, diagonal]), (("cells", 1),), depth)
    stiff_wide = coeff_wide[0]
    inverse_wide = coeff_wide[1]
    diagonal_wide = coeff_wide[2]
    stiff_rim = stiff_wide[depth - 1 : depth + rows_here + 1]

    def precondition(residual):
        residual_wide = padded_2(residual, (("cells", 2),), depth)
        update = DAMPING * inverse_wide * residual_wide
        for sweep in range(depth):
            rimmed = jnp.pad(stiff_wide * update, ((0, 0), (0, 0), (1, 1), (0, 0)))
            applied = diagonal_wide * update - stiff_wide * neighbour_sum(rimmed)
            update = update + DAMPING * inverse_wide * (residual_wide - applied)
        return update[:, :, depth : depth + rows_here]

    cell_index = lax.axis_index("cells")
    sensor_index = lax.axis_index("sensors")
    cells_here = rows_here * grid_cols
    sensors_here = forward_map.shape[2]
    local_sensors = lax.dynamic_slice_in_dim(sensor_cell, sensor_index * sensors_here, sensors_here)
    cell_ids = cell_index * cells_here + jnp.arange(cells_here, dtype=jnp.int32)
    sensor_marks = (cell_ids[:, None] == local_sensors[None, :]).astype(jnp.bfloat16)
    local_weight = lax.dynamic_slice_in_dim(noise_weight, sensor_index * sensors_here, sensors_here)
    solution = precondition(rhs)
    residual = rhs
    for iteration in range(ITERS):
        field_wide = padded_2(solution.astype(jnp.bfloat16), (("cells", 2),), 1).astype(
            solution.dtype
        )
        prior_part = diagonal * solution - stiffness * neighbour_sum(stiff_rim * field_wide)
        field_low = solution.astype(jnp.bfloat16).reshape(time_here, samples, cells_here)
        spectrum = jnp.einsum(
            "jt,tbc->jbc",
            table,
            lax.all_gather(field_low, "sensors", axis=0, tiled=True),
            preferred_element_type=jnp.float32,
        ).astype(jnp.bfloat16)
        observed = lax.psum(observe(forward_map, spectrum, sensor_marks), "cells")
        weighted = (local_weight * observed).astype(jnp.bfloat16)
        adjoint = pull_back(forward_map, weighted, sensor_marks)
        result = lax.psum_scatter(
            jnp.einsum(
                "jt,jbc->tbc",
                table_wide,
                adjoint,
                precision=lax.Precision.HIGHEST,
                preferred_element_type=jnp.float32,
            ),
            "sensors",
            scatter_dimension=0,
            tiled=True,
        )
        residual = rhs - (prior_part + result.reshape(solution.shape))
        solution = solution + precondition(residual)
    return (solution, residual)


def solution(mesh):
    placed = (
        P("sensors", None, "cells", None),
        P(None, None, "sensors", "cells"),
        P("cells", None),
        P("cells", None),
        P(),
        P(),
    )
    return jax.shard_map(
        shards,
        mesh=mesh,
        in_specs=placed,
        out_specs=(P("sensors", None, "cells", None), P("sensors", None, "cells", None)),
        check_vma=False,
    )
```

profile of v0, /device:TPU:1, one launch (start us, length us, event | category | flops | bytes accessed | tf_op | source)
XLA Modules:
  0.0 1392.7 jit_solution(18334837641370925467)
XLA Ops:
  55.3 117.3 %all-gather.3.cloned.1.call-done = bf16[256,6,4096]{2,0,1:T(8,128)(2,1)} async-done(((bf16[32,6,4096]{2,0,1:T(8,128)(2,1)}), bf16[256,6,4096]{2,0,1:T(8,128)(2,1)}) %all-gather.3.cloned.1.call-update) | async-done | bytes 12582928 | tf_op jit(solution)/shard_map/all_gather | solution.py:136
  172.5 11.1 convolution_convert_fusion.1
  183.7 10.8 fusion.261
  200.8 12.0 fusion.22
  212.9 11.7 fusion.20
  224.5 12.3 fusion.149
  238.3 10.8 fusion.164
  250.3 39.1 %all-reduce.23.cloned.1.call-done = f32[2,128,6,16]{1,3,2,0:T(8,128)} async-done(((f32[2,128,6,16]{1,3,2,0:T(8,128)}), f32[2,128,6,16]{1,3,2,0:T(8,128)}) %all-reduce.23.cloned.1.call-update) | async-done | bytes 98320 | tf_op jit(solution)/shard_map/psum | solution.py:139
  290.6 13.9 fusion.34
  304.5 13.9 fusion.16
  318.6 13.8 fusion.18
  332.4 13.9 fusion.32
  346.3 28.4 %fusion.43 = f32[128,6,4096]{2,0,1:T(8,128)} fusion(f32[128,6,4096]{2,1,0:T(8,128)} %fusion.18, f32[128,6,4096]{2,1,0:T(8,128)} %fusion.34, s32[4096]{0:T(1024)S(1)} %iota_add_fusion, s32[16]{0:T(128)S(1)} %dynamic_slice.7, bf16[2,128,6,16]{1,3,2,0:T(8,128)(2,1)S(1)} %multiply_convert_fusion.3), kind=kOutput, calls=%fused_computation.47 | convolution fusion | flops 107020288 | bytes 37790208 | tf_op jit(solution)/shard_map/fbs,cs->fbc/dot_general | solution.py:78
  374.7 28.6 %fusion.42 = f32[128,6,4096]{2,0,1:T(8,128)} fusion(f32[128,6,4096]{2,1,0:T(8,128)} %fusion.16, f32[128,6,4096]{2,1,0:T(8,128)} %fusion.32, s32[4096]{0:T(1024)S(1)} %iota_add_fusion, s32[16]{0:T(128)S(1)} %dynamic_slice.7, bf16[2,128,6,16]{1,3,2,0:T(8,128)(2,1)S(1)} %multiply_convert_fusion.3), kind=kOutput, calls=%fused_computation.45 | convolution fusion | flops 107020288 | bytes 37790208 | tf_op jit(solution)/shard_map/fbs,cs->fbc/dot_general | solution.py:78
  403.3 24.8 %fusion = f32[256,6,4096]{2,0,1:T(8,128)} fusion(f32[128,6,4096]{2,0,1:T(8,128)} %fusion.42, f32[128,6,4096]{2,0,1:T(8,128)} %fusion.43, bf16[128,256]{1,0:T(8,128)(2,1)S(1)} %copy-done.17, bf16[128,256]{1,0:T(8,128)(2,1)S(1)} %copy-done.20), kind=kOutput, calls=%fused_computation | convolution fusion | flops 19333906432 | bytes 50462720 | tf_op jit(solution)/shard_map/jt,jbc->tbc/dot_general | solution.py:143
  438.7 235.0 %reduce-scatter.3.cloned.1.call-done = f32[32,6,4096]{2,0,1:T(8,128)} async-done(((f32[256,6,4096]{2,0,1:T(8,128)}), f32[32,6,4096]{2,0,1:T(8,128)}) %reduce-scatter.3.cloned.1.call-update) | async-done | bytes 3145744 | tf_op jit(solution)/shard_map/reduce_scatter | solution.py:142
  718.3 120.2 %all-gather.5.cloned.1.call-done = bf16[256,6,4096]{2,0,1:T(8,128)(2,1)} async-done(((bf16[32,6,4096]{2,0,1:T(8,128)(2,1)}), bf16[256,6,4096]{2,0,1:T(8,128)(2,1)}) %all-gather.5.cloned.1.call-update) | async-done | bytes 12582928 | tf_op jit(solution)/shard_map/all_gather | solution.py:136
  838.5 11.5 convolution_convert_fusion
  850.0 8.4 fusion.260
  864.0 13.9 fusion.14
  878.2 11.3 fusion.12
  889.4 11.1 fusion.179
  901.0 14.0 %fusion.194 = f32[1,128,6,16]{3,2,1,0:T(8,128)S(1)} fusion(f32[128,6,16]{2,1,0:T(8,128)S(1)} %copy.47, f32[128,6,16]{2,1,0:T(8,128)S(1)} %fusion.12, bf16[2,128,16,4096]{3,2,1,0:T(8,128)(2,1)} %param.7, bf16[128,6,4096]{2,0,1:T(8,128)(2,1)} %copy-done.7), kind=kOutput, calls=%fused_computation.201 | convolution fusion | flops 100687872 | bytes 23216128 | tf_op jit(solution)/shard_map/fsc,fbc->fbs/dot_general | solution.py:54
  916.1 39.1 %all-reduce.25.cloned.1.call-done = f32[2,128,6,16]{1,3,2,0:T(8,128)} async-done(((f32[2,128,6,16]{1,3,2,0:T(8,128)}), f32[2,128,6,16]{1,3,2,0:T(8,128)}) %all-reduce.25.cloned.1.call-update) | async-done | bytes 98320 | tf_op jit(solution)/shard_map/psum | solution.py:139
  956.4 13.9 fusion.10
  970.3 13.9 fusion.24
  984.5 13.8 fusion.26
  998.3 13.8 fusion.8
  1012.1 28.6 %fusion.41 = f32[128,6,4096]{2,0,1:T(8,128)} fusion(f32[128,6,4096]{2,1,0:T(8,128)} %fusion.10, f32[128,6,4096]{2,1,0:T(8,128)} %fusion.26, s32[4096]{0:T(1024)S(1)} %iota_add_fusion, s32[16]{0:T(128)S(1)} %dynamic_slice.7, bf16[2,128,6,16]{1,3,2,0:T(8,128)(2,1)S(1)} %multiply_convert_fusion.2), kind=kOutput, calls=%fused_computation.43 | convolution fusion | flops 107020288 | bytes 37790208 | tf_op jit(solution)/shard_map/fbs,cs->fbc/dot_general | solution.py:78
  1040.7 28.3 %fusion.40 = f32[128,6,4096]{2,0,1:T(8,128)} fusion(f32[128,6,4096]{2,1,0:T(8,128)} %fusion.8, f32[128,6,4096]{2,1,0:T(8,128)} %fusion.24, s32[4096]{0:T(1024)S(1)} %iota_add_fusion, s32[16]{0:T(128)S(1)} %dynamic_slice.7, bf16[2,128,6,16]{1,3,2,0:T(8,128)(2,1)S(1)} %multiply_convert_fusion.2), kind=kOutput, calls=%fused_computation.41 | convolution fusion | flops 107020288 | bytes 37790208 | tf_op jit(solution)/shard_map/fbs,cs->fbc/dot_general | solution.py:78
  1069.1 24.8 %fusion.4 = f32[256,6,4096]{2,0,1:T(8,128)} fusion(f32[128,6,4096]{2,0,1:T(8,128)} %fusion.40, f32[128,6,4096]{2,0,1:T(8,128)} %fusion.41, bf16[128,256]{1,0:T(8,128)(2,1)S(1)} %copy-done.18, bf16[128,256]{1,0:T(8,128)(2,1)S(1)} %copy-done.21), kind=kOutput, calls=%fused_computation.4 | convolution fusion | flops 19333906432 | bytes 50462720 | tf_op jit(solution)/shard_map/jt,jbc->tbc/dot_general | solution.py:143
  1104.5 235.0 %reduce-scatter.5.cloned.1.call-done = f32[32,6,4096]{2,0,1:T(8,128)} async-done(((f32[256,6,4096]{2,0,1:T(8,128)}), f32[32,6,4096]{2,0,1:T(8,128)}) %reduce-scatter.5.cloned.1.call-update) | async-done | bytes 3145744 | tf_op jit(solution)/shard_map/reduce_scatter | solution.py:142
  (209 shorter events, 178.2 us)
Async XLA Ops:
  7.2 165.3 %all-gather.3.cloned.1.call-start = ((), (), s32[]{:S(2)}) async-start(), calls=%async_computation.2 | async-start | bytes 14155776 | tf_op jit(solution)/shard_map/all_gather | solution.py:136
  8.9 12.2 collective-permute-start
  12.8 8.3 collective-permute-start.1
  15.7 9.0 collective-permute-start.2
  19.8 14.1 %collective-permute-start.3 = (f32[32,6,3,128]{3,0,2,1:T(8,128)S(1)}, f32[32,6,3,128]{3,0,2,1:T(8,128)S(1)}, u32[]{:S(2)}, u32[]{:S(2)}) collective-permute-start(f32[32,6,3,128]{3,0,2,1:T(8,128)S(1)} %copy.139), channel_id=1, source_target_pairs={{8,0},{16,8},{24,16},{9,1},{17,9},{25,17},{10,2},{18,10},{26,18},{... | collective-permute-start | bytes 884744 | tf_op jit(solution)/shard_map/ppermute | solution.py:23
  21.9 23.8 %copy-start.31 = (f32[32,128]{1,0:T(8,128)}, f32[32,128]{1,0:T(8,128)S(1)}, u32[]{:S(2)}) copy-start(f32[32,128]{1,0:T(8,128)S(1)} %slice.347) | copy-start | bytes 49156
  21.9 23.8 %copy-start.34 = (f32[32,128]{1,0:T(8,128)}, f32[32,128]{1,0:T(8,128)S(1)}, u32[]{:S(2)}) copy-start(f32[32,128]{1,0:T(8,128)S(1)} %slice.349) | copy-start | bytes 49156
  54.3 235.1 %all-reduce.23.cloned.1.call-start = ((), (), s32[]{:S(2)}) async-start(), calls=%async_computation.3 | async-start | bytes 196608 | tf_op jit(solution)/shard_map/psum | solution.py:139
  55.2 128.4 %copy-start.16 = (bf16[128,256]{1,0:T(8,128)(2,1)}, bf16[128,256]{1,0:T(8,128)(2,1)S(1)}, u32[]{:S(2)}) copy-start(bf16[128,256]{1,0:T(8,128)(2,1)S(1)} %get-tuple-element.54) | copy-start | bytes 196612
  55.3 128.4 %copy-start.19 = (bf16[128,256]{1,0:T(8,128)(2,1)}, bf16[128,256]{1,0:T(8,128)(2,1)S(1)}, u32[]{:S(2)}) copy-start(bf16[128,256]{1,0:T(8,128)(2,1)S(1)} %get-tuple-element.55) | copy-start | bytes 196612
  250.0 423.7 %reduce-scatter.3.cloned.1.call-start = ((), (), s32[]{:S(2)}) async-start(), calls=%async_computation.4 | async-start | bytes 28311552 | tf_op jit(solution)/shard_map/reduce_scatter | solution.py:142
  250.3 54.2 %copy-start.42 = (f32[16]{0:T(128)}, f32[16]{0:T(128)S(1)}, u32[]{:S(2)}) copy-start(f32[16]{0:T(128)S(1)} %dynamic_slice.6) | copy-start | bytes 196
  374.7 28.6 %copy-start.17 = (bf16[128,256]{1,0:T(8,128)(2,1)S(1)}, bf16[128,256]{1,0:T(8,128)(2,1)}, u32[]{:S(2)}) copy-start(bf16[128,256]{1,0:T(8,128)(2,1)} %copy-done.16) | copy-start | bytes 196612
  374.7 28.6 %copy-start.20 = (bf16[128,256]{1,0:T(8,128)(2,1)S(1)}, bf16[128,256]{1,0:T(8,128)(2,1)}, u32[]{:S(2)}) copy-start(bf16[128,256]{1,0:T(8,128)(2,1)} %copy-done.19) | copy-start | bytes 196612
  428.1 245.6 %copy-start.25 = (f32[32,128]{1,0:T(8,128)S(1)}, f32[32,128]{1,0:T(8,128)}, u32[]{:S(2)}) copy-start(f32[32,128]{1,0:T(8,128)} %param.8) | copy-start | bytes 49156
  428.1 245.6 %copy-start.28 = (f32[32,128]{1,0:T(8,128)S(1)}, f32[32,128]{1,0:T(8,128)}, u32[]{:S(2)}) copy-start(f32[32,128]{1,0:T(8,128)} %copy-done.27) | copy-start | bytes 49156
  428.1 410.4 %all-gather.5.cloned.1.call-start = ((), (), s32[]{:S(2)}) async-start(), calls=%async_computation.5 | async-start | bytes 14155776 | tf_op jit(solution)/shard_map/all_gather | solution.py:136
  429.0 5.1 collective-permute-start.4
  432.0 4.8 collective-permute-start.5
  680.5 6.7 collective-permute-start.6
  683.6 11.4 collective-permute-start.7
  718.3 237.0 %all-reduce.25.cloned.1.call-start = ((), (), s32[]{:S(2)}) async-start(), calls=%async_computation.6 | async-start | bytes 196608 | tf_op jit(solution)/shard_map/psum | solution.py:139
  901.0 54.3 %copy-start.43 = (f32[16]{0:T(128)S(1)}, f32[16]{0:T(128)}, u32[]{:S(2)}) copy-start(f32[16]{0:T(128)} %copy-done.42) | copy-start | bytes 196
  915.9 423.7 %reduce-scatter.5.cloned.1.call-start = ((), (), s32[]{:S(2)}) async-start(), calls=%async_computation.7 | async-start | bytes 28311552 | tf_op jit(solution)/shard_map/reduce_scatter | solution.py:142
  1040.7 28.4 %copy-start.18 = (bf16[128,256]{1,0:T(8,128)(2,1)S(1)}, bf16[128,256]{1,0:T(8,128)(2,1)}, u32[]{:S(2)}) copy-start(bf16[128,256]{1,0:T(8,128)(2,1)} %copy-done.16) | copy-start | bytes 196612
  1040.7 28.4 %copy-start.21 = (bf16[128,256]{1,0:T(8,128)(2,1)S(1)}, bf16[128,256]{1,0:T(8,128)(2,1)}, u32[]{:S(2)}) copy-start(bf16[128,256]{1,0:T(8,128)(2,1)} %copy-done.19) | copy-start | bytes 196612
  1094.0 245.6 %copy-start.26 = (f32[32,128]{1,0:T(8,128)S(1)}, f32[32,128]{1,0:T(8,128)}, u32[]{:S(2)}) copy-start(f32[32,128]{1,0:T(8,128)} %param.8) | copy-start | bytes 49156
  1094.0 245.6 %copy-start.29 = (f32[32,128]{1,0:T(8,128)S(1)}, f32[32,128]{1,0:T(8,128)}, u32[]{:S(2)}) copy-start(f32[32,128]{1,0:T(8,128)} %copy-done.27) | copy-start | bytes 49156
  1094.8 4.3 collective-permute-start.8
  1097.9 4.8 collective-permute-start.9
  1346.3 7.9 collective-permute-start.10
  1349.4 11.4 collective-permute-start.11
  (34 other events, 316.4 us)
Sparse Core Ops, SparseCore 0:
  54.5 118.0 all-gather.2
  250.1 39.2 all-reduce.22
  428.2 245.4 reduce-scatter.2
  718.4 120.0 all-gather.4
  916.0 39.2 all-reduce.24
  1094.1 245.3 reduce-scatter.4
where the time goes:
time: 1410 us; the launch traced here: 1390 us
  waiting for transfers between devices  819 us (58%)
  matrix products  401 us (28%)
  other arithmetic  78.5 us (6%)
  local copies, waits for them, and re-layouts  49.8 us (4%)
  starting transfers between devices  28.8 us (2%)
  between operations  15.3 us (1%)
    reduce_scatter x2, waiting for transfers between devices, shards(): lax.psum_scatter(jnp.einsum('jt,jbc->tbc', table_wide, adjoint, precision...  470 us
    all_gather x2, waiting for transfers between devices, shards(): lax.all_gather(field_low, 'sensors', axis=0, tiled=True)  237 us
    dot_general x4, matrix products, place_cells(): jnp.einsum('fbs,cs->fbc', values, sensor_marks, preferred_element_type=jn...  114 us
    dot_general x8, matrix products, spread_back(): jnp.einsum('fsc,fbs->fbc', weights, values, preferred_element_type=jnp.fl...  111 us
    dot_general x8, matrix products, project(): jnp.einsum('fsc,fbc->fbs', weights, values, preferred_element_type=jnp.fl...  97.1 us
    psum x2, waiting for transfers between devices, shards(): observed = lax.psum(observe(forward_map, spectrum, sensor_marks), 'cells')  78.3 us
    dot_general x2, matrix products, shards(): jnp.einsum('jt,jbc->tbc', table_wide, adjoint, precision=lax.Precision.HI...  49.6 us
  transfers between devices with their start and end apart: 18, of which 13 were waited for; matrix products, arithmetic and copies ran while one was open for 1% of the time, Pallas kernels for 0%

commit v1 on v0

v1 whole, which is shorter than its diff:
```python
import math

import jax
import jax.numpy as jnp
from jax import lax
from jax.experimental import pallas as pl
from jax.experimental.pallas import tpu as pltpu
from jax.sharding import PartitionSpec as P

SWEEPS = 4
ITERS = 2
DAMPING = 0.8
HALO = SWEEPS
LANES = 128
SUBLANES = 8
GROUPS = 2
CHUNK_ROWS = 4
VMEM_BYTES = 40 * 2**20


def transform_table(freqs, period):
    wave = jnp.arange(freqs, dtype=jnp.int32)[:, None]
    moment = jnp.arange(period, dtype=jnp.int32)[None, :]
    phase = (wave * moment % period).astype(jnp.float32) * (2.0 * math.pi / period)
    factor = 1.0 / math.sqrt(period)
    return jnp.concatenate([jnp.cos(phase) * factor, -jnp.sin(phase) * factor], axis=0).astype(
        jnp.bfloat16
    )


def params(**kwargs):
    return pltpu.CompilerParams(vmem_limit_bytes=VMEM_BYTES, **kwargs)


def whole_block(array):
    return pl.BlockSpec(array.shape, lambda *_: (0,) * array.ndim)


def dot(left, right):
    return jnp.dot(left, right, preferred_element_type=jnp.float32)


def dot_lanes(left, right):
    return lax.dot_general(left, right, (((1,), (1,)), ((), ())), preferred_element_type=jnp.float32)


def neighbours(field):
    inner = field[1:-1]
    lane = lax.broadcasted_iota(jnp.int32, inner.shape, 2)
    before = jnp.where(lane == 0, 0.0, pltpu.roll(inner, 1, 2))
    after = jnp.where(lane == LANES - 1, 0.0, pltpu.roll(inner, LANES - 1, 2))
    return (field[2:] + field[:-2]) + (before + after)


def trim(array, width):
    return array[width : array.shape[0] - width]


def precondition(residual, coeff_ref):
    extra = (coeff_ref.shape[1] - residual.shape[0]) // 2
    coeff = [trim(coeff_ref[k], extra) for k in range(3)]
    first = coeff[0] * residual
    scaled = first
    for sweep in range(1, SWEEPS):
        scaled = (
            (1.0 - DAMPING) * scaled[1:-1]
            + trim(first, sweep)
            + trim(coeff[1], sweep) * neighbours(scaled)
        )
    return trim(coeff[2], SWEEPS - 1) * scaled


def prior(field, coeff_ref):
    extra = (coeff_ref.shape[1] - field.shape[0]) // 2
    stiffness = trim(coeff_ref[3], extra)
    diagonal = trim(coeff_ref[4], extra + 1)
    return diagonal * field[1:-1] - stiffness[1:-1] * neighbours(stiffness * field)


def time_chunks(steps, body):
    def run(index, carry):
        body(pl.ds(pl.multiple_of(index * SUBLANES, SUBLANES), SUBLANES))
        return carry

    lax.fori_loop(0, steps // SUBLANES, run, 0)


def start_kernel(rhs_ref, up_ref, down_ref, coeff_ref, iter_ref, low_ref, rest_ref, top_ref, bottom_ref):
    rows = iter_ref.shape[1]

    def body(times):
        here = jnp.swapaxes(rhs_ref[times], 0, 1)
        update = precondition(
            jnp.concatenate([up_ref[0, :, times], here, down_ref[0, :, times]], axis=0), coeff_ref
        )
        iter_ref[0, :, times] = update[1:-1]
        rest = here - prior(update, coeff_ref)
        rest_ref[0, :, times] = rest
        top_ref[0, :, times] = rest[:HALO]
        bottom_ref[0, :, times] = rest[rows - HALO :]

    time_chunks(iter_ref.shape[2], body)
    low_ref[...] = iter_ref[...].astype(low_ref.dtype)


def start(group, members, rhs, up, down, coeff):
    steps, _, rows, cols = rhs.shape
    flat = rhs.reshape(steps, -1, cols)
    field = pl.BlockSpec((1, rows, steps, cols), lambda b: (b, 0, 0, 0))
    rim = pl.BlockSpec((1, HALO, steps, cols), lambda b: (b, 0, 0, 0))
    whole_rim = pl.BlockSpec((1, HALO, steps, cols), lambda b: (b + group * members, 0, 0, 0))
    shape = (members, rows, steps, cols)
    rim_shape = (members, HALO, steps, cols)
    return pl.pallas_call(
        start_kernel,
        grid=(members,),
        in_specs=[
            pl.BlockSpec((steps, rows, cols), lambda b: (0, b + group * members, 0)),
            whole_rim,
            whole_rim,
            whole_block(coeff),
        ],
        out_specs=[field, field, field, rim, rim],
        out_shape=[
            jax.ShapeDtypeStruct(shape, jnp.float32),
            jax.ShapeDtypeStruct(shape, jnp.bfloat16),
            jax.ShapeDtypeStruct(shape, jnp.float32),
            jax.ShapeDtypeStruct(rim_shape, jnp.float32),
            jax.ShapeDtypeStruct(rim_shape, jnp.float32),
        ],
        compiler_params=params(),
        name="start",
    )(flat, up, down, coeff)


def residual_of(times, rest_refs, misfit_refs):
    parts = [
        rest[0, :, times] - misfit[0, :, times].astype(jnp.float32)
        for rest, misfit in zip(rest_refs, misfit_refs)
    ]
    return jnp.concatenate(parts, axis=0)


def step_kernel(
    up_ref, rest_ref, down_ref, mup_ref, misfit_ref, mdown_ref, iter_ref, coeff_ref,
    next_ref, low_ref, later_ref, top_ref, bottom_ref,
):
    rows = iter_ref.shape[1]

    def body(times):
        residual = residual_of(times, (up_ref, rest_ref, down_ref), (mup_ref, misfit_ref, mdown_ref))
        update = precondition(residual, coeff_ref)
        next_ref[0, :, times] = iter_ref[0, :, times] + update[1:-1]
        rest = rest_ref[0, :, times] - prior(update, coeff_ref)
        later_ref[0, :, times] = rest
        top_ref[0, :, times] = rest[:HALO]
        bottom_ref[0, :, times] = rest[rows - HALO :]

    time_chunks(iter_ref.shape[2], body)
    low_ref[...] = next_ref[...].astype(low_ref.dtype)


def step(rests, misfits, iterate, coeff):
    members, rows, steps, cols = iterate.shape
    field = pl.BlockSpec((1, rows, steps, cols), lambda b: (b, 0, 0, 0))
    rim = pl.BlockSpec((1, HALO, steps, cols), lambda b: (b, 0, 0, 0))
    rim_shape = (members, HALO, steps, cols)
    return pl.pallas_call(
        step_kernel,
        grid=(members,),
        in_specs=[rim, field, rim] * 2 + [field, whole_block(coeff)],
        out_specs=[field, field, field, rim, rim],
        out_shape=[
            jax.ShapeDtypeStruct(iterate.shape, jnp.float32),
            jax.ShapeDtypeStruct(iterate.shape, jnp.bfloat16),
            jax.ShapeDtypeStruct(iterate.shape, jnp.float32),
            jax.ShapeDtypeStruct(rim_shape, jnp.float32),
            jax.ShapeDtypeStruct(rim_shape, jnp.float32),
        ],
        compiler_params=params(),
        name="step",
    )(*rests, *misfits, iterate, coeff)


def finish_kernel(
    up_ref, rest_ref, down_ref, mup_ref, misfit_ref, mdown_ref, iter_ref, coeff_ref, *refs
):
    solution_ref, residual_ref = refs[-2:]

    def body(times):
        residual = residual_of(times, (up_ref, rest_ref, down_ref), (mup_ref, misfit_ref, mdown_ref))
        update = precondition(residual, coeff_ref)
        solution_ref[times] = jnp.swapaxes(iter_ref[0, :, times] + update[1:-1], 0, 1)
        residual_ref[times] = jnp.swapaxes(trim(residual, HALO), 0, 1)

    time_chunks(iter_ref.shape[2], body)


def finish(group, samples, rests, misfits, iterate, coeff, previous):
    members, rows, steps, cols = iterate.shape
    field = pl.BlockSpec((1, rows, steps, cols), lambda b: (b, 0, 0, 0))
    rim = pl.BlockSpec((1, HALO, steps, cols), lambda b: (b, 0, 0, 0))
    result = pl.BlockSpec((steps, rows, cols), lambda b: (0, b + group * members, 0))
    shape = jax.ShapeDtypeStruct((steps, samples * rows, cols), jnp.float32)
    first = 8
    return pl.pallas_call(
        finish_kernel,
        grid=(members,),
        in_specs=[rim, field, rim] * 2
        + [field, whole_block(coeff)]
        + [pl.BlockSpec(memory_space=pl.ANY)] * len(previous),
        out_specs=[result, result],
        out_shape=[shape, shape],
        input_output_aliases={first + k: k for k in range(len(previous))},
        compiler_params=params(),
        name="finish",
    )(*rests, *misfits, iterate, coeff, *previous)


def same_frequency(near, sensors):
    shape = (near, LANES)
    return lax.broadcasted_iota(jnp.int32, shape, 0) == (
        lax.broadcasted_iota(jnp.int32, shape, 1) // sensors
    )


def marks_of(cell_ref, width):
    first = pl.program_id(0) * width
    parts = []
    for start_lane in range(0, width, LANES):
        lane = lax.broadcasted_iota(jnp.int32, cell_ref.shape, 1) + (first + start_lane)
        parts.append(jnp.where(cell_ref[...] == lane, 1.0, 0.0).astype(jnp.bfloat16))
    return jnp.concatenate(parts, axis=1)


def observe_kernel(field_ref, map_ref, table_ref, cell_ref, real_ref, imag_ref, spec, acc, picked):
    devices, members, rows, steps, lanes = field_ref.shape
    freqs, sensors, width = map_ref.shape[1:]
    near = lanes // sensors
    chunk = pl.program_id(0)

    @pl.when(chunk == 0)
    def _():
        acc[...] = jnp.zeros_like(acc)
        picked[...] = jnp.zeros_like(picked)

    marks = marks_of(cell_ref, width)
    for b in range(members):
        history = jnp.concatenate(
            [field_ref[:, b, r].reshape(devices * steps, lanes) for r in range(rows)], axis=1
        )
        spectrum = dot(table_ref[...], history)
        spec[2 * b] = spectrum[:freqs]
        spec[2 * b + 1] = spectrum[freqs:]
    for m in range(2 * members):
        picked[m] += dot_lanes(spec[m].astype(jnp.bfloat16), marks)
    for q in range(freqs // near):
        here = slice(q * near, (q + 1) * near)
        left = spec[:, here].reshape(2 * members * near, width).astype(jnp.bfloat16)
        acc[q] += dot_lanes(left, map_ref[:, here].reshape(2 * near * sensors, width))

    @pl.when(chunk == pl.num_programs(0) - 1)
    def _():
        mask = same_frequency(near, sensors)
        for q in range(freqs // near):
            here = slice(q * near, (q + 1) * near)
            for b in range(members):
                real = acc[q, 2 * b * near : (2 * b + 1) * near]
                imag = acc[q, (2 * b + 1) * near : (2 * b + 2) * near]
                obs_real = real[:, :lanes] - imag[:, lanes:] + picked[2 * b, here]
                obs_imag = imag[:, :lanes] + real[:, lanes:] + picked[2 * b + 1, here]
                real_ref[b, q : q + 1] = jnp.sum(jnp.where(mask, obs_real, 0.0), 0, keepdims=True)
                imag_ref[b, q : q + 1] = jnp.sum(jnp.where(mask, obs_imag, 0.0), 0, keepdims=True)


def map_spec(forward_map, width):
    return pl.BlockSpec(forward_map.shape[:3] + (width,), lambda c: (0, 0, 0, c))


def observe(field, forward_map, table, local_cells):
    devices, members, rows, steps, lanes = field.shape
    _, freqs, sensors, cells = forward_map.shape
    width = CHUNK_ROWS * lanes
    near = lanes // sensors
    shape = (members, freqs // near, lanes)
    return pl.pallas_call(
        observe_kernel,
        grid=(rows // CHUNK_ROWS,),
        in_specs=[
            pl.BlockSpec((devices, members, CHUNK_ROWS, steps, lanes), lambda c: (0, 0, c, 0, 0)),
            map_spec(forward_map, width),
            whole_block(table),
            whole_block(local_cells),
        ],
        out_specs=[pl.BlockSpec(shape, lambda c: (0, 0, 0))] * 2,
        out_shape=[jax.ShapeDtypeStruct(shape, jnp.float32)] * 2,
        scratch_shapes=[
            pltpu.VMEM((2 * members, freqs, width), jnp.float32),
            pltpu.VMEM((freqs // near, 2 * members * near, 2 * lanes), jnp.float32),
            pltpu.VMEM((2 * members, freqs, lanes), jnp.float32),
        ],
        compiler_params=params(),
        cost_estimate=pl.CostEstimate(
            flops=8 * members * freqs * sensors * cells,
            bytes_accessed=2 * forward_map.size + 2 * field.size,
            transcendentals=0,
        ),
        name="observe",
    )(field, forward_map, table, local_cells)


def pull_kernel(*refs):
    reals, imags = refs[: len(refs) // 2 - 3], refs[len(refs) // 2 - 3 : -7]
    noise_ref, map_ref, back_ref, cell_ref, out_ref, weights, adjoint = refs[-7:]
    devices, members, rows, steps, lanes = out_ref.shape
    freqs, sensors, width = map_ref.shape[1:]
    near = lanes // sensors

    def total(parts, b):
        values = [part[b] for part in parts]
        while len(values) > 1:
            values = [values[k] + values[k + 1] for k in range(0, len(values), 2)]
        return (noise_ref[...] * values[0]).astype(jnp.bfloat16).astype(jnp.float32)

    @pl.when(pl.program_id(0) == 0)
    def _():
        mask = same_frequency(near, sensors)
        for b in range(members):
            real, imag = total(reals, b), total(imags, b)
            for q in range(freqs // near):
                here = slice(q * near, (q + 1) * near)
                w_real = jnp.where(mask, real[q : q + 1], 0.0)
                w_imag = jnp.where(mask, imag[q : q + 1], 0.0)
                weights[2 * b, here, :lanes] = w_real
                weights[2 * b, here, lanes:] = w_imag
                weights[2 * b + 1, here, :lanes] = w_imag
                weights[2 * b + 1, here, lanes:] = -w_real

    marks = marks_of(cell_ref, width)
    for m in range(2 * members):
        adjoint[m] = dot(weights[m, :, :lanes].astype(jnp.bfloat16), marks)
    for q in range(freqs // near):
        here = slice(q * near, (q + 1) * near)
        left = weights[:, here].reshape(2 * members * near, 2 * lanes).astype(jnp.bfloat16)
        part = dot(left, map_ref[:, here].reshape(2 * near * sensors, width))
        adjoint[:, here] += part.reshape(2 * members, near, width)
    for b in range(members):
        whole = adjoint[2 * b : 2 * b + 2].reshape(2 * freqs, width)
        high = whole.astype(jnp.bfloat16)
        low = (whole - high.astype(jnp.float32)).astype(jnp.bfloat16)
        misfit = (dot(back_ref[...], high) + dot(back_ref[...], low)).astype(out_ref.dtype)
        for r in range(rows):
            part = misfit[:, r * lanes : (r + 1) * lanes]
            out_ref[:, b, r] = part.reshape(devices, steps, lanes)


def pull_back(reals, imags, noise, forward_map, back, local_cells, shape):
    devices, members, rows, steps, lanes = shape
    _, freqs, sensors, cells = forward_map.shape
    width = CHUNK_ROWS * lanes
    small = [*reals, *imags, noise]
    return pl.pallas_call(
        pull_kernel,
        grid=(rows // CHUNK_ROWS,),
        in_specs=[whole_block(array) for array in small]
        + [map_spec(forward_map, width), whole_block(back), whole_block(local_cells)],
        out_specs=pl.BlockSpec(
            (devices, members, CHUNK_ROWS, steps, lanes), lambda c: (0, 0, c, 0, 0)
        ),
        out_shape=jax.ShapeDtypeStruct(shape, jnp.bfloat16),
        scratch_shapes=[
            pltpu.VMEM((2 * members, freqs, 2 * lanes), jnp.float32),
            pltpu.VMEM((2 * members, freqs, width), jnp.float32),
        ],
        compiler_params=params(),
        cost_estimate=pl.CostEstimate(
            flops=8 * members * freqs * sensors * cells,
            bytes_accessed=2 * forward_map.size + 2 * math.prod(shape),
            transcendentals=0,
        ),
        name="pull_back",
    )(*small, forward_map, back, local_cells)


def rims(top, bottom):
    size = lax.axis_size("cells")
    onward = [(k, k + 1) for k in range(size - 1)]
    backward = [(k + 1, k) for k in range(size - 1)]
    return lax.ppermute(bottom, "cells", onward), lax.ppermute(top, "cells", backward)


def from_all_cells(value):
    size = lax.axis_size("cells")
    if size & (size - 1):
        return [lax.psum(value, "cells")]
    return [value] + [
        lax.ppermute(value, "cells", [(k, k ^ other) for k in range(size)])
        for other in range(1, size)
    ]


def shards(rhs, forward_map, stiffness, reaction, noise_weight, sensor_cell):
    steps, samples, rows, cols = rhs.shape
    _, freqs, sensors, cells = forward_map.shape
    times_over = lax.axis_size("sensors")
    table = transform_table(freqs, 2 * freqs)
    back = table.T
    near = LANES // sensors

    diagonal = reaction + 4.0 * stiffness * stiffness
    local = jnp.stack([stiffness, diagonal])
    up, down = rims(local[:, :HALO], local[:, rows - HALO :])
    stiff, diag = jnp.concatenate([up, local, down], axis=1)
    inside = diag > 0.0
    inverse = jnp.where(inside, 1.0 / jnp.where(inside, diag, 1.0), 0.0)
    unscale = jnp.where(inside, 1.0 / jnp.where(inside, stiff, 1.0), 0.0)
    scaled = DAMPING * inverse * stiff
    coeff = jnp.stack([scaled, scaled * stiff, unscale, stiff, diag])
    coeff = jnp.broadcast_to(coeff[:, :, None, :], coeff.shape[:2] + (SUBLANES, cols))

    cell_index = lax.axis_index("cells")
    sensor_index = lax.axis_index("sensors")
    local_cells = lax.dynamic_slice_in_dim(sensor_cell, sensor_index * sensors, sensors)
    local_cells = jnp.tile(local_cells - cell_index * cells, near)[:, None]
    local_cells = jnp.broadcast_to(local_cells, (LANES, LANES))
    noise = lax.dynamic_slice_in_dim(noise_weight, sensor_index * sensors, sensors)
    noise = jnp.tile(noise, near)[None, :]

    up, down = rims(
        jnp.transpose(rhs[:, :, :HALO], (1, 2, 0, 3)),
        jnp.transpose(rhs[:, :, rows - HALO :], (1, 2, 0, 3)),
    )
    members = samples // GROUPS
    states = []
    for group in range(GROUPS):
        states.append(start(group, members, rhs, up, down, coeff))

    outputs = ()
    for iteration in range(ITERS):
        for group in range(GROUPS):
            iterate, low, rest, top, bottom = states[group]
            above, below = rims(top, bottom)
            field = lax.all_gather(low, "sensors", axis=0, tiled=False)
            real, imag = observe(field, forward_map, table, local_cells)
            misfit = pull_back(
                from_all_cells(real),
                from_all_cells(imag),
                noise,
                forward_map,
                back,
                local_cells,
                (times_over, members, rows, steps, cols),
            )
            misfit = lax.psum_scatter(misfit, "sensors", scatter_dimension=0, tiled=False)
            m_above, m_below = rims(misfit[:, :HALO], misfit[:, rows - HALO :])
            rests, misfits = (above, rest, below), (m_above, misfit, m_below)
            if iteration < ITERS - 1:
                states[group] = step(rests, misfits, iterate, coeff)
            else:
                outputs = finish(group, samples, rests, misfits, iterate, coeff, outputs)
    return tuple(out.reshape(rhs.shape) for out in outputs)


def solution(mesh):
    placed = (
        P("sensors", None, "cells", None),
        P(None, None, "sensors", "cells"),
        P("cells", None),
        P("cells", None),
        P(),
        P(),
    )
    return jax.shard_map(
        shards,
        mesh=mesh,
        in_specs=placed,
        out_specs=(P("sensors", None, "cells", None), P("sensors", None, "cells", None)),
        check_vma=False,
    )
```

time: 1410 us -> 623 us (0.44)
  waiting for transfers between devices: 819 us -> 291 us
  matrix products: 401 us -> 0 us
  Pallas kernels: 0 us -> 184 us
  other arithmetic: 78.5 us -> 2.36 us
  starting transfers between devices: 28.8 us -> 71.8 us
    dot_general x28 -> x0, matrix products: 401 us -> none  [the longest x4 114 us: place_cells(): jnp.einsum('fbs,cs->fbc', values, sensor_marks, preferred_element_type=jn...]
    reduce_scatter x2 -> x4, waiting for transfers between devices: 470 us -> 129 us  [shards(): lax.psum_scatter(misfit, 'sensors', scatter_dimension=0, tiled=False)]
    pallas_call x0 -> x14, Pallas kernels: none -> 184 us  [the longest x4 75.4 us: observe(): pl.pallas_call(observe_kernel, grid=(rows // CHUNK_ROWS,), in_specs=[pl.B...]
    all_gather x2 -> x4, waiting for transfers between devices: 237 us -> 130 us  [shards(): field = lax.all_gather(low, 'sensors', axis=0, tiled=False)]
    psum x2 -> x0, waiting for transfers between devices: 78.3 us -> none  [shards(): observed = lax.psum(observe(forward_map, spectrum, sensor_marks), 'cells')]
    ppermute x12 -> x44, starting transfers between devices: 28 us -> 71.3 us  [the longest x10 36.9 us: rims(): lax.ppermute(bottom, 'cells', onward)]
    unnamed x102 -> x78, local copies, waits for them, and re-layouts: 16 us -> 46.1 us
    mul x11 -> x1, other arithmetic: 25.7 us -> 0.02 us  [shards(): coeff = jnp.stack([scaled, scaled * stiff, unscale, stiff, diag])]
  transfers between devices with their start and end apart: 18 -> 52, of which waited for: 13 -> 28; matrix products, arithmetic and copies ran while one was open for 1% -> 1% of each run, Pallas kernels for 0% -> 28%
where the time goes in v1:
time: 623 us; the launch traced here: 617 us
  waiting for transfers between devices  291 us (47%)
  Pallas kernels  184 us (30%)
  starting transfers between devices  71.8 us (12%)
  local copies, waits for them, and re-layouts  52.6 us (8%)
  between operations  14.7 us (2%)
    all_gather x4, waiting for transfers between devices, shards(): field = lax.all_gather(low, 'sensors', axis=0, tiled=False)  130 us
    reduce_scatter x4, waiting for transfers between devices, shards(): lax.psum_scatter(misfit, 'sensors', scatter_dimension=0, tiled=False)  129 us
    pallas_call x4, Pallas kernels, observe(): pl.pallas_call(observe_kernel, grid=(rows // CHUNK_ROWS,), in_specs=[pl.B...  75.4 us
    pallas_call x4, Pallas kernels, pull_back(): pl.pallas_call(pull_kernel, grid=(rows // CHUNK_ROWS,), in_specs=[whole_b...  70.5 us
    unnamed x78, local copies, waits for them, and re-layouts  46.1 us
    ppermute x10, starting transfers between devices, rims(): lax.ppermute(bottom, 'cells', onward)  36.9 us
    ppermute x24, starting transfers between devices, from_all_cells(): lax.ppermute(value, 'cells', [(k, k ^ other) for k in range(size)])  21.5 us
    pallas_call x2, Pallas kernels, step(): pl.pallas_call(step_kernel, grid=(members,), in_specs=[rim, field, rim] *...  13.6 us
  transfers between devices with their start and end apart: 52, of which 28 were waited for; matrix products, arithmetic and copies ran while one was open for 1% of the time, Pallas kernels for 28%

profile of v1, /device:TPU:1, one launch (start us, length us, event | category | flops | bytes accessed | tf_op | source)
XLA Modules:
  0.0 617.2 jit_solution(6496769261178299388)
XLA Ops:
  8.9 3.9 collective-permute-start.2
  15.8 4.0 collective-permute-start
  21.3 5.6 collective-permute-done.up_ref
  26.9 11.3 %collective-permute-done.1.down_ref = f32[6,4,32,128]{3,2,1,0:T(8,128)S(1)} collective-permute-done((f32[6,4,32,128]{3,2,1,0:T(8,128)S(1)}, f32[6,4,32,128]{3,2,1,0:T(8,128)S(1)}, u32[]{:S(2)}, u32[]{:S(2)}) %collective-permute-start.1) | collective-permute-done | bytes 393248 | tf_op jit(solution)/shard_map/ppermute | solution.py:389
  38.2 6.9 %start.3 = (f32[3,32,32,128]{3,2,1,0:T(8,128)S(1)}, bf16[3,32,32,128]{3,2,1,0:T(8,128)(2,1)}, f32[3,32,32,128]{3,2,1,0:T(8,128)S(1)}, f32[3,4,32,128]{3,2,1,0:T(8,128)S(1)}, f32[3,4,32,128]{3,2,1,0:T(8,128)}) custom-call(f32[32,192,128]{2,1,0:T(8,128)S(1)} %bitcast.22, f32[6,4,32,128]{3,2,1,0:T(8,128)S(1)} %collective-permute-done.up_ref, ...), custom_call_target="tpu_custom_call" | custom-call | tf_op jit(solution)/shard_map/start/pallas_call | solution.py:114
  50.1 6.1 start.2
  59.9 54.4 %all-gather.13.cloned.1.call-done = bf16[24,32,32,128]{3,2,1,0:T(8,128)(2,1)} async-done(((bf16[3,32,32,128]{3,2,1,0:T(8,128)(2,1)}), bf16[24,32,32,128]{3,2,1,0:T(8,128)(2,1)}) %all-gather.13.cloned.1.call-update) | async-done | bytes 6291472 | tf_op jit(solution)/shard_map/all_gather | solution.py:443
  117.2 18.9 %observe.6 = (f32[3,16,128]{2,1,0:T(8,128)S(1)}, f32[3,16,128]{2,1,0:T(8,128)S(1)}) custom-call(bf16[8,3,32,32,128]{4,3,2,1,0:T(8,128)(2,1)S(1)} %bitcast.27, bf16[2,128,16,4096]{3,2,1,0:T(8,128)(2,1)} %refs_9_.7, bf16[256,256]{1,0:T(8,128)(2,1)S(1)} %copy.18.table_ref, s32[128,128]{1,0:T(8,128)S(1)} %broadcast_in_dim.22.cell_ref.refs_11_), custom_call_target="tpu_custom_call" | custom-call | flops 201326592 | bytes 39845888 | tf_op jit(solution)/shard_map/observe/pallas_call | solution.py:286
  144.7 17.6 %pull_back.6 = bf16[8,3,32,32,128]{4,3,2,1,0:T(8,128)(2,1)S(1)} custom-call(f32[3,16,128]{2,1,0:T(8,128)S(1)} %get-tuple-element.52.refs_0_, f32[3,16,128]{2,1,0:T(8,128)S(1)} %collective-permute-done.26.refs_1_, f32[3,16,128]{2,1,0:T(8,128)S(1)} %collective-permute-done.27.refs_2_, f32[3,16,128]{2,1,0:T(8,128)S(1)} %collective-permute-done.28.refs_3_, ...), custom_call_target="tpu_custom_call" | custom-call | flops 201326592 | bytes 39845888 | tf_op jit(solution)/shard_map/pull_back/pallas_call | solution.py:362
  165.1 14.4 %all-gather.9.cloned.1.call-done = bf16[24,32,32,128]{3,2,1,0:T(8,128)(2,1)} async-done(((bf16[3,32,32,128]{3,2,1,0:T(8,128)(2,1)}), bf16[24,32,32,128]{3,2,1,0:T(8,128)(2,1)}) %all-gather.9.cloned.1.call-update) | async-done | bytes 6291472 | tf_op jit(solution)/shard_map/all_gather | solution.py:443
  182.2 18.7 %observe.4 = (f32[3,16,128]{2,1,0:T(8,128)S(1)}, f32[3,16,128]{2,1,0:T(8,128)S(1)}) custom-call(bf16[8,3,32,32,128]{4,3,2,1,0:T(8,128)(2,1)S(1)} %bitcast.24, bf16[2,128,16,4096]{3,2,1,0:T(8,128)(2,1)} %refs_9_.7, bf16[256,256]{1,0:T(8,128)(2,1)S(1)} %copy.18.table_ref, s32[128,128]{1,0:T(8,128)S(1)} %broadcast_in_dim.22.cell_ref.refs_11_), custom_call_target="tpu_custom_call" | custom-call | flops 201326592 | bytes 39845888 | tf_op jit(solution)/shard_map/observe/pallas_call | solution.py:286
  209.3 17.6 %pull_back.4 = bf16[8,3,32,32,128]{4,3,2,1,0:T(8,128)(2,1)S(1)} custom-call(f32[3,16,128]{2,1,0:T(8,128)S(1)} %get-tuple-element.38.refs_0_, f32[3,16,128]{2,1,0:T(8,128)S(1)} %collective-permute-done.6.refs_1_, f32[3,16,128]{2,1,0:T(8,128)S(1)} %collective-permute-done.7.refs_2_, f32[3,16,128]{2,1,0:T(8,128)S(1)} %collective-permute-done.8.refs_3_, ...), custom_call_target="tpu_custom_call" | custom-call | flops 201326592 | bytes 39845888 | tf_op jit(solution)/shard_map/pull_back/pallas_call | solution.py:362
  232.9 14.9 %reduce-scatter.9.cloned.1.call-done = bf16[1,3,32,32,128]{4,3,2,1,0:T(8,128)(2,1)} async-done(((bf16[8,3,32,32,128]{4,3,2,1,0:T(8,128)(2,1)}), bf16[1,3,32,32,128]{4,3,2,1,0:T(8,128)(2,1)}) %reduce-scatter.9.cloned.1.call-update) | async-done | bytes 786448 | tf_op jit(solution)/shard_map/reduce_scatter | solution.py:454
  250.0 4.0 collective-permute-start.32
  259.9 6.8 %step.3 = (f32[3,32,32,128]{3,2,1,0:T(8,128)S(1)}, bf16[3,32,32,128]{3,2,1,0:T(8,128)(2,1)S(1)}, f32[3,32,32,128]{3,2,1,0:T(8,128)S(1)}, f32[3,4,32,128]{3,2,1,0:T(8,128)}, f32[3,4,32,128]{3,2,1,0:T(8,128)S(1)}) custom-call(f32[3,4,32,128]{3,2,1,0:T(8,128)S(1)} %collective-permute-done.24.up_ref, f32[3,32,32,128]{3,2,1,0:T(8,128)S(1)} %copy-done.19, ...), custom_call_target="tpu_custom_call" | custom-call | tf_op jit(solution)/shard_map/step/pallas_call | solution.py:168
  270.7 4.1 collective-permute-start.4
  276.1 41.9 %reduce-scatter.5.cloned.1.call-done = bf16[1,3,32,32,128]{4,3,2,1,0:T(8,128)(2,1)} async-done(((bf16[8,3,32,32,128]{4,3,2,1,0:T(8,128)(2,1)}), bf16[1,3,32,32,128]{4,3,2,1,0:T(8,128)(2,1)}) %reduce-scatter.5.cloned.1.call-update) | async-done | bytes 786448 | tf_op jit(solution)/shard_map/reduce_scatter | solution.py:454
  320.3 4.0 collective-permute-start.12
  328.7 6.8 %step.2 = (f32[3,32,32,128]{3,2,1,0:T(8,128)S(1)}, bf16[3,32,32,128]{3,2,1,0:T(8,128)(2,1)S(1)}, f32[3,32,32,128]{3,2,1,0:T(8,128)S(1)}, f32[3,4,32,128]{3,2,1,0:T(8,128)}, f32[3,4,32,128]{3,2,1,0:T(8,128)}) custom-call(f32[3,4,32,128]{3,2,1,0:T(8,128)S(1)} %collective-permute-done.4.up_ref, f32[3,32,32,128]{3,2,1,0:T(8,128)S(1)} %copy-done.11, ...), custom_call_target="tpu_custom_call" | custom-call | tf_op jit(solution)/shard_map/step/pallas_call | solution.py:168
  339.0 46.3 %all-gather.15.cloned.1.call-done = bf16[24,32,32,128]{3,2,1,0:T(8,128)(2,1)} async-done(((bf16[3,32,32,128]{3,2,1,0:T(8,128)(2,1)}), bf16[24,32,32,128]{3,2,1,0:T(8,128)(2,1)}) %all-gather.15.cloned.1.call-update) | async-done | bytes 6291472 | tf_op jit(solution)/shard_map/all_gather | solution.py:443
  388.1 19.1 %observe.7 = (f32[3,16,128]{2,1,0:T(8,128)S(1)}, f32[3,16,128]{2,1,0:T(8,128)S(1)}) custom-call(bf16[8,3,32,32,128]{4,3,2,1,0:T(8,128)(2,1)S(1)} %bitcast.26, bf16[2,128,16,4096]{3,2,1,0:T(8,128)(2,1)} %refs_9_.7, bf16[256,256]{1,0:T(8,128)(2,1)S(1)} %copy.18.table_ref, s32[128,128]{1,0:T(8,128)S(1)} %broadcast_in_dim.22.cell_ref.refs_11_), custom_call_target="tpu_custom_call" | custom-call | flops 201326592 | bytes 39845888 | tf_op jit(solution)/shard_map/observe/pallas_call | solution.py:286
  415.5 17.6 %pull_back.7 = bf16[8,3,32,32,128]{4,3,2,1,0:T(8,128)(2,1)S(1)} custom-call(f32[3,16,128]{2,1,0:T(8,128)S(1)} %get-tuple-element.59.refs_0_, f32[3,16,128]{2,1,0:T(8,128)S(1)} %collective-permute-done.36.refs_1_, f32[3,16,128]{2,1,0:T(8,128)S(1)} %collective-permute-done.37.refs_2_, f32[3,16,128]{2,1,0:T(8,128)S(1)} %collective-permute-done.38.refs_3_, ...), custom_call_target="tpu_custom_call" | custom-call | flops 201326592 | bytes 39845888 | tf_op jit(solution)/shard_map/pull_back/pallas_call | solution.py:362
  435.8 14.9 %all-gather.11.cloned.1.call-done = bf16[24,32,32,128]{3,2,1,0:T(8,128)(2,1)} async-done(((bf16[3,32,32,128]{3,2,1,0:T(8,128)(2,1)}), bf16[24,32,32,128]{3,2,1,0:T(8,128)(2,1)}) %all-gather.11.cloned.1.call-update) | async-done | bytes 6291472 | tf_op jit(solution)/shard_map/all_gather | solution.py:443
  453.6 18.7 %observe.5 = (f32[3,16,128]{2,1,0:T(8,128)S(1)}, f32[3,16,128]{2,1,0:T(8,128)S(1)}) custom-call(bf16[8,3,32,32,128]{4,3,2,1,0:T(8,128)(2,1)S(1)} %bitcast.25, bf16[2,128,16,4096]{3,2,1,0:T(8,128)(2,1)} %refs_9_.7, bf16[256,256]{1,0:T(8,128)(2,1)S(1)} %copy.18.table_ref, s32[128,128]{1,0:T(8,128)S(1)} %broadcast_in_dim.22.cell_ref.refs_11_), custom_call_target="tpu_custom_call" | custom-call | flops 201326592 | bytes 39845888 | tf_op jit(solution)/shard_map/observe/pallas_call | solution.py:286
  480.6 17.6 %pull_back.5 = bf16[8,3,32,32,128]{4,3,2,1,0:T(8,128)(2,1)S(1)} custom-call(f32[3,16,128]{2,1,0:T(8,128)S(1)} %get-tuple-element.45.refs_0_, f32[3,16,128]{2,1,0:T(8,128)S(1)} %collective-permute-done.16.refs_1_, f32[3,16,128]{2,1,0:T(8,128)S(1)} %collective-permute-done.17.refs_2_, f32[3,16,128]{2,1,0:T(8,128)S(1)} %collective-permute-done.18.refs_3_, ...), custom_call_target="tpu_custom_call" | custom-call | flops 201326592 | bytes 39845888 | tf_op jit(solution)/shard_map/pull_back/pallas_call | solution.py:362
  504.5 4.6 collective-permute-start.34
  510.4 8.7 %reduce-scatter.11.cloned.1.call-done = bf16[1,3,32,32,128]{4,3,2,1,0:T(8,128)(2,1)} async-done(((bf16[8,3,32,32,128]{4,3,2,1,0:T(8,128)(2,1)}), bf16[1,3,32,32,128]{4,3,2,1,0:T(8,128)(2,1)}) %reduce-scatter.11.cloned.1.call-update) | async-done | bytes 786448 | tf_op jit(solution)/shard_map/reduce_scatter | solution.py:454
  522.0 4.0 collective-permute-start.42
  526.0 63.5 %reduce-scatter.7.cloned.1.call-done = bf16[1,3,32,32,128]{4,3,2,1,0:T(8,128)(2,1)} async-done(((bf16[8,3,32,32,128]{4,3,2,1,0:T(8,128)(2,1)}), bf16[1,3,32,32,128]{4,3,2,1,0:T(8,128)(2,1)}) %reduce-scatter.7.cloned.1.call-update) | async-done | bytes 786448 | tf_op jit(solution)/shard_map/reduce_scatter | solution.py:454
  591.8 4.0 collective-permute-start.22
  598.4 5.9 finish.2
  604.4 5.9 finish.3
  (193 shorter events, 109.3 us)
Async XLA Ops:
  7.2 107.2 %all-gather.13.cloned.1.call-start = ((), (), s32[]{:S(2)}) async-start(), calls=%async_computation.10 | async-start | bytes 7077888 | tf_op jit(solution)/shard_map/all_gather | solution.py:443
  8.9 12.3 %collective-permute-start.2 = (f32[2,4,128]{2,1,0:T(4,128)S(1)}, f32[2,4,128]{2,1,0:T(4,128)S(1)}, u32[]{:S(2)}, u32[]{:S(2)}) collective-permute-start(f32[2,4,128]{2,1,0:T(4,128)S(1)} %get-tuple-element.81), channel_id=1, source_target_pairs={{0,8},{8,16},{16,24},{1,9},{9,17},{17,25},{2,10},{10,18},{18,26},{... | collective-permute-start | bytes 12296 | tf_op jit(solution)/shard_map/ppermute | solution.py:389
  12.8 8.3 %collective-permute-start.3 = (f32[2,4,128]{2,1,0:T(4,128)S(1)}, f32[2,4,128]{2,1,0:T(4,128)S(1)}, u32[]{:S(2)}, u32[]{:S(2)}) collective-permute-start(f32[2,4,128]{2,1,0:T(4,128)S(1)} %get-tuple-element.82), channel_id=1, source_target_pairs={{8,0},{16,8},{24,16},{9,1},{17,9},{25,17},{10,2},{18,10},{26,18},{... | collective-permute-start | bytes 12296 | tf_op jit(solution)/shard_map/ppermute | solution.py:389
  15.8 11.1 %collective-permute-start = (f32[6,4,32,128]{3,2,1,0:T(8,128)S(1)}, f32[6,4,32,128]{3,2,1,0:T(8,128)S(1)}, u32[]{:S(2)}, u32[]{:S(2)}) collective-permute-start(f32[6,4,32,128]{3,2,1,0:T(8,128)S(1)} %bitcast.38), channel_id=1, source_target_pairs={{0,8},{8,16},{16,24},{1,9},{9,17},{17,25},{2,10},{10,18},{18,26},{... | collective-permute-start | bytes 1179656 | tf_op jit(solution)/shard_map/ppermute | solution.py:389
  19.9 18.3 %collective-permute-start.1 = (f32[6,4,32,128]{3,2,1,0:T(8,128)S(1)}, f32[6,4,32,128]{3,2,1,0:T(8,128)S(1)}, u32[]{:S(2)}, u32[]{:S(2)}) collective-permute-start(f32[6,4,32,128]{3,2,1,0:T(8,128)S(1)} %bitcast.39), channel_id=1, source_target_pairs={{8,0},{16,8},{24,16},{9,1},{17,9},{25,17},{10,2},{18,10},{26,18},{... | collective-permute-start | bytes 1179656 | tf_op jit(solution)/shard_map/ppermute | solution.py:389
  48.2 131.3 %all-gather.9.cloned.1.call-start = ((), (), s32[]{:S(2)}) async-start(), calls=%async_computation.8 | async-start | bytes 7077888 | tf_op jit(solution)/shard_map/all_gather | solution.py:443
  59.0 188.8 %reduce-scatter.9.cloned.1.call-start = ((), (), s32[]{:S(2)}) async-start(), calls=%async_computation.6 | async-start | bytes 7077888 | tf_op jit(solution)/shard_map/reduce_scatter | solution.py:454
  136.2 5.2 collective-permute-start.28
  165.0 153.1 %reduce-scatter.5.cloned.1.call-start = ((), (), s32[]{:S(2)}) async-start(), calls=%async_computation.4 | async-start | bytes 7077888 | tf_op jit(solution)/shard_map/reduce_scatter | solution.py:454
  200.9 5.2 collective-permute-start.8
  229.5 155.8 %all-gather.15.cloned.1.call-start = ((), (), s32[]{:S(2)}) async-start(), calls=%async_computation.11 | async-start | bytes 7077888 | tf_op jit(solution)/shard_map/all_gather | solution.py:443
  229.5 24.5 %collective-permute-start.24 = (f32[3,4,32,128]{3,2,1,0:T(8,128)}, f32[3,4,32,128]{3,2,1,0:T(8,128)S(1)}, u32[]{:S(2)}, u32[]{:S(2)}) collective-permute-start(f32[3,4,32,128]{3,2,1,0:T(8,128)} %get-tuple-element.48), channel_id=1, source_target_pairs={{0,8},{8,16},{16,24},{1,9},{9,17},{17,25},{2,10},{10,18},{18,26},{... | collective-permute-start | bytes 589832 | tf_op jit(solution)/shard_map/ppermute | solution.py:389
  231.6 22.5 %collective-permute-start.25 = (f32[3,4,32,128]{3,2,1,0:T(8,128)}, f32[3,4,32,128]{3,2,1,0:T(8,128)S(1)}, u32[]{:S(2)}, u32[]{:S(2)}) collective-permute-start(f32[3,4,32,128]{3,2,1,0:T(8,128)} %copy-done.34), channel_id=1, source_target_pairs={{8,0},{16,8},{24,16},{9,1},{17,9},{25,17},{10,2},{18,10},{26,18},{... | collective-permute-start | bytes 589832 | tf_op jit(solution)/shard_map/ppermute | solution.py:389
  248.7 5.4 collective-permute-start.33
  250.0 5.6 collective-permute-start.32
  270.6 180.1 %all-gather.11.cloned.1.call-start = ((), (), s32[]{:S(2)}) async-start(), calls=%async_computation.9 | async-start | bytes 7077888 | tf_op jit(solution)/shard_map/all_gather | solution.py:443
  270.7 53.6 %collective-permute-start.4 = (f32[3,4,32,128]{3,2,1,0:T(8,128)}, f32[3,4,32,128]{3,2,1,0:T(8,128)S(1)}, u32[]{:S(2)}, u32[]{:S(2)}) collective-permute-start(f32[3,4,32,128]{3,2,1,0:T(8,128)} %copy-done.31), channel_id=1, source_target_pairs={{0,8},{8,16},{16,24},{1,9},{9,17},{17,25},{2,10},{10,18},{18,26},{... | collective-permute-start | bytes 589832 | tf_op jit(solution)/shard_map/ppermute | solution.py:389
  274.8 49.5 %collective-permute-start.5 = (f32[3,4,32,128]{3,2,1,0:T(8,128)S(1)}, f32[3,4,32,128]{3,2,1,0:T(8,128)S(1)}, u32[]{:S(2)}, u32[]{:S(2)}) collective-permute-start(f32[3,4,32,128]{3,2,1,0:T(8,128)S(1)} %get-tuple-element.36), channel_id=1, source_target_pairs={{8,0},{16,8},{24,16},{9,1},{17,9},{25,17},{10,2},{18,10},{26,18},{... | collective-permute-start | bytes 589832 | tf_op jit(solution)/shard_map/ppermute | solution.py:389
  319.0 5.4 collective-permute-start.13
  320.3 5.6 collective-permute-start.12
  338.8 180.3 %reduce-scatter.11.cloned.1.call-start = ((), (), s32[]{:S(2)}) async-start(), calls=%async_computation.7 | async-start | bytes 7077888 | tf_op jit(solution)/shard_map/reduce_scatter | solution.py:454
  407.2 5.1 collective-permute-start.38
  435.8 153.8 %reduce-scatter.7.cloned.1.call-start = ((), (), s32[]{:S(2)}) async-start(), calls=%async_computation.5 | async-start | bytes 7077888 | tf_op jit(solution)/shard_map/reduce_scatter | solution.py:454
  472.2 5.2 collective-permute-start.18
  501.0 103.4 %collective-permute-start.14 = (f32[3,4,32,128]{3,2,1,0:T(8,128)}, f32[3,4,32,128]{3,2,1,0:T(8,128)S(1)}, u32[]{:S(2)}, u32[]{:S(2)}) collective-permute-start(f32[3,4,32,128]{3,2,1,0:T(8,128)} %get-tuple-element.41), channel_id=1, source_target_pairs={{0,8},{8,16},{16,24},{1,9},{9,17},{17,25},{2,10},{10,18},{18,26},{... | collective-permute-start | bytes 589832 | tf_op jit(solution)/shard_map/ppermute | solution.py:389
  503.1 101.2 %collective-permute-start.15 = (f32[3,4,32,128]{3,2,1,0:T(8,128)}, f32[3,4,32,128]{3,2,1,0:T(8,128)S(1)}, u32[]{:S(2)}, u32[]{:S(2)}) collective-permute-start(f32[3,4,32,128]{3,2,1,0:T(8,128)} %get-tuple-element.43), channel_id=1, source_target_pairs={{8,0},{16,8},{24,16},{9,1},{17,9},{25,17},{10,2},{18,10},{26,18},{... | collective-permute-start | bytes 589832 | tf_op jit(solution)/shard_map/ppermute | solution.py:389
  504.5 17.6 %collective-permute-start.34 = (f32[3,4,32,128]{3,2,1,0:T(8,128)S(1)}, f32[3,4,32,128]{3,2,1,0:T(8,128)S(1)}, u32[]{:S(2)}, u32[]{:S(2)}) collective-permute-start(f32[3,4,32,128]{3,2,1,0:T(8,128)S(1)} %copy-done.33), channel_id=1, source_target_pairs={{0,8},{8,16},{16,24},{1,9},{9,17},{17,25},{2,10},{10,18},{18,26},{... | collective-permute-start | bytes 589832 | tf_op jit(solution)/shard_map/ppermute | solution.py:389
  509.1 81.4 %collective-permute-start.35 = (f32[3,4,32,128]{3,2,1,0:T(8,128)}, f32[3,4,32,128]{3,2,1,0:T(8,128)S(1)}, u32[]{:S(2)}, u32[]{:S(2)}) collective-permute-start(f32[3,4,32,128]{3,2,1,0:T(8,128)} %get-tuple-element.57), channel_id=1, source_target_pairs={{8,0},{16,8},{24,16},{9,1},{17,9},{25,17},{10,2},{18,10},{26,18},{... | collective-permute-start | bytes 589832 | tf_op jit(solution)/shard_map/ppermute | solution.py:389
  520.7 71.1 %collective-permute-start.43 = (bf16[3,4,32,128]{3,2,1,0:T(8,128)(2,1)}, bf16[3,4,32,128]{3,2,1,0:T(8,128)(2,1)S(1)}, u32[]{:S(2)}, u32[]{:S(2)}) collective-permute-start(bf16[3,4,32,128]{3,2,1,0:T(8,128)(2,1)} %get-tuple-element.70), channel_id=1, source_target_pairs={{8,0},{16,8},{24,16},{9,1},{17,9},{25,17},{10,2},{18,10},{26,18},{... | collective-permute-start | bytes 294920 | tf_op jit(solution)/shard_map/ppermute | solution.py:389
  522.0 73.8 %collective-permute-start.42 = (bf16[3,4,32,128]{3,2,1,0:T(8,128)(2,1)}, bf16[3,4,32,128]{3,2,1,0:T(8,128)(2,1)S(1)}, u32[]{:S(2)}, u32[]{:S(2)}) collective-permute-start(bf16[3,4,32,128]{3,2,1,0:T(8,128)(2,1)} %get-tuple-element.71), channel_id=1, source_target_pairs={{0,8},{8,16},{16,24},{1,9},{9,17},{17,25},{2,10},{10,18},{18,26},{... | collective-permute-start | bytes 294920 | tf_op jit(solution)/shard_map/ppermute | solution.py:389
  590.5 13.8 %collective-permute-start.23 = (bf16[3,4,32,128]{3,2,1,0:T(8,128)(2,1)S(1)}, bf16[3,4,32,128]{3,2,1,0:T(8,128)(2,1)S(1)}, u32[]{:S(2)}, u32[]{:S(2)}) collective-permute-start(bf16[3,4,32,128]{3,2,1,0:T(8,128)(2,1)S(1)} %get-tuple-element.74), channel_id=1, source_target_pairs={{8,0},{16,8},{24,16},{9,1},{17,9},{25,17},{10,2},{18,10},{26,18},{... | collective-permute-start | bytes 294920 | tf_op jit(solution)/shard_map/ppermute | solution.py:389
  591.8 12.5 %collective-permute-start.22 = (bf16[3,4,32,128]{3,2,1,0:T(8,128)(2,1)S(1)}, bf16[3,4,32,128]{3,2,1,0:T(8,128)(2,1)S(1)}, u32[]{:S(2)}, u32[]{:S(2)}) collective-permute-start(bf16[3,4,32,128]{3,2,1,0:T(8,128)(2,1)S(1)} %get-tuple-element.75), channel_id=1, source_target_pairs={{0,8},{8,16},{16,24},{1,9},{9,17},{17,25},{2,10},{10,18},{18,26},{... | collective-permute-start | bytes 294920 | tf_op jit(solution)/shard_map/ppermute | solution.py:389
  (58 other events, 309.0 us)
Sparse Core Ops, SparseCore 0:
  48.3 66.0 all-gather.12
  116.0 63.3 all-gather.8
  181.8 65.9 reduce-scatter.8
  249.9 68.0 reduce-scatter.4
  319.6 65.6 all-gather.14
  387.3 63.3 all-gather.10
  453.1 65.9 reduce-scatter.10
  521.4 68.0 reduce-scatter.6

commit v2 on v1

v2 whole, which is shorter than its diff:
```python
import math

import jax
import jax.numpy as jnp
from jax import lax
from jax.experimental import pallas as pl
from jax.experimental.pallas import tpu as pltpu
from jax.sharding import PartitionSpec as P

SWEEPS = 4
ITERS = 2
DAMPING = 0.8
HALO = SWEEPS
LANES = 128
SUBLANES = 8
GROUPS = 3
CHUNK_ROWS = 4
VMEM_BYTES = 40 * 2**20


def transform_table(freqs, moments):
    period = moments.size
    wave = jnp.arange(freqs, dtype=jnp.int32)[:, None]
    moment = moments.reshape(1, period)
    phase = (wave * moment % period).astype(jnp.float32) * (2.0 * math.pi / period)
    factor = 1.0 / math.sqrt(period)
    return jnp.concatenate([jnp.cos(phase) * factor, -jnp.sin(phase) * factor], axis=0).astype(
        jnp.bfloat16
    )


def whole_block(array):
    return pl.BlockSpec(array.shape, lambda *_: (0,) * array.ndim)


def call(kernel, core, grid, in_specs, out_specs, out_shape, scratch=(), aliases=None, **kwargs):
    grid_spec = pltpu.PrefetchScalarGridSpec(
        num_scalar_prefetch=1,
        grid=grid,
        in_specs=in_specs,
        out_specs=out_specs,
        scratch_shapes=list(scratch),
    )
    return pl.pallas_call(
        kernel,
        grid_spec=grid_spec,
        out_shape=out_shape,
        input_output_aliases=aliases or {},
        compiler_params=pltpu.CompilerParams(vmem_limit_bytes=VMEM_BYTES),
        **kwargs,
    )


def dot(left, right):
    return jnp.dot(left, right, preferred_element_type=jnp.float32)


def dot_lanes(left, right):
    return lax.dot_general(left, right, (((1,), (1,)), ((), ())), preferred_element_type=jnp.float32)


def neighbours(field):
    inner = field[1:-1]
    lane = lax.broadcasted_iota(jnp.int32, inner.shape, 2)
    before = jnp.where(lane == 0, 0.0, pltpu.roll(inner, 1, 2))
    after = jnp.where(lane == LANES - 1, 0.0, pltpu.roll(inner, LANES - 1, 2))
    return (field[2:] + field[:-2]) + (before + after)


def trim(array, width):
    return array[width : array.shape[0] - width]


def precondition(residual, coeff_ref):
    extra = (coeff_ref.shape[1] - residual.shape[0]) // 2
    coeff = [trim(coeff_ref[k], extra) for k in range(3)]
    first = coeff[0] * residual
    scaled = first
    for sweep in range(1, SWEEPS):
        scaled = (
            (1.0 - DAMPING) * scaled[1:-1]
            + trim(first, sweep)
            + trim(coeff[1], sweep) * neighbours(scaled)
        )
    return trim(coeff[2], SWEEPS - 1) * scaled


def prior(field, coeff_ref):
    extra = (coeff_ref.shape[1] - field.shape[0]) // 2
    stiffness = trim(coeff_ref[3], extra)
    diagonal = trim(coeff_ref[4], extra + 1)
    return diagonal * field[1:-1] - stiffness[1:-1] * neighbours(stiffness * field)


def time_chunks(steps, body):
    def run(index, carry):
        body(pl.ds(pl.multiple_of(index * SUBLANES, SUBLANES), SUBLANES))
        return carry

    lax.fori_loop(0, steps // SUBLANES, run, 0)


def fields(members, rows, steps, cols):
    field = pl.BlockSpec((1, rows, steps, cols), lambda b, core: (b, 0, 0, 0))
    half = pl.BlockSpec((1, rows // 2, steps, cols), lambda b, core: (b, 0, 0, 0))
    rim = pl.BlockSpec((1, HALO, steps, cols), lambda b, core: (b, 0, 0, 0))

    def shape(count, dtype):
        return jax.ShapeDtypeStruct((members, count, steps, cols), dtype)

    specs = [field, half, half, field, rim, rim]
    shapes = [
        shape(rows, jnp.float32),
        shape(rows // 2, jnp.bfloat16),
        shape(rows // 2, jnp.bfloat16),
        shape(rows, jnp.float32),
        shape(HALO, jnp.bfloat16),
        shape(HALO, jnp.bfloat16),
    ]
    return field, half, rim, specs, shapes


def put_rest(rest, times, rest_ref, top_ref, bottom_ref):
    rest_ref[0, :, times] = rest
    top_ref[0, :, times] = rest[:HALO].astype(top_ref.dtype)
    bottom_ref[0, :, times] = rest[rest.shape[0] - HALO :].astype(bottom_ref.dtype)


def put_low(core, iter_ref, keep_ref, give_ref):
    half = keep_ref.shape[1]
    keep_ref[0] = iter_ref[0, pl.ds(core * half, half)].astype(keep_ref.dtype)
    give_ref[0] = iter_ref[0, pl.ds((1 - core) * half, half)].astype(give_ref.dtype)


def start_kernel(
    core_ref, rhs_ref, up_ref, down_ref, coeff_ref,
    iter_ref, keep_ref, give_ref, rest_ref, top_ref, bottom_ref,
):
    def body(times):
        here = jnp.swapaxes(rhs_ref[times], 0, 1)
        rims_here = [ref[0, :, times].astype(jnp.float32) for ref in (up_ref, down_ref)]
        update = precondition(jnp.concatenate([rims_here[0], here, rims_here[1]], axis=0), coeff_ref)
        iter_ref[0, :, times] = update[1:-1]
        put_rest(here - prior(update, coeff_ref), times, rest_ref, top_ref, bottom_ref)

    time_chunks(iter_ref.shape[2], body)
    put_low(core_ref[0], iter_ref, keep_ref, give_ref)


def start(group, members, core, rhs, up, down, coeff):
    steps, _, rows, cols = rhs.shape
    flat = rhs.reshape(steps, -1, cols)
    field, half, rim, specs, shapes = fields(members, rows, steps, cols)
    return call(
        start_kernel,
        core,
        (members,),
        [
            pl.BlockSpec((steps, rows, cols), lambda b, core: (0, b + group * members, 0)),
            rim,
            rim,
            whole_block(coeff),
        ],
        specs,
        shapes,
        name="start",
    )(core, flat, up, down, coeff)


def residual_of(core, times, rest_refs, misfit_refs, whole_ref):
    own_ref, other_ref, same_ref, cross_ref = misfit_refs
    half = own_ref.shape[1]
    whole_ref[pl.ds(core * half, half)] = own_ref[0, :, times].astype(jnp.float32)
    whole_ref[pl.ds((1 - core) * half, half)] = other_ref[0, :, times].astype(jnp.float32)
    same = same_ref[0, :, times].astype(jnp.float32)
    cross = cross_ref[0, :, times].astype(jnp.float32)
    first = core == 0
    parts = [jnp.where(first, cross, same), whole_ref[...], jnp.where(first, same, cross)]
    rests = [ref[0, :, times].astype(jnp.float32) for ref in rest_refs]
    return jnp.concatenate([rest - part for rest, part in zip(rests, parts)], axis=0)


def step_kernel(
    core_ref, up_ref, rest_ref, down_ref, own_ref, other_ref, same_ref, cross_ref, iter_ref, coeff_ref,
    next_ref, keep_ref, give_ref, later_ref, top_ref, bottom_ref, whole_ref,
):
    def body(times):
        residual = residual_of(
            core_ref[0],
            times,
            (up_ref, rest_ref, down_ref),
            (own_ref, other_ref, same_ref, cross_ref),
            whole_ref,
        )
        update = precondition(residual, coeff_ref)
        next_ref[0, :, times] = iter_ref[0, :, times] + update[1:-1]
        put_rest(rest_ref[0, :, times] - prior(update, coeff_ref), times, later_ref, top_ref, bottom_ref)

    time_chunks(iter_ref.shape[2], body)
    put_low(core_ref[0], next_ref, keep_ref, give_ref)


def step(core, rests, misfits, iterate, coeff):
    members, rows, steps, cols = iterate.shape
    field, half, rim, specs, shapes = fields(members, rows, steps, cols)
    return call(
        step_kernel,
        core,
        (members,),
        [rim, field, rim, half, half, rim, rim, field, whole_block(coeff)],
        specs,
        shapes,
        [pltpu.VMEM((rows, SUBLANES, cols), jnp.float32)],
        name="step",
    )(core, *rests, *misfits, iterate, coeff)


def finish_kernel(
    core_ref, up_ref, rest_ref, down_ref, own_ref, other_ref, same_ref, cross_ref, iter_ref, coeff_ref,
    *refs,
):
    solution_ref, residual_ref, whole_ref = refs[-3:]

    def body(times):
        residual = residual_of(
            core_ref[0],
            times,
            (up_ref, rest_ref, down_ref),
            (own_ref, other_ref, same_ref, cross_ref),
            whole_ref,
        )
        update = precondition(residual, coeff_ref)
        solution_ref[times] = jnp.swapaxes(iter_ref[0, :, times] + update[1:-1], 0, 1)
        residual_ref[times] = jnp.swapaxes(trim(residual, HALO), 0, 1)

    time_chunks(iter_ref.shape[2], body)


def finish(group, samples, core, rests, misfits, iterate, coeff, previous):
    members, rows, steps, cols = iterate.shape
    field, half, rim, _, _ = fields(members, rows, steps, cols)
    result = pl.BlockSpec((steps, rows, cols), lambda b, core: (0, b + group * members, 0))
    shape = jax.ShapeDtypeStruct((steps, samples * rows, cols), jnp.float32)
    in_specs = [rim, field, rim, half, half, rim, rim, field, whole_block(coeff)]
    first = 1 + len(in_specs)
    return call(
        finish_kernel,
        core,
        (members,),
        in_specs + [pl.BlockSpec(memory_space=pl.ANY)] * len(previous),
        [result, result],
        [shape, shape],
        [pltpu.VMEM((rows, SUBLANES, cols), jnp.float32)],
        {first + k: k for k in range(len(previous))},
        name="finish",
    )(core, *rests, *misfits, iterate, coeff, *previous)


def same_frequency(near, sensors, lanes):
    shape = (near, lanes)
    return lax.broadcasted_iota(jnp.int32, shape, 0) == (
        lax.broadcasted_iota(jnp.int32, shape, 1) % LANES // sensors
    )


def marks_of(cell_ref, width):
    first = pl.program_id(0) * width
    parts = []
    for start_lane in range(0, width, LANES):
        lane = lax.broadcasted_iota(jnp.int32, cell_ref.shape, 1) + (first + start_lane)
        parts.append(jnp.where(cell_ref[...] == lane, 1.0, 0.0).astype(jnp.bfloat16))
    return jnp.concatenate(parts, axis=1)


def near_map(own_ref, other_ref, here):
    _, freqs, sensors, width = own_ref.shape
    parts = [
        ref[part, here].reshape(LANES, width) for part in range(2) for ref in (own_ref, other_ref)
    ]
    return jnp.concatenate(parts, axis=0)


def observe_kernel(core_ref, *refs):
    *field_refs, own_ref, other_ref, table_ref, cell_ref, out_ref, spec, acc, picked = refs
    _, members, rows, steps, lanes = field_refs[0].shape
    freqs, sensors, width = own_ref.shape[1:]
    near = lanes // sensors
    wide = 2 * lanes
    count = len(field_refs) // 2 + 1
    chunk = pl.program_id(0)

    @pl.when(chunk == 0)
    def _():
        acc[...] = jnp.zeros_like(acc)
        picked[...] = jnp.zeros_like(picked)

    marks = marks_of(cell_ref, width)

    def history(b, r):
        slots = [field_refs[0][:, b, r]]
        for k in range(1, count):
            slots.append(field_refs[k][:, b, r] + field_refs[2 * count - 1 - k][:, b, r])
        return jnp.concatenate([slot.reshape(2 * steps, lanes) for slot in slots], axis=0)

    for b in range(members):
        spectrum = dot(
            table_ref[...], jnp.concatenate([history(b, r) for r in range(rows)], axis=1)
        )
        spec[2 * b] = spectrum[:freqs]
        spec[2 * b + 1] = spectrum[freqs:]
    for m in range(2 * members):
        picked[m] += dot_lanes(spec[m].astype(jnp.bfloat16), marks)
    for q in range(freqs // near):
        here = slice(q * near, (q + 1) * near)
        left = spec[:, here].reshape(2 * members * near, width).astype(jnp.bfloat16)
        acc[q] += dot_lanes(left, near_map(own_ref, other_ref, here))

    @pl.when(chunk == pl.num_programs(0) - 1)
    def _():
        mask = same_frequency(near, sensors, wide)
        for q in range(freqs // near):
            here = slice(q * near, (q + 1) * near)
            for b in range(members):
                real = acc[q, 2 * b * near : (2 * b + 1) * near]
                imag = acc[q, (2 * b + 1) * near : (2 * b + 2) * near]
                sums = (
                    real[:, :wide] - imag[:, wide:] + picked[2 * b, here],
                    imag[:, :wide] + real[:, wide:] + picked[2 * b + 1, here],
                )
                for part, value in enumerate(sums):
                    line = jnp.sum(jnp.where(mask, value, 0.0), 0, keepdims=True)
                    out_ref[0, part, b, q : q + 1] = line[:, :lanes]
                    out_ref[1, part, b, q : q + 1] = line[:, lanes:]


def map_specs(own, other, width):
    chunks = other.shape[3] // width
    return [
        pl.BlockSpec(own.shape[:3] + (width,), lambda c, core: (0, 0, 0, core[0] * chunks + c)),
        pl.BlockSpec(other.shape[:3] + (width,), lambda c, core: (0, 0, 0, c)),
    ]


def map_cost(members, own, other, moved):
    return pl.CostEstimate(
        flops=16 * members * other.size,
        bytes_accessed=4 * other.size + 2 * moved,
        transcendentals=0,
    )


def observe(core, slots, own, other, table, local_cells):
    _, members, rows, steps, lanes = slots[0].shape
    _, freqs, sensors, cells = other.shape
    width = CHUNK_ROWS * lanes
    near = lanes // sensors
    shape = (2, 2, members, freqs // near, lanes)
    slot = pl.BlockSpec((2, members, CHUNK_ROWS, steps, lanes), lambda c, core: (0, 0, c, 0, 0))
    return call(
        observe_kernel,
        core,
        (rows // CHUNK_ROWS,),
        [slot] * len(slots)
        + map_specs(own, other, width)
        + [whole_block(table), whole_block(local_cells)],
        pl.BlockSpec(shape, lambda c, core: (0, 0, 0, 0, 0)),
        jax.ShapeDtypeStruct(shape, jnp.float32),
        [
            pltpu.VMEM((2 * members, freqs, width), jnp.float32),
            pltpu.VMEM((freqs // near, 2 * members * near, 4 * lanes), jnp.float32),
            pltpu.VMEM((2 * members, freqs, 2 * lanes), jnp.float32),
        ],
        cost_estimate=map_cost(members, own, other, len(slots) * slots[0].size),
        name="observe",
    )(core, *slots, own, other, table, local_cells)


def pull_kernel(core_ref, *refs):
    *sums, noise_ref, own_ref, other_ref, back_ref, cell_ref, out_ref, weights, adjoint = refs
    devices, _, members, rows, steps, lanes = out_ref.shape
    freqs, sensors, width = own_ref.shape[1:]
    near = lanes // sensors
    wide = 2 * lanes

    def total(part, b, which):
        values = [ref[which, part, b] for ref in sums]
        while len(values) > 1:
            values = [values[k] + values[k + 1] for k in range(0, len(values), 2)]
        noise = noise_ref[which : which + 1]
        return (noise * values[0]).astype(jnp.bfloat16).astype(jnp.float32)

    @pl.when(pl.program_id(0) == 0)
    def _():
        mask = same_frequency(near, sensors, wide)
        for b in range(members):
            real, imag = (
                jnp.concatenate([total(part, b, 0), total(part, b, 1)], axis=1) for part in range(2)
            )
            for q in range(freqs // near):
                here = slice(q * near, (q + 1) * near)
                w_real = jnp.where(mask, real[q : q + 1], 0.0)
                w_imag = jnp.where(mask, imag[q : q + 1], 0.0)
                weights[2 * b, here, :wide] = w_real
                weights[2 * b, here, wide:] = w_imag
                weights[2 * b + 1, here, :wide] = w_imag
                weights[2 * b + 1, here, wide:] = -w_real

    marks = marks_of(cell_ref, width)
    for m in range(2 * members):
        adjoint[m] = dot(weights[m, :, :wide].astype(jnp.bfloat16), marks)
    for q in range(freqs // near):
        here = slice(q * near, (q + 1) * near)
        left = weights[:, here].reshape(2 * members * near, 2 * wide).astype(jnp.bfloat16)
        part = dot(left, near_map(own_ref, other_ref, here))
        adjoint[:, here] += part.reshape(2 * members, near, width)
    for b in range(members):
        whole = adjoint[2 * b : 2 * b + 2].reshape(2 * freqs, width)
        high = whole.astype(jnp.bfloat16)
        low = (whole - high.astype(jnp.float32)).astype(jnp.bfloat16)
        misfit = (dot(back_ref[...], high) + dot(back_ref[...], low)).astype(out_ref.dtype)
        for r in range(rows):
            part = misfit[:, r * lanes : (r + 1) * lanes]
            out_ref[:, :, b, r] = part.reshape(devices, 2, steps, lanes)


def pull_back(core, sums, noise, own, other, back, local_cells, shape):
    devices, _, members, rows, steps, lanes = shape
    _, freqs, sensors, cells = other.shape
    width = CHUNK_ROWS * lanes
    small = [*sums, noise]
    return call(
        pull_kernel,
        core,
        (rows // CHUNK_ROWS,),
        [whole_block(array) for array in small]
        + map_specs(own, other, width)
        + [whole_block(back), whole_block(local_cells)],
        pl.BlockSpec(
            (devices, 2, members, CHUNK_ROWS, steps, lanes), lambda c, core: (0, 0, 0, c, 0, 0)
        ),
        jax.ShapeDtypeStruct(shape, jnp.bfloat16),
        [
            pltpu.VMEM((2 * members, freqs, 4 * lanes), jnp.float32),
            pltpu.VMEM((2 * members, freqs, width), jnp.float32),
        ],
        cost_estimate=map_cost(members, own, other, math.prod(shape)),
        name="pull_back",
    )(core, *small, own, other, back, local_cells)


def rims(top, bottom):
    size = lax.axis_size("cells")
    onward = [(k, k + 1) for k in range(size - 1)]
    backward = [(k + 1, k) for k in range(size - 1)]
    return lax.ppermute(bottom, "cells", onward), lax.ppermute(top, "cells", backward)


def misfit_rims(edge):
    size, width = lax.axis_size("cells"), lax.axis_size("sensors")
    same, cross = [], []
    for cell in range(size):
        for sensor in range(width):
            there = cell + 2 * (sensor % 2) - 1
            if 0 <= there < size:
                same.append((cell * width + sensor, there * width + sensor))
                cross.append((cell * width + sensor, there * width + (sensor ^ 1)))
    both = ("cells", "sensors")
    return lax.ppermute(edge, both, same), lax.ppermute(edge, both, cross)


def swap_cores(value):
    size = lax.axis_size("sensors")
    return lax.ppermute(value, "sensors", [(k, k ^ 1) for k in range(size)])


def from_all_cells(value):
    size = lax.axis_size("cells")
    if size & (size - 1):
        return [lax.psum(value, "cells")]
    return [value] + [
        lax.ppermute(value, "cells", [(k, k ^ other) for k in range(size)])
        for other in range(1, size)
    ]


def gather_line(value):
    size = lax.axis_size("sensors")
    chips = size // 2
    ups, downs = [value], [value]
    for hop in range(1, chips):
        onward = [(k, k + 2) for k in range(2 * hop - 2, size - 2)]
        backward = [(size - 1 - k, size - 1 - there) for k, there in onward]
        ups.append(lax.ppermute(ups[-1], "sensors", onward))
        downs.append(lax.ppermute(downs[-1], "sensors", backward))
    return [value, *ups[1:], *downs[1:]]


def shards(rhs, forward_map, stiffness, reaction, noise_weight, sensor_cell):
    steps, samples, rows, cols = rhs.shape
    _, freqs, sensors, cells = forward_map.shape
    size = lax.axis_size("sensors")
    chips = size // 2
    cell_index = lax.axis_index("cells")
    sensor_index = lax.axis_index("sensors")
    core = sensor_index % 2
    chip = sensor_index // 2
    near = LANES // sensors
    half = cells // 2

    away = lax.dynamic_slice_in_dim(forward_map, (1 - core) * half, half, axis=3)
    other_map = swap_cores(away)

    cores = jnp.stack([core, 1 - core])
    offsets = cores[None, :, None] * steps + jnp.arange(steps, dtype=jnp.int32)
    chip_steps = 2 * steps
    places = (chip - jnp.arange(chips, dtype=jnp.int32)) % chips
    table = transform_table(freqs, places[:, None, None] * chip_steps + offsets)
    places = jnp.arange(chips, dtype=jnp.int32)
    back = transform_table(freqs, places[:, None, None] * chip_steps + offsets).T

    diagonal = reaction + 4.0 * stiffness * stiffness
    local = jnp.stack([stiffness, diagonal])
    up, down = rims(local[:, :HALO], local[:, rows - HALO :])
    stiff, diag = jnp.concatenate([up, local, down], axis=1)
    inside = diag > 0.0
    inverse = jnp.where(inside, 1.0 / jnp.where(inside, diag, 1.0), 0.0)
    unscale = jnp.where(inside, 1.0 / jnp.where(inside, stiff, 1.0), 0.0)
    scaled = DAMPING * inverse * stiff
    coeff = jnp.stack([scaled, scaled * stiff, unscale, stiff, diag])
    coeff = jnp.broadcast_to(coeff[:, :, None, :], coeff.shape[:2] + (SUBLANES, cols))

    def per_lane(values):
        own = lax.dynamic_slice_in_dim(values, sensor_index * sensors, sensors)
        other = lax.dynamic_slice_in_dim(values, (sensor_index ^ 1) * sensors, sensors)
        return jnp.stack([jnp.tile(own, near), jnp.tile(other, near)])

    noise = per_lane(noise_weight)
    local_cells = per_lane(sensor_cell) - (cell_index * cells + core * half)
    local_cells = jnp.broadcast_to(local_cells.reshape(2 * LANES, 1), (2 * LANES, LANES))
    core = core.reshape(1)

    members = samples // GROUPS
    states = []
    for group in range(GROUPS):
        group_rhs = rhs[:, group * members : (group + 1) * members]
        up, down = rims(
            *(
                jnp.transpose(rim, (1, 2, 0, 3)).astype(jnp.bfloat16)
                for rim in (group_rhs[:, :, :HALO], group_rhs[:, :, rows - HALO :])
            )
        )
        states.append(start(group, members, core, rhs, up, down, coeff))

    lines = [[k for k in range(size) if k % 2 == parity] for parity in range(2)]
    outputs = ()
    for iteration in range(ITERS):
        for group in range(GROUPS):
            iterate, keep, give, rest, top, bottom = states[group]
            above, below = rims(top, bottom)
            slots = gather_line(jnp.stack([keep, swap_cores(give)]))
            sums = observe(core, slots, forward_map, other_map, table, local_cells)
            sums = from_all_cells(sums + swap_cores(sums)[::-1])
            shape = (chips, 2, members, rows // 2, steps, cols)
            misfit = pull_back(core, sums, noise, forward_map, other_map, back, local_cells, shape)
            misfit = lax.psum_scatter(
                misfit, "sensors", scatter_dimension=0, axis_index_groups=lines, tiled=False
            )
            first = (rows // 2 - HALO) * core[0]
            edge = lax.dynamic_slice_in_dim(misfit, first, HALO, axis=2)
            same, _ = misfit_rims(edge[0])
            _, cross = misfit_rims(edge[1])
            misfits = (misfit[0], swap_cores(misfit[1]), same, cross)
            rests = (above, rest, below)
            if iteration < ITERS - 1:
                states[group] = step(core, rests, misfits, iterate, coeff)
            else:
                outputs = finish(group, samples, core, rests, misfits, iterate, coeff, outputs)
    return tuple(out.reshape(rhs.shape) for out in outputs)


def solution(mesh):
    placed = (
        P("sensors", None, "cells", None),
        P(None, None, "sensors", "cells"),
        P("cells", None),
        P("cells", None),
        P(),
        P(),
    )
    return jax.shard_map(
        shards,
        mesh=mesh,
        in_specs=placed,
        out_specs=(P("sensors", None, "cells", None), P("sensors", None, "cells", None)),
        check_vma=False,
    )
```

time: 623 us -> 856 us (1.37)
  starting transfers between devices: 71.8 us -> 175 us
  waiting for transfers between devices: 291 us -> 377 us
  Pallas kernels: 184 us -> 226 us
    ppermute x0 -> x67, waiting for transfers between devices: none -> 315 us  [the longest x18 197 us: gather_line(): downs.append(lax.ppermute(downs[-1], 'sensors', backward))]
    all_gather x4 -> x0, waiting for transfers between devices: 130 us -> none  [shards(): field = lax.all_gather(low, 'sensors', axis=0, tiled=False)]
    ppermute x0 -> x67, starting transfers between devices: none -> 115 us  [the longest x12 37.1 us: misfit_rims(): return (lax.ppermute(edge, both, same), lax.ppermute(edge, both, cross))]
    reduce_scatter x4 -> x6, waiting for transfers between devices: 129 us -> 26.2 us  [shards(): lax.psum_scatter(misfit, 'sensors', scatter_dimension=0, axis_index_group...]
    pallas_call x14 -> x21, Pallas kernels: 184 us -> 226 us  [the longest x6 95.7 us: observe(): call(observe_kernel, core, (rows // CHUNK_ROWS,), [slot] * len(slots) + m...]
    unnamed x78 -> x71, local copies, waits for them, and re-layouts: 46.1 us -> 20.4 us
    dynamic_slice x1 -> x3, local copies, waits for them, and re-layouts: 0.07 us -> 14.6 us  [the longest x1 14.4 us: shards(): lax.dynamic_slice_in_dim(forward_map, (1 - core) * half, half, axis=3)]
    squeeze x0 -> x12, local copies, waits for them, and re-layouts: none -> 13.4 us  [the longest x6 8.03 us: shards(): misfits = (misfit[0], swap_cores(misfit[1]), same, cross)]
  transfers between devices with their start and end apart: 52 -> 111, of which waited for: 28 -> 60; matrix products, arithmetic and copies ran while one was open for 1% -> 2% of each run, Pallas kernels for 28% -> 22%
where the time goes in v2:
time: 856 us; the launch traced here: 845 us
  waiting for transfers between devices  377 us (44%)
  Pallas kernels  226 us (26%)
  starting transfers between devices  175 us (20%)
  local copies, waits for them, and re-layouts  49.8 us (6%)
  between operations  16 us (2%)
    ppermute x18, waiting for transfers between devices, gather_line(): downs.append(lax.ppermute(downs[-1], 'sensors', backward))  197 us
    pallas_call x6, Pallas kernels, observe(): call(observe_kernel, core, (rows // CHUNK_ROWS,), [slot] * len(slots) + m...  95.7 us
    ppermute x18, waiting for transfers between devices, gather_line(): ups.append(lax.ppermute(ups[-1], 'sensors', onward))  93 us
    pallas_call x6, Pallas kernels, pull_back(): call(pull_kernel, core, (rows // CHUNK_ROWS,), [whole_block(array) for ar...  90.2 us
    ppermute x12, starting transfers between devices, misfit_rims(): return (lax.ppermute(edge, both, same), lax.ppermute(edge, both, cross))  37.1 us
    ppermute x10, starting transfers between devices, rims(): lax.ppermute(bottom, 'cells', onward)  30.5 us
    ppermute x19, starting transfers between devices, swap_cores(): return lax.ppermute(value, 'sensors', [(k, k ^ 1) for k in range(size)])  30.4 us
    reduce_scatter x6, waiting for transfers between devices, shards(): lax.psum_scatter(misfit, 'sensors', scatter_dimension=0, axis_index_group...  26.2 us
  transfers between devices with their start and end apart: 111, of which 60 were waited for; matrix products, arithmetic and copies ran while one was open for 2% of the time, Pallas kernels for 22%

profile of v2, /device:TPU:1, one launch (start us, length us, event | category | flops | bytes accessed | tf_op | source)
XLA Modules:
  0.0 844.9 jit_solution(12061569273900324999)
XLA Ops:
  7.3 14.4 %constant_dynamic-slice_fusion = bf16[2,128,16,2048]{3,2,1,0:T(8,128)(2,1)} fusion(bf16[2,128,16,4096]{3,2,1,0:T(8,128)(2,1)} %refs_5_.11, s32[]{:T(128)S(6)} %select_n.74), kind=kLoop, calls=%fused_computation.77 | loop fusion | bytes 33554436 | tf_op jit(solution)/shard_map/dynamic_slice | solution.py:510
  53.2 9.4 %collective-permute-done.76.refs_1_ = bf16[2,2,16,32,128]{4,3,2,1,0:T(8,128)(2,1)S(1)} collective-permute-done((bf16[2,2,16,32,128]{4,3,2,1,0:T(8,128)(2,1)S(1)}, bf16[2,2,16,32,128]{4,3,2,1,0:T(8,128)(2,1)S(1)}, u32[]{:S(2)}, u32[]{:S(2)}) %collective-permute-start.76) | collective-permute-done | bytes 524320 | tf_op jit(solution)/shard_map/ppermute | solution.py:493
  70.2 11.7 %collective-permute-done.80.refs_5_ = bf16[2,2,16,32,128]{4,3,2,1,0:T(8,128)(2,1)} collective-permute-done((bf16[2,2,16,32,128]{4,3,2,1,0:T(8,128)(2,1)}, bf16[2,2,16,32,128]{4,3,2,1,0:T(8,128)(2,1)}, u32[]{:S(2)}, u32[]{:S(2)}) %collective-permute-start.80) | collective-permute-done | bytes 524320 | tf_op jit(solution)/shard_map/ppermute | solution.py:494
  84.5 11.1 %collective-permute-done.81.refs_6_ = bf16[2,2,16,32,128]{4,3,2,1,0:T(8,128)(2,1)} collective-permute-done((bf16[2,2,16,32,128]{4,3,2,1,0:T(8,128)(2,1)}, bf16[2,2,16,32,128]{4,3,2,1,0:T(8,128)(2,1)}, u32[]{:S(2)}, u32[]{:S(2)}) %collective-permute-start.81) | collective-permute-done | bytes 524320 | tf_op jit(solution)/shard_map/ppermute | solution.py:494
  95.6 16.3 %observe.10 = f32[2,2,2,16,128]{4,3,2,1,0:T(8,128)S(1)} custom-call(s32[1]{0:T(128)} %bitcast.core_ref, bf16[2,2,16,32,128]{4,3,2,1,0:T(8,128)(2,1)S(1)} %pad_maximum_fusion.4.refs_0_, bf16[2,2,16,32,128]{4,3,2,1,0:T(8,128)(2,1)S(1)} %collective-permute-done.76.refs_1_, bf16[2,2,16,32,128]{4,3,2,1,0:T(8,128)(2,1)} %collective-permute-done.77.refs_2_, ...), custom_call_target="tpu_custom_call" | custom-call | flops 268435456 | bytes 37224448 | tf_op jit(solution)/shard_map/observe/pallas_call | solution.py:359
  122.4 15.1 %pull_back.10 = bf16[4,2,2,16,32,128]{5,4,3,2,1,0:T(8,128)(2,1)} custom-call(s32[1]{0:T(128)} %bitcast.core_ref, f32[2,2,2,16,128]{4,3,2,1,0:T(8,128)S(1)} %reverse_add_fusion.1.refs_0_, f32[2,2,2,16,128]{4,3,2,1,0:T(8,128)S(1)} %collective-permute-done.83.refs_1_, f32[2,2,2,16,128]{4,3,2,1,0:T(8,128)S(1)} %collective-permute-done.84.refs_2_, ...), custom_call_target="tpu_custom_call" | custom-call | flops 268435456 | bytes 35651584 | tf_op jit(solution)/shard_map/pull_back/pallas_call | solution.py:431
  159.2 21.6 %collective-permute-done.42.refs_1_ = bf16[2,2,16,32,128]{4,3,2,1,0:T(8,128)(2,1)S(1)} collective-permute-done((bf16[2,2,16,32,128]{4,3,2,1,0:T(8,128)(2,1)S(1)}, bf16[2,2,16,32,128]{4,3,2,1,0:T(8,128)(2,1)S(1)}, u32[]{:S(2)}, u32[]{:S(2)}) %collective-permute-start.42) | collective-permute-done | bytes 524320 | tf_op jit(solution)/shard_map/ppermute | solution.py:493
  189.1 15.2 %collective-permute-done.46.refs_5_ = bf16[2,2,16,32,128]{4,3,2,1,0:T(8,128)(2,1)S(1)} collective-permute-done((bf16[2,2,16,32,128]{4,3,2,1,0:T(8,128)(2,1)S(1)}, bf16[2,2,16,32,128]{4,3,2,1,0:T(8,128)(2,1)S(1)}, u32[]{:S(2)}, u32[]{:S(2)}) %collective-permute-start.46) | collective-permute-done | bytes 524320 | tf_op jit(solution)/shard_map/ppermute | solution.py:494
  205.8 12.7 %collective-permute-done.47.refs_6_ = bf16[2,2,16,32,128]{4,3,2,1,0:T(8,128)(2,1)S(1)} collective-permute-done((bf16[2,2,16,32,128]{4,3,2,1,0:T(8,128)(2,1)S(1)}, bf16[2,2,16,32,128]{4,3,2,1,0:T(8,128)(2,1)S(1)}, u32[]{:S(2)}, u32[]{:S(2)}) %collective-permute-start.47) | collective-permute-done | bytes 524320 | tf_op jit(solution)/shard_map/ppermute | solution.py:494
  218.4 15.9 %observe.8 = f32[2,2,2,16,128]{4,3,2,1,0:T(8,128)S(1)} custom-call(s32[1]{0:T(128)} %bitcast.core_ref, bf16[2,2,16,32,128]{4,3,2,1,0:T(8,128)(2,1)S(1)} %pad_maximum_fusion.2.refs_0_, bf16[2,2,16,32,128]{4,3,2,1,0:T(8,128)(2,1)S(1)} %collective-permute-done.42.refs_1_, bf16[2,2,16,32,128]{4,3,2,1,0:T(8,128)(2,1)S(1)} %collective-permute-done.43.refs_2_, ...), custom_call_target="tpu_custom_call" | custom-call | flops 268435456 | bytes 37224448 | tf_op jit(solution)/shard_map/observe/pallas_call | solution.py:359
  243.8 15.0 %pull_back.8 = bf16[4,2,2,16,32,128]{5,4,3,2,1,0:T(8,128)(2,1)} custom-call(s32[1]{0:T(128)} %bitcast.core_ref, f32[2,2,2,16,128]{4,3,2,1,0:T(8,128)S(1)} %reverse_add_fusion.3.refs_0_, f32[2,2,2,16,128]{4,3,2,1,0:T(8,128)S(1)} %collective-permute-done.49.refs_1_, f32[2,2,2,16,128]{4,3,2,1,0:T(8,128)S(1)} %collective-permute-done.50.refs_2_, ...), custom_call_target="tpu_custom_call" | custom-call | flops 268435456 | bytes 35651584 | tf_op jit(solution)/shard_map/pull_back/pallas_call | solution.py:431
  283.7 24.8 %collective-permute-done.10.refs_4_ = bf16[2,2,16,32,128]{4,3,2,1,0:T(8,128)(2,1)S(1)} collective-permute-done((bf16[2,2,16,32,128]{4,3,2,1,0:T(8,128)(2,1)S(1)}, bf16[2,2,16,32,128]{4,3,2,1,0:T(8,128)(2,1)S(1)}, u32[]{:S(2)}, u32[]{:S(2)}) %collective-permute-start.10) | collective-permute-done | bytes 524320 | tf_op jit(solution)/shard_map/ppermute | solution.py:494
  310.6 14.2 %collective-permute-done.11.refs_5_ = bf16[2,2,16,32,128]{4,3,2,1,0:T(8,128)(2,1)S(1)} collective-permute-done((bf16[2,2,16,32,128]{4,3,2,1,0:T(8,128)(2,1)S(1)}, bf16[2,2,16,32,128]{4,3,2,1,0:T(8,128)(2,1)S(1)}, u32[]{:S(2)}, u32[]{:S(2)}) %collective-permute-start.11) | collective-permute-done | bytes 524320 | tf_op jit(solution)/shard_map/ppermute | solution.py:494
  326.8 12.2 %collective-permute-done.12.refs_6_ = bf16[2,2,16,32,128]{4,3,2,1,0:T(8,128)(2,1)S(1)} collective-permute-done((bf16[2,2,16,32,128]{4,3,2,1,0:T(8,128)(2,1)S(1)}, bf16[2,2,16,32,128]{4,3,2,1,0:T(8,128)(2,1)S(1)}, u32[]{:S(2)}, u32[]{:S(2)}) %collective-permute-start.12) | collective-permute-done | bytes 524320 | tf_op jit(solution)/shard_map/ppermute | solution.py:494
  339.0 15.9 %observe.6 = f32[2,2,2,16,128]{4,3,2,1,0:T(8,128)S(1)} custom-call(s32[1]{0:T(128)} %bitcast.core_ref, bf16[2,2,16,32,128]{4,3,2,1,0:T(8,128)(2,1)S(1)} %pad_maximum_fusion.refs_0_, bf16[2,2,16,32,128]{4,3,2,1,0:T(8,128)(2,1)S(1)} %collective-permute-done.7.refs_1_, bf16[2,2,16,32,128]{4,3,2,1,0:T(8,128)(2,1)S(1)} %collective-permute-done.8.refs_2_, ...), custom_call_target="tpu_custom_call" | custom-call | flops 268435456 | bytes 37224448 | tf_op jit(solution)/shard_map/observe/pallas_call | solution.py:359
  364.3 15.0 %pull_back.6 = bf16[4,2,2,16,32,128]{5,4,3,2,1,0:T(8,128)(2,1)} custom-call(s32[1]{0:T(128)} %bitcast.core_ref, f32[2,2,2,16,128]{4,3,2,1,0:T(8,128)S(1)} %reverse_add_fusion.5.refs_0_, f32[2,2,2,16,128]{4,3,2,1,0:T(8,128)S(1)} %collective-permute-done.15.refs_1_, f32[2,2,2,16,128]{4,3,2,1,0:T(8,128)S(1)} %collective-permute-done.16.refs_2_, ...), custom_call_target="tpu_custom_call" | custom-call | flops 268435456 | bytes 35651584 | tf_op jit(solution)/shard_map/pull_back/pallas_call | solution.py:431
  407.8 21.7 %collective-permute-done.92.refs_1_ = bf16[2,2,16,32,128]{4,3,2,1,0:T(8,128)(2,1)S(1)} collective-permute-done((bf16[2,2,16,32,128]{4,3,2,1,0:T(8,128)(2,1)S(1)}, bf16[2,2,16,32,128]{4,3,2,1,0:T(8,128)(2,1)S(1)}, u32[]{:S(2)}, u32[]{:S(2)}) %collective-permute-start.92) | collective-permute-done | bytes 524320 | tf_op jit(solution)/shard_map/ppermute | solution.py:493
  436.0 13.6 %collective-permute-done.96.refs_5_ = bf16[2,2,16,32,128]{4,3,2,1,0:T(8,128)(2,1)S(1)} collective-permute-done((bf16[2,2,16,32,128]{4,3,2,1,0:T(8,128)(2,1)S(1)}, bf16[2,2,16,32,128]{4,3,2,1,0:T(8,128)(2,1)S(1)}, u32[]{:S(2)}, u32[]{:S(2)}) %collective-permute-start.96) | collective-permute-done | bytes 524320 | tf_op jit(solution)/shard_map/ppermute | solution.py:494
  451.1 12.5 %collective-permute-done.97.refs_6_ = bf16[2,2,16,32,128]{4,3,2,1,0:T(8,128)(2,1)S(1)} collective-permute-done((bf16[2,2,16,32,128]{4,3,2,1,0:T(8,128)(2,1)S(1)}, bf16[2,2,16,32,128]{4,3,2,1,0:T(8,128)(2,1)S(1)}, u32[]{:S(2)}, u32[]{:S(2)}) %collective-permute-start.97) | collective-permute-done | bytes 524320 | tf_op jit(solution)/shard_map/ppermute | solution.py:494
  463.6 15.9 %observe.11 = f32[2,2,2,16,128]{4,3,2,1,0:T(8,128)S(1)} custom-call(s32[1]{0:T(128)} %bitcast.core_ref, bf16[2,2,16,32,128]{4,3,2,1,0:T(8,128)(2,1)S(1)} %pad_maximum_fusion.5.refs_0_, bf16[2,2,16,32,128]{4,3,2,1,0:T(8,128)(2,1)S(1)} %collective-permute-done.92.refs_1_, bf16[2,2,16,32,128]{4,3,2,1,0:T(8,128)(2,1)S(1)} %collective-permute-done.93.refs_2_, ...), custom_call_target="tpu_custom_call" | custom-call | flops 268435456 | bytes 37224448 | tf_op jit(solution)/shard_map/observe/pallas_call | solution.py:359
  489.2 15.1 %pull_back.11 = bf16[4,2,2,16,32,128]{5,4,3,2,1,0:T(8,128)(2,1)} custom-call(s32[1]{0:T(128)} %bitcast.core_ref, f32[2,2,2,16,128]{4,3,2,1,0:T(8,128)S(1)} %reverse_add_fusion.refs_0_, f32[2,2,2,16,128]{4,3,2,1,0:T(8,128)S(1)} %collective-permute-done.99.refs_1_, f32[2,2,2,16,128]{4,3,2,1,0:T(8,128)S(1)} %collective-permute-done.100.refs_2_, ...), custom_call_target="tpu_custom_call" | custom-call | flops 268435456 | bytes 35651584 | tf_op jit(solution)/shard_map/pull_back/pallas_call | solution.py:431
  532.7 21.2 %collective-permute-done.58.refs_1_ = bf16[2,2,16,32,128]{4,3,2,1,0:T(8,128)(2,1)S(1)} collective-permute-done((bf16[2,2,16,32,128]{4,3,2,1,0:T(8,128)(2,1)S(1)}, bf16[2,2,16,32,128]{4,3,2,1,0:T(8,128)(2,1)S(1)}, u32[]{:S(2)}, u32[]{:S(2)}) %collective-permute-start.58) | collective-permute-done | bytes 524320 | tf_op jit(solution)/shard_map/ppermute | solution.py:493
  557.8 14.9 %collective-permute-done.62.refs_5_ = bf16[2,2,16,32,128]{4,3,2,1,0:T(8,128)(2,1)S(1)} collective-permute-done((bf16[2,2,16,32,128]{4,3,2,1,0:T(8,128)(2,1)S(1)}, bf16[2,2,16,32,128]{4,3,2,1,0:T(8,128)(2,1)S(1)}, u32[]{:S(2)}, u32[]{:S(2)}) %collective-permute-start.62) | collective-permute-done | bytes 524320 | tf_op jit(solution)/shard_map/ppermute | solution.py:494
  574.0 12.8 %collective-permute-done.63.refs_6_ = bf16[2,2,16,32,128]{4,3,2,1,0:T(8,128)(2,1)S(1)} collective-permute-done((bf16[2,2,16,32,128]{4,3,2,1,0:T(8,128)(2,1)S(1)}, bf16[2,2,16,32,128]{4,3,2,1,0:T(8,128)(2,1)S(1)}, u32[]{:S(2)}, u32[]{:S(2)}) %collective-permute-start.63) | collective-permute-done | bytes 524320 | tf_op jit(solution)/shard_map/ppermute | solution.py:494
  586.8 15.9 %observe.9 = f32[2,2,2,16,128]{4,3,2,1,0:T(8,128)S(1)} custom-call(s32[1]{0:T(128)} %bitcast.core_ref, bf16[2,2,16,32,128]{4,3,2,1,0:T(8,128)(2,1)S(1)} %pad_maximum_fusion.3.refs_0_, bf16[2,2,16,32,128]{4,3,2,1,0:T(8,128)(2,1)S(1)} %collective-permute-done.58.refs_1_, bf16[2,2,16,32,128]{4,3,2,1,0:T(8,128)(2,1)S(1)} %collective-permute-done.59.refs_2_, ...), custom_call_target="tpu_custom_call" | custom-call | flops 268435456 | bytes 37224448 | tf_op jit(solution)/shard_map/observe/pallas_call | solution.py:359
  612.3 15.0 %pull_back.9 = bf16[4,2,2,16,32,128]{5,4,3,2,1,0:T(8,128)(2,1)} custom-call(s32[1]{0:T(128)} %bitcast.core_ref, f32[2,2,2,16,128]{4,3,2,1,0:T(8,128)S(1)} %reverse_add_fusion.2.refs_0_, f32[2,2,2,16,128]{4,3,2,1,0:T(8,128)S(1)} %collective-permute-done.65.refs_1_, f32[2,2,2,16,128]{4,3,2,1,0:T(8,128)S(1)} %collective-permute-done.66.refs_2_, ...), custom_call_target="tpu_custom_call" | custom-call | flops 268435456 | bytes 35651584 | tf_op jit(solution)/shard_map/pull_back/pallas_call | solution.py:431
  657.4 19.1 %collective-permute-done.24.refs_1_ = bf16[2,2,16,32,128]{4,3,2,1,0:T(8,128)(2,1)S(1)} collective-permute-done((bf16[2,2,16,32,128]{4,3,2,1,0:T(8,128)(2,1)S(1)}, bf16[2,2,16,32,128]{4,3,2,1,0:T(8,128)(2,1)S(1)}, u32[]{:S(2)}, u32[]{:S(2)}) %collective-permute-start.24) | collective-permute-done | bytes 524320 | tf_op jit(solution)/shard_map/ppermute | solution.py:493
  680.6 14.7 %collective-permute-done.28.refs_5_ = bf16[2,2,16,32,128]{4,3,2,1,0:T(8,128)(2,1)S(1)} collective-permute-done((bf16[2,2,16,32,128]{4,3,2,1,0:T(8,128)(2,1)S(1)}, bf16[2,2,16,32,128]{4,3,2,1,0:T(8,128)(2,1)S(1)}, u32[]{:S(2)}, u32[]{:S(2)}) %collective-permute-start.28) | collective-permute-done | bytes 524320 | tf_op jit(solution)/shard_map/ppermute | solution.py:494
  696.6 12.7 %collective-permute-done.29.refs_6_ = bf16[2,2,16,32,128]{4,3,2,1,0:T(8,128)(2,1)S(1)} collective-permute-done((bf16[2,2,16,32,128]{4,3,2,1,0:T(8,128)(2,1)S(1)}, bf16[2,2,16,32,128]{4,3,2,1,0:T(8,128)(2,1)S(1)}, u32[]{:S(2)}, u32[]{:S(2)}) %collective-permute-start.29) | collective-permute-done | bytes 524320 | tf_op jit(solution)/shard_map/ppermute | solution.py:494
  709.3 15.9 %observe.7 = f32[2,2,2,16,128]{4,3,2,1,0:T(8,128)S(1)} custom-call(s32[1]{0:T(128)} %bitcast.core_ref, bf16[2,2,16,32,128]{4,3,2,1,0:T(8,128)(2,1)S(1)} %pad_maximum_fusion.1.refs_0_, bf16[2,2,16,32,128]{4,3,2,1,0:T(8,128)(2,1)S(1)} %collective-permute-done.24.refs_1_, bf16[2,2,16,32,128]{4,3,2,1,0:T(8,128)(2,1)S(1)} %collective-permute-done.25.refs_2_, ...), custom_call_target="tpu_custom_call" | custom-call | flops 268435456 | bytes 37224448 | tf_op jit(solution)/shard_map/observe/pallas_call | solution.py:359
  734.8 15.0 %pull_back.7 = bf16[4,2,2,16,32,128]{5,4,3,2,1,0:T(8,128)(2,1)} custom-call(s32[1]{0:T(128)} %bitcast.core_ref, f32[2,2,2,16,128]{4,3,2,1,0:T(8,128)S(1)} %reverse_add_fusion.4.refs_0_, f32[2,2,2,16,128]{4,3,2,1,0:T(8,128)S(1)} %collective-permute-done.31.refs_1_, f32[2,2,2,16,128]{4,3,2,1,0:T(8,128)S(1)} %collective-permute-done.32.refs_2_, ...), custom_call_target="tpu_custom_call" | custom-call | flops 268435456 | bytes 35651584 | tf_op jit(solution)/shard_map/pull_back/pallas_call | solution.py:431
  765.4 26.1 %reduce-scatter.9.cloned.1.call-done = bf16[1,2,2,16,32,128]{5,4,3,2,1,0:T(8,128)(2,1)} async-done(((bf16[4,2,2,16,32,128]{5,4,3,2,1,0:T(8,128)(2,1)}), bf16[1,2,2,16,32,128]{5,4,3,2,1,0:T(8,128)(2,1)}) %reduce-scatter.9.cloned.1.call-update) | async-done | bytes 524304 | tf_op jit(solution)/shard_map/reduce_scatter | solution.py:565
  (344 shorter events, 326.2 us)
Async XLA Ops:
  7.2 372.3 %reduce-scatter.15.cloned.1.call-start = ((), (), s32[]{:S(2)}) async-start(), calls=%async_computation.10 | async-start | bytes 2621440 | tf_op jit(solution)/shard_map/reduce_scatter | solution.py:565
  21.7 73.8 %collective-permute-start.13 = (bf16[2,128,16,2048]{3,2,1,0:T(8,128)(2,1)}, bf16[2,128,16,2048]{3,2,1,0:T(8,128)(2,1)}, u32[]{:S(2)}, u32[]{:S(2)}) collective-permute-start(bf16[2,128,16,2048]{3,2,1,0:T(8,128)(2,1)} %constant_dynamic-slice_fusion), channel_id=1, source_target_pairs={{0,1},{1,0},{2,3},{3,2},{4,5},{5,4},{6,7},{7,6},{8,9},{9,8},{10,11... | collective-permute-start | bytes 50331656 | tf_op jit(solution)/shard_map/ppermute | solution.py:473
  137.5 366.8 %reduce-scatter.11.cloned.1.call-start = ((), (), s32[]{:S(2)}) async-start(), calls=%async_computation.8 | async-start | bytes 2621440 | tf_op jit(solution)/shard_map/reduce_scatter | solution.py:565
  156.5 24.3 %collective-permute-start.42 = (bf16[2,2,16,32,128]{4,3,2,1,0:T(8,128)(2,1)S(1)}, bf16[2,2,16,32,128]{4,3,2,1,0:T(8,128)(2,1)S(1)}, u32[]{:S(2)}, u32[]{:S(2)}) collective-permute-start(bf16[2,2,16,32,128]{4,3,2,1,0:T(8,128)(2,1)S(1)} %pad_maximum_fusion.2.refs_0_), channel_id=1, source_target_pairs={{0,2},{1,3},{2,4},{3,5},{4,6},{5,7},{8,10},{9,11},{10,12},{11,13},... | collective-permute-start | bytes 1572872 | tf_op jit(solution)/shard_map/ppermute | solution.py:493
  157.9 29.2 %collective-permute-start.45 = (bf16[2,2,16,32,128]{4,3,2,1,0:T(8,128)(2,1)S(1)}, bf16[2,2,16,32,128]{4,3,2,1,0:T(8,128)(2,1)S(1)}, u32[]{:S(2)}, u32[]{:S(2)}) collective-permute-start(bf16[2,2,16,32,128]{4,3,2,1,0:T(8,128)(2,1)S(1)} %pad_maximum_fusion.2.refs_0_), channel_id=1, source_target_pairs={{7,5},{6,4},{5,3},{4,2},{3,1},{2,0},{15,13},{14,12},{13,11},{12,10... | collective-permute-start | bytes 1572872 | tf_op jit(solution)/shard_map/ppermute | solution.py:494
  187.1 17.2 %collective-permute-start.46 = (bf16[2,2,16,32,128]{4,3,2,1,0:T(8,128)(2,1)S(1)}, bf16[2,2,16,32,128]{4,3,2,1,0:T(8,128)(2,1)S(1)}, u32[]{:S(2)}, u32[]{:S(2)}) collective-permute-start(bf16[2,2,16,32,128]{4,3,2,1,0:T(8,128)(2,1)S(1)} %collective-permute-done.45.refs_4_), channel_id=1, source_target_pairs={{5,3},{4,2},{3,1},{2,0},{13,11},{12,10},{11,9},{10,8},{21,19},{20,... | collective-permute-start | bytes 1572872 | tf_op jit(solution)/shard_map/ppermute | solution.py:494
  188.4 17.4 %collective-permute-start.44 = (bf16[2,2,16,32,128]{4,3,2,1,0:T(8,128)(2,1)S(1)}, bf16[2,2,16,32,128]{4,3,2,1,0:T(8,128)(2,1)S(1)}, u32[]{:S(2)}, u32[]{:S(2)}) collective-permute-start(bf16[2,2,16,32,128]{4,3,2,1,0:T(8,128)(2,1)S(1)} %collective-permute-done.43.refs_2_), channel_id=1, source_target_pairs={{4,6},{5,7},{12,14},{13,15},{20,22},{21,23},{28,30},{29,31}} | collective-permute-start | bytes 1572872 | tf_op jit(solution)/shard_map/ppermute | solution.py:493
  258.9 368.5 %reduce-scatter.7.cloned.1.call-start = ((), (), s32[]{:S(2)}) async-start(), calls=%async_computation.6 | async-start | bytes 2621440 | tf_op jit(solution)/shard_map/reduce_scatter | solution.py:565
  278.4 30.1 %collective-permute-start.10 = (bf16[2,2,16,32,128]{4,3,2,1,0:T(8,128)(2,1)S(1)}, bf16[2,2,16,32,128]{4,3,2,1,0:T(8,128)(2,1)S(1)}, u32[]{:S(2)}, u32[]{:S(2)}) collective-permute-start(bf16[2,2,16,32,128]{4,3,2,1,0:T(8,128)(2,1)S(1)} %pad_maximum_fusion.refs_0_), channel_id=1, source_target_pairs={{7,5},{6,4},{5,3},{4,2},{3,1},{2,0},{15,13},{14,12},{13,11},{12,10... | collective-permute-start | bytes 1572872 | tf_op jit(solution)/shard_map/ppermute | solution.py:494
  279.7 30.1 %collective-permute-start.7 = (bf16[2,2,16,32,128]{4,3,2,1,0:T(8,128)(2,1)S(1)}, bf16[2,2,16,32,128]{4,3,2,1,0:T(8,128)(2,1)S(1)}, u32[]{:S(2)}, u32[]{:S(2)}) collective-permute-start(bf16[2,2,16,32,128]{4,3,2,1,0:T(8,128)(2,1)S(1)} %pad_maximum_fusion.refs_0_), channel_id=1, source_target_pairs={{0,2},{1,3},{2,4},{3,5},{4,6},{5,7},{8,10},{9,11},{10,12},{11,13},... | collective-permute-start | bytes 1572872 | tf_op jit(solution)/shard_map/ppermute | solution.py:493
  379.4 379.4 %reduce-scatter.17.cloned.1.call-start = ((), (), s32[]{:S(2)}) async-start(), calls=%async_computation.11 | async-start | bytes 2621440 | tf_op jit(solution)/shard_map/reduce_scatter | solution.py:565
  405.2 24.3 %collective-permute-start.92 = (bf16[2,2,16,32,128]{4,3,2,1,0:T(8,128)(2,1)S(1)}, bf16[2,2,16,32,128]{4,3,2,1,0:T(8,128)(2,1)S(1)}, u32[]{:S(2)}, u32[]{:S(2)}) collective-permute-start(bf16[2,2,16,32,128]{4,3,2,1,0:T(8,128)(2,1)S(1)} %pad_maximum_fusion.5.refs_0_), channel_id=1, source_target_pairs={{0,2},{1,3},{2,4},{3,5},{4,6},{5,7},{8,10},{9,11},{10,12},{11,13},... | collective-permute-start | bytes 1572872 | tf_op jit(solution)/shard_map/ppermute | solution.py:493
  406.5 27.5 %collective-permute-start.95 = (bf16[2,2,16,32,128]{4,3,2,1,0:T(8,128)(2,1)S(1)}, bf16[2,2,16,32,128]{4,3,2,1,0:T(8,128)(2,1)S(1)}, u32[]{:S(2)}, u32[]{:S(2)}) collective-permute-start(bf16[2,2,16,32,128]{4,3,2,1,0:T(8,128)(2,1)S(1)} %pad_maximum_fusion.5.refs_0_), channel_id=1, source_target_pairs={{7,5},{6,4},{5,3},{4,2},{3,1},{2,0},{15,13},{14,12},{13,11},{12,10... | collective-permute-start | bytes 1572872 | tf_op jit(solution)/shard_map/ppermute | solution.py:494
  504.3 259.3 %reduce-scatter.13.cloned.1.call-start = ((), (), s32[]{:S(2)}) async-start(), calls=%async_computation.9 | async-start | bytes 2621440 | tf_op jit(solution)/shard_map/reduce_scatter | solution.py:565
  530.0 23.8 %collective-permute-start.58 = (bf16[2,2,16,32,128]{4,3,2,1,0:T(8,128)(2,1)S(1)}, bf16[2,2,16,32,128]{4,3,2,1,0:T(8,128)(2,1)S(1)}, u32[]{:S(2)}, u32[]{:S(2)}) collective-permute-start(bf16[2,2,16,32,128]{4,3,2,1,0:T(8,128)(2,1)S(1)} %pad_maximum_fusion.3.refs_0_), channel_id=1, source_target_pairs={{0,2},{1,3},{2,4},{3,5},{4,6},{5,7},{8,10},{9,11},{10,12},{11,13},... | collective-permute-start | bytes 1572872 | tf_op jit(solution)/shard_map/ppermute | solution.py:493
  531.4 24.4 %collective-permute-start.61 = (bf16[2,2,16,32,128]{4,3,2,1,0:T(8,128)(2,1)S(1)}, bf16[2,2,16,32,128]{4,3,2,1,0:T(8,128)(2,1)S(1)}, u32[]{:S(2)}, u32[]{:S(2)}) collective-permute-start(bf16[2,2,16,32,128]{4,3,2,1,0:T(8,128)(2,1)S(1)} %pad_maximum_fusion.3.refs_0_), channel_id=1, source_target_pairs={{7,5},{6,4},{5,3},{4,2},{3,1},{2,0},{15,13},{14,12},{13,11},{12,10... | collective-permute-start | bytes 1572872 | tf_op jit(solution)/shard_map/ppermute | solution.py:494
  555.8 17.0 %collective-permute-start.62 = (bf16[2,2,16,32,128]{4,3,2,1,0:T(8,128)(2,1)S(1)}, bf16[2,2,16,32,128]{4,3,2,1,0:T(8,128)(2,1)S(1)}, u32[]{:S(2)}, u32[]{:S(2)}) collective-permute-start(bf16[2,2,16,32,128]{4,3,2,1,0:T(8,128)(2,1)S(1)} %collective-permute-done.61.refs_4_), channel_id=1, source_target_pairs={{5,3},{4,2},{3,1},{2,0},{13,11},{12,10},{11,9},{10,8},{21,19},{20,... | collective-permute-start | bytes 1572872 | tf_op jit(solution)/shard_map/ppermute | solution.py:494
  557.1 17.0 %collective-permute-start.60 = (bf16[2,2,16,32,128]{4,3,2,1,0:T(8,128)(2,1)S(1)}, bf16[2,2,16,32,128]{4,3,2,1,0:T(8,128)(2,1)S(1)}, u32[]{:S(2)}, u32[]{:S(2)}) collective-permute-start(bf16[2,2,16,32,128]{4,3,2,1,0:T(8,128)(2,1)S(1)} %collective-permute-done.59.refs_2_), channel_id=1, source_target_pairs={{4,6},{5,7},{12,14},{13,15},{20,22},{21,23},{28,30},{29,31}} | collective-permute-start | bytes 1572872 | tf_op jit(solution)/shard_map/ppermute | solution.py:493
  627.3 164.2 %reduce-scatter.9.cloned.1.call-start = ((), (), s32[]{:S(2)}) async-start(), calls=%async_computation.7 | async-start | bytes 2621440 | tf_op jit(solution)/shard_map/reduce_scatter | solution.py:565
  654.8 21.7 %collective-permute-start.24 = (bf16[2,2,16,32,128]{4,3,2,1,0:T(8,128)(2,1)S(1)}, bf16[2,2,16,32,128]{4,3,2,1,0:T(8,128)(2,1)S(1)}, u32[]{:S(2)}, u32[]{:S(2)}) collective-permute-start(bf16[2,2,16,32,128]{4,3,2,1,0:T(8,128)(2,1)S(1)} %pad_maximum_fusion.1.refs_0_), channel_id=1, source_target_pairs={{0,2},{1,3},{2,4},{3,5},{4,6},{5,7},{8,10},{9,11},{10,12},{11,13},... | collective-permute-start | bytes 1572872 | tf_op jit(solution)/shard_map/ppermute | solution.py:493
  656.1 22.2 %collective-permute-start.27 = (bf16[2,2,16,32,128]{4,3,2,1,0:T(8,128)(2,1)S(1)}, bf16[2,2,16,32,128]{4,3,2,1,0:T(8,128)(2,1)S(1)}, u32[]{:S(2)}, u32[]{:S(2)}) collective-permute-start(bf16[2,2,16,32,128]{4,3,2,1,0:T(8,128)(2,1)S(1)} %pad_maximum_fusion.1.refs_0_), channel_id=1, source_target_pairs={{7,5},{6,4},{5,3},{4,2},{3,1},{2,0},{15,13},{14,12},{13,11},{12,10... | collective-permute-start | bytes 1572872 | tf_op jit(solution)/shard_map/ppermute | solution.py:494
  678.3 16.9 %collective-permute-start.28 = (bf16[2,2,16,32,128]{4,3,2,1,0:T(8,128)(2,1)S(1)}, bf16[2,2,16,32,128]{4,3,2,1,0:T(8,128)(2,1)S(1)}, u32[]{:S(2)}, u32[]{:S(2)}) collective-permute-start(bf16[2,2,16,32,128]{4,3,2,1,0:T(8,128)(2,1)S(1)} %collective-permute-done.27.refs_4_), channel_id=1, source_target_pairs={{5,3},{4,2},{3,1},{2,0},{13,11},{12,10},{11,9},{10,8},{21,19},{20,... | collective-permute-start | bytes 1572872 | tf_op jit(solution)/shard_map/ppermute | solution.py:494
  749.9 42.8 %collective-permute-start.89 = (bf16[2,4,32,128]{3,2,1,0:T(8,128)(2,1)}, bf16[2,4,32,128]{3,2,1,0:T(8,128)(2,1)S(1)}, u32[]{:S(2)}, u32[]{:S(2)}) collective-permute-start(bf16[2,4,32,128]{3,2,1,0:T(8,128)(2,1)} %get-tuple-element.74), channel_id=1, source_target_pairs={{0,8},{8,16},{16,24},{1,9},{9,17},{17,25},{2,10},{10,18},{18,26},{... | collective-permute-start | bytes 196616 | tf_op jit(solution)/shard_map/ppermute | solution.py:455
  752.2 42.3 %collective-permute-start.90 = (bf16[2,4,32,128]{3,2,1,0:T(8,128)(2,1)S(1)}, bf16[2,4,32,128]{3,2,1,0:T(8,128)(2,1)S(1)}, u32[]{:S(2)}, u32[]{:S(2)}) collective-permute-start(bf16[2,4,32,128]{3,2,1,0:T(8,128)(2,1)S(1)} %get-tuple-element.76), channel_id=1, source_target_pairs={{8,0},{16,8},{24,16},{9,1},{17,9},{25,17},{10,2},{18,10},{26,18},{... | collective-permute-start | bytes 196616 | tf_op jit(solution)/shard_map/ppermute | solution.py:455
  753.5 44.1 %collective-permute-start.55 = (bf16[2,4,32,128]{3,2,1,0:T(8,128)(2,1)}, bf16[2,4,32,128]{3,2,1,0:T(8,128)(2,1)S(1)}, u32[]{:S(2)}, u32[]{:S(2)}) collective-permute-start(bf16[2,4,32,128]{3,2,1,0:T(8,128)(2,1)} %copy-done.25), channel_id=1, source_target_pairs={{0,8},{8,16},{16,24},{1,9},{9,17},{17,25},{2,10},{10,18},{18,26},{... | collective-permute-start | bytes 196616 | tf_op jit(solution)/shard_map/ppermute | solution.py:455
  757.5 42.5 %collective-permute-start.56 = (bf16[2,4,32,128]{3,2,1,0:T(8,128)(2,1)}, bf16[2,4,32,128]{3,2,1,0:T(8,128)(2,1)S(1)}, u32[]{:S(2)}, u32[]{:S(2)}) collective-permute-start(bf16[2,4,32,128]{3,2,1,0:T(8,128)(2,1)} %copy-done.24), channel_id=1, source_target_pairs={{8,0},{16,8},{24,16},{9,1},{17,9},{25,17},{10,2},{18,10},{26,18},{... | collective-permute-start | bytes 196616 | tf_op jit(solution)/shard_map/ppermute | solution.py:455
  760.7 53.4 %collective-permute-start.102 = (bf16[2,16,32,128]{3,2,1,0:T(8,128)(2,1)}, bf16[2,16,32,128]{3,2,1,0:T(8,128)(2,1)}, u32[]{:S(2)}, u32[]{:S(2)}) collective-permute-start(bf16[2,16,32,128]{3,2,1,0:T(8,128)(2,1)} %get-tuple-element.96), channel_id=1, source_target_pairs={{0,1},{1,0},{2,3},{3,2},{4,5},{5,4},{6,7},{7,6},{8,9},{9,8},{10,11... | collective-permute-start | bytes 786440 | tf_op jit(solution)/shard_map/ppermute | solution.py:473
  792.7 25.4 %collective-permute-start.68 = (bf16[2,16,32,128]{3,2,1,0:T(8,128)(2,1)}, bf16[2,16,32,128]{3,2,1,0:T(8,128)(2,1)S(1)}, u32[]{:S(2)}, u32[]{:S(2)}) collective-permute-start(bf16[2,16,32,128]{3,2,1,0:T(8,128)(2,1)} %get-tuple-element.104), channel_id=1, source_target_pairs={{0,1},{1,0},{2,3},{3,2},{4,5},{5,4},{6,7},{7,6},{8,9},{9,8},{10,11... | collective-permute-start | bytes 786440 | tf_op jit(solution)/shard_map/ppermute | solution.py:473
  800.0 33.3 %collective-permute-start.34 = (bf16[2,16,32,128]{3,2,1,0:T(8,128)(2,1)S(1)}, bf16[2,16,32,128]{3,2,1,0:T(8,128)(2,1)S(1)}, u32[]{:S(2)}, u32[]{:S(2)}) collective-permute-start(bf16[2,16,32,128]{3,2,1,0:T(8,128)(2,1)S(1)} %get-tuple-element.112), channel_id=1, source_target_pairs={{0,1},{1,0},{2,3},{3,2},{4,5},{5,4},{6,7},{7,6},{8,9},{9,8},{10,11... | collective-permute-start | bytes 786440 | tf_op jit(solution)/shard_map/ppermute | solution.py:473
  808.2 25.0 %collective-permute-start.21 = (bf16[2,4,32,128]{3,2,1,0:T(8,128)(2,1)}, bf16[2,4,32,128]{3,2,1,0:T(8,128)(2,1)S(1)}, u32[]{:S(2)}, u32[]{:S(2)}) collective-permute-start(bf16[2,4,32,128]{3,2,1,0:T(8,128)(2,1)} %copy-done.27), channel_id=1, source_target_pairs={{0,8},{8,16},{16,24},{1,9},{9,17},{17,25},{2,10},{10,18},{18,26},{... | collective-permute-start | bytes 196616 | tf_op jit(solution)/shard_map/ppermute | solution.py:455
  812.7 20.5 %collective-permute-start.22 = (bf16[2,4,32,128]{3,2,1,0:T(8,128)(2,1)}, bf16[2,4,32,128]{3,2,1,0:T(8,128)(2,1)S(1)}, u32[]{:S(2)}, u32[]{:S(2)}) collective-permute-start(bf16[2,4,32,128]{3,2,1,0:T(8,128)(2,1)} %copy-done.26), channel_id=1, source_target_pairs={{8,0},{16,8},{24,16},{9,1},{17,9},{25,17},{10,2},{18,10},{26,18},{... | collective-permute-start | bytes 196616 | tf_op jit(solution)/shard_map/ppermute | solution.py:455
  814.1 19.2 %collective-permute-start.35 = (bf16[2,4,32,128]{3,2,1,0:T(8,128)(2,1)S(1)}, bf16[2,4,32,128]{3,2,1,0:T(8,128)(2,1)S(1)}, u32[]{:S(2)}, u32[]{:S(2)}) collective-permute-start(bf16[2,4,32,128]{3,2,1,0:T(8,128)(2,1)S(1)} %get-tuple-element.111), channel_id=1, source_target_pairs={{1,9},{3,11},{5,13},{7,15},{8,0},{9,17},{10,2},{11,19},{12,4},{13,... | collective-permute-start | bytes 196616 | tf_op jit(solution)/shard_map/ppermute | solution.py:468
  (114 other events, 1311.1 us)
Sparse Core Ops, SparseCore 0:
  137.6 52.4 reduce-scatter.14
  259.0 52.5 reduce-scatter.10
  379.5 53.8 reduce-scatter.6
  504.4 49.9 reduce-scatter.16
  627.5 47.4 reduce-scatter.12
  750.0 41.5 reduce-scatter.8

commit v3 on v2

--- a/solution.py
+++ b/solution.py
@@ -13,7 +13,7 @@
 HALO = SWEEPS
 LANES = 128
 SUBLANES = 8
-GROUPS = 3
+GROUPS = 2
 CHUNK_ROWS = 4
 VMEM_BYTES = 40 * 2**20
 
@@ -281,12 +281,11 @@
 
 
 def observe_kernel(core_ref, *refs):
-    *field_refs, own_ref, other_ref, table_ref, cell_ref, out_ref, spec, acc, picked = refs
-    _, members, rows, steps, lanes = field_refs[0].shape
+    field_ref, own_ref, other_ref, table_ref, cell_ref, out_ref, spec, acc, picked = refs
+    chips, _, members, rows, steps, lanes = field_ref.shape
     freqs, sensors, width = own_ref.shape[1:]
     near = lanes // sensors
     wide = 2 * lanes
-    count = len(field_refs) // 2 + 1
     chunk = pl.program_id(0)
 
     @pl.when(chunk == 0)
@@ -297,10 +296,7 @@
     marks = marks_of(cell_ref, width)
 
     def history(b, r):
-        slots = [field_refs[0][:, b, r]]
-        for k in range(1, count):
-            slots.append(field_refs[k][:, b, r] + field_refs[2 * count - 1 - k][:, b, r])
-        return jnp.concatenate([slot.reshape(2 * steps, lanes) for slot in slots], axis=0)
+        return field_ref[:, :, b, r].reshape(2 * chips * steps, lanes)
 
     for b in range(members):
         spectrum = dot(
@@ -349,18 +345,18 @@
     )
 
 
-def observe(core, slots, own, other, table, local_cells):
-    _, members, rows, steps, lanes = slots[0].shape
+def observe(core, field, own, other, table, local_cells):
+    chips, _, members, rows, steps, lanes = field.shape
     _, freqs, sensors, cells = other.shape
     width = CHUNK_ROWS * lanes
     near = lanes // sensors
     shape = (2, 2, members, freqs // near, lanes)
-    slot = pl.BlockSpec((2, members, CHUNK_ROWS, steps, lanes), lambda c, core: (0, 0, c, 0, 0))
+    block = (chips, 2, members, CHUNK_ROWS, steps, lanes)
     return call(
         observe_kernel,
         core,
         (rows // CHUNK_ROWS,),
-        [slot] * len(slots)
+        [pl.BlockSpec(block, lambda c, core: (0, 0, 0, c, 0, 0))]
         + map_specs(own, other, width)
         + [whole_block(table), whole_block(local_cells)],
         pl.BlockSpec(shape, lambda c, core: (0, 0, 0, 0, 0)),
@@ -370,9 +366,9 @@
             pltpu.VMEM((freqs // near, 2 * members * near, 4 * lanes), jnp.float32),
             pltpu.VMEM((2 * members, freqs, 2 * lanes), jnp.float32),
         ],
-        cost_estimate=map_cost(members, own, other, len(slots) * slots[0].size),
+        cost_estimate=map_cost(members, own, other, field.size),
         name="observe",
-    )(core, *slots, own, other, table, local_cells)
+    )(core, field, own, other, table, local_cells)
 
 
 def pull_kernel(core_ref, *refs):
@@ -483,18 +479,6 @@
     ]
 
 
-def gather_line(value):
-    size = lax.axis_size("sensors")
-    chips = size // 2
-    ups, downs = [value], [value]
-    for hop in range(1, chips):
-        onward = [(k, k + 2) for k in range(2 * hop - 2, size - 2)]
-        backward = [(size - 1 - k, size - 1 - there) for k, there in onward]
-        ups.append(lax.ppermute(ups[-1], "sensors", onward))
-        downs.append(lax.ppermute(downs[-1], "sensors", backward))
-    return [value, *ups[1:], *downs[1:]]
-
-
 def shards(rhs, forward_map, stiffness, reaction, noise_weight, sensor_cell):
     steps, samples, rows, cols = rhs.shape
     _, freqs, sensors, cells = forward_map.shape
@@ -503,7 +487,6 @@
     cell_index = lax.axis_index("cells")
     sensor_index = lax.axis_index("sensors")
     core = sensor_index % 2
-    chip = sensor_index // 2
     near = LANES // sensors
     half = cells // 2
 
@@ -513,10 +496,9 @@
     cores = jnp.stack([core, 1 - core])
     offsets = cores[None, :, None] * steps + jnp.arange(steps, dtype=jnp.int32)
     chip_steps = 2 * steps
-    places = (chip - jnp.arange(chips, dtype=jnp.int32)) % chips
-    table = transform_table(freqs, places[:, None, None] * chip_steps + offsets)
-    places = jnp.arange(chips, dtype=jnp.int32)
-    back = transform_table(freqs, places[:, None, None] * chip_steps + offsets).T
+    places = jnp.arange(chips, dtype=jnp.int32)[:, None, None] * chip_steps
+    table = transform_table(freqs, places + offsets)
+    back = table.T
 
     diagonal = reaction + 4.0 * stiffness * stiffness
     local = jnp.stack([stiffness, diagonal])
@@ -557,8 +539,10 @@
         for group in range(GROUPS):
             iterate, keep, give, rest, top, bottom = states[group]
             above, below = rims(top, bottom)
-            slots = gather_line(jnp.stack([keep, swap_cores(give)]))
-            sums = observe(core, slots, forward_map, other_map, table, local_cells)
+            field = lax.all_gather(
+                jnp.stack([keep, swap_cores(give)]), "sensors", axis_index_groups=lines
+            )
+            sums = observe(core, field, forward_map, other_map, table, local_cells)
             sums = from_all_cells(sums + swap_cores(sums)[::-1])
             shape = (chips, 2, members, rows // 2, steps, cols)
             misfit = pull_back(core, sums, noise, forward_map, other_map, back, local_cells, shape)

time: 856 us -> 610 us (0.71); the launches traced: 845 us -> 608 us
  waiting for transfers between devices: 377 us -> 282 us
  starting transfers between devices: 175 us -> 82.2 us
  Pallas kernels: 226 us -> 166 us
    ppermute x36 -> x0, waiting for transfers between devices: 290 us -> none  [the longest x18 197 us: gather_line(): downs.append(lax.ppermute(downs[-1], 'sensors', backward))]
    all_gather x0 -> x4, waiting for transfers between devices: none -> 113 us  [shards(): lax.all_gather(jnp.stack([keep, swap_cores(give)]), 'sensors', axis_index...]
    reduce_scatter x6 -> x4, waiting for transfers between devices: 26.2 us -> 124 us  [shards(): lax.psum_scatter(misfit, 'sensors', scatter_dimension=0, axis_index_group...]
    ppermute x36 -> x0, starting transfers between devices: 47.3 us -> none  [the longest x18 23.8 us: gather_line(): ups.append(lax.ppermute(ups[-1], 'sensors', onward))]
    pallas_call x6 -> x4, Pallas kernels: 90.2 us -> 58.7 us  [pull_back(): call(pull_kernel, core, (rows // CHUNK_ROWS,), [whole_block(array) for ar...]
    pallas_call x6 -> x4, Pallas kernels: 95.7 us -> 69.7 us  [observe(): call(observe_kernel, core, (rows // CHUNK_ROWS,), [pl.BlockSpec(block, la...]
    ppermute x19 -> x13, starting transfers between devices: 30.4 us -> 9.28 us  [swap_cores(): return lax.ppermute(value, 'sensors', [(k, k ^ 1) for k in range(size)])]
    unnamed x71 -> x65, local copies, waits for them, and re-layouts: 20.4 us -> 32.6 us
  transfers between devices with their start and end apart: 111 -> 55, of which waited for: 60 -> 34; matrix products, arithmetic and copies ran while one was open for 2% -> 3% of each run, Pallas kernels for 22% -> 26%
where the time goes in v3:
time: 610 us; the launch traced here: 608 us
  waiting for transfers between devices  282 us (46%)
  Pallas kernels  166 us (27%)
  starting transfers between devices  82.2 us (13%)
  local copies, waits for them, and re-layouts  58 us (10%)
  between operations  14.9 us (2%)
    reduce_scatter x4, waiting for transfers between devices, shards(): lax.psum_scatter(misfit, 'sensors', scatter_dimension=0, axis_index_group...  124 us
    all_gather x4, waiting for transfers between devices, shards(): lax.all_gather(jnp.stack([keep, swap_cores(give)]), 'sensors', axis_index...  113 us
    pallas_call x4, Pallas kernels, observe(): call(observe_kernel, core, (rows // CHUNK_ROWS,), [pl.BlockSpec(block, la...  69.7 us
    pallas_call x4, Pallas kernels, pull_back(): call(pull_kernel, core, (rows // CHUNK_ROWS,), [whole_block(array) for ar...  58.7 us
    unnamed x65, local copies, waits for them, and re-layouts  32.6 us
    ppermute x7, starting transfers between devices, rims(): lax.ppermute(bottom, 'cells', onward)  26.8 us
    ppermute x8, starting transfers between devices, misfit_rims(): return (lax.ppermute(edge, both, same), lax.ppermute(edge, both, cross))  25.5 us
    ppermute x12, waiting for transfers between devices, from_all_cells(): lax.ppermute(value, 'cells', [(k, k ^ other) for k in range(size)])  17.9 us
  transfers between devices with their start and end apart: 55, of which 34 were waited for; matrix products, arithmetic and copies ran while one was open for 3% of the time, Pallas kernels for 26%

profile of v3, /device:TPU:1, one launch (start us, length us, event | category | flops | bytes accessed | tf_op | source)
XLA Modules:
  0.0 608.0 jit_solution(4212003607844844821)
XLA Ops:
  7.3 14.4 %constant_dynamic-slice_fusion = bf16[2,128,16,2048]{3,2,1,0:T(8,128)(2,1)} fusion(bf16[2,128,16,4096]{3,2,1,0:T(8,128)(2,1)} %refs_5_.7, s32[]{:T(128)S(6)} %select_n.54), kind=kLoop, calls=%fused_computation.51 | loop fusion | bytes 33554436 | tf_op jit(solution)/shard_map/dynamic_slice | solution.py:493
  21.7 4.6 collective-permute-start.2
  29.5 4.0 collective-permute-start.25
  35.1 5.1 collective-permute-done.26.down_ref
  40.2 6.2 %start.3 = (f32[3,32,32,128]{3,2,1,0:T(8,128)S(1)}, bf16[3,16,32,128]{3,2,1,0:T(8,128)(2,1)S(1)}, bf16[3,16,32,128]{3,2,1,0:T(8,128)(2,1)S(1)}, f32[3,32,32,128]...) custom-call(s32[1]{0:T(128)} %bitcast.core_ref, ...), custom_call_target="tpu_custom_call" | custom-call | tf_op jit(solution)/shard_map/start/pallas_call | solution.py:154
  53.0 4.4 collective-permute-start
  64.9 6.1 %start.2 = (f32[3,32,32,128]{3,2,1,0:T(8,128)S(1)}, bf16[3,16,32,128]{3,2,1,0:T(8,128)(2,1)S(1)}, bf16[3,16,32,128]{3,2,1,0:T(8,128)(2,1)S(1)}, f32[3,32,32,128]...) custom-call(s32[1]{0:T(128)} %bitcast.core_ref, ...), custom_call_target="tpu_custom_call" | custom-call | tf_op jit(solution)/shard_map/start/pallas_call | solution.py:154
  77.5 40.3 %all-gather.13.cloned.1.call-done = bf16[8,3,16,32,128]{4,3,2,1,0:T(8,128)(2,1)} async-done(((bf16[2,3,16,32,128]{4,3,2,1,0:T(8,128)(2,1)}), bf16[8,3,16,32,128]{4,3,2,1,0:T(8,128)(2,1)}) %all-gather.13.cloned.1.call-update) | async-done | bytes 3145744 | tf_op jit(solution)/shard_map/all_gather | solution.py:542
  119.8 17.5 %observe.6 = f32[2,2,3,16,128]{4,3,2,1,0:T(8,128)S(1)} custom-call(s32[1]{0:T(128)} %bitcast.core_ref, bf16[4,2,3,16,32,128]{5,4,3,2,1,0:T(8,128)(2,1)S(1)} %bitcast.67, bf16[2,128,16,4096]{3,2,1,0:T(8,128)(2,1)} %refs_5_.7, bf16[2,128,16,2048]{3,2,1,0:T(8,128)(2,1)} %collective-permute-done.7.refs_2_.refs_6_, bf16[256,256]{1,0:T(8,128)(2,1)S(1)} %copy.16.refs_3_, ...), custom_call_target="tpu_custom_call" | custom-call | flops 402653184 | bytes 36700160 | tf_op jit(solution)/shard_map/observe/pallas_call | solution.py:355
  146.3 14.6 %pull_back.6 = bf16[4,2,3,16,32,128]{5,4,3,2,1,0:T(8,128)(2,1)S(1)} custom-call(s32[1]{0:T(128)} %bitcast.core_ref, f32[2,2,3,16,128]{4,3,2,1,0:T(8,128)S(1)} %reverse_add_fusion.1.refs_0_, f32[2,2,3,16,128]{4,3,2,1,0:T(8,128)S(1)} %collective-permute-done.31.refs_1_, f32[2,2,3,16,128]{4,3,2,1,0:T(8,128)S(1)} %collective-permute-done.32.refs_2_, ...), custom_call_target="tpu_custom_call" | custom-call | flops 402653184 | bytes 36700160 | tf_op jit(solution)/shard_map/pull_back/pallas_call | solution.py:427
  162.9 19.3 %all-gather.9.cloned.1.call-done = bf16[8,3,16,32,128]{4,3,2,1,0:T(8,128)(2,1)} async-done(((bf16[2,3,16,32,128]{4,3,2,1,0:T(8,128)(2,1)}), bf16[8,3,16,32,128]{4,3,2,1,0:T(8,128)(2,1)}) %all-gather.9.cloned.1.call-update) | async-done | bytes 3145744 | tf_op jit(solution)/shard_map/all_gather | solution.py:542
  184.0 17.3 %observe.4 = f32[2,2,3,16,128]{4,3,2,1,0:T(8,128)S(1)} custom-call(s32[1]{0:T(128)} %bitcast.core_ref, bf16[4,2,3,16,32,128]{5,4,3,2,1,0:T(8,128)(2,1)S(1)} %bitcast.66, bf16[2,128,16,4096]{3,2,1,0:T(8,128)(2,1)} %refs_5_.7, bf16[2,128,16,2048]{3,2,1,0:T(8,128)(2,1)} %collective-permute-done.7.refs_2_.refs_6_, bf16[256,256]{1,0:T(8,128)(2,1)S(1)} %copy.16.refs_3_, ...), custom_call_target="tpu_custom_call" | custom-call | flops 402653184 | bytes 36700160 | tf_op jit(solution)/shard_map/observe/pallas_call | solution.py:355
  210.4 14.7 %pull_back.4 = bf16[4,2,3,16,32,128]{5,4,3,2,1,0:T(8,128)(2,1)S(1)} custom-call(s32[1]{0:T(128)} %bitcast.core_ref, f32[2,2,3,16,128]{4,3,2,1,0:T(8,128)S(1)} %reverse_add_fusion.3.refs_0_, f32[2,2,3,16,128]{4,3,2,1,0:T(8,128)S(1)} %collective-permute-done.9.refs_1_, f32[2,2,3,16,128]{4,3,2,1,0:T(8,128)S(1)} %collective-permute-done.10.refs_2_, ...), custom_call_target="tpu_custom_call" | custom-call | flops 402653184 | bytes 36700160 | tf_op jit(solution)/shard_map/pull_back/pallas_call | solution.py:427
  226.8 17.0 %reduce-scatter.9.cloned.1.call-done = bf16[1,2,3,16,32,128]{5,4,3,2,1,0:T(8,128)(2,1)} async-done(((bf16[4,2,3,16,32,128]{5,4,3,2,1,0:T(8,128)(2,1)}), bf16[1,2,3,16,32,128]{5,4,3,2,1,0:T(8,128)(2,1)}) %reduce-scatter.9.cloned.1.call-update) | async-done | bytes 786448 | tf_op jit(solution)/shard_map/reduce_scatter | solution.py:549
  252.0 4.0 collective-permute-start.35
  265.2 7.3 %step.3 = (f32[3,32,32,128]{3,2,1,0:T(8,128)S(1)}, bf16[3,16,32,128]{3,2,1,0:T(8,128)(2,1)S(1)}, bf16[3,16,32,128]{3,2,1,0:T(8,128)(2,1)S(1)}, f32[3,32,32,128]{...) custom-call(s32[1]{0:T(128)} %bitcast.core_ref, ...), custom_call_target="tpu_custom_call" | custom-call | tf_op jit(solution)/shard_map/step/pallas_call | solution.py:206
  278.2 28.7 %reduce-scatter.5.cloned.1.call-done = bf16[1,2,3,16,32,128]{5,4,3,2,1,0:T(8,128)(2,1)} async-done(((bf16[4,2,3,16,32,128]{5,4,3,2,1,0:T(8,128)(2,1)}), bf16[1,2,3,16,32,128]{5,4,3,2,1,0:T(8,128)(2,1)}) %reduce-scatter.5.cloned.1.call-update) | async-done | bytes 786448 | tf_op jit(solution)/shard_map/reduce_scatter | solution.py:549
  314.3 4.0 collective-permute-start.13
  326.1 6.4 %step.2 = (f32[3,32,32,128]{3,2,1,0:T(8,128)S(1)}, bf16[3,16,32,128]{3,2,1,0:T(8,128)(2,1)S(1)}, bf16[3,16,32,128]{3,2,1,0:T(8,128)(2,1)S(1)}, f32[3,32,32,128]{...) custom-call(s32[1]{0:T(128)} %bitcast.core_ref, ...), custom_call_target="tpu_custom_call" | custom-call | tf_op jit(solution)/shard_map/step/pallas_call | solution.py:206
  338.2 34.3 %all-gather.15.cloned.1.call-done = bf16[8,3,16,32,128]{4,3,2,1,0:T(8,128)(2,1)} async-done(((bf16[2,3,16,32,128]{4,3,2,1,0:T(8,128)(2,1)}), bf16[8,3,16,32,128]{4,3,2,1,0:T(8,128)(2,1)}) %all-gather.15.cloned.1.call-update) | async-done | bytes 3145744 | tf_op jit(solution)/shard_map/all_gather | solution.py:542
  374.5 17.5 %observe.7 = f32[2,2,3,16,128]{4,3,2,1,0:T(8,128)S(1)} custom-call(s32[1]{0:T(128)} %bitcast.core_ref, bf16[4,2,3,16,32,128]{5,4,3,2,1,0:T(8,128)(2,1)S(1)} %bitcast.68, bf16[2,128,16,4096]{3,2,1,0:T(8,128)(2,1)} %refs_5_.7, bf16[2,128,16,2048]{3,2,1,0:T(8,128)(2,1)} %collective-permute-done.7.refs_2_.refs_6_, bf16[256,256]{1,0:T(8,128)(2,1)S(1)} %copy.16.refs_3_, ...), custom_call_target="tpu_custom_call" | custom-call | flops 402653184 | bytes 36700160 | tf_op jit(solution)/shard_map/observe/pallas_call | solution.py:355
  400.9 14.6 %pull_back.7 = bf16[4,2,3,16,32,128]{5,4,3,2,1,0:T(8,128)(2,1)S(1)} custom-call(s32[1]{0:T(128)} %bitcast.core_ref, f32[2,2,3,16,128]{4,3,2,1,0:T(8,128)S(1)} %reverse_add_fusion.refs_0_, f32[2,2,3,16,128]{4,3,2,1,0:T(8,128)S(1)} %collective-permute-done.41.refs_1_, f32[2,2,3,16,128]{4,3,2,1,0:T(8,128)S(1)} %collective-permute-done.42.refs_2_, ...), custom_call_target="tpu_custom_call" | custom-call | flops 402653184 | bytes 36700160 | tf_op jit(solution)/shard_map/pull_back/pallas_call | solution.py:427
  417.6 19.2 %all-gather.11.cloned.1.call-done = bf16[8,3,16,32,128]{4,3,2,1,0:T(8,128)(2,1)} async-done(((bf16[2,3,16,32,128]{4,3,2,1,0:T(8,128)(2,1)}), bf16[8,3,16,32,128]{4,3,2,1,0:T(8,128)(2,1)}) %all-gather.11.cloned.1.call-update) | async-done | bytes 3145744 | tf_op jit(solution)/shard_map/all_gather | solution.py:542
  438.6 17.3 %observe.5 = f32[2,2,3,16,128]{4,3,2,1,0:T(8,128)S(1)} custom-call(s32[1]{0:T(128)} %bitcast.core_ref, bf16[4,2,3,16,32,128]{5,4,3,2,1,0:T(8,128)(2,1)S(1)} %bitcast.69, bf16[2,128,16,4096]{3,2,1,0:T(8,128)(2,1)} %refs_5_.7, bf16[2,128,16,2048]{3,2,1,0:T(8,128)(2,1)} %collective-permute-done.7.refs_2_.refs_6_, bf16[256,256]{1,0:T(8,128)(2,1)S(1)} %copy.16.refs_3_, ...), custom_call_target="tpu_custom_call" | custom-call | flops 402653184 | bytes 36700160 | tf_op jit(solution)/shard_map/observe/pallas_call | solution.py:355
  464.5 14.7 %pull_back.5 = bf16[4,2,3,16,32,128]{5,4,3,2,1,0:T(8,128)(2,1)S(1)} custom-call(s32[1]{0:T(128)} %bitcast.core_ref, f32[2,2,3,16,128]{4,3,2,1,0:T(8,128)S(1)} %reverse_add_fusion.2.refs_0_, f32[2,2,3,16,128]{4,3,2,1,0:T(8,128)S(1)} %collective-permute-done.19.refs_1_, f32[2,2,3,16,128]{4,3,2,1,0:T(8,128)S(1)} %collective-permute-done.20.refs_2_, ...), custom_call_target="tpu_custom_call" | custom-call | flops 402653184 | bytes 36700160 | tf_op jit(solution)/shard_map/pull_back/pallas_call | solution.py:427
  480.9 17.5 %reduce-scatter.11.cloned.1.call-done = bf16[1,2,3,16,32,128]{5,4,3,2,1,0:T(8,128)(2,1)} async-done(((bf16[4,2,3,16,32,128]{5,4,3,2,1,0:T(8,128)(2,1)}), bf16[1,2,3,16,32,128]{5,4,3,2,1,0:T(8,128)(2,1)}) %reduce-scatter.11.cloned.1.call-update) | async-done | bytes 786448 | tf_op jit(solution)/shard_map/reduce_scatter | solution.py:549
  501.2 60.4 %reduce-scatter.7.cloned.1.call-done = bf16[1,2,3,16,32,128]{5,4,3,2,1,0:T(8,128)(2,1)} async-done(((bf16[4,2,3,16,32,128]{5,4,3,2,1,0:T(8,128)(2,1)}), bf16[1,2,3,16,32,128]{5,4,3,2,1,0:T(8,128)(2,1)}) %reduce-scatter.7.cloned.1.call-update) | async-done | bytes 786448 | tf_op jit(solution)/shard_map/reduce_scatter | solution.py:549
  569.3 4.0 collective-permute-start.45
  576.9 4.5 collective-permute-start.15
  582.7 4.0 collective-permute-start.23
  589.0 6.0 finish.2
  595.1 6.1 finish.3
  (210 shorter events, 137.0 us)
Async XLA Ops:
  7.2 110.6 %all-gather.13.cloned.1.call-start = ((), (), s32[]{:S(2)}) async-start(), calls=%async_computation.10 | async-start | bytes 3932160 | tf_op jit(solution)/shard_map/all_gather | solution.py:542
  21.7 96.2 %collective-permute-start.7 = (bf16[2,128,16,2048]{3,2,1,0:T(8,128)(2,1)}, bf16[2,128,16,2048]{3,2,1,0:T(8,128)(2,1)}, u32[]{:S(2)}, u32[]{:S(2)}) collective-permute-start(bf16[2,128,16,2048]{3,2,1,0:T(8,128)(2,1)} %constant_dynamic-slice_fusion), channel_id=1, source_target_pairs={{0,1},{1,0},{2,3},{3,2},{4,5},{5,4},{6,7},{7,6},{8,9},{9,8},{10,11... | collective-permute-start | bytes 50331656 | tf_op jit(solution)/shard_map/ppermute | solution.py:469
  21.7 13.1 %collective-permute-start.2 = (f32[2,4,128]{2,1,0:T(4,128)S(1)}, f32[2,4,128]{2,1,0:T(4,128)S(1)}, u32[]{:S(2)}, u32[]{:S(2)}) collective-permute-start(f32[2,4,128]{2,1,0:T(4,128)S(1)} %get-tuple-element.83), channel_id=1, source_target_pairs={{0,8},{8,16},{16,24},{1,9},{9,17},{17,25},{2,10},{10,18},{18,26},{... | collective-permute-start | bytes 12296 | tf_op jit(solution)/shard_map/ppermute | solution.py:451
  26.3 8.5 %collective-permute-start.3 = (f32[2,4,128]{2,1,0:T(4,128)S(1)}, f32[2,4,128]{2,1,0:T(4,128)S(1)}, u32[]{:S(2)}, u32[]{:S(2)}) collective-permute-start(f32[2,4,128]{2,1,0:T(4,128)S(1)} %get-tuple-element.84), channel_id=1, source_target_pairs={{8,0},{16,8},{24,16},{9,1},{17,9},{25,17},{10,2},{18,10},{26,18},{... | collective-permute-start | bytes 12296 | tf_op jit(solution)/shard_map/ppermute | solution.py:451
  33.5 6.7 %collective-permute-start.26 = (bf16[3,4,32,128]{3,2,1,0:T(8,128)(2,1)S(1)}, bf16[3,4,32,128]{3,2,1,0:T(8,128)(2,1)S(1)}, u32[]{:S(2)}, u32[]{:S(2)}) collective-permute-start(bf16[3,4,32,128]{3,2,1,0:T(8,128)(2,1)S(1)} %get-tuple-element.60), channel_id=1, source_target_pairs={{8,0},{16,8},{24,16},{9,1},{17,9},{25,17},{10,2},{18,10},{26,18},{... | collective-permute-start | bytes 294920 | tf_op jit(solution)/shard_map/ppermute | solution.py:451
  53.0 129.2 %all-gather.9.cloned.1.call-start = ((), (), s32[]{:S(2)}) async-start(), calls=%async_computation.8 | async-start | bytes 3932160 | tf_op jit(solution)/shard_map/all_gather | solution.py:542
  76.1 167.8 %reduce-scatter.9.cloned.1.call-start = ((), (), s32[]{:S(2)}) async-start(), calls=%async_computation.6 | async-start | bytes 3932160 | tf_op jit(solution)/shard_map/reduce_scatter | solution.py:549
  162.6 144.3 %reduce-scatter.5.cloned.1.call-start = ((), (), s32[]{:S(2)}) async-start(), calls=%async_computation.4 | async-start | bytes 3932160 | tf_op jit(solution)/shard_map/reduce_scatter | solution.py:549
  226.8 145.8 %all-gather.15.cloned.1.call-start = ((), (), s32[]{:S(2)}) async-start(), calls=%async_computation.11 | async-start | bytes 3932160 | tf_op jit(solution)/shard_map/all_gather | solution.py:542
  245.8 16.5 %collective-permute-start.34 = (bf16[3,16,32,128]{3,2,1,0:T(8,128)(2,1)}, bf16[3,16,32,128]{3,2,1,0:T(8,128)(2,1)}, u32[]{:S(2)}, u32[]{:S(2)}) collective-permute-start(bf16[3,16,32,128]{3,2,1,0:T(8,128)(2,1)} %get-tuple-element.70), channel_id=1, source_target_pairs={{0,1},{1,0},{2,3},{3,2},{4,5},{5,4},{6,7},{7,6},{8,9},{9,8},{10,11... | collective-permute-start | bytes 1179656 | tf_op jit(solution)/shard_map/ppermute | solution.py:469
  246.6 11.7 %collective-permute-start.27 = (bf16[3,4,32,128]{3,2,1,0:T(8,128)(2,1)}, bf16[3,4,32,128]{3,2,1,0:T(8,128)(2,1)S(1)}, u32[]{:S(2)}, u32[]{:S(2)}) collective-permute-start(bf16[3,4,32,128]{3,2,1,0:T(8,128)(2,1)} %copy-done.24), channel_id=1, source_target_pairs={{0,8},{8,16},{16,24},{1,9},{9,17},{17,25},{2,10},{10,18},{18,26},{... | collective-permute-start | bytes 294920 | tf_op jit(solution)/shard_map/ppermute | solution.py:451
  249.7 8.7 %collective-permute-start.28 = (bf16[3,4,32,128]{3,2,1,0:T(8,128)(2,1)S(1)}, bf16[3,4,32,128]{3,2,1,0:T(8,128)(2,1)S(1)}, u32[]{:S(2)}, u32[]{:S(2)}) collective-permute-start(bf16[3,4,32,128]{3,2,1,0:T(8,128)(2,1)S(1)} %get-tuple-element.44), channel_id=1, source_target_pairs={{8,0},{16,8},{24,16},{9,1},{17,9},{25,17},{10,2},{18,10},{26,18},{... | collective-permute-start | bytes 294920 | tf_op jit(solution)/shard_map/ppermute | solution.py:451
  252.0 6.4 %collective-permute-start.35 = (bf16[3,4,32,128]{3,2,1,0:T(8,128)(2,1)S(1)}, bf16[3,4,32,128]{3,2,1,0:T(8,128)(2,1)S(1)}, u32[]{:S(2)}, u32[]{:S(2)}) collective-permute-start(bf16[3,4,32,128]{3,2,1,0:T(8,128)(2,1)S(1)} %get-tuple-element.69), channel_id=1, source_target_pairs={{1,9},{3,11},{5,13},{7,15},{8,0},{9,17},{10,2},{11,19},{12,4},{13,... | collective-permute-start | bytes 294920 | tf_op jit(solution)/shard_map/ppermute | solution.py:464
  256.0 6.3 %collective-permute-start.36 = (bf16[3,4,32,128]{3,2,1,0:T(8,128)(2,1)S(1)}, bf16[3,4,32,128]{3,2,1,0:T(8,128)(2,1)S(1)}, u32[]{:S(2)}, u32[]{:S(2)}) collective-permute-start(bf16[3,4,32,128]{3,2,1,0:T(8,128)(2,1)S(1)} %get-tuple-element.68), channel_id=1, source_target_pairs={{1,8},{3,10},{5,12},{7,14},{8,1},{9,16},{10,3},{11,18},{12,5},{13,... | collective-permute-start | bytes 294920 | tf_op jit(solution)/shard_map/ppermute | solution.py:464
  278.2 158.6 %all-gather.11.cloned.1.call-start = ((), (), s32[]{:S(2)}) async-start(), calls=%async_computation.9 | async-start | bytes 3932160 | tf_op jit(solution)/shard_map/all_gather | solution.py:542
  308.1 16.6 %collective-permute-start.12 = (bf16[3,16,32,128]{3,2,1,0:T(8,128)(2,1)S(1)}, bf16[3,16,32,128]{3,2,1,0:T(8,128)(2,1)S(1)}, u32[]{:S(2)}, u32[]{:S(2)}) collective-permute-start(bf16[3,16,32,128]{3,2,1,0:T(8,128)(2,1)S(1)} %get-tuple-element.78), channel_id=1, source_target_pairs={{0,1},{1,0},{2,3},{3,2},{4,5},{5,4},{6,7},{7,6},{8,9},{9,8},{10,11... | collective-permute-start | bytes 1179656 | tf_op jit(solution)/shard_map/ppermute | solution.py:469
  309.0 11.8 %collective-permute-start.4 = (bf16[3,4,32,128]{3,2,1,0:T(8,128)(2,1)S(1)}, bf16[3,4,32,128]{3,2,1,0:T(8,128)(2,1)S(1)}, u32[]{:S(2)}, u32[]{:S(2)}) collective-permute-start(bf16[3,4,32,128]{3,2,1,0:T(8,128)(2,1)S(1)} %get-tuple-element.30), channel_id=1, source_target_pairs={{0,8},{8,16},{16,24},{1,9},{9,17},{17,25},{2,10},{10,18},{18,26},{... | collective-permute-start | bytes 294920 | tf_op jit(solution)/shard_map/ppermute | solution.py:451
  312.1 8.7 %collective-permute-start.5 = (bf16[3,4,32,128]{3,2,1,0:T(8,128)(2,1)S(1)}, bf16[3,4,32,128]{3,2,1,0:T(8,128)(2,1)S(1)}, u32[]{:S(2)}, u32[]{:S(2)}) collective-permute-start(bf16[3,4,32,128]{3,2,1,0:T(8,128)(2,1)S(1)} %get-tuple-element.32), channel_id=1, source_target_pairs={{8,0},{16,8},{24,16},{9,1},{17,9},{25,17},{10,2},{18,10},{26,18},{... | collective-permute-start | bytes 294920 | tf_op jit(solution)/shard_map/ppermute | solution.py:451
  314.3 6.4 %collective-permute-start.13 = (bf16[3,4,32,128]{3,2,1,0:T(8,128)(2,1)S(1)}, bf16[3,4,32,128]{3,2,1,0:T(8,128)(2,1)S(1)}, u32[]{:S(2)}, u32[]{:S(2)}) collective-permute-start(bf16[3,4,32,128]{3,2,1,0:T(8,128)(2,1)S(1)} %get-tuple-element.77), channel_id=1, source_target_pairs={{1,9},{3,11},{5,13},{7,15},{8,0},{9,17},{10,2},{11,19},{12,4},{13,... | collective-permute-start | bytes 294920 | tf_op jit(solution)/shard_map/ppermute | solution.py:464
  318.3 6.3 %collective-permute-start.14 = (bf16[3,4,32,128]{3,2,1,0:T(8,128)(2,1)S(1)}, bf16[3,4,32,128]{3,2,1,0:T(8,128)(2,1)S(1)}, u32[]{:S(2)}, u32[]{:S(2)}) collective-permute-start(bf16[3,4,32,128]{3,2,1,0:T(8,128)(2,1)S(1)} %get-tuple-element.76), channel_id=1, source_target_pairs={{1,8},{3,10},{5,12},{7,14},{8,1},{9,16},{10,3},{11,18},{12,5},{13,... | collective-permute-start | bytes 294920 | tf_op jit(solution)/shard_map/ppermute | solution.py:464
  338.2 160.3 %reduce-scatter.11.cloned.1.call-start = ((), (), s32[]{:S(2)}) async-start(), calls=%async_computation.7 | async-start | bytes 3932160 | tf_op jit(solution)/shard_map/reduce_scatter | solution.py:549
  417.3 144.3 %reduce-scatter.7.cloned.1.call-start = ((), (), s32[]{:S(2)}) async-start(), calls=%async_computation.5 | async-start | bytes 3932160 | tf_op jit(solution)/shard_map/reduce_scatter | solution.py:549
  500.4 86.4 %collective-permute-start.44 = (bf16[3,16,32,128]{3,2,1,0:T(8,128)(2,1)}, bf16[3,16,32,128]{3,2,1,0:T(8,128)(2,1)S(1)}, u32[]{:S(2)}, u32[]{:S(2)}) collective-permute-start(bf16[3,16,32,128]{3,2,1,0:T(8,128)(2,1)} %get-tuple-element.66), channel_id=1, source_target_pairs={{0,1},{1,0},{2,3},{3,2},{4,5},{5,4},{6,7},{7,6},{8,9},{9,8},{10,11... | collective-permute-start | bytes 1179656 | tf_op jit(solution)/shard_map/ppermute | solution.py:469
  562.9 32.1 %collective-permute-start.22 = (bf16[3,16,32,128]{3,2,1,0:T(8,128)(2,1)S(1)}, bf16[3,16,32,128]{3,2,1,0:T(8,128)(2,1)S(1)}, u32[]{:S(2)}, u32[]{:S(2)}) collective-permute-start(bf16[3,16,32,128]{3,2,1,0:T(8,128)(2,1)S(1)} %get-tuple-element.74), channel_id=1, source_target_pairs={{0,1},{1,0},{2,3},{3,2},{4,5},{5,4},{6,7},{7,6},{8,9},{9,8},{10,11... | collective-permute-start | bytes 1179656 | tf_op jit(solution)/shard_map/ppermute | solution.py:469
  563.8 9.5 %collective-permute-start.37 = (bf16[3,4,32,128]{3,2,1,0:T(8,128)(2,1)S(1)}, bf16[3,4,32,128]{3,2,1,0:T(8,128)(2,1)S(1)}, u32[]{:S(2)}, u32[]{:S(2)}) collective-permute-start(bf16[3,4,32,128]{3,2,1,0:T(8,128)(2,1)S(1)} %copy-done.26), channel_id=1, source_target_pairs={{0,8},{8,16},{16,24},{1,9},{9,17},{17,25},{2,10},{10,18},{18,26},{... | collective-permute-start | bytes 294920 | tf_op jit(solution)/shard_map/ppermute | solution.py:451
  567.1 9.8 %collective-permute-start.38 = (bf16[3,4,32,128]{3,2,1,0:T(8,128)(2,1)S(1)}, bf16[3,4,32,128]{3,2,1,0:T(8,128)(2,1)S(1)}, u32[]{:S(2)}, u32[]{:S(2)}) collective-permute-start(bf16[3,4,32,128]{3,2,1,0:T(8,128)(2,1)S(1)} %get-tuple-element.50), channel_id=1, source_target_pairs={{8,0},{16,8},{24,16},{9,1},{17,9},{25,17},{10,2},{18,10},{26,18},{... | collective-permute-start | bytes 294920 | tf_op jit(solution)/shard_map/ppermute | solution.py:451
  569.3 12.1 %collective-permute-start.45 = (bf16[3,4,32,128]{3,2,1,0:T(8,128)(2,1)S(1)}, bf16[3,4,32,128]{3,2,1,0:T(8,128)(2,1)S(1)}, u32[]{:S(2)}, u32[]{:S(2)}) collective-permute-start(bf16[3,4,32,128]{3,2,1,0:T(8,128)(2,1)S(1)} %get-tuple-element.65), channel_id=1, source_target_pairs={{1,9},{3,11},{5,13},{7,15},{8,0},{9,17},{10,2},{11,19},{12,4},{13,... | collective-permute-start | bytes 294920 | tf_op jit(solution)/shard_map/ppermute | solution.py:464
  573.3 9.4 %collective-permute-start.46 = (bf16[3,4,32,128]{3,2,1,0:T(8,128)(2,1)S(1)}, bf16[3,4,32,128]{3,2,1,0:T(8,128)(2,1)S(1)}, u32[]{:S(2)}, u32[]{:S(2)}) collective-permute-start(bf16[3,4,32,128]{3,2,1,0:T(8,128)(2,1)S(1)} %get-tuple-element.64), channel_id=1, source_target_pairs={{1,8},{3,10},{5,12},{7,14},{8,1},{9,16},{10,3},{11,18},{12,5},{13,... | collective-permute-start | bytes 294920 | tf_op jit(solution)/shard_map/ppermute | solution.py:464
  576.9 18.2 %collective-permute-start.15 = (bf16[3,4,32,128]{3,2,1,0:T(8,128)(2,1)}, bf16[3,4,32,128]{3,2,1,0:T(8,128)(2,1)S(1)}, u32[]{:S(2)}, u32[]{:S(2)}) collective-permute-start(bf16[3,4,32,128]{3,2,1,0:T(8,128)(2,1)} %copy-done.27), channel_id=1, source_target_pairs={{0,8},{8,16},{16,24},{1,9},{9,17},{17,25},{2,10},{10,18},{18,26},{... | collective-permute-start | bytes 294920 | tf_op jit(solution)/shard_map/ppermute | solution.py:451
  581.4 13.6 %collective-permute-start.16 = (bf16[3,4,32,128]{3,2,1,0:T(8,128)(2,1)S(1)}, bf16[3,4,32,128]{3,2,1,0:T(8,128)(2,1)S(1)}, u32[]{:S(2)}, u32[]{:S(2)}) collective-permute-start(bf16[3,4,32,128]{3,2,1,0:T(8,128)(2,1)S(1)} %get-tuple-element.38), channel_id=1, source_target_pairs={{8,0},{16,8},{24,16},{9,1},{17,9},{25,17},{10,2},{18,10},{26,18},{... | collective-permute-start | bytes 294920 | tf_op jit(solution)/shard_map/ppermute | solution.py:451
  582.7 12.3 %collective-permute-start.23 = (bf16[3,4,32,128]{3,2,1,0:T(8,128)(2,1)S(1)}, bf16[3,4,32,128]{3,2,1,0:T(8,128)(2,1)S(1)}, u32[]{:S(2)}, u32[]{:S(2)}) collective-permute-start(bf16[3,4,32,128]{3,2,1,0:T(8,128)(2,1)S(1)} %get-tuple-element.73), channel_id=1, source_target_pairs={{1,9},{3,11},{5,13},{7,15},{8,0},{9,17},{10,2},{11,19},{12,4},{13,... | collective-permute-start | bytes 294920 | tf_op jit(solution)/shard_map/ppermute | solution.py:464
  586.7 8.3 %collective-permute-start.24 = (bf16[3,4,32,128]{3,2,1,0:T(8,128)(2,1)S(1)}, bf16[3,4,32,128]{3,2,1,0:T(8,128)(2,1)S(1)}, u32[]{:S(2)}, u32[]{:S(2)}) collective-permute-start(bf16[3,4,32,128]{3,2,1,0:T(8,128)(2,1)S(1)} %get-tuple-element.72), channel_id=1, source_target_pairs={{1,8},{3,10},{5,12},{7,14},{8,1},{9,16},{10,3},{11,18},{12,5},{13,... | collective-permute-start | bytes 294920 | tf_op jit(solution)/shard_map/ppermute | solution.py:464
  (55 other events, 485.8 us)
Sparse Core Ops, SparseCore 0:
  53.1 64.6 all-gather.12
  119.9 62.1 all-gather.8
  185.0 58.7 reduce-scatter.8
  246.6 60.2 reduce-scatter.4
  308.9 63.6 all-gather.14
  374.6 62.1 all-gather.10
  439.6 58.7 reduce-scatter.10
  501.3 60.2 reduce-scatter.6

commit v4 on v2

--- a/solution.py
+++ b/solution.py
@@ -483,16 +483,37 @@
     ]
 
 
-def gather_line(value):
-    size = lax.axis_size("sensors")
-    chips = size // 2
-    ups, downs = [value], [value]
-    for hop in range(1, chips):
-        onward = [(k, k + 2) for k in range(2 * hop - 2, size - 2)]
-        backward = [(size - 1 - k, size - 1 - there) for k, there in onward]
-        ups.append(lax.ppermute(ups[-1], "sensors", onward))
-        downs.append(lax.ppermute(downs[-1], "sensors", backward))
-    return [value, *ups[1:], *downs[1:]]
+class Line:
+    def __init__(self, value):
+        self.size = lax.axis_size("sensors")
+        self.value, self.ups, self.downs = value, [], []
+        self.ends = (value, value)
+
+    def hop(self, last=False):
+        while len(self.ups) < self.size // 2 - 1:
+            start = 2 * len(self.ups)
+            onward = [(k, k + 2) for k in range(start, self.size - 2)]
+            backward = [(self.size - 1 - k, self.size - 1 - there) for k, there in onward]
+            self.sent = self.ends
+            up = lax.ppermute(self.ends[0], "sensors", onward)
+            down = lax.ppermute(self.ends[1], "sensors", backward)
+            self.ups.append(up)
+            self.downs.append(down)
+            self.ends = (up, down)
+            if not last:
+                break
+
+    def after(self, other):
+        if other is not None and self.ups:
+            self.ends, other = lax.optimization_barrier((self.ends, other))
+            self.ups[-1], self.downs[-1] = self.ends
+        return other
+
+    def mark(self):
+        return self.sent
+
+    def slots(self):
+        return [self.value, *self.ups, *self.downs]
 
 
 def shards(rhs, forward_map, stiffness, reaction, noise_weight, sensor_cell):
@@ -507,9 +528,6 @@
     near = LANES // sensors
     half = cells // 2
 
-    away = lax.dynamic_slice_in_dim(forward_map, (1 - core) * half, half, axis=3)
-    other_map = swap_cores(away)
-
     cores = jnp.stack([core, 1 - core])
     offsets = cores[None, :, None] * steps + jnp.arange(steps, dtype=jnp.int32)
     chip_steps = 2 * steps
@@ -540,41 +558,77 @@
     core = core.reshape(1)
 
     members = samples // GROUPS
+    top, bottom = (
+        jnp.transpose(rim, (1, 2, 0, 3)).astype(jnp.bfloat16)
+        for rim in (rhs[:, :, :HALO], rhs[:, :, rows - HALO :])
+    )
     states = []
     for group in range(GROUPS):
-        group_rhs = rhs[:, group * members : (group + 1) * members]
-        up, down = rims(
-            *(
-                jnp.transpose(rim, (1, 2, 0, 3)).astype(jnp.bfloat16)
-                for rim in (group_rhs[:, :, :HALO], group_rhs[:, :, rows - HALO :])
-            )
-        )
+        here = slice(group * members, (group + 1) * members)
+        up, down = rims(top[here], bottom[here])
         states.append(start(group, members, core, rhs, up, down, coeff))
+    there, *states[0] = lax.optimization_barrier(((1 - core[0]) * half, *states[0]))
+    other_map = swap_cores(lax.dynamic_slice_in_dim(forward_map, there, half, axis=3))
 
     lines = [[k for k in range(size) if k % 2 == parity] for parity in range(2)]
+    shape = (chips, 2, members, rows // 2, steps, cols)
+
+    def ready(state):
+        iterate, keep, give, rest, top, bottom = state
+        above, below = rims(top, bottom)
+        return iterate, jnp.stack([keep, swap_cores(give)]), (above, rest, below)
+
+    def edges(misfit):
+        first = (rows // 2 - HALO) * core[0]
+        edge = lax.dynamic_slice_in_dim(misfit, first, HALO, axis=2)
+        same, _ = misfit_rims(edge[0])
+        _, cross = misfit_rims(edge[1])
+        return misfit[0], swap_cores(misfit[1]), same, cross
+
+    items = [(iteration, group) for iteration in range(ITERS) for group in range(GROUPS)]
+    states = {k: ready(state) for k, state in enumerate(states)}
+    scattered = {}
     outputs = ()
-    for iteration in range(ITERS):
-        for group in range(GROUPS):
-            iterate, keep, give, rest, top, bottom = states[group]
-            above, below = rims(top, bottom)
-            slots = gather_line(jnp.stack([keep, swap_cores(give)]))
+    slots = None
+    for i in range(len(items) + 2):
+        line = None
+        if i < len(items):
+            here = states[i][1]
+            if slots is not None:
+                here, slots = lax.optimization_barrier((here, slots))
+            line = Line(here)
+            line.hop()
+        sums = None
+        if slots is not None:
             sums = observe(core, slots, forward_map, other_map, table, local_cells)
+        if line is not None:
+            sums = line.after(sums)
+            line.hop()
+        misfit = None
+        if sums is not None:
             sums = from_all_cells(sums + swap_cores(sums)[::-1])
-            shape = (chips, 2, members, rows // 2, steps, cols)
             misfit = pull_back(core, sums, noise, forward_map, other_map, back, local_cells, shape)
-            misfit = lax.psum_scatter(
+        if line is not None:
+            misfit = line.after(misfit)
+            line.hop(last=True)
+        if misfit is not None:
+            scattered[i - 1] = lax.psum_scatter(
                 misfit, "sensors", scatter_dimension=0, axis_index_groups=lines, tiled=False
             )
-            first = (rows // 2 - HALO) * core[0]
-            edge = lax.dynamic_slice_in_dim(misfit, first, HALO, axis=2)
-            same, _ = misfit_rims(edge[0])
-            _, cross = misfit_rims(edge[1])
-            misfits = (misfit[0], swap_cores(misfit[1]), same, cross)
-            rests = (above, rest, below)
+        done = i - 2
+        if done in scattered:
+            total = scattered.pop(done)
+            if line is not None:
+                total, _ = lax.optimization_barrier((total, line.mark()))
+            iteration, group = items[done]
+            iterate, _, rests = states.pop(done)
             if iteration < ITERS - 1:
-                states[group] = step(core, rests, misfits, iterate, coeff)
+                states[done + GROUPS] = ready(step(core, rests, edges(total), iterate, coeff))
             else:
-                outputs = finish(group, samples, core, rests, misfits, iterate, coeff, outputs)
+                outputs = finish(
+                    group, samples, core, rests, edges(total), iterate, coeff, outputs
+                )
+        slots = line.slots() if line is not None else None
     return tuple(out.reshape(rhs.shape) for out in outputs)
 
 

time: 856 us -> 747 us (0.87)
  waiting for transfers between devices: 377 us -> 234 us
  starting transfers between devices: 175 us -> 191 us
  local copies, waits for them, and re-layouts: 49.8 us -> 60.3 us
    ppermute x36, waiting for transfers between devices: 290 us -> 148 us  [the longest x18 137 us: hop(): down = lax.ppermute(self.ends[1], 'sensors', backward)]
    unnamed x71 -> x89, local copies, waits for them, and re-layouts: 20.4 us -> 25.7 us
  transfers between devices with their start and end apart: 111 -> 111, of which waited for: 60 -> 45; matrix products, arithmetic and copies ran while one was open for 2% -> 3% of each run, Pallas kernels for 22% -> 30%
where the time goes in v4:
time: 747 us; the launch traced here: 737 us
  waiting for transfers between devices  234 us (31%)
  Pallas kernels  229 us (31%)
  starting transfers between devices  191 us (26%)
  local copies, waits for them, and re-layouts  60.3 us (8%)
  between operations  16 us (2%)
    ppermute x18, waiting for transfers between devices, hop(): down = lax.ppermute(self.ends[1], 'sensors', backward)  137 us
    pallas_call x6, Pallas kernels, observe(): call(observe_kernel, core, (rows // CHUNK_ROWS,), [slot] * len(slots) + m...  97.3 us
    pallas_call x6, Pallas kernels, pull_back(): call(pull_kernel, core, (rows // CHUNK_ROWS,), [whole_block(array) for ar...  90.2 us
    ppermute x12, starting transfers between devices, misfit_rims(): return (lax.ppermute(edge, both, same), lax.ppermute(edge, both, cross))  37.5 us
    ppermute x10, starting transfers between devices, rims(): lax.ppermute(bottom, 'cells', onward)  36.2 us
    ppermute x19, starting transfers between devices, swap_cores(): return lax.ppermute(value, 'sensors', [(k, k ^ 1) for k in range(size)])  32.8 us
    reduce_scatter x6, waiting for transfers between devices, shards(): lax.psum_scatter(misfit, 'sensors', scatter_dimension=0, axis_index_group...  28.1 us
    ppermute x18, starting transfers between devices, hop(): up = lax.ppermute(self.ends[0], 'sensors', onward)  27.8 us
  transfers between devices with their start and end apart: 111, of which 45 were waited for; matrix products, arithmetic and copies ran while one was open for 3% of the time, Pallas kernels for 30%

profile of v4, /device:TPU:1, one launch (start us, length us, event | category | flops | bytes accessed | tf_op | source)
XLA Modules:
  0.0 736.7 jit_solution(91548776745442513)
XLA Ops:
  36.2 17.5 %constant_dynamic-slice_fusion = bf16[2,128,16,2048]{3,2,1,0:T(8,128)(2,1)} fusion(bf16[2,128,16,4096]{3,2,1,0:T(8,128)(2,1)} %refs_5_.11, s32[]{:T(128)S(6)} %select_n.74), kind=kLoop, calls=%fused_computation.73 | loop fusion | bytes 33554436 | tf_op jit(solution)/shard_map/dynamic_slice | solution.py:571
  55.7 6.5 collective-permute-done.13
  66.7 9.8 %collective-permute-done.14.refs_1_ = bf16[2,2,16,32,128]{4,3,2,1,0:T(8,128)(2,1)S(1)} collective-permute-done((bf16[2,2,16,32,128]{4,3,2,1,0:T(8,128)(2,1)S(1)}, bf16[2,2,16,32,128]{4,3,2,1,0:T(8,128)(2,1)S(1)}, u32[]{:S(2)}, u32[]{:S(2)}) %collective-permute-start.14) | collective-permute-done | bytes 524320 | tf_op jit(solution)/shard_map/ppermute | solution.py:498
  81.8 4.5 collective-permute-start.10
  93.7 4.8 start.5
  107.2 13.6 %collective-permute-done.19.refs_6_ = bf16[2,2,16,32,128]{4,3,2,1,0:T(8,128)(2,1)} collective-permute-done((bf16[2,2,16,32,128]{4,3,2,1,0:T(8,128)(2,1)}, bf16[2,2,16,32,128]{4,3,2,1,0:T(8,128)(2,1)}, u32[]{:S(2)}, u32[]{:S(2)}) %collective-permute-start.19) | collective-permute-done | bytes 524320 | tf_op jit(solution)/shard_map/ppermute | solution.py:499
  127.1 16.3 %observe.6 = f32[2,2,2,16,128]{4,3,2,1,0:T(8,128)S(1)} custom-call(s32[1]{0:T(128)} %bitcast.core_ref, bf16[2,2,16,32,128]{4,3,2,1,0:T(8,128)(2,1)S(1)} %pad_maximum_fusion.1.refs_0_, bf16[2,2,16,32,128]{4,3,2,1,0:T(8,128)(2,1)S(1)} %copy-done.26, bf16[2,2,16,32,128]{4,3,2,1,0:T(8,128)(2,1)} %collective-permute-done.15.refs_2_, ...), custom_call_target="tpu_custom_call" | custom-call | flops 268435456 | bytes 37224448 | tf_op jit(solution)/shard_map/observe/pallas_call | solution.py:359
  153.1 15.0 %pull_back.6 = bf16[4,2,2,16,32,128]{5,4,3,2,1,0:T(8,128)(2,1)} custom-call(s32[1]{0:T(128)} %bitcast.core_ref, f32[2,2,2,16,128]{4,3,2,1,0:T(8,128)S(1)} %reverse_add_fusion.5.refs_0_, f32[2,2,2,16,128]{4,3,2,1,0:T(8,128)S(1)} %collective-permute-done.26.refs_1_, f32[2,2,2,16,128]{4,3,2,1,0:T(8,128)S(1)} %collective-permute-done.27.refs_2_, ...), custom_call_target="tpu_custom_call" | custom-call | flops 268435456 | bytes 35651584 | tf_op jit(solution)/shard_map/pull_back/pallas_call | solution.py:431
  198.2 16.3 %observe.7 = f32[2,2,2,16,128]{4,3,2,1,0:T(8,128)S(1)} custom-call(s32[1]{0:T(128)} %bitcast.core_ref, bf16[2,2,16,32,128]{4,3,2,1,0:T(8,128)(2,1)S(1)} %pad_maximum_fusion.refs_0_, bf16[2,2,16,32,128]{4,3,2,1,0:T(8,128)(2,1)} %collective-permute-done.20.refs_1_, bf16[2,2,16,32,128]{4,3,2,1,0:T(8,128)(2,1)} %collective-permute-done.23.refs_2_, ...), custom_call_target="tpu_custom_call" | custom-call | flops 268435456 | bytes 37224448 | tf_op jit(solution)/shard_map/observe/pallas_call | solution.py:359
  215.3 15.4 %collective-permute-done.33.refs_4_ = bf16[2,2,16,32,128]{4,3,2,1,0:T(8,128)(2,1)} collective-permute-done((bf16[2,2,16,32,128]{4,3,2,1,0:T(8,128)(2,1)S(1)}, bf16[2,2,16,32,128]{4,3,2,1,0:T(8,128)(2,1)}, u32[]{:S(2)}, u32[]{:S(2)}) %collective-permute-start.33) | collective-permute-done | bytes 524320 | tf_op jit(solution)/shard_map/ppermute | solution.py:499
  243.6 15.0 %pull_back.7 = bf16[4,2,2,16,32,128]{5,4,3,2,1,0:T(8,128)(2,1)} custom-call(s32[1]{0:T(128)} %bitcast.core_ref, f32[2,2,2,16,128]{4,3,2,1,0:T(8,128)S(1)} %reverse_add_fusion.4.refs_0_, f32[2,2,2,16,128]{4,3,2,1,0:T(8,128)S(1)} %collective-permute-done.37.refs_1_, f32[2,2,2,16,128]{4,3,2,1,0:T(8,128)S(1)} %collective-permute-done.38.refs_2_, ...), custom_call_target="tpu_custom_call" | custom-call | flops 268435456 | bytes 35651584 | tf_op jit(solution)/shard_map/pull_back/pallas_call | solution.py:431
  280.6 4.8 step.3
  287.0 24.6 %collective-permute-done.45.refs_6_ = bf16[2,2,16,32,128]{4,3,2,1,0:T(8,128)(2,1)S(1)} collective-permute-done((bf16[2,2,16,32,128]{4,3,2,1,0:T(8,128)(2,1)}, bf16[2,2,16,32,128]{4,3,2,1,0:T(8,128)(2,1)S(1)}, u32[]{:S(2)}, u32[]{:S(2)}) %collective-permute-start.45) | collective-permute-done | bytes 524320 | tf_op jit(solution)/shard_map/ppermute | solution.py:499
  314.2 16.3 %observe.8 = f32[2,2,2,16,128]{4,3,2,1,0:T(8,128)S(1)} custom-call(s32[1]{0:T(128)} %bitcast.core_ref, bf16[2,2,16,32,128]{4,3,2,1,0:T(8,128)(2,1)S(1)} %pad_maximum_fusion.2.refs_0_, bf16[2,2,16,32,128]{4,3,2,1,0:T(8,128)(2,1)} %collective-permute-done.32.refs_1_, bf16[2,2,16,32,128]{4,3,2,1,0:T(8,128)(2,1)} %collective-permute-done.34.refs_2_, ...), custom_call_target="tpu_custom_call" | custom-call | flops 268435456 | bytes 37224448 | tf_op jit(solution)/shard_map/observe/pallas_call | solution.py:359
  341.7 15.0 %pull_back.8 = bf16[4,2,2,16,32,128]{5,4,3,2,1,0:T(8,128)(2,1)} custom-call(s32[1]{0:T(128)} %bitcast.core_ref, f32[2,2,2,16,128]{4,3,2,1,0:T(8,128)S(1)} %reverse_add_fusion.3.refs_0_, f32[2,2,2,16,128]{4,3,2,1,0:T(8,128)S(1)} %collective-permute-done.51.refs_1_, f32[2,2,2,16,128]{4,3,2,1,0:T(8,128)S(1)} %collective-permute-done.52.refs_2_, ...), custom_call_target="tpu_custom_call" | custom-call | flops 268435456 | bytes 35651584 | tf_op jit(solution)/shard_map/pull_back/pallas_call | solution.py:431
  379.7 4.8 step.4
  386.2 26.1 %collective-permute-done.61.refs_6_ = bf16[2,2,16,32,128]{4,3,2,1,0:T(8,128)(2,1)S(1)} collective-permute-done((bf16[2,2,16,32,128]{4,3,2,1,0:T(8,128)(2,1)}, bf16[2,2,16,32,128]{4,3,2,1,0:T(8,128)(2,1)S(1)}, u32[]{:S(2)}, u32[]{:S(2)}) %collective-permute-start.61) | collective-permute-done | bytes 524320 | tf_op jit(solution)/shard_map/ppermute | solution.py:499
  417.7 16.0 %observe.9 = f32[2,2,2,16,128]{4,3,2,1,0:T(8,128)S(1)} custom-call(s32[1]{0:T(128)} %bitcast.core_ref, bf16[2,2,16,32,128]{4,3,2,1,0:T(8,128)(2,1)S(1)} %pad_maximum_fusion.3.refs_0_, bf16[2,2,16,32,128]{4,3,2,1,0:T(8,128)(2,1)S(1)} %copy-done.28, bf16[2,2,16,32,128]{4,3,2,1,0:T(8,128)(2,1)} %collective-permute-done.48.refs_2_, ...), custom_call_target="tpu_custom_call" | custom-call | flops 268435456 | bytes 37224448 | tf_op jit(solution)/shard_map/observe/pallas_call | solution.py:359
  445.3 15.1 %pull_back.9 = bf16[4,2,2,16,32,128]{5,4,3,2,1,0:T(8,128)(2,1)} custom-call(s32[1]{0:T(128)} %bitcast.core_ref, f32[2,2,2,16,128]{4,3,2,1,0:T(8,128)S(1)} %reverse_add_fusion.2.refs_0_, f32[2,2,2,16,128]{4,3,2,1,0:T(8,128)S(1)} %collective-permute-done.67.refs_1_, f32[2,2,2,16,128]{4,3,2,1,0:T(8,128)S(1)} %collective-permute-done.68.refs_2_, ...), custom_call_target="tpu_custom_call" | custom-call | flops 268435456 | bytes 35651584 | tf_op jit(solution)/shard_map/pull_back/pallas_call | solution.py:431
  489.3 25.9 %collective-permute-done.77.refs_6_ = bf16[2,2,16,32,128]{4,3,2,1,0:T(8,128)(2,1)S(1)} collective-permute-done((bf16[2,2,16,32,128]{4,3,2,1,0:T(8,128)(2,1)}, bf16[2,2,16,32,128]{4,3,2,1,0:T(8,128)(2,1)S(1)}, u32[]{:S(2)}, u32[]{:S(2)}) %collective-permute-start.77) | collective-permute-done | bytes 524320 | tf_op jit(solution)/shard_map/ppermute | solution.py:499
  518.6 16.3 %observe.10 = f32[2,2,2,16,128]{4,3,2,1,0:T(8,128)S(1)} custom-call(s32[1]{0:T(128)} %bitcast.core_ref, bf16[2,2,16,32,128]{4,3,2,1,0:T(8,128)(2,1)S(1)} %pad_maximum_fusion.4.refs_0_, bf16[2,2,16,32,128]{4,3,2,1,0:T(8,128)(2,1)} %collective-permute-done.62.refs_1_, bf16[2,2,16,32,128]{4,3,2,1,0:T(8,128)(2,1)} %collective-permute-done.64.refs_2_, ...), custom_call_target="tpu_custom_call" | custom-call | flops 268435456 | bytes 37224448 | tf_op jit(solution)/shard_map/observe/pallas_call | solution.py:359
  545.8 15.0 %pull_back.10 = bf16[4,2,2,16,32,128]{5,4,3,2,1,0:T(8,128)(2,1)} custom-call(s32[1]{0:T(128)} %bitcast.core_ref, f32[2,2,2,16,128]{4,3,2,1,0:T(8,128)S(1)} %reverse_add_fusion.1.refs_0_, f32[2,2,2,16,128]{4,3,2,1,0:T(8,128)S(1)} %collective-permute-done.83.refs_1_, f32[2,2,2,16,128]{4,3,2,1,0:T(8,128)S(1)} %collective-permute-done.84.refs_2_, ...), custom_call_target="tpu_custom_call" | custom-call | flops 268435456 | bytes 35651584 | tf_op jit(solution)/shard_map/pull_back/pallas_call | solution.py:431
  562.9 25.4 %collective-permute-done.87.refs_6_ = bf16[2,2,16,32,128]{4,3,2,1,0:T(8,128)(2,1)S(1)} collective-permute-done((bf16[2,2,16,32,128]{4,3,2,1,0:T(8,128)(2,1)}, bf16[2,2,16,32,128]{4,3,2,1,0:T(8,128)(2,1)S(1)}, u32[]{:S(2)}, u32[]{:S(2)}) %collective-permute-start.87) | collective-permute-done | bytes 524320 | tf_op jit(solution)/shard_map/ppermute | solution.py:499
  588.3 16.1 %observe.11 = f32[2,2,2,16,128]{4,3,2,1,0:T(8,128)S(1)} custom-call(s32[1]{0:T(128)} %bitcast.core_ref, bf16[2,2,16,32,128]{4,3,2,1,0:T(8,128)(2,1)S(1)} %pad_maximum_fusion.5.refs_0_, bf16[2,2,16,32,128]{4,3,2,1,0:T(8,128)(2,1)} %collective-permute-done.78.refs_1_, bf16[2,2,16,32,128]{4,3,2,1,0:T(8,128)(2,1)S(1)} %collective-permute-done.80.refs_2_, ...), custom_call_target="tpu_custom_call" | custom-call | flops 268435456 | bytes 37224448 | tf_op jit(solution)/shard_map/observe/pallas_call | solution.py:359
  604.5 11.7 %collective-permute-start.88 = (f32[2,2,2,16,128]{4,3,2,1,0:T(8,128)S(1)}, f32[2,2,2,16,128]{4,3,2,1,0:T(8,128)S(1)}, u32[]{:S(2)}, u32[]{:S(2)}) collective-permute-start(f32[2,2,2,16,128]{4,3,2,1,0:T(8,128)S(1)} %observe.11), channel_id=1, source_target_pairs={{0,1},{1,0},{2,3},{3,2},{4,5},{5,4},{6,7},{7,6},{8,9},{9,8},{10,11... | collective-permute-start | bytes 196616 | tf_op jit(solution)/shard_map/ppermute | solution.py:473
  622.9 15.0 %pull_back.11 = bf16[4,2,2,16,32,128]{5,4,3,2,1,0:T(8,128)(2,1)} custom-call(s32[1]{0:T(128)} %bitcast.core_ref, f32[2,2,2,16,128]{4,3,2,1,0:T(8,128)S(1)} %reverse_add_fusion.refs_0_, f32[2,2,2,16,128]{4,3,2,1,0:T(8,128)S(1)} %collective-permute-done.89.refs_1_, f32[2,2,2,16,128]{4,3,2,1,0:T(8,128)S(1)} %collective-permute-done.90.refs_2_, ...), custom_call_target="tpu_custom_call" | custom-call | flops 268435456 | bytes 35651584 | tf_op jit(solution)/shard_map/pull_back/pallas_call | solution.py:431
  641.8 4.5 collective-permute-start.95
  655.5 28.0 %reduce-scatter.13.cloned.1.call-done = bf16[1,2,2,16,32,128]{5,4,3,2,1,0:T(8,128)(2,1)} async-done(((bf16[4,2,2,16,32,128]{5,4,3,2,1,0:T(8,128)(2,1)}), bf16[1,2,2,16,32,128]{5,4,3,2,1,0:T(8,128)(2,1)}) %reduce-scatter.13.cloned.1.call-update) | async-done | bytes 524304 | tf_op jit(solution)/shard_map/reduce_scatter | solution.py:615
  699.1 4.5 collective-permute-start.73
  714.3 5.2 finish.3
  719.6 5.4 finish.4
  725.0 4.4 finish.5
  (364 shorter events, 285.7 us)
Async XLA Ops:
  7.2 251.6 %reduce-scatter.7.cloned.1.call-start = ((), (), s32[]{:S(2)}) async-start(), calls=%async_computation.6 | async-start | bytes 2621440 | tf_op jit(solution)/shard_map/reduce_scatter | solution.py:615
  53.8 72.2 %collective-permute-start.22 = (bf16[2,128,16,2048]{3,2,1,0:T(8,128)(2,1)}, bf16[2,128,16,2048]{3,2,1,0:T(8,128)(2,1)}, u32[]{:S(2)}, u32[]{:S(2)}) collective-permute-start(bf16[2,128,16,2048]{3,2,1,0:T(8,128)(2,1)} %constant_dynamic-slice_fusion), channel_id=1, source_target_pairs={{0,1},{1,0},{2,3},{3,2},{4,5},{5,4},{6,7},{7,6},{8,9},{9,8},{10,11... | collective-permute-start | bytes 50331656 | tf_op jit(solution)/shard_map/ppermute | solution.py:473
  76.6 26.1 %collective-permute-start.15 = (bf16[2,2,16,32,128]{4,3,2,1,0:T(8,128)(2,1)S(1)}, bf16[2,2,16,32,128]{4,3,2,1,0:T(8,128)(2,1)}, u32[]{:S(2)}, u32[]{:S(2)}) collective-permute-start(bf16[2,2,16,32,128]{4,3,2,1,0:T(8,128)(2,1)S(1)} %collective-permute-done.14.refs_1_), channel_id=1, source_target_pairs={{2,4},{3,5},{4,6},{5,7},{10,12},{11,13},{12,14},{13,15},{18,20},{1... | collective-permute-start | bytes 1572872 | tf_op jit(solution)/shard_map/ppermute | solution.py:498
  80.5 23.6 %collective-permute-start.18 = (bf16[2,2,16,32,128]{4,3,2,1,0:T(8,128)(2,1)}, bf16[2,2,16,32,128]{4,3,2,1,0:T(8,128)(2,1)}, u32[]{:S(2)}, u32[]{:S(2)}) collective-permute-start(bf16[2,2,16,32,128]{4,3,2,1,0:T(8,128)(2,1)} %collective-permute-done.17.refs_4_), channel_id=1, source_target_pairs={{5,3},{4,2},{3,1},{2,0},{13,11},{12,10},{11,9},{10,8},{21,19},{20,... | collective-permute-start | bytes 1572872 | tf_op jit(solution)/shard_map/ppermute | solution.py:499
  143.5 24.6 %collective-permute-start.23 = (bf16[2,2,16,32,128]{4,3,2,1,0:T(8,128)(2,1)}, bf16[2,2,16,32,128]{4,3,2,1,0:T(8,128)(2,1)}, u32[]{:S(2)}, u32[]{:S(2)}) collective-permute-start(bf16[2,2,16,32,128]{4,3,2,1,0:T(8,128)(2,1)} %collective-permute-done.20.refs_1_), channel_id=1, source_target_pairs={{2,4},{3,5},{4,6},{5,7},{10,12},{11,13},{12,14},{13,15},{18,20},{1... | collective-permute-start | bytes 1572872 | tf_op jit(solution)/shard_map/ppermute | solution.py:498
  144.9 23.2 %collective-permute-start.24 = (bf16[2,2,16,32,128]{4,3,2,1,0:T(8,128)(2,1)}, bf16[2,2,16,32,128]{4,3,2,1,0:T(8,128)(2,1)}, u32[]{:S(2)}, u32[]{:S(2)}) collective-permute-start(bf16[2,2,16,32,128]{4,3,2,1,0:T(8,128)(2,1)} %collective-permute-done.21.refs_4_), channel_id=1, source_target_pairs={{5,3},{4,2},{3,1},{2,0},{13,11},{12,10},{11,9},{10,8},{21,19},{20,... | collective-permute-start | bytes 1572872 | tf_op jit(solution)/shard_map/ppermute | solution.py:499
  168.2 188.7 %reduce-scatter.11.cloned.1.call-start = ((), (), s32[]{:S(2)}) async-start(), calls=%async_computation.8 | async-start | bytes 2621440 | tf_op jit(solution)/shard_map/reduce_scatter | solution.py:615
  168.9 23.9 %collective-permute-start.31 = (bf16[2,2,16,32,128]{4,3,2,1,0:T(8,128)(2,1)}, bf16[2,2,16,32,128]{4,3,2,1,0:T(8,128)(2,1)S(1)}, u32[]{:S(2)}, u32[]{:S(2)}) collective-permute-start(bf16[2,2,16,32,128]{4,3,2,1,0:T(8,128)(2,1)} %collective-permute-done.24.refs_5_), channel_id=1, source_target_pairs={{3,1},{2,0},{11,9},{10,8},{19,17},{18,16},{27,25},{26,24}} | collective-permute-start | bytes 1572872 | tf_op jit(solution)/shard_map/ppermute | solution.py:499
  196.9 33.8 %collective-permute-start.33 = (bf16[2,2,16,32,128]{4,3,2,1,0:T(8,128)(2,1)S(1)}, bf16[2,2,16,32,128]{4,3,2,1,0:T(8,128)(2,1)}, u32[]{:S(2)}, u32[]{:S(2)}) collective-permute-start(bf16[2,2,16,32,128]{4,3,2,1,0:T(8,128)(2,1)S(1)} %pad_maximum_fusion.2.refs_0_), channel_id=1, source_target_pairs={{7,5},{6,4},{5,3},{4,2},{3,1},{2,0},{15,13},{14,12},{13,11},{12,10... | collective-permute-start | bytes 1572872 | tf_op jit(solution)/shard_map/ppermute | solution.py:499
  230.7 28.0 %collective-permute-start.34 = (bf16[2,2,16,32,128]{4,3,2,1,0:T(8,128)(2,1)}, bf16[2,2,16,32,128]{4,3,2,1,0:T(8,128)(2,1)}, u32[]{:S(2)}, u32[]{:S(2)}) collective-permute-start(bf16[2,2,16,32,128]{4,3,2,1,0:T(8,128)(2,1)} %collective-permute-done.32.refs_1_), channel_id=1, source_target_pairs={{2,4},{3,5},{4,6},{5,7},{10,12},{11,13},{12,14},{13,15},{18,20},{1... | collective-permute-start | bytes 1572872 | tf_op jit(solution)/shard_map/ppermute | solution.py:498
  232.1 26.6 %collective-permute-start.35 = (bf16[2,2,16,32,128]{4,3,2,1,0:T(8,128)(2,1)}, bf16[2,2,16,32,128]{4,3,2,1,0:T(8,128)(2,1)}, u32[]{:S(2)}, u32[]{:S(2)}) collective-permute-start(bf16[2,2,16,32,128]{4,3,2,1,0:T(8,128)(2,1)} %collective-permute-done.33.refs_4_), channel_id=1, source_target_pairs={{5,3},{4,2},{3,1},{2,0},{13,11},{12,10},{11,9},{10,8},{21,19},{20,... | collective-permute-start | bytes 1572872 | tf_op jit(solution)/shard_map/ppermute | solution.py:499
  258.7 201.7 %reduce-scatter.9.cloned.1.call-start = ((), (), s32[]{:S(2)}) async-start(), calls=%async_computation.7 | async-start | bytes 2621440 | tf_op jit(solution)/shard_map/reduce_scatter | solution.py:615
  267.2 44.4 %collective-permute-start.45 = (bf16[2,2,16,32,128]{4,3,2,1,0:T(8,128)(2,1)}, bf16[2,2,16,32,128]{4,3,2,1,0:T(8,128)(2,1)S(1)}, u32[]{:S(2)}, u32[]{:S(2)}) collective-permute-start(bf16[2,2,16,32,128]{4,3,2,1,0:T(8,128)(2,1)} %collective-permute-done.35.refs_5_), channel_id=1, source_target_pairs={{3,1},{2,0},{11,9},{10,8},{19,17},{18,16},{27,25},{26,24}} | collective-permute-start | bytes 1572872 | tf_op jit(solution)/shard_map/ppermute | solution.py:499
  330.6 26.2 %collective-permute-start.48 = (bf16[2,2,16,32,128]{4,3,2,1,0:T(8,128)(2,1)S(1)}, bf16[2,2,16,32,128]{4,3,2,1,0:T(8,128)(2,1)}, u32[]{:S(2)}, u32[]{:S(2)}) collective-permute-start(bf16[2,2,16,32,128]{4,3,2,1,0:T(8,128)(2,1)S(1)} %collective-permute-done.46.refs_1_), channel_id=1, source_target_pairs={{2,4},{3,5},{4,6},{5,7},{10,12},{11,13},{12,14},{13,15},{18,20},{1... | collective-permute-start | bytes 1572872 | tf_op jit(solution)/shard_map/ppermute | solution.py:498
  332.0 24.7 %collective-permute-start.49 = (bf16[2,2,16,32,128]{4,3,2,1,0:T(8,128)(2,1)S(1)}, bf16[2,2,16,32,128]{4,3,2,1,0:T(8,128)(2,1)}, u32[]{:S(2)}, u32[]{:S(2)}) collective-permute-start(bf16[2,2,16,32,128]{4,3,2,1,0:T(8,128)(2,1)S(1)} %collective-permute-done.47.refs_4_), channel_id=1, source_target_pairs={{5,3},{4,2},{3,1},{2,0},{13,11},{12,10},{11,9},{10,8},{21,19},{20,... | collective-permute-start | bytes 1572872 | tf_op jit(solution)/shard_map/ppermute | solution.py:499
  356.8 290.8 %reduce-scatter.17.cloned.1.call-start = ((), (), s32[]{:S(2)}) async-start(), calls=%async_computation.11 | async-start | bytes 2621440 | tf_op jit(solution)/shard_map/reduce_scatter | solution.py:615
  365.1 47.2 %collective-permute-start.61 = (bf16[2,2,16,32,128]{4,3,2,1,0:T(8,128)(2,1)}, bf16[2,2,16,32,128]{4,3,2,1,0:T(8,128)(2,1)S(1)}, u32[]{:S(2)}, u32[]{:S(2)}) collective-permute-start(bf16[2,2,16,32,128]{4,3,2,1,0:T(8,128)(2,1)} %collective-permute-done.49.refs_5_), channel_id=1, source_target_pairs={{3,1},{2,0},{11,9},{10,8},{19,17},{18,16},{27,25},{26,24}} | collective-permute-start | bytes 1572872 | tf_op jit(solution)/shard_map/ppermute | solution.py:499
  433.7 26.6 %collective-permute-start.64 = (bf16[2,2,16,32,128]{4,3,2,1,0:T(8,128)(2,1)}, bf16[2,2,16,32,128]{4,3,2,1,0:T(8,128)(2,1)}, u32[]{:S(2)}, u32[]{:S(2)}) collective-permute-start(bf16[2,2,16,32,128]{4,3,2,1,0:T(8,128)(2,1)} %collective-permute-done.62.refs_1_), channel_id=1, source_target_pairs={{2,4},{3,5},{4,6},{5,7},{10,12},{11,13},{12,14},{13,15},{18,20},{1... | collective-permute-start | bytes 1572872 | tf_op jit(solution)/shard_map/ppermute | solution.py:498
  435.2 25.1 %collective-permute-start.65 = (bf16[2,2,16,32,128]{4,3,2,1,0:T(8,128)(2,1)}, bf16[2,2,16,32,128]{4,3,2,1,0:T(8,128)(2,1)}, u32[]{:S(2)}, u32[]{:S(2)}) collective-permute-start(bf16[2,2,16,32,128]{4,3,2,1,0:T(8,128)(2,1)} %collective-permute-done.63.refs_4_), channel_id=1, source_target_pairs={{5,3},{4,2},{3,1},{2,0},{13,11},{12,10},{11,9},{10,8},{21,19},{20,... | collective-permute-start | bytes 1572872 | tf_op jit(solution)/shard_map/ppermute | solution.py:499
  460.4 193.2 %reduce-scatter.15.cloned.1.call-start = ((), (), s32[]{:S(2)}) async-start(), calls=%async_computation.10 | async-start | bytes 2621440 | tf_op jit(solution)/shard_map/reduce_scatter | solution.py:615
  468.7 46.5 %collective-permute-start.77 = (bf16[2,2,16,32,128]{4,3,2,1,0:T(8,128)(2,1)}, bf16[2,2,16,32,128]{4,3,2,1,0:T(8,128)(2,1)S(1)}, u32[]{:S(2)}, u32[]{:S(2)}) collective-permute-start(bf16[2,2,16,32,128]{4,3,2,1,0:T(8,128)(2,1)} %collective-permute-done.65.refs_5_), channel_id=1, source_target_pairs={{3,1},{2,0},{11,9},{10,8},{19,17},{18,16},{27,25},{26,24}} | collective-permute-start | bytes 1572872 | tf_op jit(solution)/shard_map/ppermute | solution.py:499
  534.9 25.9 %collective-permute-start.80 = (bf16[2,2,16,32,128]{4,3,2,1,0:T(8,128)(2,1)}, bf16[2,2,16,32,128]{4,3,2,1,0:T(8,128)(2,1)S(1)}, u32[]{:S(2)}, u32[]{:S(2)}) collective-permute-start(bf16[2,2,16,32,128]{4,3,2,1,0:T(8,128)(2,1)} %collective-permute-done.78.refs_1_), channel_id=1, source_target_pairs={{2,4},{3,5},{4,6},{5,7},{10,12},{11,13},{12,14},{13,15},{18,20},{1... | collective-permute-start | bytes 1572872 | tf_op jit(solution)/shard_map/ppermute | solution.py:498
  535.6 25.2 %collective-permute-start.81 = (bf16[2,2,16,32,128]{4,3,2,1,0:T(8,128)(2,1)}, bf16[2,2,16,32,128]{4,3,2,1,0:T(8,128)(2,1)}, u32[]{:S(2)}, u32[]{:S(2)}) collective-permute-start(bf16[2,2,16,32,128]{4,3,2,1,0:T(8,128)(2,1)} %collective-permute-done.79.refs_4_), channel_id=1, source_target_pairs={{5,3},{4,2},{3,1},{2,0},{13,11},{12,10},{11,9},{10,8},{21,19},{20,... | collective-permute-start | bytes 1572872 | tf_op jit(solution)/shard_map/ppermute | solution.py:499
  560.9 122.7 %reduce-scatter.13.cloned.1.call-start = ((), (), s32[]{:S(2)}) async-start(), calls=%async_computation.9 | async-start | bytes 2621440 | tf_op jit(solution)/shard_map/reduce_scatter | solution.py:615
  561.6 26.7 %collective-permute-start.87 = (bf16[2,2,16,32,128]{4,3,2,1,0:T(8,128)(2,1)}, bf16[2,2,16,32,128]{4,3,2,1,0:T(8,128)(2,1)S(1)}, u32[]{:S(2)}, u32[]{:S(2)}) collective-permute-start(bf16[2,2,16,32,128]{4,3,2,1,0:T(8,128)(2,1)} %collective-permute-done.81.refs_5_), channel_id=1, source_target_pairs={{3,1},{2,0},{11,9},{10,8},{19,17},{18,16},{27,25},{26,24}} | collective-permute-start | bytes 1572872 | tf_op jit(solution)/shard_map/ppermute | solution.py:499
  640.5 44.2 %collective-permute-start.101 = (bf16[2,4,32,128]{3,2,1,0:T(8,128)(2,1)}, bf16[2,4,32,128]{3,2,1,0:T(8,128)(2,1)S(1)}, u32[]{:S(2)}, u32[]{:S(2)}) collective-permute-start(bf16[2,4,32,128]{3,2,1,0:T(8,128)(2,1)} %get-tuple-element.238), channel_id=1, source_target_pairs={{8,0},{16,8},{24,16},{9,1},{17,9},{25,17},{10,2},{18,10},{26,18},{... | collective-permute-start | bytes 196616 | tf_op jit(solution)/shard_map/ppermute | solution.py:455
  641.8 45.9 %collective-permute-start.95 = (bf16[2,4,32,128]{3,2,1,0:T(8,128)(2,1)}, bf16[2,4,32,128]{3,2,1,0:T(8,128)(2,1)S(1)}, u32[]{:S(2)}, u32[]{:S(2)}) collective-permute-start(bf16[2,4,32,128]{3,2,1,0:T(8,128)(2,1)} %get-tuple-element.231), channel_id=1, source_target_pairs={{0,8},{8,16},{16,24},{1,9},{9,17},{17,25},{2,10},{10,18},{18,26},{... | collective-permute-start | bytes 196616 | tf_op jit(solution)/shard_map/ppermute | solution.py:455
  646.3 44.7 %collective-permute-start.96 = (bf16[2,4,32,128]{3,2,1,0:T(8,128)(2,1)}, bf16[2,4,32,128]{3,2,1,0:T(8,128)(2,1)S(1)}, u32[]{:S(2)}, u32[]{:S(2)}) collective-permute-start(bf16[2,4,32,128]{3,2,1,0:T(8,128)(2,1)} %get-tuple-element.233), channel_id=1, source_target_pairs={{8,0},{16,8},{24,16},{9,1},{17,9},{25,17},{10,2},{18,10},{26,18},{... | collective-permute-start | bytes 196616 | tf_op jit(solution)/shard_map/ppermute | solution.py:455
  649.5 49.7 %collective-permute-start.102 = (bf16[2,16,32,128]{3,2,1,0:T(8,128)(2,1)}, bf16[2,16,32,128]{3,2,1,0:T(8,128)(2,1)}, u32[]{:S(2)}, u32[]{:S(2)}) collective-permute-start(bf16[2,16,32,128]{3,2,1,0:T(8,128)(2,1)} %get-tuple-element.254), channel_id=1, source_target_pairs={{0,1},{1,0},{2,3},{3,2},{4,5},{5,4},{6,7},{7,6},{8,9},{9,8},{10,11... | collective-permute-start | bytes 786440 | tf_op jit(solution)/shard_map/ppermute | solution.py:473
  655.5 53.4 %collective-permute-start.97 = (bf16[2,16,32,128]{3,2,1,0:T(8,128)(2,1)}, bf16[2,16,32,128]{3,2,1,0:T(8,128)(2,1)}, u32[]{:S(2)}, u32[]{:S(2)}) collective-permute-start(bf16[2,16,32,128]{3,2,1,0:T(8,128)(2,1)} %get-tuple-element.258), channel_id=1, source_target_pairs={{0,1},{1,0},{2,3},{3,2},{4,5},{5,4},{6,7},{7,6},{8,9},{9,8},{10,11... | collective-permute-start | bytes 786440 | tf_op jit(solution)/shard_map/ppermute | solution.py:473
  691.0 34.0 %collective-permute-start.92 = (bf16[2,16,32,128]{3,2,1,0:T(8,128)(2,1)S(1)}, bf16[2,16,32,128]{3,2,1,0:T(8,128)(2,1)S(1)}, u32[]{:S(2)}, u32[]{:S(2)}) collective-permute-start(bf16[2,16,32,128]{3,2,1,0:T(8,128)(2,1)S(1)} %get-tuple-element.262), channel_id=1, source_target_pairs={{0,1},{1,0},{2,3},{3,2},{4,5},{5,4},{6,7},{7,6},{8,9},{9,8},{10,11... | collective-permute-start | bytes 786440 | tf_op jit(solution)/shard_map/ppermute | solution.py:473
  699.1 25.8 %collective-permute-start.73 = (bf16[2,4,32,128]{3,2,1,0:T(8,128)(2,1)}, bf16[2,4,32,128]{3,2,1,0:T(8,128)(2,1)S(1)}, u32[]{:S(2)}, u32[]{:S(2)}) collective-permute-start(bf16[2,4,32,128]{3,2,1,0:T(8,128)(2,1)} %copy-done.38), channel_id=1, source_target_pairs={{0,8},{8,16},{16,24},{1,9},{9,17},{17,25},{2,10},{10,18},{18,26},{... | collective-permute-start | bytes 196616 | tf_op jit(solution)/shard_map/ppermute | solution.py:455
  (123 other events, 1485.5 us)
Sparse Core Ops, SparseCore 0:
  168.3 62.9 reduce-scatter.6
  258.8 57.1 reduce-scatter.10
  356.9 60.4 reduce-scatter.8
  460.5 59.8 reduce-scatter.16
  561.0 54.7 reduce-scatter.14
  638.0 45.4 reduce-scatter.12

commit v5 on v3

--- a/solution.py
+++ b/solution.py
@@ -13,9 +13,9 @@
 HALO = SWEEPS
 LANES = 128
 SUBLANES = 8
-GROUPS = 2
+GROUPS = 3
 CHUNK_ROWS = 4
-VMEM_BYTES = 40 * 2**20
+VMEM_BYTES = 20 * 2**20
 
 
 def transform_table(freqs, moments):
@@ -272,18 +272,45 @@
     return jnp.concatenate(parts, axis=1)
 
 
-def near_map(own_ref, other_ref, here):
-    _, freqs, sensors, width = own_ref.shape
+def near_map(own_ref, other_ref, here, width):
+    cells = pl.ds(pl.multiple_of(pl.program_id(0) * width, LANES), width)
     parts = [
-        ref[part, here].reshape(LANES, width) for part in range(2) for ref in (own_ref, other_ref)
+        ref[part, here, :, cells].reshape(LANES, width)
+        for part in range(2)
+        for ref in (own_ref, other_ref)
     ]
     return jnp.concatenate(parts, axis=0)
+
+
+def keep_kernel(core_ref, map_ref, out_ref, sem):
+    cells = pl.ds(pl.multiple_of(core_ref[0], LANES), out_ref.shape[3])
+    copy = pltpu.make_async_copy(map_ref.at[:, :, :, cells], out_ref, sem)
+    copy.start()
+    copy.wait()
+
+
+def keep(first, forward_map, cells):
+    return call(
+        keep_kernel,
+        first,
+        (1,),
+        [pl.BlockSpec(memory_space=pl.ANY)],
+        pl.BlockSpec(memory_space=pltpu.VMEM),
+        pltpu.VMEM(forward_map.shape[:3] + (cells,), forward_map.dtype),
+        [pltpu.SemaphoreType.DMA],
+        name="keep",
+    )(first.reshape(1), forward_map)
+
+
+def resident(*maps):
+    return [pltpu.with_memory_space_constraint(part, pltpu.VMEM) for part in maps]
 
 
 def observe_kernel(core_ref, *refs):
     field_ref, own_ref, other_ref, table_ref, cell_ref, out_ref, spec, acc, picked = refs
     chips, _, members, rows, steps, lanes = field_ref.shape
-    freqs, sensors, width = own_ref.shape[1:]
+    freqs, sensors, _ = own_ref.shape[1:]
+    width = rows * lanes
     near = lanes // sensors
     wide = 2 * lanes
     chunk = pl.program_id(0)
@@ -309,7 +336,7 @@
     for q in range(freqs // near):
         here = slice(q * near, (q + 1) * near)
         left = spec[:, here].reshape(2 * members * near, width).astype(jnp.bfloat16)
-        acc[q] += dot_lanes(left, near_map(own_ref, other_ref, here))
+        acc[q] += dot_lanes(left, near_map(own_ref, other_ref, here, width))
 
     @pl.when(chunk == pl.num_programs(0) - 1)
     def _():
@@ -329,18 +356,10 @@
                     out_ref[1, part, b, q : q + 1] = line[:, lanes:]
 
 
-def map_specs(own, other, width):
-    chunks = other.shape[3] // width
-    return [
-        pl.BlockSpec(own.shape[:3] + (width,), lambda c, core: (0, 0, 0, core[0] * chunks + c)),
-        pl.BlockSpec(other.shape[:3] + (width,), lambda c, core: (0, 0, 0, c)),
-    ]
-
-
 def map_cost(members, own, other, moved):
     return pl.CostEstimate(
         flops=16 * members * other.size,
-        bytes_accessed=4 * other.size + 2 * moved,
+        bytes_accessed=2 * moved,
         transcendentals=0,
     )
 
@@ -357,7 +376,7 @@
         core,
         (rows // CHUNK_ROWS,),
         [pl.BlockSpec(block, lambda c, core: (0, 0, 0, c, 0, 0))]
-        + map_specs(own, other, width)
+        + [pl.BlockSpec(memory_space=pltpu.VMEM)] * 2
         + [whole_block(table), whole_block(local_cells)],
         pl.BlockSpec(shape, lambda c, core: (0, 0, 0, 0, 0)),
         jax.ShapeDtypeStruct(shape, jnp.float32),
@@ -368,13 +387,14 @@
         ],
         cost_estimate=map_cost(members, own, other, field.size),
         name="observe",
-    )(core, field, own, other, table, local_cells)
+    )(core, field, *resident(own, other), table, local_cells)
 
 
 def pull_kernel(core_ref, *refs):
     *sums, noise_ref, own_ref, other_ref, back_ref, cell_ref, out_ref, weights, adjoint = refs
     devices, _, members, rows, steps, lanes = out_ref.shape
-    freqs, sensors, width = own_ref.shape[1:]
+    freqs, sensors, _ = own_ref.shape[1:]
+    width = rows * lanes
     near = lanes // sensors
     wide = 2 * lanes
 
@@ -407,7 +427,7 @@
     for q in range(freqs // near):
         here = slice(q * near, (q + 1) * near)
         left = weights[:, here].reshape(2 * members * near, 2 * wide).astype(jnp.bfloat16)
-        part = dot(left, near_map(own_ref, other_ref, here))
+        part = dot(left, near_map(own_ref, other_ref, here, width))
         adjoint[:, here] += part.reshape(2 * members, near, width)
     for b in range(members):
         whole = adjoint[2 * b : 2 * b + 2].reshape(2 * freqs, width)
@@ -429,7 +449,7 @@
         core,
         (rows // CHUNK_ROWS,),
         [whole_block(array) for array in small]
-        + map_specs(own, other, width)
+        + [pl.BlockSpec(memory_space=pltpu.VMEM)] * 2
         + [whole_block(back), whole_block(local_cells)],
         pl.BlockSpec(
             (devices, 2, members, CHUNK_ROWS, steps, lanes), lambda c, core: (0, 0, 0, c, 0, 0)
@@ -441,7 +461,7 @@
         ],
         cost_estimate=map_cost(members, own, other, math.prod(shape)),
         name="pull_back",
-    )(core, *small, own, other, back, local_cells)
+    )(core, *small, *resident(own, other), back, local_cells)
 
 
 def rims(top, bottom):
@@ -490,9 +510,6 @@
     near = LANES // sensors
     half = cells // 2
 
-    away = lax.dynamic_slice_in_dim(forward_map, (1 - core) * half, half, axis=3)
-    other_map = swap_cores(away)
-
     cores = jnp.stack([core, 1 - core])
     offsets = cores[None, :, None] * steps + jnp.arange(steps, dtype=jnp.int32)
     chip_steps = 2 * steps
@@ -522,43 +539,60 @@
     core = core.reshape(1)
 
     members = samples // GROUPS
+    top, bottom = (
+        jnp.transpose(rim, (1, 2, 0, 3)).astype(jnp.bfloat16)
+        for rim in (rhs[:, :, :HALO], rhs[:, :, rows - HALO :])
+    )
     states = []
     for group in range(GROUPS):
-        group_rhs = rhs[:, group * members : (group + 1) * members]
-        up, down = rims(
-            *(
-                jnp.transpose(rim, (1, 2, 0, 3)).astype(jnp.bfloat16)
-                for rim in (group_rhs[:, :, :HALO], group_rhs[:, :, rows - HALO :])
-            )
-        )
+        here = slice(group * members, (group + 1) * members)
+        up, down = rims(top[here], bottom[here])
         states.append(start(group, members, core, rhs, up, down, coeff))
+    there, *states[0] = lax.optimization_barrier(((1 - core[0]) * half, *states[0]))
+    away = lax.dynamic_slice_in_dim(forward_map, there, half, axis=3)
+    other_map = keep(jnp.zeros_like(there), swap_cores(away), half)
+    own_map = keep(half - there, forward_map, half)
 
     lines = [[k for k in range(size) if k % 2 == parity] for parity in range(2)]
+    shape = (chips, 2, members, rows // 2, steps, cols)
+
+    def ready(state):
+        iterate, keep, give, rest, top, bottom = state
+        above, below = rims(top, bottom)
+        return iterate, jnp.stack([keep, swap_cores(give)]), (above, rest, below)
+
+    def edges(misfit):
+        first = (rows // 2 - HALO) * core[0]
+        edge = lax.dynamic_slice_in_dim(misfit, first, HALO, axis=2)
+        same, _ = misfit_rims(edge[0])
+        _, cross = misfit_rims(edge[1])
+        return misfit[0], swap_cores(misfit[1]), same, cross
+
+    states = [ready(state) for state in states]
     outputs = ()
     for iteration in range(ITERS):
+        fields = [lax.all_gather(state[1], "sensors", axis_index_groups=lines) for state in states]
+        totals = []
+        for field in fields:
+            sums = observe(core, field, own_map, other_map, table, local_cells)
+            sums = from_all_cells(sums + swap_cores(sums)[::-1])
+            misfit = pull_back(core, sums, noise, own_map, other_map, back, local_cells, shape)
+            totals.append(
+                lax.psum_scatter(
+                    misfit, "sensors", scatter_dimension=0, axis_index_groups=lines, tiled=False
+                )
+            )
         for group in range(GROUPS):
-            iterate, keep, give, rest, top, bottom = states[group]
-            above, below = rims(top, bottom)
-            field = lax.all_gather(
-                jnp.stack([keep, swap_cores(give)]), "sensors", axis_index_groups=lines
-            )
-            sums = observe(core, field, forward_map, other_map, table, local_cells)
-            sums = from_all_cells(sums + swap_cores(sums)[::-1])
-            shape = (chips, 2, members, rows // 2, steps, cols)
-            misfit = pull_back(core, sums, noise, forward_map, other_map, back, local_cells, shape)
-            misfit = lax.psum_scatter(
-                misfit, "sensors", scatter_dimension=0, axis_index_groups=lines, tiled=False
-            )
-            first = (rows // 2 - HALO) * core[0]
-            edge = lax.dynamic_slice_in_dim(misfit, first, HALO, axis=2)
-            same, _ = misfit_rims(edge[0])
-            _, cross = misfit_rims(edge[1])
-            misfits = (misfit[0], swap_cores(misfit[1]), same, cross)
-            rests = (above, rest, below)
+            iterate, _, rests = states[group]
+            total = totals[group]
             if iteration < ITERS - 1:
-                states[group] = step(core, rests, misfits, iterate, coeff)
+                states[group] = ready(step(core, rests, edges(total), iterate, coeff))
             else:
-                outputs = finish(group, samples, core, rests, misfits, iterate, coeff, outputs)
+                if outputs:
+                    total, outputs = lax.optimization_barrier((total, outputs))
+                outputs = finish(
+                    group, samples, core, rests, edges(total), iterate, coeff, outputs
+                )
     return tuple(out.reshape(rhs.shape) for out in outputs)
 
 

time: 610 us -> 658 us (1.079); the launches traced: 608 us -> 646 us
  waiting for transfers between devices: 282 us -> 163 us
  local copies, waits for them, and re-layouts: 58 us -> 157 us
  starting transfers between devices: 82.2 us -> 121 us
  Pallas kernels: 166 us -> 183 us
    unnamed x65 -> x99, local copies, waits for them, and re-layouts: 32.6 us -> 127 us
    all_gather x4 -> x6, waiting for transfers between devices: 113 us -> 25 us  [shards(): lax.all_gather(state[1], 'sensors', axis_index_groups=lines)]
    reduce_scatter x4 -> x6, waiting for transfers between devices: 124 us -> 65.5 us  [shards(): lax.psum_scatter(misfit, 'sensors', scatter_dimension=0, axis_index_group...]
    ppermute x8 -> x12, starting transfers between devices: 25.5 us -> 38.9 us  [misfit_rims(): return (lax.ppermute(edge, both, same), lax.ppermute(edge, both, cross))]
    ppermute x8 -> x12, waiting for transfers between devices: 7.85 us -> 20.5 us  [misfit_rims(): return (lax.ppermute(edge, both, same), lax.ppermute(edge, both, cross))]
    pallas_call x0 -> x2, Pallas kernels: none -> 12.1 us  [keep(): call(keep_kernel, first, (1,), [pl.BlockSpec(memory_space=pl.ANY)], pl.Bl...]
    ppermute x13 -> x19, waiting for transfers between devices: 9.68 us -> 18.6 us  [swap_cores(): return lax.ppermute(value, 'sensors', [(k, k ^ 1) for k in range(size)])]
    ppermute x13 -> x19, starting transfers between devices: 9.28 us -> 17.3 us  [swap_cores(): return lax.ppermute(value, 'sensors', [(k, k ^ 1) for k in range(size)])]
  transfers between devices with their start and end apart: 55 -> 81, of which waited for: 34 -> 46; matrix products, arithmetic and copies ran while one was open for 3% -> 3% of each run, Pallas kernels for 26% -> 27%
where the time goes in v5:
time: 658 us; the launch traced here: 646 us
  Pallas kernels  183 us (28%)
  waiting for transfers between devices  163 us (25%)
  local copies, waits for them, and re-layouts  157 us (24%)
  starting transfers between devices  121 us (18%)
  between operations  15.6 us (2%)
  other arithmetic  7.52 us (1%)
    unnamed x99, local copies, waits for them, and re-layouts  127 us
    pallas_call x6, Pallas kernels, observe(): call(observe_kernel, core, (rows // CHUNK_ROWS,), [pl.BlockSpec(block, la...  74.3 us
    reduce_scatter x6, waiting for transfers between devices, shards(): lax.psum_scatter(misfit, 'sensors', scatter_dimension=0, axis_index_group...  65.5 us
    pallas_call x6, Pallas kernels, pull_back(): call(pull_kernel, core, (rows // CHUNK_ROWS,), [whole_block(array) for ar...  58.1 us
    ppermute x12, starting transfers between devices, misfit_rims(): return (lax.ppermute(edge, both, same), lax.ppermute(edge, both, cross))  38.9 us
    ppermute x10, starting transfers between devices, rims(): lax.ppermute(bottom, 'cells', onward)  34.8 us
    all_gather x6, waiting for transfers between devices, shards(): lax.all_gather(state[1], 'sensors', axis_index_groups=lines)  25 us
    ppermute x12, waiting for transfers between devices, misfit_rims(): return (lax.ppermute(edge, both, same), lax.ppermute(edge, both, cross))  20.5 us
  transfers between devices with their start and end apart: 81, of which 46 were waited for; matrix products, arithmetic and copies ran while one was open for 3% of the time, Pallas kernels for 27%

profile of v5, /device:TPU:1, one launch (start us, length us, event | category | flops | bytes accessed | tf_op | source)
XLA Modules:
  0.0 646.3 jit_solution(11992824041995034387)
XLA Ops:
  34.9 17.5 %constant_dynamic-slice_fusion = bf16[2,128,16,2048]{3,2,1,0:T(8,128)(2,1)} fusion(bf16[2,128,16,4096]{3,2,1,0:T(8,128)(2,1)} %map_ref.1, s32[]{:T(128)S(6)} %select_n.56), kind=kLoop, calls=%fused_computation.61 | loop fusion | bytes 33554436 | tf_op jit(solution)/shard_map/dynamic_slice | solution.py:552
  53.8 6.5 %collective-permute-done.45 = bf16[2,16,32,128]{3,2,1,0:T(8,128)(2,1)S(1)} collective-permute-done((bf16[2,16,32,128]{3,2,1,0:T(8,128)(2,1)S(1)}, bf16[2,16,32,128]{3,2,1,0:T(8,128)(2,1)S(1)}, u32[]{:S(2)}, u32[]{:S(2)}) %collective-permute-start.45) | collective-permute-done | bytes 262176 | tf_op jit(solution)/shard_map/ppermute | solution.py:489
  103.4 5.8 keep.2.refs_1_.refs_5_
  109.2 5.8 copy-done
  115.0 6.3 keep.3.refs_2_.refs_6_
  127.2 5.9 copy-done.1
  133.0 5.8 copy-done.9
  138.9 12.4 %observe.10 = f32[2,2,2,16,128]{4,3,2,1,0:T(8,128)S(1)} custom-call(s32[1]{0:T(128)} %bitcast.core_ref, bf16[4,2,2,16,32,128]{5,4,3,2,1,0:T(8,128)(2,1)} %bitcast.99, bf16[2,128,16,2048]{3,2,1,0:T(8,128)(2,1)S(1)} %copy-done.1, bf16[2,128,16,2048]{3,2,1,0:T(8,128)(2,1)S(1)} %copy-done.9, bf16[256,256]{1,0:T(8,128)(2,1)S(1)} %copy.20.refs_3_, ...), custom_call_target="tpu_custom_call" | custom-call | flops 268435456 | bytes 2097152 | tf_op jit(solution)/shard_map/observe/pallas_call | solution.py:374
  157.4 5.8 copy-done.2
  163.2 6.1 copy-done.10
  169.3 9.7 %pull_back.10 = bf16[4,2,2,16,32,128]{5,4,3,2,1,0:T(8,128)(2,1)} custom-call(s32[1]{0:T(128)} %bitcast.core_ref, f32[2,2,2,16,128]{4,3,2,1,0:T(8,128)S(1)} %reverse_add_fusion.1.refs_0_, f32[2,2,2,16,128]{4,3,2,1,0:T(8,128)S(1)} %collective-permute-done.47.refs_1_, f32[2,2,2,16,128]{4,3,2,1,0:T(8,128)S(1)} %collective-permute-done.48.refs_2_, ...), custom_call_target="tpu_custom_call" | custom-call | flops 268435456 | bytes 2097152 | tf_op jit(solution)/shard_map/pull_back/pallas_call | solution.py:447
  179.3 5.8 copy-done.3
  185.1 5.9 copy-done.11
  191.0 12.4 %observe.8 = f32[2,2,2,16,128]{4,3,2,1,0:T(8,128)S(1)} custom-call(s32[1]{0:T(128)} %bitcast.core_ref, bf16[4,2,2,16,32,128]{5,4,3,2,1,0:T(8,128)(2,1)} %bitcast.97, bf16[2,128,16,2048]{3,2,1,0:T(8,128)(2,1)S(1)} %copy-done.3, bf16[2,128,16,2048]{3,2,1,0:T(8,128)(2,1)S(1)} %copy-done.11, bf16[256,256]{1,0:T(8,128)(2,1)S(1)} %copy.20.refs_3_, ...), custom_call_target="tpu_custom_call" | custom-call | flops 268435456 | bytes 2097152 | tf_op jit(solution)/shard_map/observe/pallas_call | solution.py:374
  212.8 9.7 %pull_back.8 = bf16[4,2,2,16,32,128]{5,4,3,2,1,0:T(8,128)(2,1)} custom-call(s32[1]{0:T(128)} %bitcast.core_ref, f32[2,2,2,16,128]{4,3,2,1,0:T(8,128)S(1)} %reverse_add_fusion.3.refs_0_, f32[2,2,2,16,128]{4,3,2,1,0:T(8,128)S(1)} %collective-permute-done.30.refs_1_, f32[2,2,2,16,128]{4,3,2,1,0:T(8,128)S(1)} %collective-permute-done.31.refs_2_, ...), custom_call_target="tpu_custom_call" | custom-call | flops 268435456 | bytes 2097152 | tf_op jit(solution)/shard_map/pull_back/pallas_call | solution.py:447
  222.6 5.9 copy-done.4
  228.4 5.9 copy-done.12
  234.3 12.4 %observe.6 = f32[2,2,2,16,128]{4,3,2,1,0:T(8,128)S(1)} custom-call(s32[1]{0:T(128)} %bitcast.core_ref, bf16[4,2,2,16,32,128]{5,4,3,2,1,0:T(8,128)(2,1)} %bitcast.96, bf16[2,128,16,2048]{3,2,1,0:T(8,128)(2,1)S(1)} %copy-done.4, bf16[2,128,16,2048]{3,2,1,0:T(8,128)(2,1)S(1)} %copy-done.12, bf16[256,256]{1,0:T(8,128)(2,1)S(1)} %copy.20.refs_3_, ...), custom_call_target="tpu_custom_call" | custom-call | flops 268435456 | bytes 2097152 | tf_op jit(solution)/shard_map/observe/pallas_call | solution.py:374
  254.5 9.7 %pull_back.6 = bf16[4,2,2,16,32,128]{5,4,3,2,1,0:T(8,128)(2,1)} custom-call(s32[1]{0:T(128)} %bitcast.core_ref, f32[2,2,2,16,128]{4,3,2,1,0:T(8,128)S(1)} %reverse_add_fusion.5.refs_0_, f32[2,2,2,16,128]{4,3,2,1,0:T(8,128)S(1)} %collective-permute-done.11.refs_1_, f32[2,2,2,16,128]{4,3,2,1,0:T(8,128)S(1)} %collective-permute-done.12.refs_2_, ...), custom_call_target="tpu_custom_call" | custom-call | flops 268435456 | bytes 2097152 | tf_op jit(solution)/shard_map/pull_back/pallas_call | solution.py:447
  321.2 17.5 %reduce-scatter.7.cloned.1.call-done = bf16[1,2,2,16,32,128]{5,4,3,2,1,0:T(8,128)(2,1)} async-done(((bf16[4,2,2,16,32,128]{5,4,3,2,1,0:T(8,128)(2,1)}), bf16[1,2,2,16,32,128]{5,4,3,2,1,0:T(8,128)(2,1)}) %reduce-scatter.7.cloned.1.call-update) | async-done | bytes 524304 | tf_op jit(solution)/shard_map/reduce_scatter | solution.py:581
  368.4 17.5 %all-gather.23.cloned.1.call-done = bf16[8,2,16,32,128]{4,3,2,1,0:T(8,128)(2,1)} async-done(((bf16[2,2,16,32,128]{4,3,2,1,0:T(8,128)(2,1)}), bf16[8,2,16,32,128]{4,3,2,1,0:T(8,128)(2,1)}) %all-gather.23.cloned.1.call-update) | async-done | bytes 2097168 | tf_op jit(solution)/shard_map/all_gather | solution.py:574
  391.7 6.3 copy-done.13
  398.0 12.4 %observe.11 = f32[2,2,2,16,128]{4,3,2,1,0:T(8,128)S(1)} custom-call(s32[1]{0:T(128)} %bitcast.core_ref, bf16[4,2,2,16,32,128]{5,4,3,2,1,0:T(8,128)(2,1)} %bitcast.98, bf16[2,128,16,2048]{3,2,1,0:T(8,128)(2,1)S(1)} %copy-done.5, bf16[2,128,16,2048]{3,2,1,0:T(8,128)(2,1)S(1)} %copy-done.13, bf16[256,256]{1,0:T(8,128)(2,1)S(1)} %copy.20.refs_3_, ...), custom_call_target="tpu_custom_call" | custom-call | flops 268435456 | bytes 2097152 | tf_op jit(solution)/shard_map/observe/pallas_call | solution.py:374
  418.8 9.7 %pull_back.11 = bf16[4,2,2,16,32,128]{5,4,3,2,1,0:T(8,128)(2,1)} custom-call(s32[1]{0:T(128)} %bitcast.core_ref, f32[2,2,2,16,128]{4,3,2,1,0:T(8,128)S(1)} %reverse_add_fusion.refs_0_, f32[2,2,2,16,128]{4,3,2,1,0:T(8,128)S(1)} %collective-permute-done.57.refs_1_, f32[2,2,2,16,128]{4,3,2,1,0:T(8,128)S(1)} %collective-permute-done.58.refs_2_, ...), custom_call_target="tpu_custom_call" | custom-call | flops 268435456 | bytes 2097152 | tf_op jit(solution)/shard_map/pull_back/pallas_call | solution.py:447
  438.0 6.3 copy-done.14
  444.3 12.4 %observe.9 = f32[2,2,2,16,128]{4,3,2,1,0:T(8,128)S(1)} custom-call(s32[1]{0:T(128)} %bitcast.core_ref, bf16[4,2,2,16,32,128]{5,4,3,2,1,0:T(8,128)(2,1)} %bitcast.100, bf16[2,128,16,2048]{3,2,1,0:T(8,128)(2,1)S(1)} %copy-done.6, bf16[2,128,16,2048]{3,2,1,0:T(8,128)(2,1)S(1)} %copy-done.14, bf16[256,256]{1,0:T(8,128)(2,1)S(1)} %copy.20.refs_3_, ...), custom_call_target="tpu_custom_call" | custom-call | flops 268435456 | bytes 2097152 | tf_op jit(solution)/shard_map/observe/pallas_call | solution.py:374
  465.2 9.7 %pull_back.9 = bf16[4,2,2,16,32,128]{5,4,3,2,1,0:T(8,128)(2,1)} custom-call(s32[1]{0:T(128)} %bitcast.core_ref, f32[2,2,2,16,128]{4,3,2,1,0:T(8,128)S(1)} %reverse_add_fusion.2.refs_0_, f32[2,2,2,16,128]{4,3,2,1,0:T(8,128)S(1)} %collective-permute-done.40.refs_1_, f32[2,2,2,16,128]{4,3,2,1,0:T(8,128)S(1)} %collective-permute-done.41.refs_2_, ...), custom_call_target="tpu_custom_call" | custom-call | flops 268435456 | bytes 2097152 | tf_op jit(solution)/shard_map/pull_back/pallas_call | solution.py:447
  484.9 6.2 copy-done.15
  491.1 12.4 %observe.7 = f32[2,2,2,16,128]{4,3,2,1,0:T(8,128)S(1)} custom-call(s32[1]{0:T(128)} %bitcast.core_ref, bf16[4,2,2,16,32,128]{5,4,3,2,1,0:T(8,128)(2,1)} %bitcast.101, bf16[2,128,16,2048]{3,2,1,0:T(8,128)(2,1)S(1)} %copy-done.7, bf16[2,128,16,2048]{3,2,1,0:T(8,128)(2,1)S(1)} %copy-done.15, bf16[256,256]{1,0:T(8,128)(2,1)S(1)} %copy.20.refs_3_, ...), custom_call_target="tpu_custom_call" | custom-call | flops 268435456 | bytes 2097152 | tf_op jit(solution)/shard_map/observe/pallas_call | solution.py:374
  512.0 9.7 %pull_back.7 = bf16[4,2,2,16,32,128]{5,4,3,2,1,0:T(8,128)(2,1)} custom-call(s32[1]{0:T(128)} %bitcast.core_ref, f32[2,2,2,16,128]{4,3,2,1,0:T(8,128)S(1)} %reverse_add_fusion.4.refs_0_, f32[2,2,2,16,128]{4,3,2,1,0:T(8,128)S(1)} %collective-permute-done.21.refs_1_, f32[2,2,2,16,128]{4,3,2,1,0:T(8,128)S(1)} %collective-permute-done.22.refs_2_, ...), custom_call_target="tpu_custom_call" | custom-call | flops 268435456 | bytes 2097152 | tf_op jit(solution)/shard_map/pull_back/pallas_call | solution.py:447
  548.4 21.5 %reduce-scatter.13.cloned.1.call-done = bf16[1,2,2,16,32,128]{5,4,3,2,1,0:T(8,128)(2,1)} async-done(((bf16[4,2,2,16,32,128]{5,4,3,2,1,0:T(8,128)(2,1)}), bf16[1,2,2,16,32,128]{5,4,3,2,1,0:T(8,128)(2,1)}) %reduce-scatter.13.cloned.1.call-update) | async-done | bytes 524304 | tf_op jit(solution)/shard_map/reduce_scatter | solution.py:581
  591.5 23.7 %reduce-scatter.9.cloned.1.call-done = bf16[1,2,2,16,32,128]{5,4,3,2,1,0:T(8,128)(2,1)} async-done(((bf16[4,2,2,16,32,128]{5,4,3,2,1,0:T(8,128)(2,1)}), bf16[1,2,2,16,32,128]{5,4,3,2,1,0:T(8,128)(2,1)}) %reduce-scatter.9.cloned.1.call-update) | async-done | bytes 524304 | tf_op jit(solution)/shard_map/reduce_scatter | solution.py:581
  (319 shorter events, 310.3 us)
Async XLA Ops:
  7.2 119.9 %all-gather.21.cloned.1.call-start = ((), (), s32[]{:S(2)}) async-start(), calls=%async_computation.16 | async-start | bytes 2621440 | tf_op jit(solution)/shard_map/all_gather | solution.py:574
  8.7 14.4 %collective-permute-start.2 = (f32[2,4,128]{2,1,0:T(4,128)S(1)}, f32[2,4,128]{2,1,0:T(4,128)S(1)}, u32[]{:S(2)}, u32[]{:S(2)}) collective-permute-start(f32[2,4,128]{2,1,0:T(4,128)S(1)} %get-tuple-element.149), channel_id=1, source_target_pairs={{0,8},{8,16},{16,24},{1,9},{9,17},{17,25},{2,10},{10,18},{18,26},{... | collective-permute-start | bytes 12296 | tf_op jit(solution)/shard_map/ppermute | solution.py:471
  12.6 10.4 %collective-permute-start.3 = (f32[2,4,128]{2,1,0:T(4,128)S(1)}, f32[2,4,128]{2,1,0:T(4,128)S(1)}, u32[]{:S(2)}, u32[]{:S(2)}) collective-permute-start(f32[2,4,128]{2,1,0:T(4,128)S(1)} %get-tuple-element.150), channel_id=1, source_target_pairs={{8,0},{16,8},{24,16},{9,1},{17,9},{25,17},{10,2},{18,10},{26,18},{... | collective-permute-start | bytes 12296 | tf_op jit(solution)/shard_map/ppermute | solution.py:471
  52.4 62.6 %collective-permute-start.9 = (bf16[2,128,16,2048]{3,2,1,0:T(8,128)(2,1)}, bf16[2,128,16,2048]{3,2,1,0:T(8,128)(2,1)}, u32[]{:S(2)}, u32[]{:S(2)}) collective-permute-start(bf16[2,128,16,2048]{3,2,1,0:T(8,128)(2,1)} %constant_dynamic-slice_fusion), channel_id=1, source_target_pairs={{0,1},{1,0},{2,3},{3,2},{4,5},{5,4},{6,7},{7,6},{8,9},{9,8},{10,11... | collective-permute-start | bytes 50331656 | tf_op jit(solution)/shard_map/ppermute | solution.py:489
  61.2 118.0 %all-gather.17.cloned.1.call-start = ((), (), s32[]{:S(2)}) async-start(), calls=%async_computation.14 | async-start | bytes 2621440 | tf_op jit(solution)/shard_map/all_gather | solution.py:574
  82.4 140.2 %all-gather.13.cloned.1.call-start = ((), (), s32[]{:S(2)}) async-start(), calls=%async_computation.12 | async-start | bytes 2621440 | tf_op jit(solution)/shard_map/all_gather | solution.py:574
  102.0 162.2 %reduce-scatter.15.cloned.1.call-start = ((), (), s32[]{:S(2)}) async-start(), calls=%async_computation.10 | async-start | bytes 2621440 | tf_op jit(solution)/shard_map/reduce_scatter | solution.py:581
  179.0 114.2 %reduce-scatter.11.cloned.1.call-start = ((), (), s32[]{:S(2)}) async-start(), calls=%async_computation.8 | async-start | bytes 2621440 | tf_op jit(solution)/shard_map/reduce_scatter | solution.py:581
  222.5 116.3 %reduce-scatter.7.cloned.1.call-start = ((), (), s32[]{:S(2)}) async-start(), calls=%async_computation.6 | async-start | bytes 2621440 | tf_op jit(solution)/shard_map/reduce_scatter | solution.py:581
  264.2 121.7 %all-gather.23.cloned.1.call-start = ((), (), s32[]{:S(2)}) async-start(), calls=%async_computation.17 | async-start | bytes 2621440 | tf_op jit(solution)/shard_map/all_gather | solution.py:574
  265.3 17.3 %collective-permute-start.50 = (bf16[2,16,32,128]{3,2,1,0:T(8,128)(2,1)S(1)}, bf16[2,16,32,128]{3,2,1,0:T(8,128)(2,1)S(1)}, u32[]{:S(2)}, u32[]{:S(2)}) collective-permute-start(bf16[2,16,32,128]{3,2,1,0:T(8,128)(2,1)S(1)} %get-tuple-element.130), channel_id=1, source_target_pairs={{0,1},{1,0},{2,3},{3,2},{4,5},{5,4},{6,7},{7,6},{8,9},{9,8},{10,11... | collective-permute-start | bytes 786440 | tf_op jit(solution)/shard_map/ppermute | solution.py:489
  267.4 11.4 %collective-permute-start.43 = (bf16[2,4,32,128]{3,2,1,0:T(8,128)(2,1)S(1)}, bf16[2,4,32,128]{3,2,1,0:T(8,128)(2,1)S(1)}, u32[]{:S(2)}, u32[]{:S(2)}) collective-permute-start(bf16[2,4,32,128]{3,2,1,0:T(8,128)(2,1)S(1)} %get-tuple-element.86), channel_id=1, source_target_pairs={{0,8},{8,16},{16,24},{1,9},{9,17},{17,25},{2,10},{10,18},{18,26},{... | collective-permute-start | bytes 196616 | tf_op jit(solution)/shard_map/ppermute | solution.py:471
  270.3 8.6 %collective-permute-start.44 = (bf16[2,4,32,128]{3,2,1,0:T(8,128)(2,1)S(1)}, bf16[2,4,32,128]{3,2,1,0:T(8,128)(2,1)S(1)}, u32[]{:S(2)}, u32[]{:S(2)}) collective-permute-start(bf16[2,4,32,128]{3,2,1,0:T(8,128)(2,1)S(1)} %get-tuple-element.88), channel_id=1, source_target_pairs={{8,0},{16,8},{24,16},{9,1},{17,9},{25,17},{10,2},{18,10},{26,18},{... | collective-permute-start | bytes 196616 | tf_op jit(solution)/shard_map/ppermute | solution.py:471
  293.1 139.1 %all-gather.19.cloned.1.call-start = ((), (), s32[]{:S(2)}) async-start(), calls=%async_computation.15 | async-start | bytes 2621440 | tf_op jit(solution)/shard_map/all_gather | solution.py:574
  294.2 17.2 %collective-permute-start.33 = (bf16[2,16,32,128]{3,2,1,0:T(8,128)(2,1)S(1)}, bf16[2,16,32,128]{3,2,1,0:T(8,128)(2,1)S(1)}, u32[]{:S(2)}, u32[]{:S(2)}) collective-permute-start(bf16[2,16,32,128]{3,2,1,0:T(8,128)(2,1)S(1)} %get-tuple-element.134), channel_id=1, source_target_pairs={{0,1},{1,0},{2,3},{3,2},{4,5},{5,4},{6,7},{7,6},{8,9},{9,8},{10,11... | collective-permute-start | bytes 786440 | tf_op jit(solution)/shard_map/ppermute | solution.py:489
  294.9 13.3 %collective-permute-start.26 = (bf16[2,4,32,128]{3,2,1,0:T(8,128)(2,1)S(1)}, bf16[2,4,32,128]{3,2,1,0:T(8,128)(2,1)S(1)}, u32[]{:S(2)}, u32[]{:S(2)}) collective-permute-start(bf16[2,4,32,128]{3,2,1,0:T(8,128)(2,1)S(1)} %get-tuple-element.75), channel_id=1, source_target_pairs={{0,8},{8,16},{16,24},{1,9},{9,17},{17,25},{2,10},{10,18},{18,26},{... | collective-permute-start | bytes 196616 | tf_op jit(solution)/shard_map/ppermute | solution.py:471
  299.2 9.0 %collective-permute-start.27 = (bf16[2,4,32,128]{3,2,1,0:T(8,128)(2,1)S(1)}, bf16[2,4,32,128]{3,2,1,0:T(8,128)(2,1)S(1)}, u32[]{:S(2)}, u32[]{:S(2)}) collective-permute-start(bf16[2,4,32,128]{3,2,1,0:T(8,128)(2,1)S(1)} %get-tuple-element.77), channel_id=1, source_target_pairs={{8,0},{16,8},{24,16},{9,1},{17,9},{25,17},{10,2},{18,10},{26,18},{... | collective-permute-start | bytes 196616 | tf_op jit(solution)/shard_map/ppermute | solution.py:471
  321.2 157.9 %all-gather.15.cloned.1.call-start = ((), (), s32[]{:S(2)}) async-start(), calls=%async_computation.13 | async-start | bytes 2621440 | tf_op jit(solution)/shard_map/all_gather | solution.py:574
  339.9 16.2 %collective-permute-start.14 = (bf16[2,16,32,128]{3,2,1,0:T(8,128)(2,1)S(1)}, bf16[2,16,32,128]{3,2,1,0:T(8,128)(2,1)S(1)}, u32[]{:S(2)}, u32[]{:S(2)}) collective-permute-start(bf16[2,16,32,128]{3,2,1,0:T(8,128)(2,1)S(1)} %get-tuple-element.138), channel_id=1, source_target_pairs={{0,1},{1,0},{2,3},{3,2},{4,5},{5,4},{6,7},{7,6},{8,9},{9,8},{10,11... | collective-permute-start | bytes 786440 | tf_op jit(solution)/shard_map/ppermute | solution.py:489
  340.7 11.9 %collective-permute-start.4 = (bf16[2,4,32,128]{3,2,1,0:T(8,128)(2,1)S(1)}, bf16[2,4,32,128]{3,2,1,0:T(8,128)(2,1)S(1)}, u32[]{:S(2)}, u32[]{:S(2)}) collective-permute-start(bf16[2,4,32,128]{3,2,1,0:T(8,128)(2,1)S(1)} %get-tuple-element.57), channel_id=1, source_target_pairs={{0,8},{8,16},{16,24},{1,9},{9,17},{17,25},{2,10},{10,18},{18,26},{... | collective-permute-start | bytes 196616 | tf_op jit(solution)/shard_map/ppermute | solution.py:471
  343.9 8.8 %collective-permute-start.5 = (bf16[2,4,32,128]{3,2,1,0:T(8,128)(2,1)S(1)}, bf16[2,4,32,128]{3,2,1,0:T(8,128)(2,1)S(1)}, u32[]{:S(2)}, u32[]{:S(2)}) collective-permute-start(bf16[2,4,32,128]{3,2,1,0:T(8,128)(2,1)S(1)} %get-tuple-element.59), channel_id=1, source_target_pairs={{8,0},{16,8},{24,16},{9,1},{17,9},{25,17},{10,2},{18,10},{26,18},{... | collective-permute-start | bytes 196616 | tf_op jit(solution)/shard_map/ppermute | solution.py:471
  368.4 156.0 %reduce-scatter.17.cloned.1.call-start = ((), (), s32[]{:S(2)}) async-start(), calls=%async_computation.11 | async-start | bytes 2621440 | tf_op jit(solution)/shard_map/reduce_scatter | solution.py:581
  428.5 141.4 %reduce-scatter.13.cloned.1.call-start = ((), (), s32[]{:S(2)}) async-start(), calls=%async_computation.9 | async-start | bytes 2621440 | tf_op jit(solution)/shard_map/reduce_scatter | solution.py:581
  474.9 140.3 %reduce-scatter.9.cloned.1.call-start = ((), (), s32[]{:S(2)}) async-start(), calls=%async_computation.7 | async-start | bytes 2621440 | tf_op jit(solution)/shard_map/reduce_scatter | solution.py:581
  525.5 16.2 %collective-permute-start.60 = (bf16[2,16,32,128]{3,2,1,0:T(8,128)(2,1)S(1)}, bf16[2,16,32,128]{3,2,1,0:T(8,128)(2,1)S(1)}, u32[]{:S(2)}, u32[]{:S(2)}) collective-permute-start(bf16[2,16,32,128]{3,2,1,0:T(8,128)(2,1)S(1)} %get-tuple-element.126), channel_id=1, source_target_pairs={{0,1},{1,0},{2,3},{3,2},{4,5},{5,4},{6,7},{7,6},{8,9},{9,8},{10,11... | collective-permute-start | bytes 786440 | tf_op jit(solution)/shard_map/ppermute | solution.py:489
  526.4 11.7 %collective-permute-start.53 = (bf16[2,4,32,128]{3,2,1,0:T(8,128)(2,1)S(1)}, bf16[2,4,32,128]{3,2,1,0:T(8,128)(2,1)S(1)}, u32[]{:S(2)}, u32[]{:S(2)}) collective-permute-start(bf16[2,4,32,128]{3,2,1,0:T(8,128)(2,1)S(1)} %copy-done.38), channel_id=1, source_target_pairs={{0,8},{8,16},{16,24},{1,9},{9,17},{17,25},{2,10},{10,18},{18,26},{... | collective-permute-start | bytes 196616 | tf_op jit(solution)/shard_map/ppermute | solution.py:471
  529.5 8.6 %collective-permute-start.54 = (bf16[2,4,32,128]{3,2,1,0:T(8,128)(2,1)S(1)}, bf16[2,4,32,128]{3,2,1,0:T(8,128)(2,1)S(1)}, u32[]{:S(2)}, u32[]{:S(2)}) collective-permute-start(bf16[2,4,32,128]{3,2,1,0:T(8,128)(2,1)S(1)} %get-tuple-element.94), channel_id=1, source_target_pairs={{8,0},{16,8},{24,16},{9,1},{17,9},{25,17},{10,2},{18,10},{26,18},{... | collective-permute-start | bytes 196616 | tf_op jit(solution)/shard_map/ppermute | solution.py:471
  571.0 16.2 %collective-permute-start.63 = (bf16[2,16,32,128]{3,2,1,0:T(8,128)(2,1)S(1)}, bf16[2,16,32,128]{3,2,1,0:T(8,128)(2,1)S(1)}, u32[]{:S(2)}, u32[]{:S(2)}) collective-permute-start(bf16[2,16,32,128]{3,2,1,0:T(8,128)(2,1)S(1)} %get-tuple-element.122), channel_id=1, source_target_pairs={{0,1},{1,0},{2,3},{3,2},{4,5},{5,4},{6,7},{7,6},{8,9},{9,8},{10,11... | collective-permute-start | bytes 786440 | tf_op jit(solution)/shard_map/ppermute | solution.py:489
  571.9 11.7 %collective-permute-start.36 = (bf16[2,4,32,128]{3,2,1,0:T(8,128)(2,1)}, bf16[2,4,32,128]{3,2,1,0:T(8,128)(2,1)S(1)}, u32[]{:S(2)}, u32[]{:S(2)}) collective-permute-start(bf16[2,4,32,128]{3,2,1,0:T(8,128)(2,1)} %copy-done.41), channel_id=1, source_target_pairs={{0,8},{8,16},{16,24},{1,9},{9,17},{17,25},{2,10},{10,18},{18,26},{... | collective-permute-start | bytes 196616 | tf_op jit(solution)/shard_map/ppermute | solution.py:471
  575.0 8.6 %collective-permute-start.37 = (bf16[2,4,32,128]{3,2,1,0:T(8,128)(2,1)S(1)}, bf16[2,4,32,128]{3,2,1,0:T(8,128)(2,1)S(1)}, u32[]{:S(2)}, u32[]{:S(2)}) collective-permute-start(bf16[2,4,32,128]{3,2,1,0:T(8,128)(2,1)S(1)} %copy-done.40), channel_id=1, source_target_pairs={{8,0},{16,8},{24,16},{9,1},{17,9},{25,17},{10,2},{18,10},{26,18},{... | collective-permute-start | bytes 196616 | tf_op jit(solution)/shard_map/ppermute | solution.py:471
  616.3 15.9 %collective-permute-start.66 = (bf16[2,16,32,128]{3,2,1,0:T(8,128)(2,1)S(1)}, bf16[2,16,32,128]{3,2,1,0:T(8,128)(2,1)S(1)}, u32[]{:S(2)}, u32[]{:S(2)}) collective-permute-start(bf16[2,16,32,128]{3,2,1,0:T(8,128)(2,1)S(1)} %get-tuple-element.118), channel_id=1, source_target_pairs={{0,1},{1,0},{2,3},{3,2},{4,5},{5,4},{6,7},{7,6},{8,9},{9,8},{10,11... | collective-permute-start | bytes 786440 | tf_op jit(solution)/shard_map/ppermute | solution.py:489
  617.3 11.8 %collective-permute-start.17 = (bf16[2,4,32,128]{3,2,1,0:T(8,128)(2,1)S(1)}, bf16[2,4,32,128]{3,2,1,0:T(8,128)(2,1)S(1)}, u32[]{:S(2)}, u32[]{:S(2)}) collective-permute-start(bf16[2,4,32,128]{3,2,1,0:T(8,128)(2,1)S(1)} %copy-done.45), channel_id=1, source_target_pairs={{0,8},{8,16},{16,24},{1,9},{9,17},{17,25},{2,10},{10,18},{18,26},{... | collective-permute-start | bytes 196616 | tf_op jit(solution)/shard_map/ppermute | solution.py:471
  (98 other events, 497.2 us)
Sparse Core Ops, SparseCore 0:
  61.3 47.1 all-gather.20
  110.7 44.6 all-gather.16
  157.5 44.6 all-gather.12
  204.3 42.4 reduce-scatter.14
  249.6 43.2 reduce-scatter.10
  295.6 43.1 reduce-scatter.6
  340.4 45.4 all-gather.22
  387.5 44.6 all-gather.18
  434.4 44.6 all-gather.14
  481.9 42.4 reduce-scatter.16
  526.7 43.1 reduce-scatter.12
  572.2 43.0 reduce-scatter.8

commit v6 on v3

--- a/solution.py
+++ b/solution.py
@@ -12,6 +12,7 @@
 DAMPING = 0.8
 HALO = SWEEPS
 LANES = 128
+APART = 3
 SUBLANES = 8
 GROUPS = 2
 CHUNK_ROWS = 4
@@ -280,9 +281,11 @@
     return jnp.concatenate(parts, axis=0)
 
 
-def observe_kernel(core_ref, *refs):
-    field_ref, own_ref, other_ref, table_ref, cell_ref, out_ref, spec, acc, picked = refs
-    chips, _, members, rows, steps, lanes = field_ref.shape
+def observe_kernel(core_ref, field_ref, *refs):
+    *slot_refs, own_ref, other_ref, table_ref, around_ref, cell_ref = refs[:-4]
+    out_ref, spec, acc, picked = refs[-4:]
+    chips, _, whole, rows, steps, lanes = field_ref.shape
+    members = spec.shape[0] // 2
     freqs, sensors, width = own_ref.shape[1:]
     near = lanes // sensors
     wide = 2 * lanes
@@ -296,12 +299,16 @@
     marks = marks_of(cell_ref, width)
 
     def history(b, r):
-        return field_ref[:, :, b, r].reshape(2 * chips * steps, lanes)
+        if b < whole:
+            return field_ref[:, :, b, r].reshape(2 * chips * steps, lanes)
+        slots = [slot_refs[0][:, b - whole, r]]
+        for k in range(1, chips):
+            slots.append(slot_refs[k][:, b - whole, r] + slot_refs[2 * chips - 1 - k][:, b - whole, r])
+        return jnp.concatenate([slot.reshape(2 * steps, lanes) for slot in slots], axis=0)
 
     for b in range(members):
-        spectrum = dot(
-            table_ref[...], jnp.concatenate([history(b, r) for r in range(rows)], axis=1)
-        )
+        table = table_ref[...] if b < whole else around_ref[...]
+        spectrum = dot(table, jnp.concatenate([history(b, r) for r in range(rows)], axis=1))
         spec[2 * b] = spectrum[:freqs]
         spec[2 * b + 1] = spectrum[freqs:]
     for m in range(2 * members):
@@ -329,36 +336,36 @@
                     out_ref[1, part, b, q : q + 1] = line[:, lanes:]
 
 
-def map_specs(own, other, width):
-    chunks = other.shape[3] // width
-    return [
-        pl.BlockSpec(own.shape[:3] + (width,), lambda c, core: (0, 0, 0, core[0] * chunks + c)),
-        pl.BlockSpec(other.shape[:3] + (width,), lambda c, core: (0, 0, 0, c)),
-    ]
-
-
-def map_cost(members, own, other, moved):
+def map_specs(own, width):
+    chunks = own.shape[3] // (2 * width)
+    spec = pl.BlockSpec(own.shape[:3] + (width,), lambda c, core: (0, 0, 0, core[0] * chunks + c))
+    return [spec, spec]
+
+
+def map_cost(members, own, moved):
     return pl.CostEstimate(
-        flops=16 * members * other.size,
-        bytes_accessed=4 * other.size + 2 * moved,
-        transcendentals=0,
+        flops=8 * members * own.size, bytes_accessed=2 * own.size + 2 * moved, transcendentals=0
     )
 
 
-def observe(core, field, own, other, table, local_cells):
-    chips, _, members, rows, steps, lanes = field.shape
-    _, freqs, sensors, cells = other.shape
+def observe(core, field, slots, own, other, table, around, local_cells):
+    chips, _, whole, rows, steps, lanes = field.shape
+    apart = slots[0].shape[1]
+    members = whole + apart
+    _, freqs, sensors, cells = own.shape
     width = CHUNK_ROWS * lanes
     near = lanes // sensors
     shape = (2, 2, members, freqs // near, lanes)
-    block = (chips, 2, members, CHUNK_ROWS, steps, lanes)
+    block = (chips, 2, whole, CHUNK_ROWS, steps, lanes)
+    slot = pl.BlockSpec((2, apart, CHUNK_ROWS, steps, lanes), lambda c, core: (0, 0, c, 0, 0))
     return call(
         observe_kernel,
         core,
         (rows // CHUNK_ROWS,),
         [pl.BlockSpec(block, lambda c, core: (0, 0, 0, c, 0, 0))]
-        + map_specs(own, other, width)
-        + [whole_block(table), whole_block(local_cells)],
+        + [slot] * len(slots)
+        + map_specs(own, width)
+        + [whole_block(table), whole_block(around), whole_block(local_cells)],
         pl.BlockSpec(shape, lambda c, core: (0, 0, 0, 0, 0)),
         jax.ShapeDtypeStruct(shape, jnp.float32),
         [
@@ -366,13 +373,14 @@
             pltpu.VMEM((freqs // near, 2 * members * near, 4 * lanes), jnp.float32),
             pltpu.VMEM((2 * members, freqs, 2 * lanes), jnp.float32),
         ],
-        cost_estimate=map_cost(members, own, other, field.size),
+        cost_estimate=map_cost(members, own, field.size),
         name="observe",
-    )(core, field, own, other, table, local_cells)
+    )(core, field, *slots, own, other, table, around, local_cells)
 
 
 def pull_kernel(core_ref, *refs):
-    *sums, noise_ref, own_ref, other_ref, back_ref, cell_ref, out_ref, weights, adjoint = refs
+    *sums, noise_ref, own_ref, other_ref, back_ref, cell_ref = refs[:-3]
+    out_ref, weights, adjoint = refs[-3:]
     devices, _, members, rows, steps, lanes = out_ref.shape
     freqs, sensors, width = own_ref.shape[1:]
     near = lanes // sensors
@@ -421,7 +429,7 @@
 
 def pull_back(core, sums, noise, own, other, back, local_cells, shape):
     devices, _, members, rows, steps, lanes = shape
-    _, freqs, sensors, cells = other.shape
+    _, freqs, sensors, cells = own.shape
     width = CHUNK_ROWS * lanes
     small = [*sums, noise]
     return call(
@@ -429,7 +437,7 @@
         core,
         (rows // CHUNK_ROWS,),
         [whole_block(array) for array in small]
-        + map_specs(own, other, width)
+        + map_specs(own, width)
         + [whole_block(back), whole_block(local_cells)],
         pl.BlockSpec(
             (devices, 2, members, CHUNK_ROWS, steps, lanes), lambda c, core: (0, 0, 0, c, 0, 0)
@@ -439,7 +447,7 @@
             pltpu.VMEM((2 * members, freqs, 4 * lanes), jnp.float32),
             pltpu.VMEM((2 * members, freqs, width), jnp.float32),
         ],
-        cost_estimate=map_cost(members, own, other, math.prod(shape)),
+        cost_estimate=map_cost(members, own, math.prod(shape)),
         name="pull_back",
     )(core, *small, own, other, back, local_cells)
 
@@ -479,6 +487,35 @@
     ]
 
 
+class Line:
+    def __init__(self, value):
+        self.size = lax.axis_size("sensors")
+        self.value, self.ups, self.downs = value, [], []
+        self.ends = (value, value)
+
+    def hop(self, last=False):
+        while len(self.ups) < self.size // 2 - 1:
+            start = 2 * len(self.ups)
+            onward = [(k, k + 2) for k in range(start, self.size - 2)]
+            backward = [(self.size - 1 - k, self.size - 1 - there) for k, there in onward]
+            up = lax.ppermute(self.ends[0], "sensors", onward)
+            down = lax.ppermute(self.ends[1], "sensors", backward)
+            self.ups.append(up)
+            self.downs.append(down)
+            self.ends = (up, down)
+            if not last:
+                break
+
+    def after(self, other):
+        if other is not None and self.ups:
+            self.ends, other = lax.optimization_barrier((self.ends, other))
+            self.ups[-1], self.downs[-1] = self.ends
+        return other
+
+    def slots(self):
+        return [self.value, *self.ups, *self.downs]
+
+
 def shards(rhs, forward_map, stiffness, reaction, noise_weight, sensor_cell):
     steps, samples, rows, cols = rhs.shape
     _, freqs, sensors, cells = forward_map.shape
@@ -489,9 +526,7 @@
     core = sensor_index % 2
     near = LANES // sensors
     half = cells // 2
-
-    away = lax.dynamic_slice_in_dim(forward_map, (1 - core) * half, half, axis=3)
-    other_map = swap_cores(away)
+    other_map = swap_cores(forward_map)
 
     cores = jnp.stack([core, 1 - core])
     offsets = cores[None, :, None] * steps + jnp.arange(steps, dtype=jnp.int32)
@@ -499,6 +534,9 @@
     places = jnp.arange(chips, dtype=jnp.int32)[:, None, None] * chip_steps
     table = transform_table(freqs, places + offsets)
     back = table.T
+    chip = sensor_index // 2
+    places = (chip - jnp.arange(chips, dtype=jnp.int32)) % chips
+    around = transform_table(freqs, places[:, None, None] * chip_steps + offsets)
 
     diagonal = reaction + 4.0 * stiffness * stiffness
     local = jnp.stack([stiffness, diagonal])
@@ -522,43 +560,83 @@
     core = core.reshape(1)
 
     members = samples // GROUPS
+    whole = members - members // APART
+    edge_rows = lax.optimization_barrier((rhs[:, :, :HALO], rhs[:, :, rows - HALO :]))
+    top, bottom = (jnp.transpose(rim, (1, 2, 0, 3)).astype(jnp.bfloat16) for rim in edge_rows)
+    lines = [[k for k in range(size) if k % 2 == parity] for parity in range(2)]
+    shape = (chips, 2, members, rows // 2, steps, cols)
+
+    def ready(state):
+        iterate, keep, give, rest, top, bottom = state
+        above, below = rims(top, bottom)
+        pair = jnp.stack([keep, swap_cores(give)])
+        parts = lax.optimization_barrier((pair[:, :whole], pair[:, whole:]))
+        return iterate, *parts, (above, rest, below)
+
+    def edges(misfit):
+        first = (rows // 2 - HALO) * core[0]
+        edge = lax.dynamic_slice_in_dim(misfit, first, HALO, axis=2)
+        same, _ = misfit_rims(edge[0])
+        _, cross = misfit_rims(edge[1])
+        return misfit[0], swap_cores(misfit[1]), same, cross
+
     states = []
     for group in range(GROUPS):
-        group_rhs = rhs[:, group * members : (group + 1) * members]
-        up, down = rims(
-            *(
-                jnp.transpose(rim, (1, 2, 0, 3)).astype(jnp.bfloat16)
-                for rim in (group_rhs[:, :, :HALO], group_rhs[:, :, rows - HALO :])
-            )
-        )
-        states.append(start(group, members, core, rhs, up, down, coeff))
-
-    lines = [[k for k in range(size) if k % 2 == parity] for parity in range(2)]
+        here = slice(group * members, (group + 1) * members)
+        ends = (top[here], bottom[here])
+        if states:
+            iterate, pair, *others = states[0]
+            pair, ends = lax.optimization_barrier((pair, ends))
+            states[0] = (iterate, pair, *others)
+        begun = start(group, members, core, rhs, *rims(*ends), coeff)
+        states.append(ready(begun))
+
+    line = Line(states[0][2])
     outputs = ()
     for iteration in range(ITERS):
+        fields = [lax.all_gather(state[1], "sensors", axis_index_groups=lines) for state in states]
+        line.hop(last=True)
+        totals = []
         for group in range(GROUPS):
-            iterate, keep, give, rest, top, bottom = states[group]
-            above, below = rims(top, bottom)
-            field = lax.all_gather(
-                jnp.stack([keep, swap_cores(give)]), "sensors", axis_index_groups=lines
+            iterate, _, _, rests = states[group]
+            field, rests = lax.optimization_barrier((fields[group], rests))
+            states[group] = iterate, rests
+            slots, line = line.slots(), None
+            if group + 1 < GROUPS:
+                line = Line(states[group + 1][2])
+                line.hop()
+            sums = observe(
+                core, field, slots, forward_map, other_map, table, around, local_cells
             )
-            sums = observe(core, field, forward_map, other_map, table, local_cells)
+            if line is not None:
+                sums = line.after(sums)
+                line.hop()
             sums = from_all_cells(sums + swap_cores(sums)[::-1])
-            shape = (chips, 2, members, rows // 2, steps, cols)
             misfit = pull_back(core, sums, noise, forward_map, other_map, back, local_cells, shape)
-            misfit = lax.psum_scatter(
-                misfit, "sensors", scatter_dimension=0, axis_index_groups=lines, tiled=False
+            if line is not None:
+                misfit = line.after(misfit)
+                line.hop(last=True)
+            totals.append(
+                lax.psum_scatter(
+                    misfit, "sensors", scatter_dimension=0, axis_index_groups=lines, tiled=False
+                )
             )
-            first = (rows // 2 - HALO) * core[0]
-            edge = lax.dynamic_slice_in_dim(misfit, first, HALO, axis=2)
-            same, _ = misfit_rims(edge[0])
-            _, cross = misfit_rims(edge[1])
-            misfits = (misfit[0], swap_cores(misfit[1]), same, cross)
-            rests = (above, rest, below)
+        for group in range(GROUPS):
+            iterate, rests = states[group]
+            total = totals[group]
             if iteration < ITERS - 1:
-                states[group] = step(core, rests, misfits, iterate, coeff)
+                if group == 1:
+                    line.hop()
+                    total = line.after(total)
+                states[group] = ready(step(core, rests, edges(total), iterate, coeff))
+                if group == 0:
+                    line = Line(states[0][2])
             else:
-                outputs = finish(group, samples, core, rests, misfits, iterate, coeff, outputs)
+                if outputs:
+                    total, outputs = lax.optimization_barrier((total, outputs))
+                outputs = finish(
+                    group, samples, core, rests, edges(total), iterate, coeff, outputs
+                )
     return tuple(out.reshape(rhs.shape) for out in outputs)
 
 

time: 610 us -> 600 us (0.984)
  waiting for transfers between devices: 282 us -> 184 us
  starting transfers between devices: 82.2 us -> 163 us
  other arithmetic: 4.78 us -> 11.1 us
    all_gather x4, waiting for transfers between devices: 113 us -> 0.03 us  [shards(): lax.all_gather(state[1], 'sensors', axis_index_groups=lines)]
    reduce_scatter x4, waiting for transfers between devices: 124 us -> 75.2 us  [shards(): lax.psum_scatter(misfit, 'sensors', scatter_dimension=0, axis_index_group...]
    ppermute x0 -> x24, starting transfers between devices: none -> 46.7 us  [the longest x12 31.1 us: hop(): up = lax.ppermute(self.ends[0], 'sensors', onward)]
    ppermute x0 -> x24, waiting for transfers between devices: none -> 35.4 us  [the longest x12 35.4 us: hop(): down = lax.ppermute(self.ends[1], 'sensors', backward)]
    ppermute x13, starting transfers between devices: 9.28 us -> 38.3 us  [swap_cores(): return lax.ppermute(value, 'sensors', [(k, k ^ 1) for k in range(size)])]
    dynamic_slice x1 -> x0, local copies, waits for them, and re-layouts: 14.4 us -> none  [shards(): lax.dynamic_slice_in_dim(forward_map, (1 - core) * half, half, axis=3)]
    ppermute x13, waiting for transfers between devices: 9.68 us -> 23 us  [swap_cores(): return lax.ppermute(value, 'sensors', [(k, k ^ 1) for k in range(size)])]
    ppermute x7, waiting for transfers between devices: 8.65 us -> 20.6 us  [rims(): lax.ppermute(top, 'cells', backward)]
  transfers between devices with their start and end apart: 55 -> 79, of which waited for: 34 -> 40; matrix products, arithmetic and copies ran while one was open for 3% -> 4% of each run, Pallas kernels for 26% -> 27%
where the time goes in v6:
time: 600 us; the launch traced here: 596 us
  waiting for transfers between devices  184 us (31%)
  Pallas kernels  167 us (28%)
  starting transfers between devices  163 us (27%)
  local copies, waits for them, and re-layouts  55.5 us (9%)
  between operations  15.1 us (3%)
  other arithmetic  11.1 us (2%)
    reduce_scatter x4, waiting for transfers between devices, shards(): lax.psum_scatter(misfit, 'sensors', scatter_dimension=0, axis_index_group...  75.2 us
    pallas_call x4, Pallas kernels, observe(): call(observe_kernel, core, (rows // CHUNK_ROWS,), [pl.BlockSpec(block, la...  70.4 us
    pallas_call x4, Pallas kernels, pull_back(): call(pull_kernel, core, (rows // CHUNK_ROWS,), [whole_block(array) for ar...  58.3 us
    unnamed x86, local copies, waits for them, and re-layouts  42.6 us
    ppermute x13, starting transfers between devices, swap_cores(): return lax.ppermute(value, 'sensors', [(k, k ^ 1) for k in range(size)])  38.3 us
    ppermute x12, waiting for transfers between devices, hop(): down = lax.ppermute(self.ends[1], 'sensors', backward)  35.4 us
    ppermute x12, starting transfers between devices, hop(): up = lax.ppermute(self.ends[0], 'sensors', onward)  31.1 us
    ppermute x7, starting transfers between devices, rims(): lax.ppermute(bottom, 'cells', onward)  27.7 us
  transfers between devices with their start and end apart: 79, of which 40 were waited for; matrix products, arithmetic and copies ran while one was open for 4% of the time, Pallas kernels for 27%

profile of v6, /device:TPU:1, one launch (start us, length us, event | category | flops | bytes accessed | tf_op | source)
XLA Modules:
  0.0 596.3 jit_solution(11039526464655192403)
XLA Ops:
  8.8 4.6 collective-permute-start.2
  28.9 6.1 %start.2 = (f32[3,32,32,128]{3,2,1,0:T(8,128)S(1)}, bf16[3,16,32,128]{3,2,1,0:T(8,128)(2,1)S(1)}, bf16[3,16,32,128]{3,2,1,0:T(8,128)(2,1)S(1)}, f32[3,32,32,128]...) custom-call(s32[1]{0:T(128)} %bitcast.core_ref, ...), custom_call_target="tpu_custom_call" | custom-call | tf_op jit(solution)/shard_map/start/pallas_call | solution.py:155
  39.9 17.1 %collective-permute-done.4 = bf16[3,16,32,128]{3,2,1,0:T(8,128)(2,1)S(1)} collective-permute-done((bf16[3,16,32,128]{3,2,1,0:T(8,128)(2,1)S(1)}, bf16[3,16,32,128]{3,2,1,0:T(8,128)(2,1)S(1)}, u32[]{:S(2)}, u32[]{:S(2)}) %collective-permute-start.4) | collective-permute-done | bytes 393248 | tf_op jit(solution)/shard_map/ppermute | solution.py:477
  57.9 4.3 collective-permute-start.5
  69.6 6.1 %start.3 = (f32[3,32,32,128]{3,2,1,0:T(8,128)S(1)}, bf16[3,16,32,128]{3,2,1,0:T(8,128)(2,1)S(1)}, bf16[3,16,32,128]{3,2,1,0:T(8,128)(2,1)S(1)}, f32[3,32,32,128]...) custom-call(s32[1]{0:T(128)} %bitcast.core_ref, ...), custom_call_target="tpu_custom_call" | custom-call | tf_op jit(solution)/shard_map/start/pallas_call | solution.py:155
  83.6 4.0 collective-permute-start.14
  88.3 15.2 %collective-permute-done.17.refs_4_ = bf16[2,1,16,32,128]{4,3,2,1,0:T(8,128)(2,1)S(1)} collective-permute-done((bf16[2,1,16,32,128]{4,3,2,1,0:T(8,128)(2,1)S(1)}, bf16[2,1,16,32,128]{4,3,2,1,0:T(8,128)(2,1)S(1)}, u32[]{:S(2)}, u32[]{:S(2)}) %collective-permute-start.17) | collective-permute-done | bytes 262176 | tf_op jit(solution)/shard_map/ppermute | solution.py:502
  109.0 4.5 collective-permute-start.10
  120.2 8.6 %collective-permute-start.12 = (bf16[2,1,16,32,128]{4,3,2,1,0:T(8,128)(2,1)S(1)}, bf16[2,1,16,32,128]{4,3,2,1,0:T(8,128)(2,1)}, u32[]{:S(2)}, u32[]{:S(2)}) collective-permute-start(bf16[2,1,16,32,128]{4,3,2,1,0:T(8,128)(2,1)S(1)} %pad_maximum_fusion.2.refs_0_), channel_id=1, source_target_pairs={{0,2},{1,3},{2,4},{3,5},{4,6},{5,7},{8,10},{9,11},{10,12},{11,13},... | collective-permute-start | bytes 786440 | tf_op jit(solution)/shard_map/ppermute | solution.py:501
  133.5 17.6 %observe.4 = f32[2,2,3,16,128]{4,3,2,1,0:T(8,128)S(1)} custom-call(s32[1]{0:T(128)} %bitcast.core_ref, bf16[4,2,2,16,32,128]{5,4,3,2,1,0:T(8,128)(2,1)S(1)} %bitcast.67, bf16[2,1,16,32,128]{4,3,2,1,0:T(8,128)(2,1)S(1)} %pad_maximum_fusion.3.refs_0_, bf16[2,1,16,32,128]{4,3,2,1,0:T(8,128)(2,1)S(1)} %copy-done.27, ...), custom_call_target="tpu_custom_call" | custom-call | flops 402653184 | bytes 35651584 | tf_op jit(solution)/shard_map/observe/pallas_call | solution.py:361
  151.2 12.3 %collective-permute-start.23 = (f32[2,2,3,16,128]{4,3,2,1,0:T(8,128)S(1)}, f32[2,2,3,16,128]{4,3,2,1,0:T(8,128)}, u32[]{:S(2)}, u32[]{:S(2)}) collective-permute-start(f32[2,2,3,16,128]{4,3,2,1,0:T(8,128)S(1)} %observe.4), channel_id=1, source_target_pairs={{0,1},{1,0},{2,3},{3,2},{4,5},{5,4},{6,7},{7,6},{8,9},{9,8},{10,11... | collective-permute-start | bytes 294920 | tf_op jit(solution)/shard_map/ppermute | solution.py:477
  166.7 4.1 collective-permute-start.25
  176.5 14.5 %pull_back.4 = bf16[4,2,3,16,32,128]{5,4,3,2,1,0:T(8,128)(2,1)S(1)} custom-call(s32[1]{0:T(128)} %bitcast.core_ref, f32[2,2,3,16,128]{4,3,2,1,0:T(8,128)S(1)} %reverse_add_fusion.3.refs_0_, f32[2,2,3,16,128]{4,3,2,1,0:T(8,128)S(1)} %collective-permute-done.24.refs_1_, f32[2,2,3,16,128]{4,3,2,1,0:T(8,128)S(1)} %collective-permute-done.25.refs_2_, ...), custom_call_target="tpu_custom_call" | custom-call | flops 402653184 | bytes 36700160 | tf_op jit(solution)/shard_map/pull_back/pallas_call | solution.py:435
  206.6 17.8 %observe.5 = f32[2,2,3,16,128]{4,3,2,1,0:T(8,128)S(1)} custom-call(s32[1]{0:T(128)} %bitcast.core_ref, bf16[4,2,2,16,32,128]{5,4,3,2,1,0:T(8,128)(2,1)S(1)} %bitcast.66, bf16[2,1,16,32,128]{4,3,2,1,0:T(8,128)(2,1)S(1)} %pad_maximum_fusion.2.refs_0_, bf16[2,1,16,32,128]{4,3,2,1,0:T(8,128)(2,1)} %collective-permute-done.12.refs_1_, ...), custom_call_target="tpu_custom_call" | custom-call | flops 402653184 | bytes 35651584 | tf_op jit(solution)/shard_map/observe/pallas_call | solution.py:361
  224.3 5.2 collective-permute-start.35
  239.8 14.6 %pull_back.5 = bf16[4,2,3,16,32,128]{5,4,3,2,1,0:T(8,128)(2,1)S(1)} custom-call(s32[1]{0:T(128)} %bitcast.core_ref, f32[2,2,3,16,128]{4,3,2,1,0:T(8,128)S(1)} %reverse_add_fusion.2.refs_0_, f32[2,2,3,16,128]{4,3,2,1,0:T(8,128)S(1)} %collective-permute-done.36.refs_1_, f32[2,2,3,16,128]{4,3,2,1,0:T(8,128)S(1)} %collective-permute-done.37.refs_2_, ...), custom_call_target="tpu_custom_call" | custom-call | flops 402653184 | bytes 36700160 | tf_op jit(solution)/shard_map/pull_back/pallas_call | solution.py:435
  270.8 7.3 %step.2 = (f32[3,32,32,128]{3,2,1,0:T(8,128)S(1)}, bf16[3,16,32,128]{3,2,1,0:T(8,128)(2,1)S(1)}, bf16[3,16,32,128]{3,2,1,0:T(8,128)(2,1)S(1)}, f32[3,32,32,128]{...) custom-call(s32[1]{0:T(128)} %bitcast.core_ref, ...), custom_call_target="tpu_custom_call" | custom-call | tf_op jit(solution)/shard_map/step/pallas_call | solution.py:207
  287.2 4.7 collective-permute-start.31
  291.9 32.2 %reduce-scatter.7.cloned.1.call-done = bf16[1,2,3,16,32,128]{5,4,3,2,1,0:T(8,128)(2,1)} async-done(((bf16[4,2,3,16,32,128]{5,4,3,2,1,0:T(8,128)(2,1)}), bf16[1,2,3,16,32,128]{5,4,3,2,1,0:T(8,128)(2,1)}) %reduce-scatter.7.cloned.1.call-update) | async-done | bytes 786448 | tf_op jit(solution)/shard_map/reduce_scatter | solution.py:620
  337.2 6.9 %step.3 = (f32[3,32,32,128]{3,2,1,0:T(8,128)S(1)}, bf16[3,16,32,128]{3,2,1,0:T(8,128)(2,1)S(1)}, bf16[3,16,32,128]{3,2,1,0:T(8,128)(2,1)S(1)}, f32[3,32,32,128]{...) custom-call(s32[1]{0:T(128)} %bitcast.core_ref, ...), custom_call_target="tpu_custom_call" | custom-call | tf_op jit(solution)/shard_map/step/pallas_call | solution.py:207
  353.0 20.1 %collective-permute-done.51.refs_5_ = bf16[2,1,16,32,128]{4,3,2,1,0:T(8,128)(2,1)S(1)} collective-permute-done((bf16[2,1,16,32,128]{4,3,2,1,0:T(8,128)(2,1)S(1)}, bf16[2,1,16,32,128]{4,3,2,1,0:T(8,128)(2,1)S(1)}, u32[]{:S(2)}, u32[]{:S(2)}) %collective-permute-start.51) | collective-permute-done | bytes 262176 | tf_op jit(solution)/shard_map/ppermute | solution.py:502
  375.7 6.3 %collective-permute-start.45 = (bf16[2,1,16,32,128]{4,3,2,1,0:T(8,128)(2,1)S(1)}, bf16[2,1,16,32,128]{4,3,2,1,0:T(8,128)(2,1)S(1)}, u32[]{:S(2)}, u32[]{:S(2)}) collective-permute-start(bf16[2,1,16,32,128]{4,3,2,1,0:T(8,128)(2,1)S(1)} %pad_maximum_fusion.refs_0_), channel_id=1, source_target_pairs={{0,2},{1,3},{2,4},{3,5},{4,6},{5,7},{8,10},{9,11},{10,12},{11,13},... | collective-permute-start | bytes 786440 | tf_op jit(solution)/shard_map/ppermute | solution.py:501
  382.0 4.0 collective-permute-start.47
  389.3 5.3 collective-permute-done.48.down_ref
  396.9 17.5 %observe.6 = f32[2,2,3,16,128]{4,3,2,1,0:T(8,128)S(1)} custom-call(s32[1]{0:T(128)} %bitcast.core_ref, bf16[4,2,2,16,32,128]{5,4,3,2,1,0:T(8,128)(2,1)S(1)} %bitcast.69, bf16[2,1,16,32,128]{4,3,2,1,0:T(8,128)(2,1)S(1)} %pad_maximum_fusion.1.refs_0_, bf16[2,1,16,32,128]{4,3,2,1,0:T(8,128)(2,1)} %collective-permute-done.31.refs_1_, ...), custom_call_target="tpu_custom_call" | custom-call | flops 402653184 | bytes 35651584 | tf_op jit(solution)/shard_map/observe/pallas_call | solution.py:361
  427.8 14.5 %pull_back.6 = bf16[4,2,3,16,32,128]{5,4,3,2,1,0:T(8,128)(2,1)S(1)} custom-call(s32[1]{0:T(128)} %bitcast.core_ref, f32[2,2,3,16,128]{4,3,2,1,0:T(8,128)S(1)} %reverse_add_fusion.1.refs_0_, f32[2,2,3,16,128]{4,3,2,1,0:T(8,128)S(1)} %collective-permute-done.56.refs_1_, f32[2,2,3,16,128]{4,3,2,1,0:T(8,128)S(1)} %collective-permute-done.57.refs_2_, ...), custom_call_target="tpu_custom_call" | custom-call | flops 402653184 | bytes 36700160 | tf_op jit(solution)/shard_map/pull_back/pallas_call | solution.py:435
  457.1 17.5 %observe.7 = f32[2,2,3,16,128]{4,3,2,1,0:T(8,128)S(1)} custom-call(s32[1]{0:T(128)} %bitcast.core_ref, bf16[4,2,2,16,32,128]{5,4,3,2,1,0:T(8,128)(2,1)S(1)} %bitcast.68, bf16[2,1,16,32,128]{4,3,2,1,0:T(8,128)(2,1)S(1)} %pad_maximum_fusion.refs_0_, bf16[2,1,16,32,128]{4,3,2,1,0:T(8,128)(2,1)S(1)} %collective-permute-done.45.refs_1_, ...), custom_call_target="tpu_custom_call" | custom-call | flops 402653184 | bytes 35651584 | tf_op jit(solution)/shard_map/observe/pallas_call | solution.py:361
  474.6 8.8 %collective-permute-start.61 = (f32[2,2,3,16,128]{4,3,2,1,0:T(8,128)S(1)}, f32[2,2,3,16,128]{4,3,2,1,0:T(8,128)S(1)}, u32[]{:S(2)}, u32[]{:S(2)}) collective-permute-start(f32[2,2,3,16,128]{4,3,2,1,0:T(8,128)S(1)} %observe.7), channel_id=1, source_target_pairs={{0,1},{1,0},{2,3},{3,2},{4,5},{5,4},{6,7},{7,6},{8,9},{9,8},{10,11... | collective-permute-start | bytes 294920 | tf_op jit(solution)/shard_map/ppermute | solution.py:477
  492.2 14.6 %pull_back.7 = bf16[4,2,3,16,32,128]{5,4,3,2,1,0:T(8,128)(2,1)S(1)} custom-call(s32[1]{0:T(128)} %bitcast.core_ref, f32[2,2,3,16,128]{4,3,2,1,0:T(8,128)S(1)} %reverse_add_fusion.refs_0_, f32[2,2,3,16,128]{4,3,2,1,0:T(8,128)S(1)} %collective-permute-done.62.refs_1_, f32[2,2,3,16,128]{4,3,2,1,0:T(8,128)S(1)} %collective-permute-done.63.refs_2_, ...), custom_call_target="tpu_custom_call" | custom-call | flops 402653184 | bytes 36700160 | tf_op jit(solution)/shard_map/pull_back/pallas_call | solution.py:435
  521.2 6.0 %finish.2 = (f32[32,192,128]{2,1,0:T(8,128)}, f32[32,192,128]{2,1,0:T(8,128)}) custom-call(s32[1]{0:T(128)} %bitcast.core_ref, bf16[3,4,32,128]{3,2,1,0:T(8,128)(2,1)S(1)} %collective-permute-done.47.up_ref, f32[3,32,32,128]{3,2,1,0:T(8,128)S(1)} %copy-done.19, bf16[3,4,32,128]{3,2,1,0:T(8,128)(2,1)S(1)} %copy-done.31, ...), custom_call_target="tpu_custom_call" | custom-call | tf_op jit(solution)/shard_map/finish/pallas_call | solution.py:247
  527.2 42.7 %reduce-scatter.9.cloned.1.call-done = bf16[1,2,3,16,32,128]{5,4,3,2,1,0:T(8,128)(2,1)} async-done(((bf16[4,2,3,16,32,128]{5,4,3,2,1,0:T(8,128)(2,1)}), bf16[1,2,3,16,32,128]{5,4,3,2,1,0:T(8,128)(2,1)}) %reduce-scatter.9.cloned.1.call-update) | async-done | bytes 786448 | tf_op jit(solution)/shard_map/reduce_scatter | solution.py:620
  583.5 6.0 %finish.3 = (f32[32,192,128]{2,1,0:T(8,128)}, f32[32,192,128]{2,1,0:T(8,128)}) custom-call(s32[1]{0:T(128)} %bitcast.core_ref, bf16[3,4,32,128]{3,2,1,0:T(8,128)(2,1)S(1)} %collective-permute-done.43.up_ref, f32[3,32,32,128]{3,2,1,0:T(8,128)S(1)} %copy-done.23, ...), custom_call_target="tpu_custom_call", output_to_operand_aliasing={{0}: (10, {}), {1}: (11, {})} | custom-call | tf_op jit(solution)/shard_map/finish/pallas_call | solution.py:247
  (289 shorter events, 209.9 us)
Async XLA Ops:
  7.2 122.7 %all-gather.11.cloned.1.call-start = ((), (), s32[]{:S(2)}) async-start(), calls=%async_computation.9 | async-start | bytes 2621440 | tf_op jit(solution)/shard_map/all_gather | solution.py:597
  7.2 122.7 %collective-permute-start.20 = (bf16[2,128,16,4096]{3,2,1,0:T(8,128)(2,1)}, bf16[2,128,16,4096]{3,2,1,0:T(8,128)(2,1)}, u32[]{:S(2)}, u32[]{:S(2)}) collective-permute-start(bf16[2,128,16,4096]{3,2,1,0:T(8,128)(2,1)} %refs_5_.7), channel_id=1, source_target_pairs={{0,1},{1,0},{2,3},{3,2},{4,5},{5,4},{6,7},{7,6},{8,9},{9,8},{10,11... | collective-permute-start | bytes 100663304 | tf_op jit(solution)/shard_map/ppermute | solution.py:477
  8.8 12.8 %collective-permute-start.2 = (f32[2,4,128]{2,1,0:T(4,128)S(1)}, f32[2,4,128]{2,1,0:T(4,128)S(1)}, u32[]{:S(2)}, u32[]{:S(2)}) collective-permute-start(f32[2,4,128]{2,1,0:T(4,128)S(1)} %get-tuple-element.179), channel_id=1, source_target_pairs={{0,8},{8,16},{16,24},{1,9},{9,17},{17,25},{2,10},{10,18},{18,26},{... | collective-permute-start | bytes 12296 | tf_op jit(solution)/shard_map/ppermute | solution.py:459
  38.6 18.3 %collective-permute-start.4 = (bf16[3,16,32,128]{3,2,1,0:T(8,128)(2,1)S(1)}, bf16[3,16,32,128]{3,2,1,0:T(8,128)(2,1)S(1)}, u32[]{:S(2)}, u32[]{:S(2)}) collective-permute-start(bf16[3,16,32,128]{3,2,1,0:T(8,128)(2,1)S(1)} %get-tuple-element.80), channel_id=1, source_target_pairs={{0,1},{1,0},{2,3},{3,2},{4,5},{5,4},{6,7},{7,6},{8,9},{9,8},{10,11... | collective-permute-start | bytes 1179656 | tf_op jit(solution)/shard_map/ppermute | solution.py:477
  57.9 147.1 %all-gather.9.cloned.1.call-start = ((), (), s32[]{:S(2)}) async-start(), calls=%async_computation.8 | async-start | bytes 2621440 | tf_op jit(solution)/shard_map/all_gather | solution.py:597
  82.0 174.3 %reduce-scatter.5.cloned.1.call-start = ((), (), s32[]{:S(2)}) async-start(), calls=%async_computation.4 | async-start | bytes 3932160 | tf_op jit(solution)/shard_map/reduce_scatter | solution.py:620
  82.3 21.3 %collective-permute-start.17 = (bf16[2,1,16,32,128]{4,3,2,1,0:T(8,128)(2,1)S(1)}, bf16[2,1,16,32,128]{4,3,2,1,0:T(8,128)(2,1)S(1)}, u32[]{:S(2)}, u32[]{:S(2)}) collective-permute-start(bf16[2,1,16,32,128]{4,3,2,1,0:T(8,128)(2,1)S(1)} %pad_maximum_fusion.3.refs_0_), channel_id=1, source_target_pairs={{7,5},{6,4},{5,3},{4,2},{3,1},{2,0},{15,13},{14,12},{13,11},{12,10... | collective-permute-start | bytes 786440 | tf_op jit(solution)/shard_map/ppermute | solution.py:502
  83.6 21.3 %collective-permute-start.14 = (bf16[2,1,16,32,128]{4,3,2,1,0:T(8,128)(2,1)S(1)}, bf16[2,1,16,32,128]{4,3,2,1,0:T(8,128)(2,1)S(1)}, u32[]{:S(2)}, u32[]{:S(2)}) collective-permute-start(bf16[2,1,16,32,128]{4,3,2,1,0:T(8,128)(2,1)S(1)} %pad_maximum_fusion.3.refs_0_), channel_id=1, source_target_pairs={{0,2},{1,3},{2,4},{3,5},{4,6},{5,7},{8,10},{9,11},{10,12},{11,13},... | collective-permute-start | bytes 786440 | tf_op jit(solution)/shard_map/ppermute | solution.py:501
  103.6 11.3 %collective-permute-start.18 = (bf16[2,1,16,32,128]{4,3,2,1,0:T(8,128)(2,1)S(1)}, bf16[2,1,16,32,128]{4,3,2,1,0:T(8,128)(2,1)}, u32[]{:S(2)}, u32[]{:S(2)}) collective-permute-start(bf16[2,1,16,32,128]{4,3,2,1,0:T(8,128)(2,1)S(1)} %collective-permute-done.17.refs_4_), channel_id=1, source_target_pairs={{5,3},{4,2},{3,1},{2,0},{13,11},{12,10},{11,9},{10,8},{21,19},{20,... | collective-permute-start | bytes 786440 | tf_op jit(solution)/shard_map/ppermute | solution.py:502
  114.9 14.9 %collective-permute-start.19 = (bf16[2,1,16,32,128]{4,3,2,1,0:T(8,128)(2,1)}, bf16[2,1,16,32,128]{4,3,2,1,0:T(8,128)(2,1)}, u32[]{:S(2)}, u32[]{:S(2)}) collective-permute-start(bf16[2,1,16,32,128]{4,3,2,1,0:T(8,128)(2,1)} %collective-permute-done.18.refs_5_), channel_id=1, source_target_pairs={{3,1},{2,0},{11,9},{10,8},{19,17},{18,16},{27,25},{26,24}} | collective-permute-start | bytes 786440 | tf_op jit(solution)/shard_map/ppermute | solution.py:502
  116.2 13.6 %collective-permute-start.16 = (bf16[2,1,16,32,128]{4,3,2,1,0:T(8,128)(2,1)}, bf16[2,1,16,32,128]{4,3,2,1,0:T(8,128)(2,1)}, u32[]{:S(2)}, u32[]{:S(2)}) collective-permute-start(bf16[2,1,16,32,128]{4,3,2,1,0:T(8,128)(2,1)} %collective-permute-done.15.refs_2_), channel_id=1, source_target_pairs={{4,6},{5,7},{12,14},{13,15},{20,22},{21,23},{28,30},{29,31}} | collective-permute-start | bytes 786440 | tf_op jit(solution)/shard_map/ppermute | solution.py:501
  118.9 32.3 %collective-permute-start.13 = (bf16[2,1,16,32,128]{4,3,2,1,0:T(8,128)(2,1)S(1)}, bf16[2,1,16,32,128]{4,3,2,1,0:T(8,128)(2,1)}, u32[]{:S(2)}, u32[]{:S(2)}) collective-permute-start(bf16[2,1,16,32,128]{4,3,2,1,0:T(8,128)(2,1)S(1)} %pad_maximum_fusion.2.refs_0_), channel_id=1, source_target_pairs={{7,5},{6,4},{5,3},{4,2},{3,1},{2,0},{15,13},{14,12},{13,11},{12,10... | collective-permute-start | bytes 786440 | tf_op jit(solution)/shard_map/ppermute | solution.py:502
  120.2 31.0 %collective-permute-start.12 = (bf16[2,1,16,32,128]{4,3,2,1,0:T(8,128)(2,1)S(1)}, bf16[2,1,16,32,128]{4,3,2,1,0:T(8,128)(2,1)}, u32[]{:S(2)}, u32[]{:S(2)}) collective-permute-start(bf16[2,1,16,32,128]{4,3,2,1,0:T(8,128)(2,1)S(1)} %pad_maximum_fusion.2.refs_0_), channel_id=1, source_target_pairs={{0,2},{1,3},{2,4},{3,5},{4,6},{5,7},{8,10},{9,11},{10,12},{11,13},... | collective-permute-start | bytes 786440 | tf_op jit(solution)/shard_map/ppermute | solution.py:501
  151.2 14.5 %collective-permute-start.23 = (f32[2,2,3,16,128]{4,3,2,1,0:T(8,128)S(1)}, f32[2,2,3,16,128]{4,3,2,1,0:T(8,128)}, u32[]{:S(2)}, u32[]{:S(2)}) collective-permute-start(f32[2,2,3,16,128]{4,3,2,1,0:T(8,128)S(1)} %observe.4), channel_id=1, source_target_pairs={{0,1},{1,0},{2,3},{3,2},{4,5},{5,4},{6,7},{7,6},{8,9},{9,8},{10,11... | collective-permute-start | bytes 294920 | tf_op jit(solution)/shard_map/ppermute | solution.py:477
  163.7 29.0 %collective-permute-start.21 = (bf16[2,1,16,32,128]{4,3,2,1,0:T(8,128)(2,1)}, bf16[2,1,16,32,128]{4,3,2,1,0:T(8,128)(2,1)S(1)}, u32[]{:S(2)}, u32[]{:S(2)}) collective-permute-start(bf16[2,1,16,32,128]{4,3,2,1,0:T(8,128)(2,1)} %collective-permute-done.12.refs_1_), channel_id=1, source_target_pairs={{2,4},{3,5},{4,6},{5,7},{10,12},{11,13},{12,14},{13,15},{18,20},{1... | collective-permute-start | bytes 786440 | tf_op jit(solution)/shard_map/ppermute | solution.py:501
  164.4 28.3 %collective-permute-start.22 = (bf16[2,1,16,32,128]{4,3,2,1,0:T(8,128)(2,1)}, bf16[2,1,16,32,128]{4,3,2,1,0:T(8,128)(2,1)}, u32[]{:S(2)}, u32[]{:S(2)}) collective-permute-start(bf16[2,1,16,32,128]{4,3,2,1,0:T(8,128)(2,1)} %collective-permute-done.13.refs_4_), channel_id=1, source_target_pairs={{5,3},{4,2},{3,1},{2,0},{13,11},{12,10},{11,9},{10,8},{21,19},{20,... | collective-permute-start | bytes 786440 | tf_op jit(solution)/shard_map/ppermute | solution.py:502
  192.8 131.3 %reduce-scatter.7.cloned.1.call-start = ((), (), s32[]{:S(2)}) async-start(), calls=%async_computation.5 | async-start | bytes 3932160 | tf_op jit(solution)/shard_map/reduce_scatter | solution.py:620
  192.8 12.2 %collective-permute-start.33 = (bf16[2,1,16,32,128]{4,3,2,1,0:T(8,128)(2,1)S(1)}, bf16[2,1,16,32,128]{4,3,2,1,0:T(8,128)(2,1)}, u32[]{:S(2)}, u32[]{:S(2)}) collective-permute-start(bf16[2,1,16,32,128]{4,3,2,1,0:T(8,128)(2,1)S(1)} %collective-permute-done.21.refs_2_), channel_id=1, source_target_pairs={{4,6},{5,7},{12,14},{13,15},{20,22},{21,23},{28,30},{29,31}} | collective-permute-start | bytes 786440 | tf_op jit(solution)/shard_map/ppermute | solution.py:501
  256.1 139.1 %all-gather.15.cloned.1.call-start = ((), (), s32[]{:S(2)}) async-start(), calls=%async_computation.11 | async-start | bytes 2621440 | tf_op jit(solution)/shard_map/all_gather | solution.py:597
  285.8 169.7 %all-gather.13.cloned.1.call-start = ((), (), s32[]{:S(2)}) async-start(), calls=%async_computation.10 | async-start | bytes 2621440 | tf_op jit(solution)/shard_map/all_gather | solution.py:597
  285.9 38.2 %collective-permute-start.32 = (bf16[2,1,16,32,128]{4,3,2,1,0:T(8,128)(2,1)S(1)}, bf16[2,1,16,32,128]{4,3,2,1,0:T(8,128)(2,1)S(1)}, u32[]{:S(2)}, u32[]{:S(2)}) collective-permute-start(bf16[2,1,16,32,128]{4,3,2,1,0:T(8,128)(2,1)S(1)} %pad_maximum_fusion.1.refs_0_), channel_id=1, source_target_pairs={{7,5},{6,4},{5,3},{4,2},{3,1},{2,0},{15,13},{14,12},{13,11},{12,10... | collective-permute-start | bytes 786440 | tf_op jit(solution)/shard_map/ppermute | solution.py:502
  287.2 36.9 %collective-permute-start.31 = (bf16[2,1,16,32,128]{4,3,2,1,0:T(8,128)(2,1)S(1)}, bf16[2,1,16,32,128]{4,3,2,1,0:T(8,128)(2,1)}, u32[]{:S(2)}, u32[]{:S(2)}) collective-permute-start(bf16[2,1,16,32,128]{4,3,2,1,0:T(8,128)(2,1)S(1)} %pad_maximum_fusion.1.refs_0_), channel_id=1, source_target_pairs={{0,2},{1,3},{2,4},{3,5},{4,6},{5,7},{8,10},{9,11},{10,12},{11,13},... | collective-permute-start | bytes 786440 | tf_op jit(solution)/shard_map/ppermute | solution.py:501
  350.3 158.3 %reduce-scatter.11.cloned.1.call-start = ((), (), s32[]{:S(2)}) async-start(), calls=%async_computation.7 | async-start | bytes 3932160 | tf_op jit(solution)/shard_map/reduce_scatter | solution.py:620
  351.0 22.1 %collective-permute-start.51 = (bf16[2,1,16,32,128]{4,3,2,1,0:T(8,128)(2,1)S(1)}, bf16[2,1,16,32,128]{4,3,2,1,0:T(8,128)(2,1)S(1)}, u32[]{:S(2)}, u32[]{:S(2)}) collective-permute-start(bf16[2,1,16,32,128]{4,3,2,1,0:T(8,128)(2,1)S(1)} %collective-permute-done.32.refs_4_), channel_id=1, source_target_pairs={{5,3},{4,2},{3,1},{2,0},{13,11},{12,10},{11,9},{10,8},{21,19},{20,... | collective-permute-start | bytes 786440 | tf_op jit(solution)/shard_map/ppermute | solution.py:502
  352.3 42.9 %collective-permute-start.50 = (bf16[2,1,16,32,128]{4,3,2,1,0:T(8,128)(2,1)S(1)}, bf16[2,1,16,32,128]{4,3,2,1,0:T(8,128)(2,1)S(1)}, u32[]{:S(2)}, u32[]{:S(2)}) collective-permute-start(bf16[2,1,16,32,128]{4,3,2,1,0:T(8,128)(2,1)S(1)} %collective-permute-done.49.refs_2_), channel_id=1, source_target_pairs={{4,6},{5,7},{12,14},{13,15},{20,22},{21,23},{28,30},{29,31}} | collective-permute-start | bytes 786440 | tf_op jit(solution)/shard_map/ppermute | solution.py:501
  373.1 22.1 %collective-permute-start.52 = (bf16[2,1,16,32,128]{4,3,2,1,0:T(8,128)(2,1)S(1)}, bf16[2,1,16,32,128]{4,3,2,1,0:T(8,128)(2,1)}, u32[]{:S(2)}, u32[]{:S(2)}) collective-permute-start(bf16[2,1,16,32,128]{4,3,2,1,0:T(8,128)(2,1)S(1)} %collective-permute-done.51.refs_5_), channel_id=1, source_target_pairs={{3,1},{2,0},{11,9},{10,8},{19,17},{18,16},{27,25},{26,24}} | collective-permute-start | bytes 786440 | tf_op jit(solution)/shard_map/ppermute | solution.py:502
  374.4 40.0 %collective-permute-start.46 = (bf16[2,1,16,32,128]{4,3,2,1,0:T(8,128)(2,1)S(1)}, bf16[2,1,16,32,128]{4,3,2,1,0:T(8,128)(2,1)S(1)}, u32[]{:S(2)}, u32[]{:S(2)}) collective-permute-start(bf16[2,1,16,32,128]{4,3,2,1,0:T(8,128)(2,1)S(1)} %pad_maximum_fusion.refs_0_), channel_id=1, source_target_pairs={{7,5},{6,4},{5,3},{4,2},{3,1},{2,0},{15,13},{14,12},{13,11},{12,10... | collective-permute-start | bytes 786440 | tf_op jit(solution)/shard_map/ppermute | solution.py:502
  375.7 38.7 %collective-permute-start.45 = (bf16[2,1,16,32,128]{4,3,2,1,0:T(8,128)(2,1)S(1)}, bf16[2,1,16,32,128]{4,3,2,1,0:T(8,128)(2,1)S(1)}, u32[]{:S(2)}, u32[]{:S(2)}) collective-permute-start(bf16[2,1,16,32,128]{4,3,2,1,0:T(8,128)(2,1)S(1)} %pad_maximum_fusion.refs_0_), channel_id=1, source_target_pairs={{0,2},{1,3},{2,4},{3,5},{4,6},{5,7},{8,10},{9,11},{10,12},{11,13},... | collective-permute-start | bytes 786440 | tf_op jit(solution)/shard_map/ppermute | solution.py:501
  416.7 27.4 %collective-permute-start.53 = (bf16[2,1,16,32,128]{4,3,2,1,0:T(8,128)(2,1)S(1)}, bf16[2,1,16,32,128]{4,3,2,1,0:T(8,128)(2,1)S(1)}, u32[]{:S(2)}, u32[]{:S(2)}) collective-permute-start(bf16[2,1,16,32,128]{4,3,2,1,0:T(8,128)(2,1)S(1)} %collective-permute-done.45.refs_1_), channel_id=1, source_target_pairs={{2,4},{3,5},{4,6},{5,7},{10,12},{11,13},{12,14},{13,15},{18,20},{1... | collective-permute-start | bytes 786440 | tf_op jit(solution)/shard_map/ppermute | solution.py:501
  417.3 26.7 %collective-permute-start.54 = (bf16[2,1,16,32,128]{4,3,2,1,0:T(8,128)(2,1)S(1)}, bf16[2,1,16,32,128]{4,3,2,1,0:T(8,128)(2,1)S(1)}, u32[]{:S(2)}, u32[]{:S(2)}) collective-permute-start(bf16[2,1,16,32,128]{4,3,2,1,0:T(8,128)(2,1)S(1)} %collective-permute-done.46.refs_4_), channel_id=1, source_target_pairs={{5,3},{4,2},{3,1},{2,0},{13,11},{12,10},{11,9},{10,8},{21,19},{20,... | collective-permute-start | bytes 786440 | tf_op jit(solution)/shard_map/ppermute | solution.py:502
  444.1 125.8 %reduce-scatter.9.cloned.1.call-start = ((), (), s32[]{:S(2)}) async-start(), calls=%async_computation.6 | async-start | bytes 3932160 | tf_op jit(solution)/shard_map/reduce_scatter | solution.py:620
  444.1 11.4 %collective-permute-start.59 = (bf16[2,1,16,32,128]{4,3,2,1,0:T(8,128)(2,1)S(1)}, bf16[2,1,16,32,128]{4,3,2,1,0:T(8,128)(2,1)S(1)}, u32[]{:S(2)}, u32[]{:S(2)}) collective-permute-start(bf16[2,1,16,32,128]{4,3,2,1,0:T(8,128)(2,1)S(1)} %collective-permute-done.53.refs_2_), channel_id=1, source_target_pairs={{4,6},{5,7},{12,14},{13,15},{20,22},{21,23},{28,30},{29,31}} | collective-permute-start | bytes 786440 | tf_op jit(solution)/shard_map/ppermute | solution.py:501
  (90 other events, 509.3 us)
Sparse Core Ops, SparseCore 0:
  58.0 54.7 all-gather.10
  115.0 52.5 all-gather.8
  192.9 63.4 reduce-scatter.4
  259.1 64.9 reduce-scatter.6
  325.5 51.6 all-gather.14
  378.6 45.3 all-gather.12
  444.2 64.1 reduce-scatter.10
  510.6 59.2 reduce-scatter.8

commit v7 on v6

--- a/solution.py
+++ b/solution.py
@@ -526,7 +526,6 @@
     core = sensor_index % 2
     near = LANES // sensors
     half = cells // 2
-    other_map = swap_cores(forward_map)
 
     cores = jnp.stack([core, 1 - core])
     offsets = cores[None, :, None] * steps + jnp.arange(steps, dtype=jnp.int32)
@@ -580,41 +579,45 @@
         _, cross = misfit_rims(edge[1])
         return misfit[0], swap_cores(misfit[1]), same, cross
 
-    states = []
-    for group in range(GROUPS):
-        here = slice(group * members, (group + 1) * members)
-        ends = (top[here], bottom[here])
-        if states:
-            iterate, pair, *others = states[0]
-            pair, ends = lax.optimization_barrier((pair, ends))
-            states[0] = (iterate, pair, *others)
-        begun = start(group, members, core, rhs, *rims(*ends), coeff)
-        states.append(ready(begun))
-
-    line = Line(states[0][2])
+    def begin(group, ends):
+        return ready(start(group, members, core, rhs, *rims(*ends), coeff))
+
+    groups = [slice(group * members, (group + 1) * members) for group in range(GROUPS)]
+    states = [begin(0, (top[groups[0]], bottom[groups[0]]))]
+    iterate, pair, apart, rests = states[0]
+    pair, apart, whole_map = lax.optimization_barrier((pair, apart, forward_map))
+    other_map = swap_cores(whole_map)
+    line = Line(apart)
+    line.hop()
+    for group in range(1, GROUPS):
+        ends = (top[groups[group]], bottom[groups[group]])
+        rests, ends = line.after((rests, ends))
+        states.append(begin(group, ends))
+    states[0] = iterate, pair, apart, rests
+
     outputs = ()
     for iteration in range(ITERS):
         fields = [lax.all_gather(state[1], "sensors", axis_index_groups=lines) for state in states]
         line.hop(last=True)
         totals = []
         for group in range(GROUPS):
-            iterate, _, _, rests = states[group]
-            field, rests = lax.optimization_barrier((fields[group], rests))
-            states[group] = iterate, rests
             slots, line = line.slots(), None
             if group + 1 < GROUPS:
                 line = Line(states[group + 1][2])
                 line.hop()
             sums = observe(
-                core, field, slots, forward_map, other_map, table, around, local_cells
+                core, fields[group], slots, forward_map, other_map, table, around, local_cells
             )
             if line is not None:
-                sums = line.after(sums)
+                iterate, pair, apart, rests = states[group + 1]
+                sums, rests = lax.optimization_barrier((sums, rests))
+                line.after(sums)
+                states[group + 1] = iterate, pair, apart, rests
                 line.hop()
             sums = from_all_cells(sums + swap_cores(sums)[::-1])
             misfit = pull_back(core, sums, noise, forward_map, other_map, back, local_cells, shape)
             if line is not None:
-                misfit = line.after(misfit)
+                line.after(misfit)
                 line.hop(last=True)
             totals.append(
                 lax.psum_scatter(
@@ -622,15 +625,17 @@
                 )
             )
         for group in range(GROUPS):
-            iterate, rests = states[group]
+            iterate, _, _, rests = states[group]
             total = totals[group]
             if iteration < ITERS - 1:
                 if group == 1:
+                    before = states[0]
+                    line = Line(before[2])
                     line.hop()
-                    total = line.after(total)
+                    line.hop()
+                    total, earlier = line.after((total, before[3]))
+                    states[0] = (*before[:3], earlier)
                 states[group] = ready(step(core, rests, edges(total), iterate, coeff))
-                if group == 0:
-                    line = Line(states[0][2])
             else:
                 if outputs:
                     total, outputs = lax.optimization_barrier((total, outputs))

time: 600 us -> 671 us (1.12)
  waiting for transfers between devices: 184 us -> 268 us
  starting transfers between devices: 163 us -> 152 us
    ppermute x12, waiting for transfers between devices: 35.4 us -> 154 us  [hop(): down = lax.ppermute(self.ends[1], 'sensors', backward)]
    reduce_scatter x4, waiting for transfers between devices: 75.2 us -> 43.2 us  [shards(): lax.psum_scatter(misfit, 'sensors', scatter_dimension=0, axis_index_group...]
    ppermute x12, waiting for transfers between devices: 0.03 us -> 8.46 us  [hop(): up = lax.ppermute(self.ends[0], 'sensors', onward)]
    ppermute x13, starting transfers between devices: 38.3 us -> 30.7 us  [swap_cores(): return lax.ppermute(value, 'sensors', [(k, k ^ 1) for k in range(size)])]
    unnamed x86 -> x92, local copies, waits for them, and re-layouts: 42.6 us -> 41.4 us
  transfers between devices with their start and end apart: 79 -> 79, of which waited for: 40 -> 47; matrix products, arithmetic and copies ran while one was open for 4% -> 3% of each run, Pallas kernels for 27% -> 23%
where the time goes in v7:
time: 671 us; the launch traced here: 668 us
  waiting for transfers between devices  268 us (40%)
  Pallas kernels  168 us (25%)
  starting transfers between devices  152 us (23%)
  local copies, waits for them, and re-layouts  54.3 us (8%)
  between operations  15.1 us (2%)
  other arithmetic  10.1 us (2%)
    ppermute x12, waiting for transfers between devices, hop(): down = lax.ppermute(self.ends[1], 'sensors', backward)  154 us
    pallas_call x4, Pallas kernels, observe(): call(observe_kernel, core, (rows // CHUNK_ROWS,), [pl.BlockSpec(block, la...  70.5 us
    pallas_call x4, Pallas kernels, pull_back(): call(pull_kernel, core, (rows // CHUNK_ROWS,), [whole_block(array) for ar...  58.3 us
    reduce_scatter x4, waiting for transfers between devices, shards(): lax.psum_scatter(misfit, 'sensors', scatter_dimension=0, axis_index_group...  43.2 us
    unnamed x92, local copies, waits for them, and re-layouts  41.4 us
    ppermute x7, starting transfers between devices, rims(): lax.ppermute(bottom, 'cells', onward)  32.6 us
    ppermute x13, starting transfers between devices, swap_cores(): return lax.ppermute(value, 'sensors', [(k, k ^ 1) for k in range(size)])  30.7 us
    ppermute x12, starting transfers between devices, hop(): up = lax.ppermute(self.ends[0], 'sensors', onward)  25.5 us
  transfers between devices with their start and end apart: 79, of which 47 were waited for; matrix products, arithmetic and copies ran while one was open for 3% of the time, Pallas kernels for 23%

profile of v7, /device:TPU:1, one launch (start us, length us, event | category | flops | bytes accessed | tf_op | source)
XLA Modules:
  0.0 668.3 jit_solution(6306733798846748564)
XLA Ops:
  28.7 6.1 start.2
  68.0 6.8 %start.3 = (f32[3,32,32,128]{3,2,1,0:T(8,128)S(1)}, bf16[3,16,32,128]{3,2,1,0:T(8,128)(2,1)S(1)}, bf16[3,16,32,128]{3,2,1,0:T(8,128)(2,1)S(1)}, f32[3,32,32,128]...) custom-call(s32[1]{0:T(128)} %bitcast.core_ref, f32[32,192,128]{2,1,0:T(8,128)S(1)} %bitcast.65, ...), custom_call_target="tpu_custom_call" | custom-call | tf_op jit(solution)/shard_map/start/pallas_call | solution.py:155
  78.4 12.1 %collective-permute-done.30 = bf16[3,16,32,128]{3,2,1,0:T(8,128)(2,1)S(1)} collective-permute-done((bf16[3,16,32,128]{3,2,1,0:T(8,128)(2,1)S(1)}, bf16[3,16,32,128]{3,2,1,0:T(8,128)(2,1)S(1)}, u32[]{:S(2)}, u32[]{:S(2)}) %collective-permute-start.30) | collective-permute-done | bytes 393248 | tf_op jit(solution)/shard_map/ppermute | solution.py:477
  98.4 10.2 %collective-permute-done.11.refs_5_ = bf16[2,1,16,32,128]{4,3,2,1,0:T(8,128)(2,1)} collective-permute-done((bf16[2,1,16,32,128]{4,3,2,1,0:T(8,128)(2,1)S(1)}, bf16[2,1,16,32,128]{4,3,2,1,0:T(8,128)(2,1)}, u32[]{:S(2)}, u32[]{:S(2)}) %collective-permute-start.11) | collective-permute-done | bytes 262176 | tf_op jit(solution)/shard_map/ppermute | solution.py:502
  112.2 7.2 %collective-permute-start.16 = (bf16[3,4,32,128]{3,2,1,0:T(8,128)(2,1)}, bf16[3,4,32,128]{3,2,1,0:T(8,128)(2,1)}, u32[]{:S(2)}, u32[]{:S(2)}) collective-permute-start(bf16[3,4,32,128]{3,2,1,0:T(8,128)(2,1)} %get-tuple-element.94), channel_id=1, source_target_pairs={{0,8},{8,16},{16,24},{1,9},{9,17},{17,25},{2,10},{10,18},{18,26},{... | collective-permute-start | bytes 294920 | tf_op jit(solution)/shard_map/ppermute | solution.py:459
  120.7 13.6 %collective-permute-done.12.refs_6_ = bf16[2,1,16,32,128]{4,3,2,1,0:T(8,128)(2,1)} collective-permute-done((bf16[2,1,16,32,128]{4,3,2,1,0:T(8,128)(2,1)}, bf16[2,1,16,32,128]{4,3,2,1,0:T(8,128)(2,1)}, u32[]{:S(2)}, u32[]{:S(2)}) %collective-permute-start.12) | collective-permute-done | bytes 262176 | tf_op jit(solution)/shard_map/ppermute | solution.py:502
  137.9 17.6 %observe.4 = f32[2,2,3,16,128]{4,3,2,1,0:T(8,128)S(1)} custom-call(s32[1]{0:T(128)} %bitcast.core_ref, bf16[4,2,2,16,32,128]{5,4,3,2,1,0:T(8,128)(2,1)S(1)} %bitcast.67, bf16[2,1,16,32,128]{4,3,2,1,0:T(8,128)(2,1)S(1)} %pad_maximum_fusion.3.refs_0_, bf16[2,1,16,32,128]{4,3,2,1,0:T(8,128)(2,1)S(1)} %copy-done.27, ...), custom_call_target="tpu_custom_call" | custom-call | flops 402653184 | bytes 35651584 | tf_op jit(solution)/shard_map/observe/pallas_call | solution.py:361
  155.5 8.8 %collective-permute-start.18 = (f32[2,2,3,16,128]{4,3,2,1,0:T(8,128)S(1)}, f32[2,2,3,16,128]{4,3,2,1,0:T(8,128)S(1)}, u32[]{:S(2)}, u32[]{:S(2)}) collective-permute-start(f32[2,2,3,16,128]{4,3,2,1,0:T(8,128)S(1)} %observe.4), channel_id=1, source_target_pairs={{0,1},{1,0},{2,3},{3,2},{4,5},{5,4},{6,7},{7,6},{8,9},{9,8},{10,11... | collective-permute-start | bytes 294920 | tf_op jit(solution)/shard_map/ppermute | solution.py:477
  165.3 6.2 collective-permute-start.20
  175.0 14.5 %pull_back.4 = bf16[4,2,3,16,32,128]{5,4,3,2,1,0:T(8,128)(2,1)S(1)} custom-call(s32[1]{0:T(128)} %bitcast.core_ref, f32[2,2,3,16,128]{4,3,2,1,0:T(8,128)S(1)} %reverse_add_fusion.3.refs_0_, f32[2,2,3,16,128]{4,3,2,1,0:T(8,128)S(1)} %collective-permute-done.19.refs_1_, f32[2,2,3,16,128]{4,3,2,1,0:T(8,128)S(1)} %collective-permute-done.20.refs_2_, ...), custom_call_target="tpu_custom_call" | custom-call | flops 402653184 | bytes 36700160 | tf_op jit(solution)/shard_map/pull_back/pallas_call | solution.py:435
  199.3 7.6 %collective-permute-done.31.refs_1_ = bf16[2,1,16,32,128]{4,3,2,1,0:T(8,128)(2,1)S(1)} collective-permute-done((bf16[2,1,16,32,128]{4,3,2,1,0:T(8,128)(2,1)S(1)}, bf16[2,1,16,32,128]{4,3,2,1,0:T(8,128)(2,1)S(1)}, u32[]{:S(2)}, u32[]{:S(2)}) %collective-permute-start.31) | collective-permute-done | bytes 262176 | tf_op jit(solution)/shard_map/ppermute | solution.py:501
  210.2 24.0 %collective-permute-done.34.refs_5_ = bf16[2,1,16,32,128]{4,3,2,1,0:T(8,128)(2,1)} collective-permute-done((bf16[2,1,16,32,128]{4,3,2,1,0:T(8,128)(2,1)S(1)}, bf16[2,1,16,32,128]{4,3,2,1,0:T(8,128)(2,1)}, u32[]{:S(2)}, u32[]{:S(2)}) %collective-permute-start.34) | collective-permute-done | bytes 262176 | tf_op jit(solution)/shard_map/ppermute | solution.py:502
  237.1 19.2 %collective-permute-done.36.refs_6_ = bf16[2,1,16,32,128]{4,3,2,1,0:T(8,128)(2,1)} collective-permute-done((bf16[2,1,16,32,128]{4,3,2,1,0:T(8,128)(2,1)}, bf16[2,1,16,32,128]{4,3,2,1,0:T(8,128)(2,1)}, u32[]{:S(2)}, u32[]{:S(2)}) %collective-permute-start.36) | collective-permute-done | bytes 262176 | tf_op jit(solution)/shard_map/ppermute | solution.py:502
  258.8 17.6 %observe.5 = f32[2,2,3,16,128]{4,3,2,1,0:T(8,128)S(1)} custom-call(s32[1]{0:T(128)} %bitcast.core_ref, bf16[4,2,2,16,32,128]{5,4,3,2,1,0:T(8,128)(2,1)S(1)} %bitcast.66, bf16[2,1,16,32,128]{4,3,2,1,0:T(8,128)(2,1)S(1)} %pad_maximum_fusion.1.refs_0_, bf16[2,1,16,32,128]{4,3,2,1,0:T(8,128)(2,1)S(1)} %copy-done.29, ...), custom_call_target="tpu_custom_call" | custom-call | flops 402653184 | bytes 35651584 | tf_op jit(solution)/shard_map/observe/pallas_call | solution.py:361
  276.4 6.9 %collective-permute-start.37 = (f32[2,2,3,16,128]{4,3,2,1,0:T(8,128)S(1)}, f32[2,2,3,16,128]{4,3,2,1,0:T(8,128)S(1)}, u32[]{:S(2)}, u32[]{:S(2)}) collective-permute-start(f32[2,2,3,16,128]{4,3,2,1,0:T(8,128)S(1)} %observe.5), channel_id=1, source_target_pairs={{0,1},{1,0},{2,3},{3,2},{4,5},{5,4},{6,7},{7,6},{8,9},{9,8},{10,11... | collective-permute-start | bytes 294920 | tf_op jit(solution)/shard_map/ppermute | solution.py:477
  291.0 14.5 %pull_back.5 = bf16[4,2,3,16,32,128]{5,4,3,2,1,0:T(8,128)(2,1)S(1)} custom-call(s32[1]{0:T(128)} %bitcast.core_ref, f32[2,2,3,16,128]{4,3,2,1,0:T(8,128)S(1)} %reverse_add_fusion.2.refs_0_, f32[2,2,3,16,128]{4,3,2,1,0:T(8,128)S(1)} %collective-permute-done.38.refs_1_, f32[2,2,3,16,128]{4,3,2,1,0:T(8,128)S(1)} %collective-permute-done.39.refs_2_, ...), custom_call_target="tpu_custom_call" | custom-call | flops 402653184 | bytes 36700160 | tf_op jit(solution)/shard_map/pull_back/pallas_call | solution.py:435
  321.5 7.3 %step.2 = (f32[3,32,32,128]{3,2,1,0:T(8,128)S(1)}, bf16[3,16,32,128]{3,2,1,0:T(8,128)(2,1)S(1)}, bf16[3,16,32,128]{3,2,1,0:T(8,128)(2,1)S(1)}, f32[3,32,32,128]{...) custom-call(s32[1]{0:T(128)} %bitcast.core_ref, ...), custom_call_target="tpu_custom_call" | custom-call | tf_op jit(solution)/shard_map/step/pallas_call | solution.py:207
  338.0 4.7 collective-permute-start.26
  342.7 14.2 %collective-permute-done.28.refs_4_ = bf16[2,1,16,32,128]{4,3,2,1,0:T(8,128)(2,1)S(1)} collective-permute-done((bf16[2,1,16,32,128]{4,3,2,1,0:T(8,128)(2,1)S(1)}, bf16[2,1,16,32,128]{4,3,2,1,0:T(8,128)(2,1)S(1)}, u32[]{:S(2)}, u32[]{:S(2)}) %collective-permute-start.28) | collective-permute-done | bytes 262176 | tf_op jit(solution)/shard_map/ppermute | solution.py:502
  359.5 5.7 collective-permute-start.41
  389.0 7.1 %step.3 = (f32[3,32,32,128]{3,2,1,0:T(8,128)S(1)}, bf16[3,16,32,128]{3,2,1,0:T(8,128)(2,1)S(1)}, bf16[3,16,32,128]{3,2,1,0:T(8,128)(2,1)S(1)}, f32[3,32,32,128]{...) custom-call(s32[1]{0:T(128)} %bitcast.core_ref, ...), custom_call_target="tpu_custom_call" | custom-call | tf_op jit(solution)/shard_map/step/pallas_call | solution.py:207
  404.3 4.5 collective-permute-start.48
  410.3 16.5 %collective-permute-done.44.refs_6_ = bf16[2,1,16,32,128]{4,3,2,1,0:T(8,128)(2,1)S(1)} collective-permute-done((bf16[2,1,16,32,128]{4,3,2,1,0:T(8,128)(2,1)}, bf16[2,1,16,32,128]{4,3,2,1,0:T(8,128)(2,1)S(1)}, u32[]{:S(2)}, u32[]{:S(2)}) %collective-permute-start.44) | collective-permute-done | bytes 262176 | tf_op jit(solution)/shard_map/ppermute | solution.py:502
  430.0 17.8 %observe.6 = f32[2,2,3,16,128]{4,3,2,1,0:T(8,128)S(1)} custom-call(s32[1]{0:T(128)} %bitcast.core_ref, bf16[4,2,2,16,32,128]{5,4,3,2,1,0:T(8,128)(2,1)S(1)} %bitcast.68, bf16[2,1,16,32,128]{4,3,2,1,0:T(8,128)(2,1)S(1)} %pad_maximum_fusion.2.refs_0_, bf16[2,1,16,32,128]{4,3,2,1,0:T(8,128)(2,1)} %collective-permute-done.26.refs_1_, ...), custom_call_target="tpu_custom_call" | custom-call | flops 402653184 | bytes 35651584 | tf_op jit(solution)/shard_map/observe/pallas_call | solution.py:361
  457.2 14.6 %pull_back.6 = bf16[4,2,3,16,32,128]{5,4,3,2,1,0:T(8,128)(2,1)S(1)} custom-call(s32[1]{0:T(128)} %bitcast.core_ref, f32[2,2,3,16,128]{4,3,2,1,0:T(8,128)S(1)} %reverse_add_fusion.1.refs_0_, f32[2,2,3,16,128]{4,3,2,1,0:T(8,128)S(1)} %collective-permute-done.56.refs_1_, f32[2,2,3,16,128]{4,3,2,1,0:T(8,128)S(1)} %collective-permute-done.57.refs_2_, ...), custom_call_target="tpu_custom_call" | custom-call | flops 402653184 | bytes 36700160 | tf_op jit(solution)/shard_map/pull_back/pallas_call | solution.py:435
  485.5 26.9 %collective-permute-done.54.refs_5_ = bf16[2,1,16,32,128]{4,3,2,1,0:T(8,128)(2,1)S(1)} collective-permute-done((bf16[2,1,16,32,128]{4,3,2,1,0:T(8,128)(2,1)S(1)}, bf16[2,1,16,32,128]{4,3,2,1,0:T(8,128)(2,1)S(1)}, u32[]{:S(2)}, u32[]{:S(2)}) %collective-permute-start.54) | collective-permute-done | bytes 262176 | tf_op jit(solution)/shard_map/ppermute | solution.py:502
  514.4 22.1 %collective-permute-done.60.refs_6_ = bf16[2,1,16,32,128]{4,3,2,1,0:T(8,128)(2,1)S(1)} collective-permute-done((bf16[2,1,16,32,128]{4,3,2,1,0:T(8,128)(2,1)S(1)}, bf16[2,1,16,32,128]{4,3,2,1,0:T(8,128)(2,1)S(1)}, u32[]{:S(2)}, u32[]{:S(2)}) %collective-permute-start.60) | collective-permute-done | bytes 262176 | tf_op jit(solution)/shard_map/ppermute | solution.py:502
  538.1 17.5 %observe.7 = f32[2,2,3,16,128]{4,3,2,1,0:T(8,128)S(1)} custom-call(s32[1]{0:T(128)} %bitcast.core_ref, bf16[4,2,2,16,32,128]{5,4,3,2,1,0:T(8,128)(2,1)S(1)} %bitcast.69, bf16[2,1,16,32,128]{4,3,2,1,0:T(8,128)(2,1)S(1)} %pad_maximum_fusion.refs_0_, bf16[2,1,16,32,128]{4,3,2,1,0:T(8,128)(2,1)S(1)} %collective-permute-done.51.refs_1_, ...), custom_call_target="tpu_custom_call" | custom-call | flops 402653184 | bytes 35651584 | tf_op jit(solution)/shard_map/observe/pallas_call | solution.py:361
  568.0 14.5 %pull_back.7 = bf16[4,2,3,16,32,128]{5,4,3,2,1,0:T(8,128)(2,1)S(1)} custom-call(s32[1]{0:T(128)} %bitcast.core_ref, f32[2,2,3,16,128]{4,3,2,1,0:T(8,128)S(1)} %reverse_add_fusion.refs_0_, f32[2,2,3,16,128]{4,3,2,1,0:T(8,128)S(1)} %collective-permute-done.62.refs_1_, f32[2,2,3,16,128]{4,3,2,1,0:T(8,128)S(1)} %collective-permute-done.63.refs_2_, ...), custom_call_target="tpu_custom_call" | custom-call | flops 402653184 | bytes 36700160 | tf_op jit(solution)/shard_map/pull_back/pallas_call | solution.py:435
  596.3 6.0 finish.2
  602.3 39.5 %reduce-scatter.9.cloned.1.call-done = bf16[1,2,3,16,32,128]{5,4,3,2,1,0:T(8,128)(2,1)} async-done(((bf16[4,2,3,16,32,128]{5,4,3,2,1,0:T(8,128)(2,1)}), bf16[1,2,3,16,32,128]{5,4,3,2,1,0:T(8,128)(2,1)}) %reduce-scatter.9.cloned.1.call-update) | async-done | bytes 786448 | tf_op jit(solution)/shard_map/reduce_scatter | solution.py:623
  655.4 6.0 finish.3
  (296 shorter events, 235.4 us)
Async XLA Ops:
  7.2 127.1 %all-gather.9.cloned.1.call-start = ((), (), s32[]{:S(2)}) async-start(), calls=%async_computation.8 | async-start | bytes 2621440 | tf_op jit(solution)/shard_map/all_gather | solution.py:600
  8.7 12.2 %collective-permute-start.2 = (f32[2,4,128]{2,1,0:T(4,128)S(1)}, f32[2,4,128]{2,1,0:T(4,128)S(1)}, u32[]{:S(2)}, u32[]{:S(2)}) collective-permute-start(f32[2,4,128]{2,1,0:T(4,128)S(1)} %get-tuple-element.175), channel_id=1, source_target_pairs={{0,8},{8,16},{16,24},{1,9},{9,17},{17,25},{2,10},{10,18},{18,26},{... | collective-permute-start | bytes 12296 | tf_op jit(solution)/shard_map/ppermute | solution.py:459
  40.8 93.5 %collective-permute-start.13 = (bf16[2,128,16,4096]{3,2,1,0:T(8,128)(2,1)}, bf16[2,128,16,4096]{3,2,1,0:T(8,128)(2,1)}, u32[]{:S(2)}, u32[]{:S(2)}) collective-permute-start(bf16[2,128,16,4096]{3,2,1,0:T(8,128)(2,1)} %refs_5_.7), channel_id=1, source_target_pairs={{0,1},{1,0},{2,3},{3,2},{4,5},{5,4},{6,7},{7,6},{8,9},{9,8},{10,11... | collective-permute-start | bytes 100663304 | tf_op jit(solution)/shard_map/ppermute | solution.py:477
  41.2 195.9 %all-gather.13.cloned.1.call-start = ((), (), s32[]{:S(2)}) async-start(), calls=%async_computation.10 | async-start | bytes 2621440 | tf_op jit(solution)/shard_map/all_gather | solution.py:600
  41.2 16.1 %collective-permute-start.6 = (bf16[2,1,16,32,128]{4,3,2,1,0:T(8,128)(2,1)S(1)}, bf16[2,1,16,32,128]{4,3,2,1,0:T(8,128)(2,1)S(1)}, u32[]{:S(2)}, u32[]{:S(2)}) collective-permute-start(bf16[2,1,16,32,128]{4,3,2,1,0:T(8,128)(2,1)S(1)} %pad_maximum_fusion.3.refs_0_), channel_id=1, source_target_pairs={{7,5},{6,4},{5,3},{4,2},{3,1},{2,0},{15,13},{14,12},{13,11},{12,10... | collective-permute-start | bytes 786440 | tf_op jit(solution)/shard_map/ppermute | solution.py:502
  42.5 14.8 %collective-permute-start.5 = (bf16[2,1,16,32,128]{4,3,2,1,0:T(8,128)(2,1)S(1)}, bf16[2,1,16,32,128]{4,3,2,1,0:T(8,128)(2,1)S(1)}, u32[]{:S(2)}, u32[]{:S(2)}) collective-permute-start(bf16[2,1,16,32,128]{4,3,2,1,0:T(8,128)(2,1)S(1)} %pad_maximum_fusion.3.refs_0_), channel_id=1, source_target_pairs={{0,2},{1,3},{2,4},{3,5},{4,6},{5,7},{8,10},{9,11},{10,12},{11,13},... | collective-permute-start | bytes 786440 | tf_op jit(solution)/shard_map/ppermute | solution.py:501
  75.9 14.6 %collective-permute-start.30 = (bf16[3,16,32,128]{3,2,1,0:T(8,128)(2,1)S(1)}, bf16[3,16,32,128]{3,2,1,0:T(8,128)(2,1)S(1)}, u32[]{:S(2)}, u32[]{:S(2)}) collective-permute-start(bf16[3,16,32,128]{3,2,1,0:T(8,128)(2,1)S(1)} %get-tuple-element.104), channel_id=1, source_target_pairs={{0,1},{1,0},{2,3},{3,2},{4,5},{5,4},{6,7},{7,6},{8,9},{9,8},{10,11... | collective-permute-start | bytes 1179656 | tf_op jit(solution)/shard_map/ppermute | solution.py:477
  91.4 216.0 %reduce-scatter.5.cloned.1.call-start = ((), (), s32[]{:S(2)}) async-start(), calls=%async_computation.4 | async-start | bytes 3932160 | tf_op jit(solution)/shard_map/reduce_scatter | solution.py:623
  93.8 14.9 %collective-permute-start.11 = (bf16[2,1,16,32,128]{4,3,2,1,0:T(8,128)(2,1)S(1)}, bf16[2,1,16,32,128]{4,3,2,1,0:T(8,128)(2,1)}, u32[]{:S(2)}, u32[]{:S(2)}) collective-permute-start(bf16[2,1,16,32,128]{4,3,2,1,0:T(8,128)(2,1)S(1)} %collective-permute-done.6.refs_4_), channel_id=1, source_target_pairs={{5,3},{4,2},{3,1},{2,0},{13,11},{12,10},{11,9},{10,8},{21,19},{20,... | collective-permute-start | bytes 786440 | tf_op jit(solution)/shard_map/ppermute | solution.py:502
  97.0 23.6 %collective-permute-start.10 = (bf16[2,1,16,32,128]{4,3,2,1,0:T(8,128)(2,1)}, bf16[2,1,16,32,128]{4,3,2,1,0:T(8,128)(2,1)}, u32[]{:S(2)}, u32[]{:S(2)}) collective-permute-start(bf16[2,1,16,32,128]{4,3,2,1,0:T(8,128)(2,1)} %collective-permute-done.9.refs_2_), channel_id=1, source_target_pairs={{4,6},{5,7},{12,14},{13,15},{20,22},{21,23},{28,30},{29,31}} | collective-permute-start | bytes 786440 | tf_op jit(solution)/shard_map/ppermute | solution.py:501
  108.6 25.6 %collective-permute-start.12 = (bf16[2,1,16,32,128]{4,3,2,1,0:T(8,128)(2,1)}, bf16[2,1,16,32,128]{4,3,2,1,0:T(8,128)(2,1)}, u32[]{:S(2)}, u32[]{:S(2)}) collective-permute-start(bf16[2,1,16,32,128]{4,3,2,1,0:T(8,128)(2,1)} %collective-permute-done.11.refs_5_), channel_id=1, source_target_pairs={{3,1},{2,0},{11,9},{10,8},{19,17},{18,16},{27,25},{26,24}} | collective-permute-start | bytes 786440 | tf_op jit(solution)/shard_map/ppermute | solution.py:502
  112.2 43.3 %collective-permute-start.16 = (bf16[3,4,32,128]{3,2,1,0:T(8,128)(2,1)}, bf16[3,4,32,128]{3,2,1,0:T(8,128)(2,1)}, u32[]{:S(2)}, u32[]{:S(2)}) collective-permute-start(bf16[3,4,32,128]{3,2,1,0:T(8,128)(2,1)} %get-tuple-element.94), channel_id=1, source_target_pairs={{0,8},{8,16},{16,24},{1,9},{9,17},{17,25},{2,10},{10,18},{18,26},{... | collective-permute-start | bytes 294920 | tf_op jit(solution)/shard_map/ppermute | solution.py:459
  119.4 36.1 %collective-permute-start.17 = (bf16[3,4,32,128]{3,2,1,0:T(8,128)(2,1)}, bf16[3,4,32,128]{3,2,1,0:T(8,128)(2,1)}, u32[]{:S(2)}, u32[]{:S(2)}) collective-permute-start(bf16[3,4,32,128]{3,2,1,0:T(8,128)(2,1)} %get-tuple-element.96), channel_id=1, source_target_pairs={{8,0},{16,8},{24,16},{9,1},{17,9},{25,17},{10,2},{18,10},{26,18},{... | collective-permute-start | bytes 294920 | tf_op jit(solution)/shard_map/ppermute | solution.py:459
  155.5 9.8 %collective-permute-start.18 = (f32[2,2,3,16,128]{4,3,2,1,0:T(8,128)S(1)}, f32[2,2,3,16,128]{4,3,2,1,0:T(8,128)S(1)}, u32[]{:S(2)}, u32[]{:S(2)}) collective-permute-start(f32[2,2,3,16,128]{4,3,2,1,0:T(8,128)S(1)} %observe.4), channel_id=1, source_target_pairs={{0,1},{1,0},{2,3},{3,2},{4,5},{5,4},{6,7},{7,6},{8,9},{9,8},{10,11... | collective-permute-start | bytes 294920 | tf_op jit(solution)/shard_map/ppermute | solution.py:477
  191.2 184.3 %reduce-scatter.7.cloned.1.call-start = ((), (), s32[]{:S(2)}) async-start(), calls=%async_computation.5 | async-start | bytes 3932160 | tf_op jit(solution)/shard_map/reduce_scatter | solution.py:623
  192.6 14.3 %collective-permute-start.31 = (bf16[2,1,16,32,128]{4,3,2,1,0:T(8,128)(2,1)S(1)}, bf16[2,1,16,32,128]{4,3,2,1,0:T(8,128)(2,1)S(1)}, u32[]{:S(2)}, u32[]{:S(2)}) collective-permute-start(bf16[2,1,16,32,128]{4,3,2,1,0:T(8,128)(2,1)S(1)} %pad_maximum_fusion.1.refs_0_), channel_id=1, source_target_pairs={{0,2},{1,3},{2,4},{3,5},{4,6},{5,7},{8,10},{9,11},{10,12},{11,13},... | collective-permute-start | bytes 786440 | tf_op jit(solution)/shard_map/ppermute | solution.py:501
  208.9 25.3 %collective-permute-start.34 = (bf16[2,1,16,32,128]{4,3,2,1,0:T(8,128)(2,1)S(1)}, bf16[2,1,16,32,128]{4,3,2,1,0:T(8,128)(2,1)}, u32[]{:S(2)}, u32[]{:S(2)}) collective-permute-start(bf16[2,1,16,32,128]{4,3,2,1,0:T(8,128)(2,1)S(1)} %collective-permute-done.32.refs_4_), channel_id=1, source_target_pairs={{5,3},{4,2},{3,1},{2,0},{13,11},{12,10},{11,9},{10,8},{21,19},{20,... | collective-permute-start | bytes 786440 | tf_op jit(solution)/shard_map/ppermute | solution.py:502
  235.6 20.7 %collective-permute-start.36 = (bf16[2,1,16,32,128]{4,3,2,1,0:T(8,128)(2,1)}, bf16[2,1,16,32,128]{4,3,2,1,0:T(8,128)(2,1)}, u32[]{:S(2)}, u32[]{:S(2)}) collective-permute-start(bf16[2,1,16,32,128]{4,3,2,1,0:T(8,128)(2,1)} %collective-permute-done.34.refs_5_), channel_id=1, source_target_pairs={{3,1},{2,0},{11,9},{10,8},{19,17},{18,16},{27,25},{26,24}} | collective-permute-start | bytes 786440 | tf_op jit(solution)/shard_map/ppermute | solution.py:502
  307.3 121.1 %all-gather.11.cloned.1.call-start = ((), (), s32[]{:S(2)}) async-start(), calls=%async_computation.9 | async-start | bytes 2621440 | tf_op jit(solution)/shard_map/all_gather | solution.py:600
  336.6 199.9 %all-gather.15.cloned.1.call-start = ((), (), s32[]{:S(2)}) async-start(), calls=%async_computation.11 | async-start | bytes 2621440 | tf_op jit(solution)/shard_map/all_gather | solution.py:600
  336.7 20.2 %collective-permute-start.28 = (bf16[2,1,16,32,128]{4,3,2,1,0:T(8,128)(2,1)S(1)}, bf16[2,1,16,32,128]{4,3,2,1,0:T(8,128)(2,1)S(1)}, u32[]{:S(2)}, u32[]{:S(2)}) collective-permute-start(bf16[2,1,16,32,128]{4,3,2,1,0:T(8,128)(2,1)S(1)} %pad_maximum_fusion.2.refs_0_), channel_id=1, source_target_pairs={{7,5},{6,4},{5,3},{4,2},{3,1},{2,0},{15,13},{14,12},{13,11},{12,10... | collective-permute-start | bytes 786440 | tf_op jit(solution)/shard_map/ppermute | solution.py:502
  338.0 20.2 %collective-permute-start.26 = (bf16[2,1,16,32,128]{4,3,2,1,0:T(8,128)(2,1)S(1)}, bf16[2,1,16,32,128]{4,3,2,1,0:T(8,128)(2,1)}, u32[]{:S(2)}, u32[]{:S(2)}) collective-permute-start(bf16[2,1,16,32,128]{4,3,2,1,0:T(8,128)(2,1)S(1)} %pad_maximum_fusion.2.refs_0_), channel_id=1, source_target_pairs={{0,2},{1,3},{2,4},{3,5},{4,6},{5,7},{8,10},{9,11},{10,12},{11,13},... | collective-permute-start | bytes 786440 | tf_op jit(solution)/shard_map/ppermute | solution.py:501
  356.9 19.7 %collective-permute-start.29 = (bf16[2,1,16,32,128]{4,3,2,1,0:T(8,128)(2,1)S(1)}, bf16[2,1,16,32,128]{4,3,2,1,0:T(8,128)(2,1)}, u32[]{:S(2)}, u32[]{:S(2)}) collective-permute-start(bf16[2,1,16,32,128]{4,3,2,1,0:T(8,128)(2,1)S(1)} %collective-permute-done.28.refs_4_), channel_id=1, source_target_pairs={{5,3},{4,2},{3,1},{2,0},{13,11},{12,10},{11,9},{10,8},{21,19},{20,... | collective-permute-start | bytes 786440 | tf_op jit(solution)/shard_map/ppermute | solution.py:502
  358.2 18.5 %collective-permute-start.27 = (bf16[2,1,16,32,128]{4,3,2,1,0:T(8,128)(2,1)}, bf16[2,1,16,32,128]{4,3,2,1,0:T(8,128)(2,1)}, u32[]{:S(2)}, u32[]{:S(2)}) collective-permute-start(bf16[2,1,16,32,128]{4,3,2,1,0:T(8,128)(2,1)} %collective-permute-done.26.refs_1_), channel_id=1, source_target_pairs={{2,4},{3,5},{4,6},{5,7},{10,12},{11,13},{12,14},{13,15},{18,20},{1... | collective-permute-start | bytes 786440 | tf_op jit(solution)/shard_map/ppermute | solution.py:501
  377.8 9.7 %collective-permute-start.45 = (bf16[3,16,32,128]{3,2,1,0:T(8,128)(2,1)S(1)}, bf16[3,16,32,128]{3,2,1,0:T(8,128)(2,1)S(1)}, u32[]{:S(2)}, u32[]{:S(2)}) collective-permute-start(bf16[3,16,32,128]{3,2,1,0:T(8,128)(2,1)S(1)} %get-tuple-element.162), channel_id=1, source_target_pairs={{0,1},{1,0},{2,3},{3,2},{4,5},{5,4},{6,7},{7,6},{8,9},{9,8},{10,11... | collective-permute-start | bytes 1179656 | tf_op jit(solution)/shard_map/ppermute | solution.py:477
  402.3 182.1 %reduce-scatter.11.cloned.1.call-start = ((), (), s32[]{:S(2)}) async-start(), calls=%async_computation.7 | async-start | bytes 3932160 | tf_op jit(solution)/shard_map/reduce_scatter | solution.py:623
  403.0 23.8 %collective-permute-start.44 = (bf16[2,1,16,32,128]{4,3,2,1,0:T(8,128)(2,1)}, bf16[2,1,16,32,128]{4,3,2,1,0:T(8,128)(2,1)S(1)}, u32[]{:S(2)}, u32[]{:S(2)}) collective-permute-start(bf16[2,1,16,32,128]{4,3,2,1,0:T(8,128)(2,1)} %collective-permute-done.29.refs_5_), channel_id=1, source_target_pairs={{3,1},{2,0},{11,9},{10,8},{19,17},{18,16},{27,25},{26,24}} | collective-permute-start | bytes 786440 | tf_op jit(solution)/shard_map/ppermute | solution.py:502
  404.3 43.5 %collective-permute-start.48 = (bf16[3,4,32,128]{3,2,1,0:T(8,128)(2,1)}, bf16[3,4,32,128]{3,2,1,0:T(8,128)(2,1)S(1)}, u32[]{:S(2)}, u32[]{:S(2)}) collective-permute-start(bf16[3,4,32,128]{3,2,1,0:T(8,128)(2,1)} %copy-done.41), channel_id=1, source_target_pairs={{0,8},{8,16},{16,24},{1,9},{9,17},{17,25},{2,10},{10,18},{18,26},{... | collective-permute-start | bytes 294920 | tf_op jit(solution)/shard_map/ppermute | solution.py:459
  408.8 39.1 %collective-permute-start.49 = (bf16[3,4,32,128]{3,2,1,0:T(8,128)(2,1)}, bf16[3,4,32,128]{3,2,1,0:T(8,128)(2,1)S(1)}, u32[]{:S(2)}, u32[]{:S(2)}) collective-permute-start(bf16[3,4,32,128]{3,2,1,0:T(8,128)(2,1)} %copy-done.40), channel_id=1, source_target_pairs={{8,0},{16,8},{24,16},{9,1},{17,9},{25,17},{10,2},{18,10},{26,18},{... | collective-permute-start | bytes 294920 | tf_op jit(solution)/shard_map/ppermute | solution.py:459
  473.5 168.3 %reduce-scatter.9.cloned.1.call-start = ((), (), s32[]{:S(2)}) async-start(), calls=%async_computation.6 | async-start | bytes 3932160 | tf_op jit(solution)/shard_map/reduce_scatter | solution.py:623
  484.2 28.2 %collective-permute-start.54 = (bf16[2,1,16,32,128]{4,3,2,1,0:T(8,128)(2,1)S(1)}, bf16[2,1,16,32,128]{4,3,2,1,0:T(8,128)(2,1)S(1)}, u32[]{:S(2)}, u32[]{:S(2)}) collective-permute-start(bf16[2,1,16,32,128]{4,3,2,1,0:T(8,128)(2,1)S(1)} %collective-permute-done.52.refs_4_), channel_id=1, source_target_pairs={{5,3},{4,2},{3,1},{2,0},{13,11},{12,10},{11,9},{10,8},{21,19},{20,... | collective-permute-start | bytes 786440 | tf_op jit(solution)/shard_map/ppermute | solution.py:502
  513.1 23.4 %collective-permute-start.60 = (bf16[2,1,16,32,128]{4,3,2,1,0:T(8,128)(2,1)S(1)}, bf16[2,1,16,32,128]{4,3,2,1,0:T(8,128)(2,1)S(1)}, u32[]{:S(2)}, u32[]{:S(2)}) collective-permute-start(bf16[2,1,16,32,128]{4,3,2,1,0:T(8,128)(2,1)S(1)} %collective-permute-done.54.refs_5_), channel_id=1, source_target_pairs={{3,1},{2,0},{11,9},{10,8},{19,17},{18,16},{27,25},{26,24}} | collective-permute-start | bytes 786440 | tf_op jit(solution)/shard_map/ppermute | solution.py:502
  (93 other events, 606.4 us)
Sparse Core Ops, SparseCore 0:
  41.3 46.9 all-gather.8
  91.5 54.4 all-gather.12
  191.4 73.1 reduce-scatter.4
  307.4 68.0 reduce-scatter.6
  377.0 51.4 all-gather.10
  429.9 45.8 all-gather.14
  478.7 69.7 reduce-scatter.10
  584.4 57.3 reduce-scatter.8

commit v8 on v7

--- a/solution.py
+++ b/solution.py
@@ -350,7 +350,7 @@
 
 def observe(core, field, slots, own, other, table, around, local_cells):
     chips, _, whole, rows, steps, lanes = field.shape
-    apart = slots[0].shape[1]
+    apart = slots[0].shape[1] if slots else 0
     members = whole + apart
     _, freqs, sensors, cells = own.shape
     width = CHUNK_ROWS * lanes
@@ -565,7 +565,7 @@
     lines = [[k for k in range(size) if k % 2 == parity] for parity in range(2)]
     shape = (chips, 2, members, rows // 2, steps, cols)
 
-    def ready(state):
+    def ready(state, whole):
         iterate, keep, give, rest, top, bottom = state
         above, below = rims(top, bottom)
         pair = jnp.stack([keep, swap_cores(give)])
@@ -579,53 +579,56 @@
         _, cross = misfit_rims(edge[1])
         return misfit[0], swap_cores(misfit[1]), same, cross
 
-    def begin(group, ends):
-        return ready(start(group, members, core, rhs, *rims(*ends), coeff))
+    def begin(group, ends, whole):
+        return ready(start(group, members, core, rhs, *rims(*ends), coeff), whole)
 
     groups = [slice(group * members, (group + 1) * members) for group in range(GROUPS)]
-    states = [begin(0, (top[groups[0]], bottom[groups[0]]))]
+    states = [begin(0, (top[groups[0]], bottom[groups[0]]), members)]
     iterate, pair, apart, rests = states[0]
-    pair, apart, whole_map = lax.optimization_barrier((pair, apart, forward_map))
+    pair, whole_map = lax.optimization_barrier((pair, forward_map))
     other_map = swap_cores(whole_map)
-    line = Line(apart)
-    line.hop()
     for group in range(1, GROUPS):
         ends = (top[groups[group]], bottom[groups[group]])
-        rests, ends = line.after((rests, ends))
-        states.append(begin(group, ends))
+        _, rests, ends = lax.optimization_barrier((pair, rests, ends))
+        states.append(begin(group, ends, whole))
     states[0] = iterate, pair, apart, rests
+    line = None
 
     outputs = ()
     for iteration in range(ITERS):
         fields = [lax.all_gather(state[1], "sensors", axis_index_groups=lines) for state in states]
-        line.hop(last=True)
+        if line is not None:
+            line.hop(last=True)
         totals = []
         for group in range(GROUPS):
-            slots, line = line.slots(), None
+            iterate, _, _, rests = states[group]
+            field = fields[group]
+            slots, line = (line.slots() if line is not None else []), None
+            if group > 0:
+                field, rests = lax.optimization_barrier((field, rests))
+            states[group] = iterate, rests
             if group + 1 < GROUPS:
                 line = Line(states[group + 1][2])
                 line.hop()
+                field = line.after(field)
+                line.hop()
             sums = observe(
-                core, fields[group], slots, forward_map, other_map, table, around, local_cells
+                core, field, slots, forward_map, other_map, table, around, local_cells
             )
             if line is not None:
-                iterate, pair, apart, rests = states[group + 1]
-                sums, rests = lax.optimization_barrier((sums, rests))
-                line.after(sums)
-                states[group + 1] = iterate, pair, apart, rests
-                line.hop()
+                sums = line.after(sums)
+                line.hop(last=True)
             sums = from_all_cells(sums + swap_cores(sums)[::-1])
             misfit = pull_back(core, sums, noise, forward_map, other_map, back, local_cells, shape)
             if line is not None:
-                line.after(misfit)
-                line.hop(last=True)
+                misfit = line.after(misfit)
             totals.append(
                 lax.psum_scatter(
                     misfit, "sensors", scatter_dimension=0, axis_index_groups=lines, tiled=False
                 )
             )
         for group in range(GROUPS):
-            iterate, _, _, rests = states[group]
+            iterate, rests = states[group]
             total = totals[group]
             if iteration < ITERS - 1:
                 if group == 1:
@@ -635,7 +638,7 @@
                     line.hop()
                     total, earlier = line.after((total, before[3]))
                     states[0] = (*before[:3], earlier)
-                states[group] = ready(step(core, rests, edges(total), iterate, coeff))
+                states[group] = ready(step(core, rests, edges(total), iterate, coeff), whole)
             else:
                 if outputs:
                     total, outputs = lax.optimization_barrier((total, outputs))

time: 671 us -> 557 us (0.83)
  waiting for transfers between devices: 268 us -> 188 us
  starting transfers between devices: 152 us -> 121 us
    ppermute x12 -> x9, waiting for transfers between devices: 154 us -> 42.3 us  [hop(): down = lax.ppermute(self.ends[1], 'sensors', backward)]
    reduce_scatter x4, waiting for transfers between devices: 43.2 us -> 73 us  [shards(): lax.psum_scatter(misfit, 'sensors', scatter_dimension=0, axis_index_group...]
    ppermute x13, starting transfers between devices: 30.7 us -> 15.1 us  [swap_cores(): return lax.ppermute(value, 'sensors', [(k, k ^ 1) for k in range(size)])]
    ppermute x12 -> x9, waiting for transfers between devices: 8.46 us -> 0.02 us  [hop(): up = lax.ppermute(self.ends[0], 'sensors', onward)]
    ppermute x12 -> x9, starting transfers between devices: 25.5 us -> 19.6 us  [hop(): up = lax.ppermute(self.ends[0], 'sensors', onward)]
    ppermute x12 -> x9, starting transfers between devices: 15.6 us -> 11.8 us  [hop(): down = lax.ppermute(self.ends[1], 'sensors', backward)]
    unnamed x92 -> x78, local copies, waits for them, and re-layouts: 41.4 us -> 41 us
  transfers between devices with their start and end apart: 79 -> 73, of which waited for: 47 -> 41; matrix products, arithmetic and copies ran while one was open for 3% -> 3% of each run, Pallas kernels for 23% -> 28%
where the time goes in v8:
time: 557 us; the launch traced here: 554 us
  waiting for transfers between devices  188 us (34%)
  Pallas kernels  168 us (30%)
  starting transfers between devices  121 us (22%)
  local copies, waits for them, and re-layouts  52.9 us (9%)
  between operations  15 us (3%)
  other arithmetic  8.98 us (2%)
    reduce_scatter x4, waiting for transfers between devices, shards(): lax.psum_scatter(misfit, 'sensors', scatter_dimension=0, axis_index_group...  73 us
    pallas_call x4, Pallas kernels, observe(): call(observe_kernel, core, (rows // CHUNK_ROWS,), [pl.BlockSpec(block, la...  70.4 us
    pallas_call x4, Pallas kernels, pull_back(): call(pull_kernel, core, (rows // CHUNK_ROWS,), [whole_block(array) for ar...  58.5 us
    ppermute x9, waiting for transfers between devices, hop(): down = lax.ppermute(self.ends[1], 'sensors', backward)  42.3 us
    unnamed x78, local copies, waits for them, and re-layouts  41 us
    ppermute x7, starting transfers between devices, rims(): lax.ppermute(bottom, 'cells', onward)  27.8 us
    ppermute x8, starting transfers between devices, misfit_rims(): return (lax.ppermute(edge, both, same), lax.ppermute(edge, both, cross))  23.5 us
    ppermute x13, waiting for transfers between devices, swap_cores(): return lax.ppermute(value, 'sensors', [(k, k ^ 1) for k in range(size)])  22.9 us
  transfers between devices with their start and end apart: 73, of which 41 were waited for; matrix products, arithmetic and copies ran while one was open for 3% of the time, Pallas kernels for 28%

profile of v8, /device:TPU:1, one launch (start us, length us, event | category | flops | bytes accessed | tf_op | source)
XLA Modules:
  0.0 554.4 jit_solution(11989683085853370521)
XLA Ops:
  8.7 3.9 collective-permute-start.2
  15.5 4.0 collective-permute-start
  22.4 4.4 collective-permute-done.1.down_ref
  28.7 6.1 %start.2 = (f32[3,32,32,128]{3,2,1,0:T(8,128)S(1)}, bf16[3,16,32,128]{3,2,1,0:T(8,128)(2,1)S(1)}, bf16[3,16,32,128]{3,2,1,0:T(8,128)(2,1)S(1)}, f32[3,32,32,128]...) custom-call(s32[1]{0:T(128)} %bitcast.core_ref, ...), custom_call_target="tpu_custom_call" | custom-call | tf_op jit(solution)/shard_map/start/pallas_call | solution.py:155
  41.3 4.4 collective-permute-start.5
  57.0 4.1 collective-permute-done.8.down_ref
  63.1 6.1 %start.3 = (f32[3,32,32,128]{3,2,1,0:T(8,128)S(1)}, bf16[3,16,32,128]{3,2,1,0:T(8,128)(2,1)S(1)}, bf16[3,16,32,128]{3,2,1,0:T(8,128)(2,1)S(1)}, f32[3,32,32,128]...) custom-call(s32[1]{0:T(128)} %bitcast.core_ref, ...), custom_call_target="tpu_custom_call" | custom-call | tf_op jit(solution)/shard_map/start/pallas_call | solution.py:155
  73.6 16.9 %collective-permute-done.9 = bf16[3,16,32,128]{3,2,1,0:T(8,128)(2,1)S(1)} collective-permute-done((bf16[3,16,32,128]{3,2,1,0:T(8,128)(2,1)S(1)}, bf16[3,16,32,128]{3,2,1,0:T(8,128)(2,1)S(1)}, u32[]{:S(2)}, u32[]{:S(2)}) %collective-permute-start.9) | collective-permute-done | bytes 393248 | tf_op jit(solution)/shard_map/ppermute | solution.py:477
  93.8 4.7 collective-permute-start.12
  99.5 10.0 %collective-permute-done.13.refs_4_ = bf16[2,1,16,32,128]{4,3,2,1,0:T(8,128)(2,1)S(1)} collective-permute-done((bf16[2,1,16,32,128]{4,3,2,1,0:T(8,128)(2,1)S(1)}, bf16[2,1,16,32,128]{4,3,2,1,0:T(8,128)(2,1)S(1)}, u32[]{:S(2)}, u32[]{:S(2)}) %collective-permute-start.13) | collective-permute-done | bytes 262176 | tf_op jit(solution)/shard_map/ppermute | solution.py:502
  114.4 17.3 %observe.4 = f32[2,2,3,16,128]{4,3,2,1,0:T(8,128)S(1)} custom-call(s32[1]{0:T(128)} %bitcast.core_ref, bf16[4,2,3,16,32,128]{5,4,3,2,1,0:T(8,128)(2,1)S(1)} %bitcast.66, bf16[2,128,16,4096]{3,2,1,0:T(8,128)(2,1)} %refs_5_.7, bf16[2,128,16,4096]{3,2,1,0:T(8,128)(2,1)} %collective-permute-done.16.refs_1_.refs_6_.refs_8_, ...), custom_call_target="tpu_custom_call" | custom-call | flops 402653184 | bytes 36700160 | tf_op jit(solution)/shard_map/observe/pallas_call | solution.py:361
  136.6 4.0 collective-permute-start.22
  146.0 14.6 %pull_back.4 = bf16[4,2,3,16,32,128]{5,4,3,2,1,0:T(8,128)(2,1)S(1)} custom-call(s32[1]{0:T(128)} %bitcast.core_ref, f32[2,2,3,16,128]{4,3,2,1,0:T(8,128)S(1)} %reverse_add_fusion.3.refs_0_, f32[2,2,3,16,128]{4,3,2,1,0:T(8,128)S(1)} %collective-permute-done.20.refs_1_, f32[2,2,3,16,128]{4,3,2,1,0:T(8,128)S(1)} %collective-permute-done.21.refs_2_, ...), custom_call_target="tpu_custom_call" | custom-call | flops 402653184 | bytes 36700160 | tf_op jit(solution)/shard_map/pull_back/pallas_call | solution.py:435
  173.9 17.7 %observe.5 = f32[2,2,3,16,128]{4,3,2,1,0:T(8,128)S(1)} custom-call(s32[1]{0:T(128)} %bitcast.core_ref, bf16[4,2,2,16,32,128]{5,4,3,2,1,0:T(8,128)(2,1)S(1)} %bitcast.67, bf16[2,1,16,32,128]{4,3,2,1,0:T(8,128)(2,1)S(1)} %pad_maximum_fusion.3.refs_0_, bf16[2,1,16,32,128]{4,3,2,1,0:T(8,128)(2,1)} %collective-permute-done.12.refs_1_, ...), custom_call_target="tpu_custom_call" | custom-call | flops 402653184 | bytes 35651584 | tf_op jit(solution)/shard_map/observe/pallas_call | solution.py:361
  202.2 14.6 %pull_back.5 = bf16[4,2,3,16,32,128]{5,4,3,2,1,0:T(8,128)(2,1)S(1)} custom-call(s32[1]{0:T(128)} %bitcast.core_ref, f32[2,2,3,16,128]{4,3,2,1,0:T(8,128)S(1)} %reverse_add_fusion.2.refs_0_, f32[2,2,3,16,128]{4,3,2,1,0:T(8,128)S(1)} %collective-permute-done.32.refs_1_, f32[2,2,3,16,128]{4,3,2,1,0:T(8,128)S(1)} %collective-permute-done.33.refs_2_, ...), custom_call_target="tpu_custom_call" | custom-call | flops 402653184 | bytes 36700160 | tf_op jit(solution)/shard_map/pull_back/pallas_call | solution.py:435
  218.6 7.4 %reduce-scatter.5.cloned.1.call-done = bf16[1,2,3,16,32,128]{5,4,3,2,1,0:T(8,128)(2,1)} async-done(((bf16[4,2,3,16,32,128]{5,4,3,2,1,0:T(8,128)(2,1)}), bf16[1,2,3,16,32,128]{5,4,3,2,1,0:T(8,128)(2,1)}) %reduce-scatter.5.cloned.1.call-update) | async-done | bytes 786448 | tf_op jit(solution)/shard_map/reduce_scatter | solution.py:626
  240.3 7.3 %step.2 = (f32[3,32,32,128]{3,2,1,0:T(8,128)S(1)}, bf16[3,16,32,128]{3,2,1,0:T(8,128)(2,1)S(1)}, bf16[3,16,32,128]{3,2,1,0:T(8,128)(2,1)S(1)}, f32[3,32,32,128]{...) custom-call(s32[1]{0:T(128)} %bitcast.core_ref, ...), custom_call_target="tpu_custom_call" | custom-call | tf_op jit(solution)/shard_map/step/pallas_call | solution.py:207
  255.7 4.7 collective-permute-start.27
  260.4 14.3 %collective-permute-done.29.refs_4_ = bf16[2,1,16,32,128]{4,3,2,1,0:T(8,128)(2,1)S(1)} collective-permute-done((bf16[2,1,16,32,128]{4,3,2,1,0:T(8,128)(2,1)S(1)}, bf16[2,1,16,32,128]{4,3,2,1,0:T(8,128)(2,1)S(1)}, u32[]{:S(2)}, u32[]{:S(2)}) %collective-permute-start.29) | collective-permute-done | bytes 262176 | tf_op jit(solution)/shard_map/ppermute | solution.py:502
  277.4 6.3 %collective-permute-start.35 = (bf16[3,4,32,128]{3,2,1,0:T(8,128)(2,1)}, bf16[3,4,32,128]{3,2,1,0:T(8,128)(2,1)S(1)}, u32[]{:S(2)}, u32[]{:S(2)}) collective-permute-start(bf16[3,4,32,128]{3,2,1,0:T(8,128)(2,1)} %copy-done.36), channel_id=1, source_target_pairs={{0,8},{8,16},{16,24},{1,9},{9,17},{17,25},{2,10},{10,18},{18,26},{... | collective-permute-start | bytes 294920 | tf_op jit(solution)/shard_map/ppermute | solution.py:459
  285.1 14.4 %reduce-scatter.7.cloned.1.call-done = bf16[1,2,3,16,32,128]{5,4,3,2,1,0:T(8,128)(2,1)} async-done(((bf16[4,2,3,16,32,128]{5,4,3,2,1,0:T(8,128)(2,1)}), bf16[1,2,3,16,32,128]{5,4,3,2,1,0:T(8,128)(2,1)}) %reduce-scatter.7.cloned.1.call-update) | async-done | bytes 786448 | tf_op jit(solution)/shard_map/reduce_scatter | solution.py:626
  312.7 7.0 %step.3 = (f32[3,32,32,128]{3,2,1,0:T(8,128)S(1)}, bf16[3,16,32,128]{3,2,1,0:T(8,128)(2,1)S(1)}, bf16[3,16,32,128]{3,2,1,0:T(8,128)(2,1)S(1)}, f32[3,32,32,128]{...) custom-call(s32[1]{0:T(128)} %bitcast.core_ref, ...), custom_call_target="tpu_custom_call" | custom-call | tf_op jit(solution)/shard_map/step/pallas_call | solution.py:207
  327.9 4.1 collective-permute-start.43
  333.9 15.1 %collective-permute-done.44.refs_4_ = bf16[2,1,16,32,128]{4,3,2,1,0:T(8,128)(2,1)S(1)} collective-permute-done((bf16[2,1,16,32,128]{4,3,2,1,0:T(8,128)(2,1)S(1)}, bf16[2,1,16,32,128]{4,3,2,1,0:T(8,128)(2,1)S(1)}, u32[]{:S(2)}, u32[]{:S(2)}) %collective-permute-start.44) | collective-permute-done | bytes 262176 | tf_op jit(solution)/shard_map/ppermute | solution.py:502
  357.7 18.0 %observe.6 = f32[2,2,3,16,128]{4,3,2,1,0:T(8,128)S(1)} custom-call(s32[1]{0:T(128)} %bitcast.core_ref, bf16[4,2,2,16,32,128]{5,4,3,2,1,0:T(8,128)(2,1)S(1)} %bitcast.68, bf16[2,1,16,32,128]{4,3,2,1,0:T(8,128)(2,1)S(1)} %pad_maximum_fusion.2.refs_0_, bf16[2,1,16,32,128]{4,3,2,1,0:T(8,128)(2,1)} %collective-permute-done.27.refs_1_, ...), custom_call_target="tpu_custom_call" | custom-call | flops 402653184 | bytes 35651584 | tf_op jit(solution)/shard_map/observe/pallas_call | solution.py:361
  386.6 14.6 %pull_back.6 = bf16[4,2,3,16,32,128]{5,4,3,2,1,0:T(8,128)(2,1)S(1)} custom-call(s32[1]{0:T(128)} %bitcast.core_ref, f32[2,2,3,16,128]{4,3,2,1,0:T(8,128)S(1)} %reverse_add_fusion.1.refs_0_, f32[2,2,3,16,128]{4,3,2,1,0:T(8,128)S(1)} %collective-permute-done.52.refs_1_, f32[2,2,3,16,128]{4,3,2,1,0:T(8,128)S(1)} %collective-permute-done.53.refs_2_, ...), custom_call_target="tpu_custom_call" | custom-call | flops 402653184 | bytes 36700160 | tf_op jit(solution)/shard_map/pull_back/pallas_call | solution.py:435
  413.3 17.4 %observe.7 = f32[2,2,3,16,128]{4,3,2,1,0:T(8,128)S(1)} custom-call(s32[1]{0:T(128)} %bitcast.core_ref, bf16[4,2,2,16,32,128]{5,4,3,2,1,0:T(8,128)(2,1)S(1)} %bitcast.69, bf16[2,1,16,32,128]{4,3,2,1,0:T(8,128)(2,1)S(1)} %pad_maximum_fusion.1.refs_0_, bf16[2,1,16,32,128]{4,3,2,1,0:T(8,128)(2,1)S(1)} %collective-permute-done.43.refs_1_, ...), custom_call_target="tpu_custom_call" | custom-call | flops 402653184 | bytes 35651584 | tf_op jit(solution)/shard_map/observe/pallas_call | solution.py:361
  441.3 14.7 %pull_back.7 = bf16[4,2,3,16,32,128]{5,4,3,2,1,0:T(8,128)(2,1)S(1)} custom-call(s32[1]{0:T(128)} %bitcast.core_ref, f32[2,2,3,16,128]{4,3,2,1,0:T(8,128)S(1)} %reverse_add_fusion.refs_0_, f32[2,2,3,16,128]{4,3,2,1,0:T(8,128)S(1)} %collective-permute-done.56.refs_1_, f32[2,2,3,16,128]{4,3,2,1,0:T(8,128)S(1)} %collective-permute-done.57.refs_2_, ...), custom_call_target="tpu_custom_call" | custom-call | flops 402653184 | bytes 36700160 | tf_op jit(solution)/shard_map/pull_back/pallas_call | solution.py:435
  457.7 7.6 %reduce-scatter.11.cloned.1.call-done = bf16[1,2,3,16,32,128]{5,4,3,2,1,0:T(8,128)(2,1)} async-done(((bf16[4,2,3,16,32,128]{5,4,3,2,1,0:T(8,128)(2,1)}), bf16[1,2,3,16,32,128]{5,4,3,2,1,0:T(8,128)(2,1)}) %reduce-scatter.11.cloned.1.call-update) | async-done | bytes 786448 | tf_op jit(solution)/shard_map/reduce_scatter | solution.py:626
  477.5 6.8 %finish.2 = (f32[32,192,128]{2,1,0:T(8,128)}, f32[32,192,128]{2,1,0:T(8,128)}) custom-call(s32[1]{0:T(128)} %bitcast.core_ref, bf16[3,4,32,128]{3,2,1,0:T(8,128)(2,1)S(1)} %collective-permute-done.35.up_ref, f32[3,32,32,128]{3,2,1,0:T(8,128)S(1)} %copy-done.19, bf16[3,4,32,128]{3,2,1,0:T(8,128)(2,1)} %collective-permute-done.36.down_ref, ...), custom_call_target="tpu_custom_call" | custom-call | tf_op jit(solution)/shard_map/finish/pallas_call | solution.py:247
  484.3 43.6 %reduce-scatter.9.cloned.1.call-done = bf16[1,2,3,16,32,128]{5,4,3,2,1,0:T(8,128)(2,1)} async-done(((bf16[4,2,3,16,32,128]{5,4,3,2,1,0:T(8,128)(2,1)}), bf16[1,2,3,16,32,128]{5,4,3,2,1,0:T(8,128)(2,1)}) %reduce-scatter.9.cloned.1.call-update) | async-done | bytes 786448 | tf_op jit(solution)/shard_map/reduce_scatter | solution.py:626
  541.5 6.0 %finish.3 = (f32[32,192,128]{2,1,0:T(8,128)}, f32[32,192,128]{2,1,0:T(8,128)}) custom-call(s32[1]{0:T(128)} %bitcast.core_ref, bf16[3,4,32,128]{3,2,1,0:T(8,128)(2,1)S(1)} %collective-permute-done.41.up_ref, f32[3,32,32,128]{3,2,1,0:T(8,128)S(1)} %copy-done.23, ...), custom_call_target="tpu_custom_call", output_to_operand_aliasing={{0}: (10, {}), {1}: (11, {})} | custom-call | tf_op jit(solution)/shard_map/finish/pallas_call | solution.py:247
  (269 shorter events, 197.2 us)
Async XLA Ops:
  7.2 102.4 %all-gather.11.cloned.1.call-start = ((), (), s32[]{:S(2)}) async-start(), calls=%async_computation.9 | async-start | bytes 3932160 | tf_op jit(solution)/shard_map/all_gather | solution.py:599
  8.7 12.2 %collective-permute-start.2 = (f32[2,4,128]{2,1,0:T(4,128)S(1)}, f32[2,4,128]{2,1,0:T(4,128)S(1)}, u32[]{:S(2)}, u32[]{:S(2)}) collective-permute-start(f32[2,4,128]{2,1,0:T(4,128)S(1)} %get-tuple-element.185), channel_id=1, source_target_pairs={{0,8},{8,16},{16,24},{1,9},{9,17},{17,25},{2,10},{10,18},{18,26},{... | collective-permute-start | bytes 12296 | tf_op jit(solution)/shard_map/ppermute | solution.py:459
  40.8 71.6 %collective-permute-start.16 = (bf16[2,128,16,4096]{3,2,1,0:T(8,128)(2,1)}, bf16[2,128,16,4096]{3,2,1,0:T(8,128)(2,1)}, u32[]{:S(2)}, u32[]{:S(2)}) collective-permute-start(bf16[2,128,16,4096]{3,2,1,0:T(8,128)(2,1)} %refs_5_.7), channel_id=1, source_target_pairs={{0,1},{1,0},{2,3},{3,2},{4,5},{5,4},{6,7},{7,6},{8,9},{9,8},{10,11... | collective-permute-start | bytes 100663304 | tf_op jit(solution)/shard_map/ppermute | solution.py:477
  41.2 130.8 %all-gather.9.cloned.1.call-start = ((), (), s32[]{:S(2)}) async-start(), calls=%async_computation.8 | async-start | bytes 2621440 | tf_op jit(solution)/shard_map/all_gather | solution.py:599
  71.7 18.9 %collective-permute-start.9 = (bf16[3,16,32,128]{3,2,1,0:T(8,128)(2,1)S(1)}, bf16[3,16,32,128]{3,2,1,0:T(8,128)(2,1)S(1)}, u32[]{:S(2)}, u32[]{:S(2)}) collective-permute-start(bf16[3,16,32,128]{3,2,1,0:T(8,128)(2,1)S(1)} %get-tuple-element.91), channel_id=1, source_target_pairs={{0,1},{1,0},{2,3},{3,2},{4,5},{5,4},{6,7},{7,6},{8,9},{9,8},{10,11... | collective-permute-start | bytes 1179656 | tf_op jit(solution)/shard_map/ppermute | solution.py:477
  91.4 134.5 %reduce-scatter.5.cloned.1.call-start = ((), (), s32[]{:S(2)}) async-start(), calls=%async_computation.4 | async-start | bytes 3932160 | tf_op jit(solution)/shard_map/reduce_scatter | solution.py:626
  92.5 17.1 %collective-permute-start.13 = (bf16[2,1,16,32,128]{4,3,2,1,0:T(8,128)(2,1)S(1)}, bf16[2,1,16,32,128]{4,3,2,1,0:T(8,128)(2,1)S(1)}, u32[]{:S(2)}, u32[]{:S(2)}) collective-permute-start(bf16[2,1,16,32,128]{4,3,2,1,0:T(8,128)(2,1)S(1)} %pad_maximum_fusion.3.refs_0_), channel_id=1, source_target_pairs={{7,5},{6,4},{5,3},{4,2},{3,1},{2,0},{15,13},{14,12},{13,11},{12,10... | collective-permute-start | bytes 786440 | tf_op jit(solution)/shard_map/ppermute | solution.py:502
  93.8 15.8 %collective-permute-start.12 = (bf16[2,1,16,32,128]{4,3,2,1,0:T(8,128)(2,1)S(1)}, bf16[2,1,16,32,128]{4,3,2,1,0:T(8,128)(2,1)}, u32[]{:S(2)}, u32[]{:S(2)}) collective-permute-start(bf16[2,1,16,32,128]{4,3,2,1,0:T(8,128)(2,1)S(1)} %pad_maximum_fusion.3.refs_0_), channel_id=1, source_target_pairs={{0,2},{1,3},{2,4},{3,5},{4,6},{5,7},{8,10},{9,11},{10,12},{11,13},... | collective-permute-start | bytes 786440 | tf_op jit(solution)/shard_map/ppermute | solution.py:501
  109.6 22.1 %collective-permute-start.14 = (bf16[2,1,16,32,128]{4,3,2,1,0:T(8,128)(2,1)}, bf16[2,1,16,32,128]{4,3,2,1,0:T(8,128)(2,1)}, u32[]{:S(2)}, u32[]{:S(2)}) collective-permute-start(bf16[2,1,16,32,128]{4,3,2,1,0:T(8,128)(2,1)} %collective-permute-done.12.refs_1_), channel_id=1, source_target_pairs={{2,4},{3,5},{4,6},{5,7},{10,12},{11,13},{12,14},{13,15},{18,20},{1... | collective-permute-start | bytes 786440 | tf_op jit(solution)/shard_map/ppermute | solution.py:501
  110.9 20.8 %collective-permute-start.15 = (bf16[2,1,16,32,128]{4,3,2,1,0:T(8,128)(2,1)S(1)}, bf16[2,1,16,32,128]{4,3,2,1,0:T(8,128)(2,1)}, u32[]{:S(2)}, u32[]{:S(2)}) collective-permute-start(bf16[2,1,16,32,128]{4,3,2,1,0:T(8,128)(2,1)S(1)} %collective-permute-done.13.refs_4_), channel_id=1, source_target_pairs={{5,3},{4,2},{3,1},{2,0},{13,11},{12,10},{11,9},{10,8},{21,19},{20,... | collective-permute-start | bytes 786440 | tf_op jit(solution)/shard_map/ppermute | solution.py:502
  133.0 29.3 %collective-permute-start.17 = (bf16[2,1,16,32,128]{4,3,2,1,0:T(8,128)(2,1)}, bf16[2,1,16,32,128]{4,3,2,1,0:T(8,128)(2,1)}, u32[]{:S(2)}, u32[]{:S(2)}) collective-permute-start(bf16[2,1,16,32,128]{4,3,2,1,0:T(8,128)(2,1)} %collective-permute-done.14.refs_2_), channel_id=1, source_target_pairs={{4,6},{5,7},{12,14},{13,15},{20,22},{21,23},{28,30},{29,31}} | collective-permute-start | bytes 786440 | tf_op jit(solution)/shard_map/ppermute | solution.py:501
  134.3 28.5 %collective-permute-start.18 = (bf16[2,1,16,32,128]{4,3,2,1,0:T(8,128)(2,1)}, bf16[2,1,16,32,128]{4,3,2,1,0:T(8,128)(2,1)}, u32[]{:S(2)}, u32[]{:S(2)}) collective-permute-start(bf16[2,1,16,32,128]{4,3,2,1,0:T(8,128)(2,1)} %collective-permute-done.15.refs_5_), channel_id=1, source_target_pairs={{3,1},{2,0},{11,9},{10,8},{19,17},{18,16},{27,25},{26,24}} | collective-permute-start | bytes 786440 | tf_op jit(solution)/shard_map/ppermute | solution.py:502
  162.8 136.7 %reduce-scatter.7.cloned.1.call-start = ((), (), s32[]{:S(2)}) async-start(), calls=%async_computation.5 | async-start | bytes 3932160 | tf_op jit(solution)/shard_map/reduce_scatter | solution.py:626
  218.6 133.3 %all-gather.15.cloned.1.call-start = ((), (), s32[]{:S(2)}) async-start(), calls=%async_computation.11 | async-start | bytes 2621440 | tf_op jit(solution)/shard_map/all_gather | solution.py:599
  254.4 157.1 %all-gather.13.cloned.1.call-start = ((), (), s32[]{:S(2)}) async-start(), calls=%async_computation.10 | async-start | bytes 2621440 | tf_op jit(solution)/shard_map/all_gather | solution.py:599
  254.4 20.3 %collective-permute-start.29 = (bf16[2,1,16,32,128]{4,3,2,1,0:T(8,128)(2,1)S(1)}, bf16[2,1,16,32,128]{4,3,2,1,0:T(8,128)(2,1)S(1)}, u32[]{:S(2)}, u32[]{:S(2)}) collective-permute-start(bf16[2,1,16,32,128]{4,3,2,1,0:T(8,128)(2,1)S(1)} %pad_maximum_fusion.2.refs_0_), channel_id=1, source_target_pairs={{7,5},{6,4},{5,3},{4,2},{3,1},{2,0},{15,13},{14,12},{13,11},{12,10... | collective-permute-start | bytes 786440 | tf_op jit(solution)/shard_map/ppermute | solution.py:502
  255.7 20.3 %collective-permute-start.27 = (bf16[2,1,16,32,128]{4,3,2,1,0:T(8,128)(2,1)S(1)}, bf16[2,1,16,32,128]{4,3,2,1,0:T(8,128)(2,1)}, u32[]{:S(2)}, u32[]{:S(2)}) collective-permute-start(bf16[2,1,16,32,128]{4,3,2,1,0:T(8,128)(2,1)S(1)} %pad_maximum_fusion.2.refs_0_), channel_id=1, source_target_pairs={{0,2},{1,3},{2,4},{3,5},{4,6},{5,7},{8,10},{9,11},{10,12},{11,13},... | collective-permute-start | bytes 786440 | tf_op jit(solution)/shard_map/ppermute | solution.py:501
  274.8 24.7 %collective-permute-start.30 = (bf16[2,1,16,32,128]{4,3,2,1,0:T(8,128)(2,1)S(1)}, bf16[2,1,16,32,128]{4,3,2,1,0:T(8,128)(2,1)}, u32[]{:S(2)}, u32[]{:S(2)}) collective-permute-start(bf16[2,1,16,32,128]{4,3,2,1,0:T(8,128)(2,1)S(1)} %collective-permute-done.29.refs_4_), channel_id=1, source_target_pairs={{5,3},{4,2},{3,1},{2,0},{13,11},{12,10},{11,9},{10,8},{21,19},{20,... | collective-permute-start | bytes 786440 | tf_op jit(solution)/shard_map/ppermute | solution.py:502
  276.1 23.4 %collective-permute-start.28 = (bf16[2,1,16,32,128]{4,3,2,1,0:T(8,128)(2,1)}, bf16[2,1,16,32,128]{4,3,2,1,0:T(8,128)(2,1)}, u32[]{:S(2)}, u32[]{:S(2)}) collective-permute-start(bf16[2,1,16,32,128]{4,3,2,1,0:T(8,128)(2,1)} %collective-permute-done.27.refs_1_), channel_id=1, source_target_pairs={{2,4},{3,5},{4,6},{5,7},{10,12},{11,13},{12,14},{13,15},{18,20},{1... | collective-permute-start | bytes 786440 | tf_op jit(solution)/shard_map/ppermute | solution.py:501
  277.4 22.1 %collective-permute-start.35 = (bf16[3,4,32,128]{3,2,1,0:T(8,128)(2,1)}, bf16[3,4,32,128]{3,2,1,0:T(8,128)(2,1)S(1)}, u32[]{:S(2)}, u32[]{:S(2)}) collective-permute-start(bf16[3,4,32,128]{3,2,1,0:T(8,128)(2,1)} %copy-done.36), channel_id=1, source_target_pairs={{0,8},{8,16},{16,24},{1,9},{9,17},{17,25},{2,10},{10,18},{18,26},{... | collective-permute-start | bytes 294920 | tf_op jit(solution)/shard_map/ppermute | solution.py:459
  283.8 15.7 %collective-permute-start.36 = (bf16[3,4,32,128]{3,2,1,0:T(8,128)(2,1)}, bf16[3,4,32,128]{3,2,1,0:T(8,128)(2,1)}, u32[]{:S(2)}, u32[]{:S(2)}) collective-permute-start(bf16[3,4,32,128]{3,2,1,0:T(8,128)(2,1)} %copy-done.35), channel_id=1, source_target_pairs={{8,0},{16,8},{24,16},{9,1},{17,9},{25,17},{10,2},{18,10},{26,18},{... | collective-permute-start | bytes 294920 | tf_op jit(solution)/shard_map/ppermute | solution.py:459
  326.5 138.8 %reduce-scatter.11.cloned.1.call-start = ((), (), s32[]{:S(2)}) async-start(), calls=%async_computation.7 | async-start | bytes 3932160 | tf_op jit(solution)/shard_map/reduce_scatter | solution.py:626
  326.6 22.5 %collective-permute-start.44 = (bf16[2,1,16,32,128]{4,3,2,1,0:T(8,128)(2,1)S(1)}, bf16[2,1,16,32,128]{4,3,2,1,0:T(8,128)(2,1)S(1)}, u32[]{:S(2)}, u32[]{:S(2)}) collective-permute-start(bf16[2,1,16,32,128]{4,3,2,1,0:T(8,128)(2,1)S(1)} %pad_maximum_fusion.1.refs_0_), channel_id=1, source_target_pairs={{7,5},{6,4},{5,3},{4,2},{3,1},{2,0},{15,13},{14,12},{13,11},{12,10... | collective-permute-start | bytes 786440 | tf_op jit(solution)/shard_map/ppermute | solution.py:502
  327.9 21.2 %collective-permute-start.43 = (bf16[2,1,16,32,128]{4,3,2,1,0:T(8,128)(2,1)S(1)}, bf16[2,1,16,32,128]{4,3,2,1,0:T(8,128)(2,1)S(1)}, u32[]{:S(2)}, u32[]{:S(2)}) collective-permute-start(bf16[2,1,16,32,128]{4,3,2,1,0:T(8,128)(2,1)S(1)} %pad_maximum_fusion.1.refs_0_), channel_id=1, source_target_pairs={{0,2},{1,3},{2,4},{3,5},{4,6},{5,7},{8,10},{9,11},{10,12},{11,13},... | collective-permute-start | bytes 786440 | tf_op jit(solution)/shard_map/ppermute | solution.py:501
  331.9 21.9 %collective-permute-start.47 = (bf16[2,1,16,32,128]{4,3,2,1,0:T(8,128)(2,1)}, bf16[2,1,16,32,128]{4,3,2,1,0:T(8,128)(2,1)S(1)}, u32[]{:S(2)}, u32[]{:S(2)}) collective-permute-start(bf16[2,1,16,32,128]{4,3,2,1,0:T(8,128)(2,1)} %collective-permute-done.28.refs_2_), channel_id=1, source_target_pairs={{4,6},{5,7},{12,14},{13,15},{20,22},{21,23},{28,30},{29,31}} | collective-permute-start | bytes 786440 | tf_op jit(solution)/shard_map/ppermute | solution.py:501
  332.6 23.5 %collective-permute-start.48 = (bf16[2,1,16,32,128]{4,3,2,1,0:T(8,128)(2,1)}, bf16[2,1,16,32,128]{4,3,2,1,0:T(8,128)(2,1)}, u32[]{:S(2)}, u32[]{:S(2)}) collective-permute-start(bf16[2,1,16,32,128]{4,3,2,1,0:T(8,128)(2,1)} %collective-permute-done.30.refs_5_), channel_id=1, source_target_pairs={{3,1},{2,0},{11,9},{10,8},{19,17},{18,16},{27,25},{26,24}} | collective-permute-start | bytes 786440 | tf_op jit(solution)/shard_map/ppermute | solution.py:502
  351.9 23.9 %collective-permute-start.45 = (bf16[2,1,16,32,128]{4,3,2,1,0:T(8,128)(2,1)S(1)}, bf16[2,1,16,32,128]{4,3,2,1,0:T(8,128)(2,1)S(1)}, u32[]{:S(2)}, u32[]{:S(2)}) collective-permute-start(bf16[2,1,16,32,128]{4,3,2,1,0:T(8,128)(2,1)S(1)} %collective-permute-done.43.refs_1_), channel_id=1, source_target_pairs={{2,4},{3,5},{4,6},{5,7},{10,12},{11,13},{12,14},{13,15},{18,20},{1... | collective-permute-start | bytes 786440 | tf_op jit(solution)/shard_map/ppermute | solution.py:501
  352.6 23.2 %collective-permute-start.46 = (bf16[2,1,16,32,128]{4,3,2,1,0:T(8,128)(2,1)S(1)}, bf16[2,1,16,32,128]{4,3,2,1,0:T(8,128)(2,1)S(1)}, u32[]{:S(2)}, u32[]{:S(2)}) collective-permute-start(bf16[2,1,16,32,128]{4,3,2,1,0:T(8,128)(2,1)S(1)} %collective-permute-done.44.refs_4_), channel_id=1, source_target_pairs={{5,3},{4,2},{3,1},{2,0},{13,11},{12,10},{11,9},{10,8},{21,19},{20,... | collective-permute-start | bytes 786440 | tf_op jit(solution)/shard_map/ppermute | solution.py:502
  376.4 26.4 %collective-permute-start.49 = (bf16[2,1,16,32,128]{4,3,2,1,0:T(8,128)(2,1)S(1)}, bf16[2,1,16,32,128]{4,3,2,1,0:T(8,128)(2,1)S(1)}, u32[]{:S(2)}, u32[]{:S(2)}) collective-permute-start(bf16[2,1,16,32,128]{4,3,2,1,0:T(8,128)(2,1)S(1)} %collective-permute-done.45.refs_2_), channel_id=1, source_target_pairs={{4,6},{5,7},{12,14},{13,15},{20,22},{21,23},{28,30},{29,31}} | collective-permute-start | bytes 786440 | tf_op jit(solution)/shard_map/ppermute | solution.py:501
  377.1 25.7 %collective-permute-start.50 = (bf16[2,1,16,32,128]{4,3,2,1,0:T(8,128)(2,1)S(1)}, bf16[2,1,16,32,128]{4,3,2,1,0:T(8,128)(2,1)S(1)}, u32[]{:S(2)}, u32[]{:S(2)}) collective-permute-start(bf16[2,1,16,32,128]{4,3,2,1,0:T(8,128)(2,1)S(1)} %collective-permute-done.46.refs_5_), channel_id=1, source_target_pairs={{3,1},{2,0},{11,9},{10,8},{19,17},{18,16},{27,25},{26,24}} | collective-permute-start | bytes 786440 | tf_op jit(solution)/shard_map/ppermute | solution.py:502
  402.8 125.0 %reduce-scatter.9.cloned.1.call-start = ((), (), s32[]{:S(2)}) async-start(), calls=%async_computation.6 | async-start | bytes 3932160 | tf_op jit(solution)/shard_map/reduce_scatter | solution.py:626
  466.5 9.6 %collective-permute-start.59 = (bf16[3,16,32,128]{3,2,1,0:T(8,128)(2,1)S(1)}, bf16[3,16,32,128]{3,2,1,0:T(8,128)(2,1)S(1)}, u32[]{:S(2)}, u32[]{:S(2)}) collective-permute-start(bf16[3,16,32,128]{3,2,1,0:T(8,128)(2,1)S(1)} %get-tuple-element.168), channel_id=1, source_target_pairs={{0,1},{1,0},{2,3},{3,2},{4,5},{5,4},{6,7},{7,6},{8,9},{9,8},{10,11... | collective-permute-start | bytes 1179656 | tf_op jit(solution)/shard_map/ppermute | solution.py:477
  (80 other events, 414.8 us)
Sparse Core Ops, SparseCore 0:
  41.3 67.8 all-gather.10
  110.8 52.7 all-gather.8
  166.5 59.4 reduce-scatter.4
  228.7 70.7 reduce-scatter.6
  300.9 50.9 all-gather.14
  353.3 50.1 all-gather.12
  406.4 58.8 reduce-scatter.10
  467.6 60.2 reduce-scatter.8

commit v9 on v7

--- a/solution.py
+++ b/solution.py
@@ -12,7 +12,6 @@
 DAMPING = 0.8
 HALO = SWEEPS
 LANES = 128
-APART = 3
 SUBLANES = 8
 GROUPS = 2
 CHUNK_ROWS = 4
@@ -109,11 +108,10 @@
     def shape(count, dtype):
         return jax.ShapeDtypeStruct((members, count, steps, cols), dtype)
 
-    specs = [field, half, half, field, rim, rim]
+    specs = [field, field, field, rim, rim]
     shapes = [
         shape(rows, jnp.float32),
-        shape(rows // 2, jnp.bfloat16),
-        shape(rows // 2, jnp.bfloat16),
+        shape(rows, jnp.bfloat16),
         shape(rows, jnp.float32),
         shape(HALO, jnp.bfloat16),
         shape(HALO, jnp.bfloat16),
@@ -127,15 +125,9 @@
     bottom_ref[0, :, times] = rest[rest.shape[0] - HALO :].astype(bottom_ref.dtype)
 
 
-def put_low(core, iter_ref, keep_ref, give_ref):
-    half = keep_ref.shape[1]
-    keep_ref[0] = iter_ref[0, pl.ds(core * half, half)].astype(keep_ref.dtype)
-    give_ref[0] = iter_ref[0, pl.ds((1 - core) * half, half)].astype(give_ref.dtype)
-
-
 def start_kernel(
     core_ref, rhs_ref, up_ref, down_ref, coeff_ref,
-    iter_ref, keep_ref, give_ref, rest_ref, top_ref, bottom_ref,
+    iter_ref, low_ref, rest_ref, top_ref, bottom_ref,
 ):
     def body(times):
         here = jnp.swapaxes(rhs_ref[times], 0, 1)
@@ -145,7 +137,7 @@
         put_rest(here - prior(update, coeff_ref), times, rest_ref, top_ref, bottom_ref)
 
     time_chunks(iter_ref.shape[2], body)
-    put_low(core_ref[0], iter_ref, keep_ref, give_ref)
+    low_ref[...] = iter_ref[...].astype(low_ref.dtype)
 
 
 def start(group, members, core, rhs, up, down, coeff):
@@ -183,7 +175,7 @@
 
 def step_kernel(
     core_ref, up_ref, rest_ref, down_ref, own_ref, other_ref, same_ref, cross_ref, iter_ref, coeff_ref,
-    next_ref, keep_ref, give_ref, later_ref, top_ref, bottom_ref, whole_ref,
+    next_ref, low_ref, later_ref, top_ref, bottom_ref, whole_ref,
 ):
     def body(times):
         residual = residual_of(
@@ -198,7 +190,7 @@
         put_rest(rest_ref[0, :, times] - prior(update, coeff_ref), times, later_ref, top_ref, bottom_ref)
 
     time_chunks(iter_ref.shape[2], body)
-    put_low(core_ref[0], next_ref, keep_ref, give_ref)
+    low_ref[...] = next_ref[...].astype(low_ref.dtype)
 
 
 def step(core, rests, misfits, iterate, coeff):
@@ -281,11 +273,9 @@
     return jnp.concatenate(parts, axis=0)
 
 
-def observe_kernel(core_ref, field_ref, *refs):
-    *slot_refs, own_ref, other_ref, table_ref, around_ref, cell_ref = refs[:-4]
-    out_ref, spec, acc, picked = refs[-4:]
-    chips, _, whole, rows, steps, lanes = field_ref.shape
-    members = spec.shape[0] // 2
+def observe_kernel(core_ref, *refs):
+    *field_refs, own_ref, other_ref, table_ref, cell_ref, out_ref, spec, acc, picked = refs
+    parts, members, rows, steps, lanes = field_refs[0].shape
     freqs, sensors, width = own_ref.shape[1:]
     near = lanes // sensors
     wide = 2 * lanes
@@ -299,16 +289,18 @@
     marks = marks_of(cell_ref, width)
 
     def history(b, r):
-        if b < whole:
-            return field_ref[:, :, b, r].reshape(2 * chips * steps, lanes)
-        slots = [slot_refs[0][:, b - whole, r]]
+        if len(field_refs) == 1:
+            return field_refs[0][:, b, r].reshape(parts * steps, lanes)
+        chips = (len(field_refs) + 1) // 2
+        slots = [field_refs[0][:, b, r]]
         for k in range(1, chips):
-            slots.append(slot_refs[k][:, b - whole, r] + slot_refs[2 * chips - 1 - k][:, b - whole, r])
-        return jnp.concatenate([slot.reshape(2 * steps, lanes) for slot in slots], axis=0)
+            slots.append(field_refs[k][:, b, r] + field_refs[2 * chips - 1 - k][:, b, r])
+        return jnp.concatenate([slot.reshape(parts * steps, lanes) for slot in slots], axis=0)
 
     for b in range(members):
-        table = table_ref[...] if b < whole else around_ref[...]
-        spectrum = dot(table, jnp.concatenate([history(b, r) for r in range(rows)], axis=1))
+        spectrum = dot(
+            table_ref[...], jnp.concatenate([history(b, r) for r in range(rows)], axis=1)
+        )
         spec[2 * b] = spectrum[:freqs]
         spec[2 * b + 1] = spectrum[freqs:]
     for m in range(2 * members):
@@ -348,24 +340,25 @@
     )
 
 
-def observe(core, field, slots, own, other, table, around, local_cells):
-    chips, _, whole, rows, steps, lanes = field.shape
-    apart = slots[0].shape[1]
-    members = whole + apart
+def observe(core, fields, own, other, table, local_cells):
+    parts, members, rows, steps, lanes = fields[0].shape
     _, freqs, sensors, cells = own.shape
     width = CHUNK_ROWS * lanes
     near = lanes // sensors
+    chunks = cells // (2 * width)
+    first = chunks if len(fields) == 1 else 0
     shape = (2, 2, members, freqs // near, lanes)
-    block = (chips, 2, whole, CHUNK_ROWS, steps, lanes)
-    slot = pl.BlockSpec((2, apart, CHUNK_ROWS, steps, lanes), lambda c, core: (0, 0, c, 0, 0))
+    block = pl.BlockSpec(
+        (parts, members, CHUNK_ROWS, steps, lanes),
+        lambda c, core: (0, 0, core[0] * first + c, 0, 0),
+    )
     return call(
         observe_kernel,
         core,
-        (rows // CHUNK_ROWS,),
-        [pl.BlockSpec(block, lambda c, core: (0, 0, 0, c, 0, 0))]
-        + [slot] * len(slots)
+        (chunks,),
+        [block] * len(fields)
         + map_specs(own, width)
-        + [whole_block(table), whole_block(around), whole_block(local_cells)],
+        + [whole_block(table), whole_block(local_cells)],
         pl.BlockSpec(shape, lambda c, core: (0, 0, 0, 0, 0)),
         jax.ShapeDtypeStruct(shape, jnp.float32),
         [
@@ -373,9 +366,9 @@
             pltpu.VMEM((freqs // near, 2 * members * near, 4 * lanes), jnp.float32),
             pltpu.VMEM((2 * members, freqs, 2 * lanes), jnp.float32),
         ],
-        cost_estimate=map_cost(members, own, field.size),
+        cost_estimate=map_cost(members, own, len(fields) * fields[0].size),
         name="observe",
-    )(core, field, *slots, own, other, table, around, local_cells)
+    )(core, *fields, own, other, table, local_cells)
 
 
 def pull_kernel(core_ref, *refs):
@@ -516,6 +509,46 @@
         return [self.value, *self.ups, *self.downs]
 
 
+class Scatter:
+    def __init__(self, parts):
+        self.size, self.parts = lax.axis_size("sensors"), parts
+        self.chip = lax.axis_index("sensors") // 2
+        self.hops, self.ends = 0, (None, None)
+
+    def part(self, place, received):
+        place = jnp.clip(place, 0, self.parts.shape[0] - 1)
+        value = lax.dynamic_index_in_dim(self.parts, place, keepdims=False)
+        if received is None:
+            return value
+        total = value.astype(jnp.float32) + received.astype(jnp.float32)
+        return total.astype(value.dtype)
+
+    def hop(self, last=False):
+        chips = self.parts.shape[0]
+        while self.hops < chips - 1:
+            self.hops += 1
+            far = chips - self.hops
+            onward = [(k, k + 2) for k in range(2 * self.hops)]
+            backward = [(self.size - 1 - k, self.size - 1 - there) for k, there in onward]
+            up = self.part(self.chip + far, self.ends[0])
+            down = self.part(self.chip - far, self.ends[1])
+            self.ends = (
+                lax.ppermute(up, "sensors", onward),
+                lax.ppermute(down, "sensors", backward),
+            )
+            if not last:
+                break
+
+    def after(self, other):
+        self.ends, other = lax.optimization_barrier((self.ends, other))
+        return other
+
+    def total(self):
+        up, down = (end.astype(jnp.float32) for end in self.ends)
+        own = lax.dynamic_index_in_dim(self.parts, self.chip, keepdims=False)
+        return (own.astype(jnp.float32) + (up + down)).astype(own.dtype)
+
+
 def shards(rhs, forward_map, stiffness, reaction, noise_weight, sensor_cell):
     steps, samples, rows, cols = rhs.shape
     _, freqs, sensors, cells = forward_map.shape
@@ -531,8 +564,8 @@
     offsets = cores[None, :, None] * steps + jnp.arange(steps, dtype=jnp.int32)
     chip_steps = 2 * steps
     places = jnp.arange(chips, dtype=jnp.int32)[:, None, None] * chip_steps
-    table = transform_table(freqs, places + offsets)
-    back = table.T
+    back = transform_table(freqs, places + offsets).T
+    table = transform_table(freqs, jnp.arange(2 * freqs, dtype=jnp.int32))
     chip = sensor_index // 2
     places = (chip - jnp.arange(chips, dtype=jnp.int32)) % chips
     around = transform_table(freqs, places[:, None, None] * chip_steps + offsets)
@@ -559,18 +592,33 @@
     core = core.reshape(1)
 
     members = samples // GROUPS
-    whole = members - members // APART
     edge_rows = lax.optimization_barrier((rhs[:, :, :HALO], rhs[:, :, rows - HALO :]))
     top, bottom = (jnp.transpose(rim, (1, 2, 0, 3)).astype(jnp.bfloat16) for rim in edge_rows)
     lines = [[k for k in range(size) if k % 2 == parity] for parity in range(2)]
     shape = (chips, 2, members, rows // 2, steps, cols)
 
     def ready(state):
-        iterate, keep, give, rest, top, bottom = state
+        iterate, low, rest, top, bottom = state
         above, below = rims(top, bottom)
-        pair = jnp.stack([keep, swap_cores(give)])
-        parts = lax.optimization_barrier((pair[:, :whole], pair[:, whole:]))
-        return iterate, *parts, (above, rest, below)
+        return iterate, low, (above, rest, below)
+
+    def begin(group, ends):
+        return ready(start(group, members, core, rhs, *rims(*ends), coeff))
+
+    def gather(low):
+        return [lax.all_gather(low, "sensors")]
+
+    def both_cores(low):
+        keep, give = (
+            lax.dynamic_slice_in_dim(low, first * (rows // 2), rows // 2, axis=1)
+            for first in (core[0], 1 - core[0])
+        )
+        return jnp.stack([keep, swap_cores(give)])
+
+    def scatter(misfit):
+        return lax.psum_scatter(
+            misfit, "sensors", scatter_dimension=0, axis_index_groups=lines, tiled=False
+        )
 
     def edges(misfit):
         first = (rows // 2 - HALO) * core[0]
@@ -579,69 +627,69 @@
         _, cross = misfit_rims(edge[1])
         return misfit[0], swap_cores(misfit[1]), same, cross
 
-    def begin(group, ends):
-        return ready(start(group, members, core, rhs, *rims(*ends), coeff))
-
     groups = [slice(group * members, (group + 1) * members) for group in range(GROUPS)]
     states = [begin(0, (top[groups[0]], bottom[groups[0]]))]
-    iterate, pair, apart, rests = states[0]
-    pair, apart, whole_map = lax.optimization_barrier((pair, apart, forward_map))
+    iterate, low, rests = states[0]
+    low, whole_map = lax.optimization_barrier((low, forward_map))
     other_map = swap_cores(whole_map)
-    line = Line(apart)
-    line.hop()
     for group in range(1, GROUPS):
         ends = (top[groups[group]], bottom[groups[group]])
-        rests, ends = line.after((rests, ends))
+        _, rests, ends = lax.optimization_barrier((low, rests, ends))
         states.append(begin(group, ends))
-    states[0] = iterate, pair, apart, rests
+    states[0] = iterate, low, rests
+    fields = [gather(state[1]) for state in states]
+
+    def hessian(fields, table):
+        sums = observe(core, fields, forward_map, other_map, table, local_cells)
+        sums = from_all_cells(sums + swap_cores(sums)[::-1])
+        return pull_back(core, sums, noise, forward_map, other_map, back, local_cells, shape)
 
     outputs = ()
     for iteration in range(ITERS):
-        fields = [lax.all_gather(state[1], "sensors", axis_index_groups=lines) for state in states]
-        line.hop(last=True)
-        totals = []
+        misfits = []
         for group in range(GROUPS):
-            slots, line = line.slots(), None
-            if group + 1 < GROUPS:
-                line = Line(states[group + 1][2])
-                line.hop()
-            sums = observe(
-                core, fields[group], slots, forward_map, other_map, table, around, local_cells
-            )
-            if line is not None:
-                iterate, pair, apart, rests = states[group + 1]
-                sums, rests = lax.optimization_barrier((sums, rests))
-                line.after(sums)
-                states[group + 1] = iterate, pair, apart, rests
-                line.hop()
-            sums = from_all_cells(sums + swap_cores(sums)[::-1])
-            misfit = pull_back(core, sums, noise, forward_map, other_map, back, local_cells, shape)
-            if line is not None:
-                line.after(misfit)
-                line.hop(last=True)
-            totals.append(
-                lax.psum_scatter(
-                    misfit, "sensors", scatter_dimension=0, axis_index_groups=lines, tiled=False
-                )
-            )
-        for group in range(GROUPS):
-            iterate, _, _, rests = states[group]
-            total = totals[group]
-            if iteration < ITERS - 1:
-                if group == 1:
-                    before = states[0]
-                    line = Line(before[2])
-                    line.hop()
-                    line.hop()
-                    total, earlier = line.after((total, before[3]))
-                    states[0] = (*before[:3], earlier)
-                states[group] = ready(step(core, rests, edges(total), iterate, coeff))
-            else:
+            iterate, low, rests = states[group]
+            field = fields[group]
+            if group > 0:
+                field, rests = lax.optimization_barrier((field, rests))
+            states[group] = iterate, low, rests
+            misfits.append(hessian(field, table if len(field) == 1 else around))
+        if iteration == ITERS - 1:
+            for group in range(GROUPS):
+                iterate, _, rests = states[group]
+                total = scatter(misfits[group])
                 if outputs:
                     total, outputs = lax.optimization_barrier((total, outputs))
                 outputs = finish(
                     group, samples, core, rests, edges(total), iterate, coeff, outputs
                 )
+            break
+        line, back_line = None, Scatter(misfits[-1])
+        for group in range(GROUPS):
+            iterate, _, rests = states[group]
+            if group < GROUPS - 1:
+                parts = edges(scatter(misfits[group]))
+                if group == 0:
+                    back_line.hop()
+                    parts = back_line.after(parts)
+                    back_line.hop()
+            else:
+                back_line.hop(last=True)
+                ends = back_line.after(line.ends)
+                line.ends = ends
+                line.ups[-1], line.downs[-1] = ends
+                total = back_line.total()
+                line.hop()
+                before = states[0]
+                parts, earlier = line.after((edges(total), before[2]))
+                states[0] = (*before[:2], earlier)
+                line.hop(last=True)
+            states[group] = ready(step(core, rests, parts, iterate, coeff))
+            if group == 0:
+                pair = back_line.after(both_cores(states[0][1]))
+                line = Line(pair)
+                line.hop()
+        fields = [line.slots()] + [gather(state[1]) for state in states[1:]]
     return tuple(out.reshape(rhs.shape) for out in outputs)
 
 

time: 671 us -> 616 us (0.918)
  starting transfers between devices: 152 us -> 109 us
  waiting for transfers between devices: 268 us -> 261 us
    ppermute x12 -> x3, waiting for transfers between devices: 154 us -> 61.1 us  [hop(): down = lax.ppermute(self.ends[1], 'sensors', backward)]
    all_gather x4 -> x3, waiting for transfers between devices: 1.63 us -> 44.2 us  [gather(): return [lax.all_gather(low, 'sensors')]]
    ppermute x13 -> x10, starting transfers between devices: 30.7 us -> 6.05 us  [swap_cores(): return lax.ppermute(value, 'sensors', [(k, k ^ 1) for k in range(size)])]
    reduce_scatter x4 -> x3, waiting for transfers between devices: 43.2 us -> 63.3 us  [scatter(): lax.psum_scatter(misfit, 'sensors', scatter_dimension=0, axis_index_group...]
    ppermute x12 -> x3, starting transfers between devices: 25.5 us -> 6.3 us  [hop(): up = lax.ppermute(self.ends[0], 'sensors', onward)]
    ppermute x0 -> x6, starting transfers between devices: none -> 17.2 us  [the longest x3 12.8 us: hop(): lax.ppermute(up, 'sensors', onward)]
    ppermute x0 -> x6, waiting for transfers between devices: none -> 15.1 us  [the longest x3 10.1 us: hop(): lax.ppermute(up, 'sensors', onward)]
    ppermute x13 -> x10, waiting for transfers between devices: 19.7 us -> 5.98 us  [swap_cores(): return lax.ppermute(value, 'sensors', [(k, k ^ 1) for k in range(size)])]
  transfers between devices with their start and end apart: 79 -> 62, of which waited for: 47 -> 40; matrix products, arithmetic and copies ran while one was open for 3% -> 2% of each run, Pallas kernels for 23% -> 24%
where the time goes in v9:
time: 616 us; the launch traced here: 614 us
  waiting for transfers between devices  261 us (42%)
  Pallas kernels  167 us (27%)
  starting transfers between devices  109 us (18%)
  local copies, waits for them, and re-layouts  48.4 us (8%)
  between operations  15 us (2%)
  other arithmetic  13.7 us (2%)
    pallas_call x4, Pallas kernels, observe(): call(observe_kernel, core, (chunks,), [block] * len(fields) + map_specs(o...  70.2 us
    reduce_scatter x3, waiting for transfers between devices, scatter(): lax.psum_scatter(misfit, 'sensors', scatter_dimension=0, axis_index_group...  63.3 us
    ppermute x3, waiting for transfers between devices, hop(): down = lax.ppermute(self.ends[1], 'sensors', backward)  61.1 us
    pallas_call x4, Pallas kernels, pull_back(): call(pull_kernel, core, (rows // CHUNK_ROWS,), [whole_block(array) for ar...  58.7 us
    all_gather x3, waiting for transfers between devices, gather(): return [lax.all_gather(low, 'sensors')]  44.2 us
    unnamed x68, local copies, waits for them, and re-layouts  37.5 us
    ppermute x7, starting transfers between devices, rims(): lax.ppermute(bottom, 'cells', onward)  27.3 us
    ppermute x8, starting transfers between devices, misfit_rims(): return (lax.ppermute(edge, both, same), lax.ppermute(edge, both, cross))  25.3 us
  transfers between devices with their start and end apart: 62, of which 40 were waited for; matrix products, arithmetic and copies ran while one was open for 2% of the time, Pallas kernels for 24%

profile of v9, /device:TPU:1, one launch (start us, length us, event | category | flops | bytes accessed | tf_op | source)
XLA Modules:
  0.0 614.4 jit_solution(4534171703617207911)
XLA Ops:
  21.2 5.6 collective-permute-done.1.down_ref
  28.7 6.9 %start.2 = (f32[3,32,32,128]{3,2,1,0:T(8,128)S(1)}, bf16[3,32,32,128]{3,2,1,0:T(8,128)(2,1)}, f32[3,32,32,128]{3,2,1,0:T(8,128)S(1)}, bf16[3,4,32,128]{3,2,1,0:T(8,128)(2,1)S(1)}, bf16[3,4,32,128]{3,2,1,0:T(8,128)(2,1)S(1)}) custom-call(s32[1]{0:T(128)} %bitcast.core_ref, f32[32,192,128]{2,1,0:T(8,128)S(1)} %bitcast.76, ...), custom_call_target="tpu_custom_call" | custom-call | tf_op jit(solution)/shard_map/start/pallas_call | solution.py:147
  39.3 4.4 collective-permute-start.4
  60.7 6.9 %start.3 = (f32[3,32,32,128]{3,2,1,0:T(8,128)S(1)}, bf16[3,32,32,128]{3,2,1,0:T(8,128)(2,1)}, f32[3,32,32,128]{3,2,1,0:T(8,128)S(1)}, bf16[3,4,32,128]{3,2,1,0:T(8,128)(2,1)S(1)}, bf16[3,4,32,128]{3,2,1,0:T(8,128)(2,1)S(1)}) custom-call(s32[1]{0:T(128)} %bitcast.core_ref, f32[32,192,128]{2,1,0:T(8,128)S(1)} %bitcast.77, ...), custom_call_target="tpu_custom_call" | custom-call | tf_op jit(solution)/shard_map/start/pallas_call | solution.py:147
  72.1 33.6 %all-gather.9.cloned.1.call-done = bf16[24,32,32,128]{3,2,1,0:T(8,128)(2,1)} async-done(((bf16[3,32,32,128]{3,2,1,0:T(8,128)(2,1)}), bf16[24,32,32,128]{3,2,1,0:T(8,128)(2,1)}) %all-gather.9.cloned.1.call-update) | async-done | bytes 6291472 | tf_op jit(solution)/shard_map/all_gather | solution.py:609
  108.5 17.3 %observe.5 = f32[2,2,3,16,128]{4,3,2,1,0:T(8,128)S(1)} custom-call(s32[1]{0:T(128)} %bitcast.core_ref, bf16[8,3,32,32,128]{4,3,2,1,0:T(8,128)(2,1)S(1)} %bitcast.79, bf16[2,128,16,4096]{3,2,1,0:T(8,128)(2,1)} %refs_5_.7, bf16[2,128,16,4096]{3,2,1,0:T(8,128)(2,1)} %collective-permute-done.10.refs_2_.refs_6_.refs_8_, bf16[256,256]{1,0:T(8,128)(2,1)S(1)} %copy.18.refs_3_, ...), custom_call_target="tpu_custom_call" | custom-call | flops 402653184 | bytes 39845888 | tf_op jit(solution)/shard_map/observe/pallas_call | solution.py:355
  134.5 14.8 %pull_back.5 = bf16[4,2,3,16,32,128]{5,4,3,2,1,0:T(8,128)(2,1)S(1)} custom-call(s32[1]{0:T(128)} %bitcast.core_ref, f32[2,2,3,16,128]{4,3,2,1,0:T(8,128)S(1)} %reverse_add_fusion.2.refs_0_, f32[2,2,3,16,128]{4,3,2,1,0:T(8,128)S(1)} %collective-permute-done.18.refs_1_, f32[2,2,3,16,128]{4,3,2,1,0:T(8,128)S(1)} %collective-permute-done.19.refs_2_, ...), custom_call_target="tpu_custom_call" | custom-call | flops 402653184 | bytes 36700160 | tf_op jit(solution)/shard_map/pull_back/pallas_call | solution.py:428
  156.0 4.7 collective-permute-done.9.down_ref
  160.7 10.6 %all-gather.7.cloned.1.call-done = bf16[24,32,32,128]{3,2,1,0:T(8,128)(2,1)} async-done(((bf16[3,32,32,128]{3,2,1,0:T(8,128)(2,1)}), bf16[24,32,32,128]{3,2,1,0:T(8,128)(2,1)}) %all-gather.7.cloned.1.call-update) | async-done | bytes 6291472 | tf_op jit(solution)/shard_map/all_gather | solution.py:609
  174.1 17.3 %observe.4 = f32[2,2,3,16,128]{4,3,2,1,0:T(8,128)S(1)} custom-call(s32[1]{0:T(128)} %bitcast.core_ref, bf16[8,3,32,32,128]{4,3,2,1,0:T(8,128)(2,1)S(1)} %bitcast.78, bf16[2,128,16,4096]{3,2,1,0:T(8,128)(2,1)} %refs_5_.7, bf16[2,128,16,4096]{3,2,1,0:T(8,128)(2,1)} %collective-permute-done.10.refs_2_.refs_6_.refs_8_, bf16[256,256]{1,0:T(8,128)(2,1)S(1)} %copy.18.refs_3_, ...), custom_call_target="tpu_custom_call" | custom-call | flops 402653184 | bytes 39845888 | tf_op jit(solution)/shard_map/observe/pallas_call | solution.py:355
  200.0 14.7 %pull_back.4 = bf16[4,2,3,16,32,128]{5,4,3,2,1,0:T(8,128)(2,1)S(1)} custom-call(s32[1]{0:T(128)} %bitcast.core_ref, f32[2,2,3,16,128]{4,3,2,1,0:T(8,128)S(1)} %reverse_add_fusion.3.refs_0_, f32[2,2,3,16,128]{4,3,2,1,0:T(8,128)S(1)} %collective-permute-done.12.refs_1_, f32[2,2,3,16,128]{4,3,2,1,0:T(8,128)S(1)} %collective-permute-done.13.refs_2_, ...), custom_call_target="tpu_custom_call" | custom-call | flops 402653184 | bytes 36700160 | tf_op jit(solution)/shard_map/pull_back/pallas_call | solution.py:428
  220.6 19.9 %reduce-scatter.4.cloned.1.call-done = bf16[1,2,3,16,32,128]{5,4,3,2,1,0:T(8,128)(2,1)} async-done(((bf16[4,2,3,16,32,128]{5,4,3,2,1,0:T(8,128)(2,1)}), bf16[1,2,3,16,32,128]{5,4,3,2,1,0:T(8,128)(2,1)}) %reduce-scatter.4.cloned.1.call-update) | async-done | bytes 786448 | tf_op jit(solution)/shard_map/reduce_scatter | solution.py:619
  249.1 4.6 collective-permute-done.23.cross_ref
  263.7 6.3 %step.2 = (f32[3,32,32,128]{3,2,1,0:T(8,128)S(1)}, bf16[3,32,32,128]{3,2,1,0:T(8,128)(2,1)S(1)}, f32[3,32,32,128]{3,2,1,0:T(8,128)S(1)}, bf16[3,4,32,128]{3,2,1,0:T(8,128)(2,1)S(1)}, bf16[3,4,32,128]{3,2,1,0:T(8,128)(2,1)S(1)}) custom-call(s32[1]{0:T(128)} %bitcast.core_ref, bf16[3,4,32,128]{3,2,1,0:T(8,128)(2,1)S(1)} %collective-permute-done.4.up_ref, ...), custom_call_target="tpu_custom_call" | custom-call | tf_op jit(solution)/shard_map/step/pallas_call | solution.py:199
  279.5 8.4 %collective-permute-start.27 = (bf16[2,3,16,32,128]{4,3,2,1,0:T(8,128)(2,1)}, bf16[2,3,16,32,128]{4,3,2,1,0:T(8,128)(2,1)}, u32[]{:S(2)}, u32[]{:S(2)}) collective-permute-start(bf16[2,3,16,32,128]{4,3,2,1,0:T(8,128)(2,1)} %get-tuple-element.137), channel_id=1, source_target_pairs={{0,2},{1,3},{2,4},{3,5},{4,6},{5,7},{8,10},{9,11},{10,12},{11,13},... | collective-permute-start | bytes 2359304 | tf_op jit(solution)/shard_map/ppermute | solution.py:536
  294.6 10.1 %collective-permute-done.27 = bf16[2,3,16,32,128]{4,3,2,1,0:T(8,128)(2,1)} collective-permute-done((bf16[2,3,16,32,128]{4,3,2,1,0:T(8,128)(2,1)}, bf16[2,3,16,32,128]{4,3,2,1,0:T(8,128)(2,1)}, u32[]{:S(2)}, u32[]{:S(2)}) %collective-permute-start.27) | collective-permute-done | bytes 786464 | tf_op jit(solution)/shard_map/ppermute | solution.py:536
  304.7 5.0 collective-permute-done.28
  309.7 10.8 %collective-permute-done.29.refs_1_ = bf16[2,3,16,32,128]{4,3,2,1,0:T(8,128)(2,1)S(1)} collective-permute-done((bf16[2,3,16,32,128]{4,3,2,1,0:T(8,128)(2,1)S(1)}, bf16[2,3,16,32,128]{4,3,2,1,0:T(8,128)(2,1)S(1)}, u32[]{:S(2)}, u32[]{:S(2)}) %collective-permute-start.29) | collective-permute-done | bytes 786464 | tf_op jit(solution)/shard_map/ppermute | solution.py:494
  320.4 5.1 collective-permute-done.30.refs_4_
  329.8 6.3 %collective-permute-start.36 = (bf16[3,4,32,128]{3,2,1,0:T(8,128)(2,1)S(1)}, bf16[3,4,32,128]{3,2,1,0:T(8,128)(2,1)S(1)}, u32[]{:S(2)}, u32[]{:S(2)}) collective-permute-start(bf16[3,4,32,128]{3,2,1,0:T(8,128)(2,1)S(1)} %get-tuple-element.104), channel_id=1, source_target_pairs={{0,8},{8,16},{16,24},{1,9},{9,17},{17,25},{2,10},{10,18},{18,26},{... | collective-permute-start | bytes 294920 | tf_op jit(solution)/shard_map/ppermute | solution.py:452
  342.3 4.5 collective-permute-start.35
  350.8 6.3 %step.3 = (f32[3,32,32,128]{3,2,1,0:T(8,128)S(1)}, bf16[3,32,32,128]{3,2,1,0:T(8,128)(2,1)S(1)}, f32[3,32,32,128]{3,2,1,0:T(8,128)S(1)}, bf16[3,4,32,128]{3,2,1,0:T(8,128)(2,1)S(1)}, bf16[3,4,32,128]{3,2,1,0:T(8,128)(2,1)S(1)}) custom-call(s32[1]{0:T(128)} %bitcast.core_ref, bf16[3,4,32,128]{3,2,1,0:T(8,128)(2,1)S(1)} %collective-permute-done.8.up_ref, ...), custom_call_target="tpu_custom_call" | custom-call | tf_op jit(solution)/shard_map/step/pallas_call | solution.py:199
  364.3 56.0 %collective-permute-done.45.refs_6_ = bf16[2,3,16,32,128]{4,3,2,1,0:T(8,128)(2,1)} collective-permute-done((bf16[2,3,16,32,128]{4,3,2,1,0:T(8,128)(2,1)}, bf16[2,3,16,32,128]{4,3,2,1,0:T(8,128)(2,1)}, u32[]{:S(2)}, u32[]{:S(2)}) %collective-permute-start.45) | collective-permute-done | bytes 786464 | tf_op jit(solution)/shard_map/ppermute | solution.py:495
  422.6 18.2 %observe.7 = f32[2,2,3,16,128]{4,3,2,1,0:T(8,128)S(1)} custom-call(s32[1]{0:T(128)} %bitcast.core_ref, bf16[2,3,16,32,128]{4,3,2,1,0:T(8,128)(2,1)S(1)} %pad_maximum_fusion.refs_0_, bf16[2,3,16,32,128]{4,3,2,1,0:T(8,128)(2,1)S(1)} %collective-permute-done.29.refs_1_, bf16[2,3,16,32,128]{4,3,2,1,0:T(8,128)(2,1)S(1)} %copy-done.26, ...), custom_call_target="tpu_custom_call" | custom-call | flops 402653184 | bytes 39059456 | tf_op jit(solution)/shard_map/observe/pallas_call | solution.py:355
  450.8 14.5 %pull_back.7 = bf16[4,2,3,16,32,128]{5,4,3,2,1,0:T(8,128)(2,1)S(1)} custom-call(s32[1]{0:T(128)} %bitcast.core_ref, f32[2,2,3,16,128]{4,3,2,1,0:T(8,128)S(1)} %reverse_add_fusion.refs_0_, f32[2,2,3,16,128]{4,3,2,1,0:T(8,128)S(1)} %collective-permute-done.47.refs_1_, f32[2,2,3,16,128]{4,3,2,1,0:T(8,128)S(1)} %collective-permute-done.48.refs_2_, ...), custom_call_target="tpu_custom_call" | custom-call | flops 402653184 | bytes 36700160 | tf_op jit(solution)/shard_map/pull_back/pallas_call | solution.py:428
  471.0 5.2 collective-permute-done.39.down_ref
  479.0 17.3 %observe.6 = f32[2,2,3,16,128]{4,3,2,1,0:T(8,128)S(1)} custom-call(s32[1]{0:T(128)} %bitcast.core_ref, bf16[8,3,32,32,128]{4,3,2,1,0:T(8,128)(2,1)S(1)} %bitcast.80, bf16[2,128,16,4096]{3,2,1,0:T(8,128)(2,1)} %refs_5_.7, bf16[2,128,16,4096]{3,2,1,0:T(8,128)(2,1)} %collective-permute-done.10.refs_2_.refs_6_.refs_8_, bf16[256,256]{1,0:T(8,128)(2,1)S(1)} %copy.18.refs_3_, ...), custom_call_target="tpu_custom_call" | custom-call | flops 402653184 | bytes 39845888 | tf_op jit(solution)/shard_map/observe/pallas_call | solution.py:355
  507.3 14.6 %pull_back.6 = bf16[4,2,3,16,32,128]{5,4,3,2,1,0:T(8,128)(2,1)S(1)} custom-call(s32[1]{0:T(128)} %bitcast.core_ref, f32[2,2,3,16,128]{4,3,2,1,0:T(8,128)S(1)} %reverse_add_fusion.1.refs_0_, f32[2,2,3,16,128]{4,3,2,1,0:T(8,128)S(1)} %collective-permute-done.41.refs_1_, f32[2,2,3,16,128]{4,3,2,1,0:T(8,128)S(1)} %collective-permute-done.42.refs_2_, ...), custom_call_target="tpu_custom_call" | custom-call | flops 402653184 | bytes 36700160 | tf_op jit(solution)/shard_map/pull_back/pallas_call | solution.py:428
  533.5 4.6 collective-permute-done.52.cross_ref
  539.5 6.0 finish.2
  545.5 42.0 %reduce-scatter.6.cloned.1.call-done = bf16[1,2,3,16,32,128]{5,4,3,2,1,0:T(8,128)(2,1)} async-done(((bf16[4,2,3,16,32,128]{5,4,3,2,1,0:T(8,128)(2,1)}), bf16[1,2,3,16,32,128]{5,4,3,2,1,0:T(8,128)(2,1)}) %reduce-scatter.6.cloned.1.call-update) | async-done | bytes 786448 | tf_op jit(solution)/shard_map/reduce_scatter | solution.py:619
  601.6 6.0 finish.3
  (236 shorter events, 190.9 us)
Async XLA Ops:
  7.2 98.5 %all-gather.9.cloned.1.call-start = ((), (), s32[]{:S(2)}) async-start(), calls=%async_computation.7 | async-start | bytes 7077888 | tf_op jit(solution)/shard_map/all_gather | solution.py:609
  8.7 12.2 %collective-permute-start.2 = (f32[2,4,128]{2,1,0:T(4,128)S(1)}, f32[2,4,128]{2,1,0:T(4,128)S(1)}, u32[]{:S(2)}, u32[]{:S(2)}) collective-permute-start(f32[2,4,128]{2,1,0:T(4,128)S(1)} %get-tuple-element.167), channel_id=1, source_target_pairs={{0,8},{8,16},{16,24},{1,9},{9,17},{17,25},{2,10},{10,18},{18,26},{... | collective-permute-start | bytes 12296 | tf_op jit(solution)/shard_map/ppermute | solution.py:452
  12.6 8.3 %collective-permute-start.3 = (f32[2,4,128]{2,1,0:T(4,128)S(1)}, f32[2,4,128]{2,1,0:T(4,128)S(1)}, u32[]{:S(2)}, u32[]{:S(2)}) collective-permute-start(f32[2,4,128]{2,1,0:T(4,128)S(1)} %get-tuple-element.168), channel_id=1, source_target_pairs={{8,0},{16,8},{24,16},{9,1},{17,9},{25,17},{10,2},{18,10},{26,18},{... | collective-permute-start | bytes 12296 | tf_op jit(solution)/shard_map/ppermute | solution.py:452
  19.6 7.2 %collective-permute-start.1 = (bf16[3,4,32,128]{3,2,1,0:T(8,128)(2,1)S(1)}, bf16[3,4,32,128]{3,2,1,0:T(8,128)(2,1)S(1)}, u32[]{:S(2)}, u32[]{:S(2)}) collective-permute-start(bf16[3,4,32,128]{3,2,1,0:T(8,128)(2,1)S(1)} %get-tuple-element.165), channel_id=1, source_target_pairs={{8,0},{16,8},{24,16},{9,1},{17,9},{25,17},{10,2},{18,10},{26,18},{... | collective-permute-start | bytes 294920 | tf_op jit(solution)/shard_map/ppermute | solution.py:452
  37.9 67.8 %collective-permute-start.10 = (bf16[2,128,16,4096]{3,2,1,0:T(8,128)(2,1)}, bf16[2,128,16,4096]{3,2,1,0:T(8,128)(2,1)}, u32[]{:S(2)}, u32[]{:S(2)}) collective-permute-start(bf16[2,128,16,4096]{3,2,1,0:T(8,128)(2,1)} %refs_5_.7), channel_id=1, source_target_pairs={{0,1},{1,0},{2,3},{3,2},{4,5},{5,4},{6,7},{7,6},{8,9},{9,8},{10,11... | collective-permute-start | bytes 100663304 | tf_op jit(solution)/shard_map/ppermute | solution.py:470
  39.3 132.0 %all-gather.7.cloned.1.call-start = ((), (), s32[]{:S(2)}) async-start(), calls=%async_computation.6 | async-start | bytes 7077888 | tf_op jit(solution)/shard_map/all_gather | solution.py:609
  39.3 6.7 %collective-permute-start.4 = (bf16[3,4,32,128]{3,2,1,0:T(8,128)(2,1)S(1)}, bf16[3,4,32,128]{3,2,1,0:T(8,128)(2,1)S(1)}, u32[]{:S(2)}, u32[]{:S(2)}) collective-permute-start(bf16[3,4,32,128]{3,2,1,0:T(8,128)(2,1)S(1)} %get-tuple-element.72), channel_id=1, source_target_pairs={{0,8},{8,16},{16,24},{1,9},{9,17},{17,25},{2,10},{10,18},{18,26},{... | collective-permute-start | bytes 294920 | tf_op jit(solution)/shard_map/ppermute | solution.py:452
  69.8 170.7 %reduce-scatter.4.cloned.1.call-start = ((), (), s32[]{:S(2)}) async-start(), calls=%async_computation.3 | async-start | bytes 3932160 | tf_op jit(solution)/shard_map/reduce_scatter | solution.py:619
  151.1 325.1 %all-gather.11.cloned.1.call-start = ((), (), s32[]{:S(2)}) async-start(), calls=%async_computation.8 | async-start | bytes 7077888 | tf_op jit(solution)/shard_map/all_gather | solution.py:609
  216.9 32.2 %collective-permute-start.15 = (bf16[2,3,16,32,128]{4,3,2,1,0:T(8,128)(2,1)}, bf16[2,3,16,32,128]{4,3,2,1,0:T(8,128)(2,1)}, u32[]{:S(2)}, u32[]{:S(2)}) collective-permute-start(bf16[2,3,16,32,128]{4,3,2,1,0:T(8,128)(2,1)} %get-tuple-element.141), channel_id=1, source_target_pairs={{0,2},{1,3},{8,10},{9,11},{16,18},{17,19},{24,26},{25,27}} | collective-permute-start | bytes 2359304 | tf_op jit(solution)/shard_map/ppermute | solution.py:536
  219.0 30.0 %collective-permute-start.16 = (bf16[2,3,16,32,128]{4,3,2,1,0:T(8,128)(2,1)}, bf16[2,3,16,32,128]{4,3,2,1,0:T(8,128)(2,1)}, u32[]{:S(2)}, u32[]{:S(2)}) collective-permute-start(bf16[2,3,16,32,128]{4,3,2,1,0:T(8,128)(2,1)} %get-tuple-element.140), channel_id=1, source_target_pairs={{7,5},{6,4},{15,13},{14,12},{23,21},{22,20},{31,29},{30,28}} | collective-permute-start | bytes 2359304 | tf_op jit(solution)/shard_map/ppermute | solution.py:537
  241.7 11.9 %collective-permute-start.21 = (bf16[3,16,32,128]{3,2,1,0:T(8,128)(2,1)S(1)}, bf16[3,16,32,128]{3,2,1,0:T(8,128)(2,1)S(1)}, u32[]{:S(2)}, u32[]{:S(2)}) collective-permute-start(bf16[3,16,32,128]{3,2,1,0:T(8,128)(2,1)S(1)} %get-tuple-element.160), channel_id=1, source_target_pairs={{0,1},{1,0},{2,3},{3,2},{4,5},{5,4},{6,7},{7,6},{8,9},{9,8},{10,11... | collective-permute-start | bytes 1179656 | tf_op jit(solution)/shard_map/ppermute | solution.py:470
  257.1 18.9 %collective-permute-start.24 = (bf16[2,3,16,32,128]{4,3,2,1,0:T(8,128)(2,1)}, bf16[2,3,16,32,128]{4,3,2,1,0:T(8,128)(2,1)}, u32[]{:S(2)}, u32[]{:S(2)}) collective-permute-start(bf16[2,3,16,32,128]{4,3,2,1,0:T(8,128)(2,1)} %get-tuple-element.139), channel_id=1, source_target_pairs={{0,2},{1,3},{2,4},{3,5},{8,10},{9,11},{10,12},{11,13},{16,18},{17,... | collective-permute-start | bytes 2359304 | tf_op jit(solution)/shard_map/ppermute | solution.py:536
  259.3 16.7 %collective-permute-start.25 = (bf16[2,3,16,32,128]{4,3,2,1,0:T(8,128)(2,1)}, bf16[2,3,16,32,128]{4,3,2,1,0:T(8,128)(2,1)}, u32[]{:S(2)}, u32[]{:S(2)}) collective-permute-start(bf16[2,3,16,32,128]{4,3,2,1,0:T(8,128)(2,1)} %get-tuple-element.138), channel_id=1, source_target_pairs={{7,5},{6,4},{5,3},{4,2},{15,13},{14,12},{13,11},{12,10},{23,21},{2... | collective-permute-start | bytes 2359304 | tf_op jit(solution)/shard_map/ppermute | solution.py:537
  279.5 25.2 %collective-permute-start.27 = (bf16[2,3,16,32,128]{4,3,2,1,0:T(8,128)(2,1)}, bf16[2,3,16,32,128]{4,3,2,1,0:T(8,128)(2,1)}, u32[]{:S(2)}, u32[]{:S(2)}) collective-permute-start(bf16[2,3,16,32,128]{4,3,2,1,0:T(8,128)(2,1)} %get-tuple-element.137), channel_id=1, source_target_pairs={{0,2},{1,3},{2,4},{3,5},{4,6},{5,7},{8,10},{9,11},{10,12},{11,13},... | collective-permute-start | bytes 2359304 | tf_op jit(solution)/shard_map/ppermute | solution.py:536
  288.0 21.7 %collective-permute-start.28 = (bf16[2,3,16,32,128]{4,3,2,1,0:T(8,128)(2,1)}, bf16[2,3,16,32,128]{4,3,2,1,0:T(8,128)(2,1)}, u32[]{:S(2)}, u32[]{:S(2)}) collective-permute-start(bf16[2,3,16,32,128]{4,3,2,1,0:T(8,128)(2,1)} %get-tuple-element.136), channel_id=1, source_target_pairs={{7,5},{6,4},{5,3},{4,2},{3,1},{2,0},{15,13},{14,12},{13,11},{12,10... | collective-permute-start | bytes 2359304 | tf_op jit(solution)/shard_map/ppermute | solution.py:537
  289.2 31.2 %collective-permute-start.29 = (bf16[2,3,16,32,128]{4,3,2,1,0:T(8,128)(2,1)S(1)}, bf16[2,3,16,32,128]{4,3,2,1,0:T(8,128)(2,1)S(1)}, u32[]{:S(2)}, u32[]{:S(2)}) collective-permute-start(bf16[2,3,16,32,128]{4,3,2,1,0:T(8,128)(2,1)S(1)} %pad_maximum_fusion.refs_0_), channel_id=1, source_target_pairs={{0,2},{1,3},{2,4},{3,5},{4,6},{5,7},{8,10},{9,11},{10,12},{11,13},... | collective-permute-start | bytes 2359304 | tf_op jit(solution)/shard_map/ppermute | solution.py:494
  293.3 32.3 %collective-permute-start.30 = (bf16[2,3,16,32,128]{4,3,2,1,0:T(8,128)(2,1)S(1)}, bf16[2,3,16,32,128]{4,3,2,1,0:T(8,128)(2,1)}, u32[]{:S(2)}, u32[]{:S(2)}) collective-permute-start(bf16[2,3,16,32,128]{4,3,2,1,0:T(8,128)(2,1)S(1)} %pad_maximum_fusion.refs_0_), channel_id=1, source_target_pairs={{7,5},{6,4},{5,3},{4,2},{3,1},{2,0},{15,13},{14,12},{13,11},{12,10... | collective-permute-start | bytes 2359304 | tf_op jit(solution)/shard_map/ppermute | solution.py:495
  325.5 24.1 %collective-permute-start.31 = (bf16[2,3,16,32,128]{4,3,2,1,0:T(8,128)(2,1)S(1)}, bf16[2,3,16,32,128]{4,3,2,1,0:T(8,128)(2,1)S(1)}, u32[]{:S(2)}, u32[]{:S(2)}) collective-permute-start(bf16[2,3,16,32,128]{4,3,2,1,0:T(8,128)(2,1)S(1)} %collective-permute-done.29.refs_1_), channel_id=1, source_target_pairs={{2,4},{3,5},{4,6},{5,7},{10,12},{11,13},{12,14},{13,15},{18,20},{1... | collective-permute-start | bytes 2359304 | tf_op jit(solution)/shard_map/ppermute | solution.py:494
  326.2 23.4 %collective-permute-start.32 = (bf16[2,3,16,32,128]{4,3,2,1,0:T(8,128)(2,1)}, bf16[2,3,16,32,128]{4,3,2,1,0:T(8,128)(2,1)S(1)}, u32[]{:S(2)}, u32[]{:S(2)}) collective-permute-start(bf16[2,3,16,32,128]{4,3,2,1,0:T(8,128)(2,1)} %collective-permute-done.30.refs_4_), channel_id=1, source_target_pairs={{5,3},{4,2},{3,1},{2,0},{13,11},{12,10},{11,9},{10,8},{21,19},{20,... | collective-permute-start | bytes 2359304 | tf_op jit(solution)/shard_map/ppermute | solution.py:495
  329.7 19.9 %collective-permute-start.33 = (bf16[3,16,32,128]{3,2,1,0:T(8,128)(2,1)S(1)}, bf16[3,16,32,128]{3,2,1,0:T(8,128)(2,1)S(1)}, u32[]{:S(2)}, u32[]{:S(2)}) collective-permute-start(bf16[3,16,32,128]{3,2,1,0:T(8,128)(2,1)S(1)} %get-tuple-element.154), channel_id=1, source_target_pairs={{0,1},{1,0},{2,3},{3,2},{4,5},{5,4},{6,7},{7,6},{8,9},{9,8},{10,11... | collective-permute-start | bytes 1179656 | tf_op jit(solution)/shard_map/ppermute | solution.py:470
  329.8 8.3 %collective-permute-start.36 = (bf16[3,4,32,128]{3,2,1,0:T(8,128)(2,1)S(1)}, bf16[3,4,32,128]{3,2,1,0:T(8,128)(2,1)S(1)}, u32[]{:S(2)}, u32[]{:S(2)}) collective-permute-start(bf16[3,4,32,128]{3,2,1,0:T(8,128)(2,1)S(1)} %get-tuple-element.104), channel_id=1, source_target_pairs={{0,8},{8,16},{16,24},{1,9},{9,17},{17,25},{2,10},{10,18},{18,26},{... | collective-permute-start | bytes 294920 | tf_op jit(solution)/shard_map/ppermute | solution.py:452
  338.1 8.6 %collective-permute-start.34 = (bf16[3,4,32,128]{3,2,1,0:T(8,128)(2,1)S(1)}, bf16[3,4,32,128]{3,2,1,0:T(8,128)(2,1)S(1)}, u32[]{:S(2)}, u32[]{:S(2)}) collective-permute-start(bf16[3,4,32,128]{3,2,1,0:T(8,128)(2,1)S(1)} %get-tuple-element.153), channel_id=1, source_target_pairs={{1,9},{3,11},{5,13},{7,15},{8,0},{9,17},{10,2},{11,19},{12,4},{13,... | collective-permute-start | bytes 294920 | tf_op jit(solution)/shard_map/ppermute | solution.py:465
  342.3 7.3 %collective-permute-start.35 = (bf16[3,4,32,128]{3,2,1,0:T(8,128)(2,1)S(1)}, bf16[3,4,32,128]{3,2,1,0:T(8,128)(2,1)S(1)}, u32[]{:S(2)}, u32[]{:S(2)}) collective-permute-start(bf16[3,4,32,128]{3,2,1,0:T(8,128)(2,1)S(1)} %get-tuple-element.152), channel_id=1, source_target_pairs={{1,8},{3,10},{5,12},{7,14},{8,1},{9,16},{10,3},{11,18},{12,5},{13,... | collective-permute-start | bytes 294920 | tf_op jit(solution)/shard_map/ppermute | solution.py:465
  360.3 164.6 %reduce-scatter.8.cloned.1.call-start = ((), (), s32[]{:S(2)}) async-start(), calls=%async_computation.5 | async-start | bytes 3932160 | tf_op jit(solution)/shard_map/reduce_scatter | solution.py:619
  362.0 58.3 %collective-permute-start.45 = (bf16[2,3,16,32,128]{4,3,2,1,0:T(8,128)(2,1)}, bf16[2,3,16,32,128]{4,3,2,1,0:T(8,128)(2,1)}, u32[]{:S(2)}, u32[]{:S(2)}) collective-permute-start(bf16[2,3,16,32,128]{4,3,2,1,0:T(8,128)(2,1)} %copy-done.27), channel_id=1, source_target_pairs={{3,1},{2,0},{11,9},{10,8},{19,17},{18,16},{27,25},{26,24}} | collective-permute-start | bytes 2359304 | tf_op jit(solution)/shard_map/ppermute | solution.py:495
  467.1 120.4 %reduce-scatter.6.cloned.1.call-start = ((), (), s32[]{:S(2)}) async-start(), calls=%async_computation.4 | async-start | bytes 3932160 | tf_op jit(solution)/shard_map/reduce_scatter | solution.py:619
  469.3 6.8 %collective-permute-start.39 = (bf16[3,4,32,128]{3,2,1,0:T(8,128)(2,1)S(1)}, bf16[3,4,32,128]{3,2,1,0:T(8,128)(2,1)S(1)}, u32[]{:S(2)}, u32[]{:S(2)}) collective-permute-start(bf16[3,4,32,128]{3,2,1,0:T(8,128)(2,1)S(1)} %get-tuple-element.115), channel_id=1, source_target_pairs={{8,0},{16,8},{24,16},{9,1},{17,9},{25,17},{10,2},{18,10},{26,18},{... | collective-permute-start | bytes 294920 | tf_op jit(solution)/shard_map/ppermute | solution.py:452
  526.2 11.9 %collective-permute-start.50 = (bf16[3,16,32,128]{3,2,1,0:T(8,128)(2,1)S(1)}, bf16[3,16,32,128]{3,2,1,0:T(8,128)(2,1)S(1)}, u32[]{:S(2)}, u32[]{:S(2)}) collective-permute-start(bf16[3,16,32,128]{3,2,1,0:T(8,128)(2,1)S(1)} %get-tuple-element.150), channel_id=1, source_target_pairs={{0,1},{1,0},{2,3},{3,2},{4,5},{5,4},{6,7},{7,6},{8,9},{9,8},{10,11... | collective-permute-start | bytes 1179656 | tf_op jit(solution)/shard_map/ppermute | solution.py:470
  531.2 6.9 %collective-permute-start.52 = (bf16[3,4,32,128]{3,2,1,0:T(8,128)(2,1)S(1)}, bf16[3,4,32,128]{3,2,1,0:T(8,128)(2,1)S(1)}, u32[]{:S(2)}, u32[]{:S(2)}) collective-permute-start(bf16[3,4,32,128]{3,2,1,0:T(8,128)(2,1)S(1)} %get-tuple-element.148), channel_id=1, source_target_pairs={{1,8},{3,10},{5,12},{7,14},{8,1},{9,16},{10,3},{11,18},{12,5},{13,... | collective-permute-start | bytes 294920 | tf_op jit(solution)/shard_map/ppermute | solution.py:465
  588.7 11.5 %collective-permute-start.53 = (bf16[3,16,32,128]{3,2,1,0:T(8,128)(2,1)S(1)}, bf16[3,16,32,128]{3,2,1,0:T(8,128)(2,1)S(1)}, u32[]{:S(2)}, u32[]{:S(2)}) collective-permute-start(bf16[3,16,32,128]{3,2,1,0:T(8,128)(2,1)S(1)} %get-tuple-element.146), channel_id=1, source_target_pairs={{0,1},{1,0},{2,3},{3,2},{4,5},{5,4},{6,7},{7,6},{8,9},{9,8},{10,11... | collective-permute-start | bytes 1179656 | tf_op jit(solution)/shard_map/ppermute | solution.py:470
  593.6 6.5 %collective-permute-start.55 = (bf16[3,4,32,128]{3,2,1,0:T(8,128)(2,1)S(1)}, bf16[3,4,32,128]{3,2,1,0:T(8,128)(2,1)S(1)}, u32[]{:S(2)}, u32[]{:S(2)}) collective-permute-start(bf16[3,4,32,128]{3,2,1,0:T(8,128)(2,1)S(1)} %get-tuple-element.144), channel_id=1, source_target_pairs={{1,8},{3,10},{5,12},{7,14},{8,1},{9,16},{10,3},{11,18},{12,5},{13,... | collective-permute-start | bytes 294920 | tf_op jit(solution)/shard_map/ppermute | solution.py:465
  (64 other events, 348.8 us)
Sparse Core Ops, SparseCore 0:
  39.4 66.2 all-gather.8
  107.8 63.3 all-gather.6
  174.2 66.3 reduce-scatter.3
  360.5 74.4 all-gather.10
  467.2 57.7 reduce-scatter.7
  527.1 60.2 reduce-scatter.5

commit v10 on v8

--- a/solution.py
+++ b/solution.py
@@ -103,22 +103,24 @@
 
 def fields(members, rows, steps, cols):
     field = pl.BlockSpec((1, rows, steps, cols), lambda b, core: (b, 0, 0, 0))
-    half = pl.BlockSpec((1, rows // 2, steps, cols), lambda b, core: (b, 0, 0, 0))
     rim = pl.BlockSpec((1, HALO, steps, cols), lambda b, core: (b, 0, 0, 0))
+    misfits = [
+        pl.BlockSpec((None, 1, count, steps, cols), lambda b, core, place=place: (place, b, 0, 0, 0))
+        for place, count in ((0, rows // 2), (1, rows // 2), (0, HALO), (1, HALO))
+    ]
 
     def shape(count, dtype):
         return jax.ShapeDtypeStruct((members, count, steps, cols), dtype)
 
-    specs = [field, half, half, field, rim, rim]
+    specs = [field, field, field, rim, rim]
     shapes = [
         shape(rows, jnp.float32),
-        shape(rows // 2, jnp.bfloat16),
-        shape(rows // 2, jnp.bfloat16),
+        shape(rows, jnp.bfloat16),
         shape(rows, jnp.float32),
         shape(HALO, jnp.bfloat16),
         shape(HALO, jnp.bfloat16),
     ]
-    return field, half, rim, specs, shapes
+    return field, rim, misfits, specs, shapes
 
 
 def put_rest(rest, times, rest_ref, top_ref, bottom_ref):
@@ -127,15 +129,9 @@
     bottom_ref[0, :, times] = rest[rest.shape[0] - HALO :].astype(bottom_ref.dtype)
 
 
-def put_low(core, iter_ref, keep_ref, give_ref):
-    half = keep_ref.shape[1]
-    keep_ref[0] = iter_ref[0, pl.ds(core * half, half)].astype(keep_ref.dtype)
-    give_ref[0] = iter_ref[0, pl.ds((1 - core) * half, half)].astype(give_ref.dtype)
-
-
 def start_kernel(
     core_ref, rhs_ref, up_ref, down_ref, coeff_ref,
-    iter_ref, keep_ref, give_ref, rest_ref, top_ref, bottom_ref,
+    iter_ref, low_ref, rest_ref, top_ref, bottom_ref,
 ):
     def body(times):
         here = jnp.swapaxes(rhs_ref[times], 0, 1)
@@ -145,13 +141,13 @@
         put_rest(here - prior(update, coeff_ref), times, rest_ref, top_ref, bottom_ref)
 
     time_chunks(iter_ref.shape[2], body)
-    put_low(core_ref[0], iter_ref, keep_ref, give_ref)
+    low_ref[...] = iter_ref[...].astype(low_ref.dtype)
 
 
 def start(group, members, core, rhs, up, down, coeff):
     steps, _, rows, cols = rhs.shape
     flat = rhs.reshape(steps, -1, cols)
-    field, half, rim, specs, shapes = fields(members, rows, steps, cols)
+    _, rim, _, specs, shapes = fields(members, rows, steps, cols)
     return call(
         start_kernel,
         core,
@@ -183,7 +179,7 @@
 
 def step_kernel(
     core_ref, up_ref, rest_ref, down_ref, own_ref, other_ref, same_ref, cross_ref, iter_ref, coeff_ref,
-    next_ref, keep_ref, give_ref, later_ref, top_ref, bottom_ref, whole_ref,
+    next_ref, low_ref, later_ref, top_ref, bottom_ref, whole_ref,
 ):
     def body(times):
         residual = residual_of(
@@ -198,17 +194,17 @@
         put_rest(rest_ref[0, :, times] - prior(update, coeff_ref), times, later_ref, top_ref, bottom_ref)
 
     time_chunks(iter_ref.shape[2], body)
-    put_low(core_ref[0], next_ref, keep_ref, give_ref)
+    low_ref[...] = next_ref[...].astype(low_ref.dtype)
 
 
 def step(core, rests, misfits, iterate, coeff):
     members, rows, steps, cols = iterate.shape
-    field, half, rim, specs, shapes = fields(members, rows, steps, cols)
+    field, rim, parts, specs, shapes = fields(members, rows, steps, cols)
     return call(
         step_kernel,
         core,
         (members,),
-        [rim, field, rim, half, half, rim, rim, field, whole_block(coeff)],
+        [rim, field, rim, *parts, field, whole_block(coeff)],
         specs,
         shapes,
         [pltpu.VMEM((rows, SUBLANES, cols), jnp.float32)],
@@ -239,10 +235,10 @@
 
 def finish(group, samples, core, rests, misfits, iterate, coeff, previous):
     members, rows, steps, cols = iterate.shape
-    field, half, rim, _, _ = fields(members, rows, steps, cols)
+    field, rim, parts, _, _ = fields(members, rows, steps, cols)
     result = pl.BlockSpec((steps, rows, cols), lambda b, core: (0, b + group * members, 0))
     shape = jax.ShapeDtypeStruct((steps, samples * rows, cols), jnp.float32)
-    in_specs = [rim, field, rim, half, half, rim, rim, field, whole_block(coeff)]
+    in_specs = [rim, field, rim, *parts, field, whole_block(coeff)]
     first = 1 + len(in_specs)
     return call(
         finish_kernel,
@@ -284,8 +280,10 @@
 def observe_kernel(core_ref, field_ref, *refs):
     *slot_refs, own_ref, other_ref, table_ref, around_ref, cell_ref = refs[:-4]
     out_ref, spec, acc, picked = refs[-4:]
-    chips, _, whole, rows, steps, lanes = field_ref.shape
+    rows, steps, lanes = field_ref.shape[-3:]
     members = spec.shape[0] // 2
+    chips = table_ref.shape[1] // (2 * steps)
+    whole = field_ref.shape[-4]
     freqs, sensors, width = own_ref.shape[1:]
     near = lanes // sensors
     wide = 2 * lanes
@@ -300,7 +298,8 @@
 
     def history(b, r):
         if b < whole:
-            return field_ref[:, :, b, r].reshape(2 * chips * steps, lanes)
+            here = field_ref[..., b, r, :, :]
+            return here.reshape(2 * chips * steps, lanes)
         slots = [slot_refs[0][:, b - whole, r]]
         for k in range(1, chips):
             slots.append(slot_refs[k][:, b - whole, r] + slot_refs[2 * chips - 1 - k][:, b - whole, r])
@@ -349,20 +348,23 @@
 
 
 def observe(core, field, slots, own, other, table, around, local_cells):
-    chips, _, whole, rows, steps, lanes = field.shape
+    *sources, whole, rows, steps, lanes = field.shape
     apart = slots[0].shape[1] if slots else 0
     members = whole + apart
     _, freqs, sensors, cells = own.shape
     width = CHUNK_ROWS * lanes
     near = lanes // sensors
     shape = (2, 2, members, freqs // near, lanes)
-    block = (chips, 2, whole, CHUNK_ROWS, steps, lanes)
+    chunks = cells // (2 * width)
+    first = chunks if len(sources) == 1 else 0
+    block = (*sources, whole, CHUNK_ROWS, steps, lanes)
+    lead = (0,) * len(sources) + (0,)
     slot = pl.BlockSpec((2, apart, CHUNK_ROWS, steps, lanes), lambda c, core: (0, 0, c, 0, 0))
     return call(
         observe_kernel,
         core,
-        (rows // CHUNK_ROWS,),
-        [pl.BlockSpec(block, lambda c, core: (0, 0, 0, c, 0, 0))]
+        (chunks,),
+        [pl.BlockSpec(block, lambda c, core: (*lead, core[0] * first + c, 0, 0))]
         + [slot] * len(slots)
         + map_specs(own, width)
         + [whole_block(table), whole_block(around), whole_block(local_cells)],
@@ -533,13 +535,34 @@
     places = jnp.arange(chips, dtype=jnp.int32)[:, None, None] * chip_steps
     table = transform_table(freqs, places + offsets)
     back = table.T
+    in_order = transform_table(freqs, jnp.arange(2 * freqs, dtype=jnp.int32))
     chip = sensor_index // 2
     places = (chip - jnp.arange(chips, dtype=jnp.int32)) % chips
     around = transform_table(freqs, places[:, None, None] * chip_steps + offsets)
 
     diagonal = reaction + 4.0 * stiffness * stiffness
     local = jnp.stack([stiffness, diagonal])
-    up, down = rims(local[:, :HALO], local[:, rows - HALO :])
+    members = samples // GROUPS
+    groups = [slice(group * members, (group + 1) * members) for group in range(GROUPS)]
+
+    def rim_rows(here, first):
+        part = lax.slice_in_dim(rhs[:, here], first, first + HALO, axis=2)
+        return jnp.transpose(lax.optimization_barrier(part), (1, 2, 0, 3))
+
+    def packed(first):
+        part = rim_rows(groups[0], first).reshape(members * HALO, steps, cols)
+        extra = local[:, first : first + HALO].reshape(2 * HALO, cols)
+        extra = jnp.pad(extra, ((0, -2 * HALO % steps), (0, 0))).reshape(-1, steps, cols)
+        return jnp.concatenate([part, extra], axis=0)
+
+    def unpacked(value):
+        part = value[: members * HALO].reshape(members, HALO, steps, cols)
+        extra = value[members * HALO :].reshape(-1, cols)[: 2 * HALO].reshape(2, HALO, cols)
+        return part, extra
+
+    (up_first, up), (down_first, down) = (
+        unpacked(value) for value in rims(packed(0), packed(rows - HALO))
+    )
     stiff, diag = jnp.concatenate([up, local, down], axis=1)
     inside = diag > 0.0
     inverse = jnp.where(inside, 1.0 / jnp.where(inside, diag, 1.0), 0.0)
@@ -558,45 +581,49 @@
     local_cells = jnp.broadcast_to(local_cells.reshape(2 * LANES, 1), (2 * LANES, LANES))
     core = core.reshape(1)
 
-    members = samples // GROUPS
     whole = members - members // APART
-    edge_rows = lax.optimization_barrier((rhs[:, :, :HALO], rhs[:, :, rows - HALO :]))
-    top, bottom = (jnp.transpose(rim, (1, 2, 0, 3)).astype(jnp.bfloat16) for rim in edge_rows)
     lines = [[k for k in range(size) if k % 2 == parity] for parity in range(2)]
     shape = (chips, 2, members, rows // 2, steps, cols)
 
-    def ready(state, whole):
-        iterate, keep, give, rest, top, bottom = state
+    def both_cores(low):
+        keep, give = (
+            lax.dynamic_slice_in_dim(low, first * (rows // 2), rows // 2, axis=1)
+            for first in (core[0], 1 - core[0])
+        )
+        return jnp.stack([keep, swap_cores(give)])
+
+    def ready(state):
+        iterate, low, rest, top, bottom = state
         above, below = rims(top, bottom)
-        pair = jnp.stack([keep, swap_cores(give)])
+        pair = both_cores(low)
         parts = lax.optimization_barrier((pair[:, :whole], pair[:, whole:]))
         return iterate, *parts, (above, rest, below)
 
     def edges(misfit):
         first = (rows // 2 - HALO) * core[0]
         edge = lax.dynamic_slice_in_dim(misfit, first, HALO, axis=2)
-        same, _ = misfit_rims(edge[0])
-        _, cross = misfit_rims(edge[1])
-        return misfit[0], swap_cores(misfit[1]), same, cross
-
-    def begin(group, ends, whole):
-        return ready(start(group, members, core, rhs, *rims(*ends), coeff), whole)
-
-    groups = [slice(group * members, (group + 1) * members) for group in range(GROUPS)]
-    states = [begin(0, (top[groups[0]], bottom[groups[0]]), members)]
-    iterate, pair, apart, rests = states[0]
-    pair, whole_map = lax.optimization_barrier((pair, forward_map))
+        return misfit, swap_cores(misfit), *misfit_rims(edge)
+
+    iterate, low, rest, *ends = start(0, members, core, rhs, up_first, down_first, coeff)
+    low, whole_map = lax.optimization_barrier((low, forward_map))
     other_map = swap_cores(whole_map)
+    above, below = rims(*ends)
+    states = [(iterate, low, None, (above, rest, below))]
     for group in range(1, GROUPS):
-        ends = (top[groups[group]], bottom[groups[group]])
-        _, rests, ends = lax.optimization_barrier((pair, rests, ends))
-        states.append(begin(group, ends, whole))
-    states[0] = iterate, pair, apart, rests
+        ends = tuple(
+            rim_rows(groups[group], first).astype(jnp.bfloat16) for first in (0, rows - HALO)
+        )
+        _, rests, ends = lax.optimization_barrier((low, states[0][3], ends))
+        states[0] = (*states[0][:3], rests)
+        states.append(ready(start(group, members, core, rhs, *rims(*ends), coeff)))
     line = None
 
     outputs = ()
     for iteration in range(ITERS):
-        fields = [lax.all_gather(state[1], "sensors", axis_index_groups=lines) for state in states]
+        fields = [
+            lax.all_gather(state[1], "sensors", axis_index_groups=None if state[2] is None else lines)
+            for state in states
+        ]
         if line is not None:
             line.hop(last=True)
         totals = []
@@ -613,7 +640,14 @@
                 field = line.after(field)
                 line.hop()
             sums = observe(
-                core, field, slots, forward_map, other_map, table, around, local_cells
+                core,
+                field,
+                slots,
+                forward_map,
+                other_map,
+                table if slots else in_order,
+                around,
+                local_cells,
             )
             if line is not None:
                 sums = line.after(sums)
@@ -638,7 +672,7 @@
                     line.hop()
                     total, earlier = line.after((total, before[3]))
                     states[0] = (*before[:3], earlier)
-                states[group] = ready(step(core, rests, edges(total), iterate, coeff), whole)
+                states[group] = ready(step(core, rests, edges(total), iterate, coeff))
             else:
                 if outputs:
                     total, outputs = lax.optimization_barrier((total, outputs))

time: 557 us -> 561 us (level)
    squeeze x8 -> x0, local copies, waits for them, and re-layouts: 9.3 us -> none  [the longest x4 5.49 us: edges(): return (misfit[0], swap_cores(misfit[1]), same, cross)]
    ppermute x7 -> x6, starting transfers between devices: 27.8 us -> 20.1 us  [rims(): lax.ppermute(bottom, 'cells', onward)]
    ppermute x13 -> x12, starting transfers between devices: 15.1 us -> 21.4 us  [swap_cores(): return lax.ppermute(value, 'sensors', [(k, k ^ 1) for k in range(size)])]
    unnamed x78 -> x102, local copies, waits for them, and re-layouts: 41 us -> 45.8 us
    ppermute x7 -> x6, waiting for transfers between devices: 18.9 us -> 21.1 us  [rims(): lax.ppermute(top, 'cells', backward)]
    ppermute x13 -> x12, waiting for transfers between devices: 22.9 us -> 23.4 us  [swap_cores(): return lax.ppermute(value, 'sensors', [(k, k ^ 1) for k in range(size)])]
  transfers between devices with their start and end apart: 73 -> 70, of which waited for: 41 -> 35; matrix products, arithmetic and copies ran while one was open for 3% -> 2% of each run, Pallas kernels for 28% -> 28%
where the time goes in v10:
time: 561 us; the launch traced here: 554 us
  waiting for transfers between devices  186 us (33%)
  Pallas kernels  168 us (30%)
  starting transfers between devices  122 us (22%)
  local copies, waits for them, and re-layouts  54.2 us (10%)
  between operations  15.1 us (3%)
  other arithmetic  8.43 us (2%)
    pallas_call x4, Pallas kernels, observe(): call(observe_kernel, core, (chunks,), [pl.BlockSpec(block, lambda c, core...  70.4 us
    reduce_scatter x4, waiting for transfers between devices, shards(): lax.psum_scatter(misfit, 'sensors', scatter_dimension=0, axis_index_group...  68.4 us
    pallas_call x4, Pallas kernels, pull_back(): call(pull_kernel, core, (rows // CHUNK_ROWS,), [whole_block(array) for ar...  58.4 us
    unnamed x102, local copies, waits for them, and re-layouts  45.8 us
    ppermute x9, waiting for transfers between devices, hop(): down = lax.ppermute(self.ends[1], 'sensors', backward)  38.3 us
    ppermute x8, starting transfers between devices, misfit_rims(): return (lax.ppermute(edge, both, same), lax.ppermute(edge, both, cross))  24.5 us
    ppermute x12, waiting for transfers between devices, swap_cores(): return lax.ppermute(value, 'sensors', [(k, k ^ 1) for k in range(size)])  23.4 us
    ppermute x9, starting transfers between devices, hop(): up = lax.ppermute(self.ends[0], 'sensors', onward)  21.6 us
  transfers between devices with their start and end apart: 70, of which 35 were waited for; matrix products, arithmetic and copies ran while one was open for 2% of the time, Pallas kernels for 28%

profile of v10, /device:TPU:1, one launch (start us, length us, event | category | flops | bytes accessed | tf_op | source)
XLA Modules:
  0.0 553.9 jit_solution(6029319155495249349)
XLA Ops:
  9.9 4.0 collective-permute-start
  17.8 6.5 %collective-permute-done.1 = f32[13,32,128]{2,1,0:T(8,128)S(1)} collective-permute-done((f32[13,32,128]{2,1,0:T(8,128)S(1)}, f32[13,32,128]{2,1,0:T(8,128)S(1)}, u32[]{:S(2)}, u32[]{:S(2)}) %collective-permute-start.1) | collective-permute-done | bytes 213024 | tf_op jit(solution)/shard_map/ppermute | solution.py:461
  27.8 6.2 %start.2 = (f32[3,32,32,128]{3,2,1,0:T(8,128)S(1)}, bf16[3,32,32,128]{3,2,1,0:T(8,128)(2,1)S(1)}, f32[3,32,32,128]{3,2,1,0:T(8,128)S(1)}, bf16[3,4,32,128]{3,2,1,0:T(8,128)(2,1)S(1)}, bf16[3,4,32,128]{3,2,1,0:T(8,128)(2,1)S(1)}) custom-call(s32[1]{0:T(128)} %bitcast.core_ref, f32[32,192,128]{2,1,0:T(8,128)S(1)} %bitcast.55, f32[3,4,32,128]{3,2,1,0:T(8,128)S(1)} %bitcast.71, ...), custom_call_target="tpu_custom_call" | custom-call | tf_op jit(solution)/shard_map/start/pallas_call | solution.py:151
  51.5 4.1 collective-permute-done.5.down_ref
  57.6 6.8 %start.3 = (f32[3,32,32,128]{3,2,1,0:T(8,128)S(1)}, bf16[3,32,32,128]{3,2,1,0:T(8,128)(2,1)S(1)}, f32[3,32,32,128]{3,2,1,0:T(8,128)S(1)}, bf16[3,4,32,128]{3,2,1,0:T(8,128)(2,1)}, bf16[3,4,32,128]{3,2,1,0:T(8,128)(2,1)}) custom-call(s32[1]{0:T(128)} %bitcast.core_ref, f32[32,192,128]{2,1,0:T(8,128)S(1)} %bitcast.56, ...), custom_call_target="tpu_custom_call" | custom-call | tf_op jit(solution)/shard_map/start/pallas_call | solution.py:151
  68.6 18.8 %collective-permute-done.6 = bf16[3,16,32,128]{3,2,1,0:T(8,128)(2,1)S(1)} collective-permute-done((bf16[3,16,32,128]{3,2,1,0:T(8,128)(2,1)S(1)}, bf16[3,16,32,128]{3,2,1,0:T(8,128)(2,1)S(1)}, u32[]{:S(2)}, u32[]{:S(2)}) %collective-permute-start.6) | collective-permute-done | bytes 393248 | tf_op jit(solution)/shard_map/ppermute | solution.py:479
  91.3 4.7 collective-permute-start.9
  96.8 7.7 %collective-permute-done.10.refs_4_ = bf16[2,1,16,32,128]{4,3,2,1,0:T(8,128)(2,1)S(1)} collective-permute-done((bf16[2,1,16,32,128]{4,3,2,1,0:T(8,128)(2,1)S(1)}, bf16[2,1,16,32,128]{4,3,2,1,0:T(8,128)(2,1)S(1)}, u32[]{:S(2)}, u32[]{:S(2)}) %collective-permute-start.10) | collective-permute-done | bytes 262176 | tf_op jit(solution)/shard_map/ppermute | solution.py:504
  111.9 17.4 %observe.4 = f32[2,2,3,16,128]{4,3,2,1,0:T(8,128)S(1)} custom-call(s32[1]{0:T(128)} %bitcast.core_ref, bf16[8,3,32,32,128]{4,3,2,1,0:T(8,128)(2,1)S(1)} %bitcast.57, bf16[2,128,16,4096]{3,2,1,0:T(8,128)(2,1)} %refs_5_.7, bf16[2,128,16,4096]{3,2,1,0:T(8,128)(2,1)} %collective-permute-done.13.refs_1_.refs_6_.refs_8_, bf16[256,256]{1,0:T(8,128)(2,1)S(1)} %copy.38.refs_2_, ...), custom_call_target="tpu_custom_call" | custom-call | flops 402653184 | bytes 39845888 | tf_op jit(solution)/shard_map/observe/pallas_call | solution.py:363
  133.0 4.5 collective-permute-start.19
  142.7 14.6 %pull_back.4 = bf16[4,2,3,16,32,128]{5,4,3,2,1,0:T(8,128)(2,1)S(1)} custom-call(s32[1]{0:T(128)} %bitcast.core_ref, f32[2,2,3,16,128]{4,3,2,1,0:T(8,128)S(1)} %reverse_add_fusion.3.refs_0_, f32[2,2,3,16,128]{4,3,2,1,0:T(8,128)S(1)} %collective-permute-done.17.refs_1_, f32[2,2,3,16,128]{4,3,2,1,0:T(8,128)S(1)} %collective-permute-done.18.refs_2_, ...), custom_call_target="tpu_custom_call" | custom-call | flops 402653184 | bytes 36700160 | tf_op jit(solution)/shard_map/pull_back/pallas_call | solution.py:437
  159.2 3.7 collective-permute-start.7
  170.8 17.7 %observe.5 = f32[2,2,3,16,128]{4,3,2,1,0:T(8,128)S(1)} custom-call(s32[1]{0:T(128)} %bitcast.core_ref, bf16[4,2,2,16,32,128]{5,4,3,2,1,0:T(8,128)(2,1)S(1)} %bitcast.58, bf16[2,1,16,32,128]{4,3,2,1,0:T(8,128)(2,1)S(1)} %pad_maximum_fusion.2.refs_0_, bf16[2,1,16,32,128]{4,3,2,1,0:T(8,128)(2,1)} %collective-permute-done.9.refs_1_, ...), custom_call_target="tpu_custom_call" | custom-call | flops 402653184 | bytes 35651584 | tf_op jit(solution)/shard_map/observe/pallas_call | solution.py:363
  199.1 14.6 %pull_back.5 = bf16[4,2,3,16,32,128]{5,4,3,2,1,0:T(8,128)(2,1)S(1)} custom-call(s32[1]{0:T(128)} %bitcast.core_ref, f32[2,2,3,16,128]{4,3,2,1,0:T(8,128)S(1)} %reverse_add_fusion.2.refs_0_, f32[2,2,3,16,128]{4,3,2,1,0:T(8,128)S(1)} %collective-permute-done.29.refs_1_, f32[2,2,3,16,128]{4,3,2,1,0:T(8,128)S(1)} %collective-permute-done.30.refs_2_, ...), custom_call_target="tpu_custom_call" | custom-call | flops 402653184 | bytes 36700160 | tf_op jit(solution)/shard_map/pull_back/pallas_call | solution.py:437
  215.5 7.5 %reduce-scatter.5.cloned.1.call-done = bf16[1,2,3,16,32,128]{5,4,3,2,1,0:T(8,128)(2,1)} async-done(((bf16[4,2,3,16,32,128]{5,4,3,2,1,0:T(8,128)(2,1)}), bf16[1,2,3,16,32,128]{5,4,3,2,1,0:T(8,128)(2,1)}) %reduce-scatter.5.cloned.1.call-update) | async-done | bytes 786448 | tf_op jit(solution)/shard_map/reduce_scatter | solution.py:660
  236.2 7.3 %step.2 = (f32[3,32,32,128]{3,2,1,0:T(8,128)S(1)}, bf16[3,32,32,128]{3,2,1,0:T(8,128)(2,1)S(1)}, f32[3,32,32,128]{3,2,1,0:T(8,128)S(1)}, bf16[3,4,32,128]{3,2,1,0:T(8,128)(2,1)S(1)}, bf16[3,4,32,128]{3,2,1,0:T(8,128)(2,1)S(1)}) custom-call(s32[1]{0:T(128)} %bitcast.core_ref, bf16[3,4,32,128]{3,2,1,0:T(8,128)(2,1)S(1)} %collective-permute-done.2.up_ref, ...), custom_call_target="tpu_custom_call" | custom-call | tf_op jit(solution)/shard_map/step/pallas_call | solution.py:203
  245.8 5.0 collective-permute-start.23
  254.4 4.0 collective-permute-start.24
  258.4 16.8 %collective-permute-done.26.refs_4_ = bf16[2,1,16,32,128]{4,3,2,1,0:T(8,128)(2,1)S(1)} collective-permute-done((bf16[2,1,16,32,128]{4,3,2,1,0:T(8,128)(2,1)S(1)}, bf16[2,1,16,32,128]{4,3,2,1,0:T(8,128)(2,1)S(1)}, u32[]{:S(2)}, u32[]{:S(2)}) %collective-permute-start.26) | collective-permute-done | bytes 262176 | tf_op jit(solution)/shard_map/ppermute | solution.py:504
  282.4 12.8 %reduce-scatter.7.cloned.1.call-done = bf16[1,2,3,16,32,128]{5,4,3,2,1,0:T(8,128)(2,1)} async-done(((bf16[4,2,3,16,32,128]{5,4,3,2,1,0:T(8,128)(2,1)}), bf16[1,2,3,16,32,128]{5,4,3,2,1,0:T(8,128)(2,1)}) %reduce-scatter.7.cloned.1.call-update) | async-done | bytes 786448 | tf_op jit(solution)/shard_map/reduce_scatter | solution.py:660
  310.8 7.1 %step.3 = (f32[3,32,32,128]{3,2,1,0:T(8,128)S(1)}, bf16[3,32,32,128]{3,2,1,0:T(8,128)(2,1)S(1)}, f32[3,32,32,128]{3,2,1,0:T(8,128)S(1)}, bf16[3,4,32,128]{3,2,1,0:T(8,128)(2,1)S(1)}, bf16[3,4,32,128]{3,2,1,0:T(8,128)(2,1)S(1)}) custom-call(s32[1]{0:T(128)} %bitcast.core_ref, bf16[3,4,32,128]{3,2,1,0:T(8,128)(2,1)} %collective-permute-done.7.up_ref, ...), custom_call_target="tpu_custom_call" | custom-call | tf_op jit(solution)/shard_map/step/pallas_call | solution.py:203
  319.2 4.9 collective-permute-start.37
  327.7 5.4 collective-permute-start.40
  335.8 11.4 %collective-permute-done.41.refs_4_ = bf16[2,1,16,32,128]{4,3,2,1,0:T(8,128)(2,1)S(1)} collective-permute-done((bf16[2,1,16,32,128]{4,3,2,1,0:T(8,128)(2,1)S(1)}, bf16[2,1,16,32,128]{4,3,2,1,0:T(8,128)(2,1)S(1)}, u32[]{:S(2)}, u32[]{:S(2)}) %collective-permute-start.41) | collective-permute-done | bytes 262176 | tf_op jit(solution)/shard_map/ppermute | solution.py:504
  358.3 17.5 %observe.6 = f32[2,2,3,16,128]{4,3,2,1,0:T(8,128)S(1)} custom-call(s32[1]{0:T(128)} %bitcast.core_ref, bf16[4,2,2,16,32,128]{5,4,3,2,1,0:T(8,128)(2,1)S(1)} %bitcast.59, bf16[2,1,16,32,128]{4,3,2,1,0:T(8,128)(2,1)S(1)} %pad_maximum_fusion.1.refs_0_, bf16[2,1,16,32,128]{4,3,2,1,0:T(8,128)(2,1)S(1)} %copy-done.30, bf16[2,1,16,32,128]{4,3,2,1,0:T(8,128)(2,1)S(1)} %copy-done.34, ...), custom_call_target="tpu_custom_call" | custom-call | flops 402653184 | bytes 35651584 | tf_op jit(solution)/shard_map/observe/pallas_call | solution.py:363
  387.1 14.6 %pull_back.6 = bf16[4,2,3,16,32,128]{5,4,3,2,1,0:T(8,128)(2,1)S(1)} custom-call(s32[1]{0:T(128)} %bitcast.core_ref, f32[2,2,3,16,128]{4,3,2,1,0:T(8,128)S(1)} %reverse_add_fusion.1.refs_0_, f32[2,2,3,16,128]{4,3,2,1,0:T(8,128)S(1)} %collective-permute-done.49.refs_1_, f32[2,2,3,16,128]{4,3,2,1,0:T(8,128)S(1)} %collective-permute-done.50.refs_2_, ...), custom_call_target="tpu_custom_call" | custom-call | flops 402653184 | bytes 36700160 | tf_op jit(solution)/shard_map/pull_back/pallas_call | solution.py:437
  414.3 17.7 %observe.7 = f32[2,2,3,16,128]{4,3,2,1,0:T(8,128)S(1)} custom-call(s32[1]{0:T(128)} %bitcast.core_ref, bf16[4,2,2,16,32,128]{5,4,3,2,1,0:T(8,128)(2,1)S(1)} %bitcast.60, bf16[2,1,16,32,128]{4,3,2,1,0:T(8,128)(2,1)S(1)} %pad_maximum_fusion.refs_0_, bf16[2,1,16,32,128]{4,3,2,1,0:T(8,128)(2,1)} %collective-permute-done.40.refs_1_, ...), custom_call_target="tpu_custom_call" | custom-call | flops 402653184 | bytes 35651584 | tf_op jit(solution)/shard_map/observe/pallas_call | solution.py:363
  442.9 14.6 %pull_back.7 = bf16[4,2,3,16,32,128]{5,4,3,2,1,0:T(8,128)(2,1)S(1)} custom-call(s32[1]{0:T(128)} %bitcast.core_ref, f32[2,2,3,16,128]{4,3,2,1,0:T(8,128)S(1)} %reverse_add_fusion.refs_0_, f32[2,2,3,16,128]{4,3,2,1,0:T(8,128)S(1)} %collective-permute-done.53.refs_1_, f32[2,2,3,16,128]{4,3,2,1,0:T(8,128)S(1)} %collective-permute-done.54.refs_2_, ...), custom_call_target="tpu_custom_call" | custom-call | flops 402653184 | bytes 36700160 | tf_op jit(solution)/shard_map/pull_back/pallas_call | solution.py:437
  459.2 6.0 %reduce-scatter.11.cloned.1.call-done = bf16[1,2,3,16,32,128]{5,4,3,2,1,0:T(8,128)(2,1)} async-done(((bf16[4,2,3,16,32,128]{5,4,3,2,1,0:T(8,128)(2,1)}), bf16[1,2,3,16,32,128]{5,4,3,2,1,0:T(8,128)(2,1)}) %reduce-scatter.11.cloned.1.call-update) | async-done | bytes 786448 | tf_op jit(solution)/shard_map/reduce_scatter | solution.py:660
  479.9 6.0 %finish.2 = (f32[32,192,128]{2,1,0:T(8,128)}, f32[32,192,128]{2,1,0:T(8,128)}) custom-call(s32[1]{0:T(128)} %bitcast.core_ref, bf16[3,4,32,128]{3,2,1,0:T(8,128)(2,1)S(1)} %copy-done.42, f32[3,32,32,128]{3,2,1,0:T(8,128)S(1)} %copy-done.21, bf16[3,4,32,128]{3,2,1,0:T(8,128)(2,1)S(1)} %copy-done.44, bf16[2,3,16,32,128]{4,3,2,1,0:T(8,128)(2,1)S(1)} %bitcast.67, ...), custom_call_target="tpu_custom_call" | custom-call | tf_op jit(solution)/shard_map/finish/pallas_call | solution.py:243
  485.9 42.0 %reduce-scatter.9.cloned.1.call-done = bf16[1,2,3,16,32,128]{5,4,3,2,1,0:T(8,128)(2,1)} async-done(((bf16[4,2,3,16,32,128]{5,4,3,2,1,0:T(8,128)(2,1)}), bf16[1,2,3,16,32,128]{5,4,3,2,1,0:T(8,128)(2,1)}) %reduce-scatter.9.cloned.1.call-update) | async-done | bytes 786448 | tf_op jit(solution)/shard_map/reduce_scatter | solution.py:660
  541.1 6.0 %finish.3 = (f32[32,192,128]{2,1,0:T(8,128)}, f32[32,192,128]{2,1,0:T(8,128)}) custom-call(s32[1]{0:T(128)} %bitcast.core_ref, bf16[3,4,32,128]{3,2,1,0:T(8,128)(2,1)S(1)} %collective-permute-done.38.up_ref, f32[3,32,32,128]{3,2,1,0:T(8,128)S(1)} %copy-done.11, ...), custom_call_target="tpu_custom_call", output_to_operand_aliasing={{0}: (10, {}), {1}: (11, {})} | custom-call | tf_op jit(solution)/shard_map/finish/pallas_call | solution.py:243
  (293 shorter events, 200.9 us)
Async XLA Ops:
  7.2 98.5 %all-gather.11.cloned.1.call-start = ((), (), s32[]{:S(2)}) async-start(), calls=%async_computation.9 | async-start | bytes 7077888 | tf_op jit(solution)/shard_map/all_gather | solution.py:624
  36.0 73.0 %collective-permute-start.13 = (bf16[2,128,16,4096]{3,2,1,0:T(8,128)(2,1)}, bf16[2,128,16,4096]{3,2,1,0:T(8,128)(2,1)}, u32[]{:S(2)}, u32[]{:S(2)}) collective-permute-start(bf16[2,128,16,4096]{3,2,1,0:T(8,128)(2,1)} %refs_5_.7), channel_id=1, source_target_pairs={{0,1},{1,0},{2,3},{3,2},{4,5},{5,4},{6,7},{7,6},{8,9},{9,8},{10,11... | collective-permute-start | bytes 100663304 | tf_op jit(solution)/shard_map/ppermute | solution.py:479
  37.6 131.3 %all-gather.9.cloned.1.call-start = ((), (), s32[]{:S(2)}) async-start(), calls=%async_computation.8 | async-start | bytes 2621440 | tf_op jit(solution)/shard_map/all_gather | solution.py:624
  66.8 20.7 %collective-permute-start.6 = (bf16[3,16,32,128]{3,2,1,0:T(8,128)(2,1)S(1)}, bf16[3,16,32,128]{3,2,1,0:T(8,128)(2,1)S(1)}, u32[]{:S(2)}, u32[]{:S(2)}) collective-permute-start(bf16[3,16,32,128]{3,2,1,0:T(8,128)(2,1)S(1)} %get-tuple-element.156), channel_id=1, source_target_pairs={{0,1},{1,0},{2,3},{3,2},{4,5},{5,4},{6,7},{7,6},{8,9},{9,8},{10,11... | collective-permute-start | bytes 1179656 | tf_op jit(solution)/shard_map/ppermute | solution.py:479
  88.3 134.6 %reduce-scatter.5.cloned.1.call-start = ((), (), s32[]{:S(2)}) async-start(), calls=%async_computation.4 | async-start | bytes 3932160 | tf_op jit(solution)/shard_map/reduce_scatter | solution.py:660
  90.0 14.4 %collective-permute-start.10 = (bf16[2,1,16,32,128]{4,3,2,1,0:T(8,128)(2,1)S(1)}, bf16[2,1,16,32,128]{4,3,2,1,0:T(8,128)(2,1)S(1)}, u32[]{:S(2)}, u32[]{:S(2)}) collective-permute-start(bf16[2,1,16,32,128]{4,3,2,1,0:T(8,128)(2,1)S(1)} %pad_maximum_fusion.2.refs_0_), channel_id=1, source_target_pairs={{7,5},{6,4},{5,3},{4,2},{3,1},{2,0},{15,13},{14,12},{13,11},{12,10... | collective-permute-start | bytes 786440 | tf_op jit(solution)/shard_map/ppermute | solution.py:504
  91.3 13.1 %collective-permute-start.9 = (bf16[2,1,16,32,128]{4,3,2,1,0:T(8,128)(2,1)S(1)}, bf16[2,1,16,32,128]{4,3,2,1,0:T(8,128)(2,1)}, u32[]{:S(2)}, u32[]{:S(2)}) collective-permute-start(bf16[2,1,16,32,128]{4,3,2,1,0:T(8,128)(2,1)S(1)} %pad_maximum_fusion.2.refs_0_), channel_id=1, source_target_pairs={{0,2},{1,3},{2,4},{3,5},{4,6},{5,7},{8,10},{9,11},{10,12},{11,13},... | collective-permute-start | bytes 786440 | tf_op jit(solution)/shard_map/ppermute | solution.py:503
  105.7 23.6 %collective-permute-start.11 = (bf16[2,1,16,32,128]{4,3,2,1,0:T(8,128)(2,1)}, bf16[2,1,16,32,128]{4,3,2,1,0:T(8,128)(2,1)}, u32[]{:S(2)}, u32[]{:S(2)}) collective-permute-start(bf16[2,1,16,32,128]{4,3,2,1,0:T(8,128)(2,1)} %collective-permute-done.9.refs_1_), channel_id=1, source_target_pairs={{2,4},{3,5},{4,6},{5,7},{10,12},{11,13},{12,14},{13,15},{18,20},{1... | collective-permute-start | bytes 786440 | tf_op jit(solution)/shard_map/ppermute | solution.py:503
  107.1 22.2 %collective-permute-start.12 = (bf16[2,1,16,32,128]{4,3,2,1,0:T(8,128)(2,1)S(1)}, bf16[2,1,16,32,128]{4,3,2,1,0:T(8,128)(2,1)}, u32[]{:S(2)}, u32[]{:S(2)}) collective-permute-start(bf16[2,1,16,32,128]{4,3,2,1,0:T(8,128)(2,1)S(1)} %collective-permute-done.10.refs_4_), channel_id=1, source_target_pairs={{5,3},{4,2},{3,1},{2,0},{13,11},{12,10},{11,9},{10,8},{21,19},{20,... | collective-permute-start | bytes 786440 | tf_op jit(solution)/shard_map/ppermute | solution.py:504
  130.3 28.6 %collective-permute-start.14 = (bf16[2,1,16,32,128]{4,3,2,1,0:T(8,128)(2,1)}, bf16[2,1,16,32,128]{4,3,2,1,0:T(8,128)(2,1)}, u32[]{:S(2)}, u32[]{:S(2)}) collective-permute-start(bf16[2,1,16,32,128]{4,3,2,1,0:T(8,128)(2,1)} %collective-permute-done.11.refs_2_), channel_id=1, source_target_pairs={{4,6},{5,7},{12,14},{13,15},{20,22},{21,23},{28,30},{29,31}} | collective-permute-start | bytes 786440 | tf_op jit(solution)/shard_map/ppermute | solution.py:503
  131.7 27.4 %collective-permute-start.15 = (bf16[2,1,16,32,128]{4,3,2,1,0:T(8,128)(2,1)}, bf16[2,1,16,32,128]{4,3,2,1,0:T(8,128)(2,1)}, u32[]{:S(2)}, u32[]{:S(2)}) collective-permute-start(bf16[2,1,16,32,128]{4,3,2,1,0:T(8,128)(2,1)} %collective-permute-done.12.refs_5_), channel_id=1, source_target_pairs={{3,1},{2,0},{11,9},{10,8},{19,17},{18,16},{27,25},{26,24}} | collective-permute-start | bytes 786440 | tf_op jit(solution)/shard_map/ppermute | solution.py:504
  159.1 136.1 %reduce-scatter.7.cloned.1.call-start = ((), (), s32[]{:S(2)}) async-start(), calls=%async_computation.5 | async-start | bytes 3932160 | tf_op jit(solution)/shard_map/reduce_scatter | solution.py:660
  215.4 132.4 %all-gather.15.cloned.1.call-start = ((), (), s32[]{:S(2)}) async-start(), calls=%async_computation.11 | async-start | bytes 2621440 | tf_op jit(solution)/shard_map/all_gather | solution.py:624
  223.0 10.7 %collective-permute-start.20 = (bf16[2,3,16,32,128]{4,3,2,1,0:T(8,128)(2,1)}, bf16[2,3,16,32,128]{4,3,2,1,0:T(8,128)(2,1)}, u32[]{:S(2)}, u32[]{:S(2)}) collective-permute-start(bf16[2,3,16,32,128]{4,3,2,1,0:T(8,128)(2,1)} %bitcast.64), channel_id=1, source_target_pairs={{0,1},{1,0},{2,3},{3,2},{4,5},{5,4},{6,7},{7,6},{8,9},{9,8},{10,11... | collective-permute-start | bytes 2359304 | tf_op jit(solution)/shard_map/ppermute | solution.py:479
  253.1 159.7 %all-gather.13.cloned.1.call-start = ((), (), s32[]{:S(2)}) async-start(), calls=%async_computation.10 | async-start | bytes 2621440 | tf_op jit(solution)/shard_map/all_gather | solution.py:624
  253.1 22.1 %collective-permute-start.26 = (bf16[2,1,16,32,128]{4,3,2,1,0:T(8,128)(2,1)S(1)}, bf16[2,1,16,32,128]{4,3,2,1,0:T(8,128)(2,1)S(1)}, u32[]{:S(2)}, u32[]{:S(2)}) collective-permute-start(bf16[2,1,16,32,128]{4,3,2,1,0:T(8,128)(2,1)S(1)} %pad_maximum_fusion.1.refs_0_), channel_id=1, source_target_pairs={{7,5},{6,4},{5,3},{4,2},{3,1},{2,0},{15,13},{14,12},{13,11},{12,10... | collective-permute-start | bytes 786440 | tf_op jit(solution)/shard_map/ppermute | solution.py:504
  254.4 22.1 %collective-permute-start.24 = (bf16[2,1,16,32,128]{4,3,2,1,0:T(8,128)(2,1)S(1)}, bf16[2,1,16,32,128]{4,3,2,1,0:T(8,128)(2,1)S(1)}, u32[]{:S(2)}, u32[]{:S(2)}) collective-permute-start(bf16[2,1,16,32,128]{4,3,2,1,0:T(8,128)(2,1)S(1)} %pad_maximum_fusion.1.refs_0_), channel_id=1, source_target_pairs={{0,2},{1,3},{2,4},{3,5},{4,6},{5,7},{8,10},{9,11},{10,12},{11,13},... | collective-permute-start | bytes 786440 | tf_op jit(solution)/shard_map/ppermute | solution.py:503
  275.2 20.7 %collective-permute-start.27 = (bf16[2,1,16,32,128]{4,3,2,1,0:T(8,128)(2,1)S(1)}, bf16[2,1,16,32,128]{4,3,2,1,0:T(8,128)(2,1)S(1)}, u32[]{:S(2)}, u32[]{:S(2)}) collective-permute-start(bf16[2,1,16,32,128]{4,3,2,1,0:T(8,128)(2,1)S(1)} %collective-permute-done.26.refs_4_), channel_id=1, source_target_pairs={{5,3},{4,2},{3,1},{2,0},{13,11},{12,10},{11,9},{10,8},{21,19},{20,... | collective-permute-start | bytes 786440 | tf_op jit(solution)/shard_map/ppermute | solution.py:504
  276.5 19.4 %collective-permute-start.25 = (bf16[2,1,16,32,128]{4,3,2,1,0:T(8,128)(2,1)S(1)}, bf16[2,1,16,32,128]{4,3,2,1,0:T(8,128)(2,1)S(1)}, u32[]{:S(2)}, u32[]{:S(2)}) collective-permute-start(bf16[2,1,16,32,128]{4,3,2,1,0:T(8,128)(2,1)S(1)} %collective-permute-done.24.refs_1_), channel_id=1, source_target_pairs={{2,4},{3,5},{4,6},{5,7},{10,12},{11,13},{12,14},{13,15},{18,20},{1... | collective-permute-start | bytes 786440 | tf_op jit(solution)/shard_map/ppermute | solution.py:503
  277.9 17.3 %collective-permute-start.32 = (bf16[3,4,32,128]{3,2,1,0:T(8,128)(2,1)S(1)}, bf16[3,4,32,128]{3,2,1,0:T(8,128)(2,1)S(1)}, u32[]{:S(2)}, u32[]{:S(2)}) collective-permute-start(bf16[3,4,32,128]{3,2,1,0:T(8,128)(2,1)S(1)} %get-tuple-element.107), channel_id=1, source_target_pairs={{0,8},{8,16},{16,24},{1,9},{9,17},{17,25},{2,10},{10,18},{18,26},{... | collective-permute-start | bytes 294920 | tf_op jit(solution)/shard_map/ppermute | solution.py:461
  281.1 14.2 %collective-permute-start.33 = (bf16[3,4,32,128]{3,2,1,0:T(8,128)(2,1)S(1)}, bf16[3,4,32,128]{3,2,1,0:T(8,128)(2,1)S(1)}, u32[]{:S(2)}, u32[]{:S(2)}) collective-permute-start(bf16[3,4,32,128]{3,2,1,0:T(8,128)(2,1)S(1)} %get-tuple-element.109), channel_id=1, source_target_pairs={{8,0},{16,8},{24,16},{9,1},{17,9},{25,17},{10,2},{18,10},{26,18},{... | collective-permute-start | bytes 294920 | tf_op jit(solution)/shard_map/ppermute | solution.py:461
  295.9 10.8 %collective-permute-start.34 = (bf16[2,3,16,32,128]{4,3,2,1,0:T(8,128)(2,1)}, bf16[2,3,16,32,128]{4,3,2,1,0:T(8,128)(2,1)S(1)}, u32[]{:S(2)}, u32[]{:S(2)}) collective-permute-start(bf16[2,3,16,32,128]{4,3,2,1,0:T(8,128)(2,1)} %bitcast.61), channel_id=1, source_target_pairs={{0,1},{1,0},{2,3},{3,2},{4,5},{5,4},{6,7},{7,6},{8,9},{9,8},{10,11... | collective-permute-start | bytes 2359304 | tf_op jit(solution)/shard_map/ppermute | solution.py:479
  326.4 138.9 %reduce-scatter.11.cloned.1.call-start = ((), (), s32[]{:S(2)}) async-start(), calls=%async_computation.7 | async-start | bytes 3932160 | tf_op jit(solution)/shard_map/reduce_scatter | solution.py:660
  326.4 20.7 %collective-permute-start.41 = (bf16[2,1,16,32,128]{4,3,2,1,0:T(8,128)(2,1)S(1)}, bf16[2,1,16,32,128]{4,3,2,1,0:T(8,128)(2,1)S(1)}, u32[]{:S(2)}, u32[]{:S(2)}) collective-permute-start(bf16[2,1,16,32,128]{4,3,2,1,0:T(8,128)(2,1)S(1)} %pad_maximum_fusion.refs_0_), channel_id=1, source_target_pairs={{7,5},{6,4},{5,3},{4,2},{3,1},{2,0},{15,13},{14,12},{13,11},{12,10... | collective-permute-start | bytes 786440 | tf_op jit(solution)/shard_map/ppermute | solution.py:504
  327.7 20.1 %collective-permute-start.40 = (bf16[2,1,16,32,128]{4,3,2,1,0:T(8,128)(2,1)S(1)}, bf16[2,1,16,32,128]{4,3,2,1,0:T(8,128)(2,1)}, u32[]{:S(2)}, u32[]{:S(2)}) collective-permute-start(bf16[2,1,16,32,128]{4,3,2,1,0:T(8,128)(2,1)S(1)} %pad_maximum_fusion.refs_0_), channel_id=1, source_target_pairs={{0,2},{1,3},{2,4},{3,5},{4,6},{5,7},{8,10},{9,11},{10,12},{11,13},... | collective-permute-start | bytes 786440 | tf_op jit(solution)/shard_map/ppermute | solution.py:503
  333.1 17.4 %collective-permute-start.44 = (bf16[2,1,16,32,128]{4,3,2,1,0:T(8,128)(2,1)}, bf16[2,1,16,32,128]{4,3,2,1,0:T(8,128)(2,1)}, u32[]{:S(2)}, u32[]{:S(2)}) collective-permute-start(bf16[2,1,16,32,128]{4,3,2,1,0:T(8,128)(2,1)} %copy-done.33), channel_id=1, source_target_pairs={{4,6},{5,7},{12,14},{13,15},{20,22},{21,23},{28,30},{29,31}} | collective-permute-start | bytes 786440 | tf_op jit(solution)/shard_map/ppermute | solution.py:503
  334.5 18.3 %collective-permute-start.45 = (bf16[2,1,16,32,128]{4,3,2,1,0:T(8,128)(2,1)}, bf16[2,1,16,32,128]{4,3,2,1,0:T(8,128)(2,1)}, u32[]{:S(2)}, u32[]{:S(2)}) collective-permute-start(bf16[2,1,16,32,128]{4,3,2,1,0:T(8,128)(2,1)} %copy-done.31), channel_id=1, source_target_pairs={{3,1},{2,0},{11,9},{10,8},{19,17},{18,16},{27,25},{26,24}} | collective-permute-start | bytes 786440 | tf_op jit(solution)/shard_map/ppermute | solution.py:504
  347.9 27.9 %collective-permute-start.42 = (bf16[2,1,16,32,128]{4,3,2,1,0:T(8,128)(2,1)}, bf16[2,1,16,32,128]{4,3,2,1,0:T(8,128)(2,1)}, u32[]{:S(2)}, u32[]{:S(2)}) collective-permute-start(bf16[2,1,16,32,128]{4,3,2,1,0:T(8,128)(2,1)} %collective-permute-done.40.refs_1_), channel_id=1, source_target_pairs={{2,4},{3,5},{4,6},{5,7},{10,12},{11,13},{12,14},{13,15},{18,20},{1... | collective-permute-start | bytes 786440 | tf_op jit(solution)/shard_map/ppermute | solution.py:503
  349.3 26.6 %collective-permute-start.43 = (bf16[2,1,16,32,128]{4,3,2,1,0:T(8,128)(2,1)}, bf16[2,1,16,32,128]{4,3,2,1,0:T(8,128)(2,1)}, u32[]{:S(2)}, u32[]{:S(2)}) collective-permute-start(bf16[2,1,16,32,128]{4,3,2,1,0:T(8,128)(2,1)} %copy-done.35), channel_id=1, source_target_pairs={{5,3},{4,2},{3,1},{2,0},{13,11},{12,10},{11,9},{10,8},{21,19},{20,... | collective-permute-start | bytes 786440 | tf_op jit(solution)/shard_map/ppermute | solution.py:504
  376.3 27.1 %collective-permute-start.46 = (bf16[2,1,16,32,128]{4,3,2,1,0:T(8,128)(2,1)}, bf16[2,1,16,32,128]{4,3,2,1,0:T(8,128)(2,1)}, u32[]{:S(2)}, u32[]{:S(2)}) collective-permute-start(bf16[2,1,16,32,128]{4,3,2,1,0:T(8,128)(2,1)} %collective-permute-done.42.refs_2_), channel_id=1, source_target_pairs={{4,6},{5,7},{12,14},{13,15},{20,22},{21,23},{28,30},{29,31}} | collective-permute-start | bytes 786440 | tf_op jit(solution)/shard_map/ppermute | solution.py:503
  377.6 25.7 %collective-permute-start.47 = (bf16[2,1,16,32,128]{4,3,2,1,0:T(8,128)(2,1)}, bf16[2,1,16,32,128]{4,3,2,1,0:T(8,128)(2,1)}, u32[]{:S(2)}, u32[]{:S(2)}) collective-permute-start(bf16[2,1,16,32,128]{4,3,2,1,0:T(8,128)(2,1)} %collective-permute-done.43.refs_5_), channel_id=1, source_target_pairs={{3,1},{2,0},{11,9},{10,8},{19,17},{18,16},{27,25},{26,24}} | collective-permute-start | bytes 786440 | tf_op jit(solution)/shard_map/ppermute | solution.py:504
  403.4 124.5 %reduce-scatter.9.cloned.1.call-start = ((), (), s32[]{:S(2)}) async-start(), calls=%async_computation.6 | async-start | bytes 3932160 | tf_op jit(solution)/shard_map/reduce_scatter | solution.py:660
  (87 other events, 572.4 us)
Sparse Core Ops, SparseCore 0:
  37.7 67.9 all-gather.10
  107.3 52.1 all-gather.8
  162.3 60.6 reduce-scatter.4
  225.7 69.4 reduce-scatter.6
  296.6 49.3 all-gather.14
  347.5 52.2 all-gather.12
  403.5 61.6 reduce-scatter.10
  467.6 60.2 reduce-scatter.8

commit v11 on v10

--- a/solution.py
+++ b/solution.py
@@ -105,8 +105,8 @@
     field = pl.BlockSpec((1, rows, steps, cols), lambda b, core: (b, 0, 0, 0))
     rim = pl.BlockSpec((1, HALO, steps, cols), lambda b, core: (b, 0, 0, 0))
     misfits = [
-        pl.BlockSpec((None, 1, count, steps, cols), lambda b, core, place=place: (place, b, 0, 0, 0))
-        for place, count in ((0, rows // 2), (1, rows // 2), (0, HALO), (1, HALO))
+        pl.BlockSpec((None, 1, count, steps, cols), lambda b, core: (0, b, 0, 0, 0))
+        for count in (rows // 2, rows // 2, HALO, HALO)
     ]
 
     def shape(count, dtype):
@@ -528,6 +528,7 @@
     core = sensor_index % 2
     near = LANES // sensors
     half = cells // 2
+    other_map = swap_cores(forward_map)
 
     cores = jnp.stack([core, 1 - core])
     offsets = cores[None, :, None] * steps + jnp.arange(steps, dtype=jnp.int32)
@@ -550,15 +551,20 @@
         return jnp.transpose(lax.optimization_barrier(part), (1, 2, 0, 3))
 
     def packed(first):
-        part = rim_rows(groups[0], first).reshape(members * HALO, steps, cols)
-        extra = local[:, first : first + HALO].reshape(2 * HALO, cols)
-        extra = jnp.pad(extra, ((0, -2 * HALO % steps), (0, 0))).reshape(-1, steps, cols)
+        part = rim_rows(groups[0], first).astype(jnp.bfloat16).reshape(members * HALO, steps, cols)
+        value, terms = local[:, first : first + HALO].reshape(2 * HALO, cols), []
+        for _ in range(3):
+            terms.append(lax.optimization_barrier(value.astype(jnp.bfloat16)))
+            value = value - terms[-1].astype(jnp.float32)
+        extra = jnp.concatenate(terms, axis=0)
+        extra = jnp.pad(extra, ((0, -6 * HALO % steps), (0, 0))).reshape(-1, steps, cols)
         return jnp.concatenate([part, extra], axis=0)
 
     def unpacked(value):
         part = value[: members * HALO].reshape(members, HALO, steps, cols)
-        extra = value[members * HALO :].reshape(-1, cols)[: 2 * HALO].reshape(2, HALO, cols)
-        return part, extra
+        extra = value[members * HALO :].reshape(-1, cols)[: 6 * HALO].astype(jnp.float32)
+        high, middle, low = extra.reshape(3, 2, HALO, cols)
+        return part, high + (middle + low)
 
     (up_first, up), (down_first, down) = (
         unpacked(value) for value in rims(packed(0), packed(rows - HALO))
@@ -602,11 +608,11 @@
     def edges(misfit):
         first = (rows // 2 - HALO) * core[0]
         edge = lax.dynamic_slice_in_dim(misfit, first, HALO, axis=2)
-        return misfit, swap_cores(misfit), *misfit_rims(edge)
+        same, _ = misfit_rims(edge[:1])
+        _, cross = misfit_rims(edge[1:])
+        return misfit, swap_cores(misfit[1:]), same, cross
 
     iterate, low, rest, *ends = start(0, members, core, rhs, up_first, down_first, coeff)
-    low, whole_map = lax.optimization_barrier((low, forward_map))
-    other_map = swap_cores(whole_map)
     above, below = rims(*ends)
     states = [(iterate, low, None, (above, rest, below))]
     for group in range(1, GROUPS):

time: 561 us -> 557 us (level)
  waiting for transfers between devices: 186 us -> 207 us
  starting transfers between devices: 122 us -> 102 us
    ppermute x9, waiting for transfers between devices: 0.02 us -> 27.9 us  [hop(): up = lax.ppermute(self.ends[0], 'sensors', onward)]
    ppermute x12, waiting for transfers between devices: 23.4 us -> 6.76 us  [swap_cores(): return lax.ppermute(value, 'sensors', [(k, k ^ 1) for k in range(size)])]
    all_gather x4, waiting for transfers between devices: 1.26 us -> 14.5 us  [shards(): lax.all_gather(state[1], 'sensors', axis_index_groups=None if state[2] is...]
    ppermute x12, starting transfers between devices: 21.4 us -> 11.7 us  [swap_cores(): return lax.ppermute(value, 'sensors', [(k, k ^ 1) for k in range(size)])]
    slice x2 -> x8, local copies, waits for them, and re-layouts: 0.01 us -> 8.65 us  [the longest x4 4.83 us: edges(): return (misfit, swap_cores(misfit[1:]), same, cross)]
    ppermute x9, waiting for transfers between devices: 38.3 us -> 30.6 us  [hop(): down = lax.ppermute(self.ends[1], 'sensors', backward)]
    ppermute x9, starting transfers between devices: 21.6 us -> 15 us  [hop(): up = lax.ppermute(self.ends[0], 'sensors', onward)]
    ppermute x8, waiting for transfers between devices: 10.9 us -> 17.5 us  [misfit_rims(): return (lax.ppermute(edge, both, same), lax.ppermute(edge, both, cross))]
  transfers between devices with their start and end apart: 70 -> 70, of which waited for: 35 -> 44; matrix products, arithmetic and copies ran while one was open for 2% -> 4% of each run, Pallas kernels for 28% -> 30%
where the time goes in v11:
time: 557 us; the launch traced here: 555 us
  waiting for transfers between devices  207 us (37%)
  Pallas kernels  170 us (31%)
  starting transfers between devices  102 us (18%)
  local copies, waits for them, and re-layouts  52.3 us (9%)
  between operations  15.1 us (3%)
  other arithmetic  8.41 us (2%)
    pallas_call x4, Pallas kernels, observe(): call(observe_kernel, core, (chunks,), [pl.BlockSpec(block, lambda c, core...  70.8 us
    reduce_scatter x4, waiting for transfers between devices, shards(): lax.psum_scatter(misfit, 'sensors', scatter_dimension=0, axis_index_group...  69.6 us
    pallas_call x4, Pallas kernels, pull_back(): call(pull_kernel, core, (rows // CHUNK_ROWS,), [whole_block(array) for ar...  58.4 us
    unnamed x74, local copies, waits for them, and re-layouts  39.9 us
    ppermute x9, waiting for transfers between devices, hop(): down = lax.ppermute(self.ends[1], 'sensors', backward)  30.6 us
    ppermute x9, waiting for transfers between devices, hop(): up = lax.ppermute(self.ends[0], 'sensors', onward)  27.9 us
    ppermute x8, starting transfers between devices, misfit_rims(): return (lax.ppermute(edge, both, same), lax.ppermute(edge, both, cross))  21.9 us
    ppermute x6, starting transfers between devices, rims(): lax.ppermute(bottom, 'cells', onward)  21.8 us
  transfers between devices with their start and end apart: 70, of which 44 were waited for; matrix products, arithmetic and copies ran while one was open for 4% of the time, Pallas kernels for 30%

profile of v11, /device:TPU:1, one launch (start us, length us, event | category | flops | bytes accessed | tf_op | source)
XLA Modules:
  0.0 554.8 jit_solution(13399043073623174955)
XLA Ops:
  10.4 4.6 collective-permute-start
  24.8 6.9 %start.2 = (f32[3,32,32,128]{3,2,1,0:T(8,128)S(1)}, bf16[3,32,32,128]{3,2,1,0:T(8,128)(2,1)}, f32[3,32,32,128]{3,2,1,0:T(8,128)S(1)}, bf16[3,4,32,128]{3,2,1,0:T(8,128)(2,1)S(1)}, bf16[3,4,32,128]{3,2,1,0:T(8,128)(2,1)S(1)}) custom-call(s32[1]{0:T(128)} %bitcast.core_ref, f32[32,192,128]{2,1,0:T(8,128)S(1)} %bitcast.63, ...), custom_call_target="tpu_custom_call" | custom-call | tf_op jit(solution)/shard_map/start/pallas_call | solution.py:151
  34.0 4.0 collective-permute-start.2
  48.7 4.6 collective-permute-done.5.down_ref
  55.2 6.8 %start.3 = (f32[3,32,32,128]{3,2,1,0:T(8,128)S(1)}, bf16[3,32,32,128]{3,2,1,0:T(8,128)(2,1)S(1)}, f32[3,32,32,128]{3,2,1,0:T(8,128)S(1)}, bf16[3,4,32,128]{3,2,1,0:T(8,128)(2,1)}, bf16[3,4,32,128]{3,2,1,0:T(8,128)(2,1)}) custom-call(s32[1]{0:T(128)} %bitcast.core_ref, f32[32,192,128]{2,1,0:T(8,128)S(1)} %bitcast.64, ...), custom_call_target="tpu_custom_call" | custom-call | tf_op jit(solution)/shard_map/start/pallas_call | solution.py:151
  75.6 9.3 %collective-permute-done.9.refs_1_ = bf16[2,1,16,32,128]{4,3,2,1,0:T(8,128)(2,1)S(1)} collective-permute-done((bf16[2,1,16,32,128]{4,3,2,1,0:T(8,128)(2,1)S(1)}, bf16[2,1,16,32,128]{4,3,2,1,0:T(8,128)(2,1)S(1)}, u32[]{:S(2)}, u32[]{:S(2)}) %collective-permute-start.9) | collective-permute-done | bytes 262176 | tf_op jit(solution)/shard_map/ppermute | solution.py:503
  84.9 9.6 %collective-permute-done.10.refs_4_ = bf16[2,1,16,32,128]{4,3,2,1,0:T(8,128)(2,1)} collective-permute-done((bf16[2,1,16,32,128]{4,3,2,1,0:T(8,128)(2,1)S(1)}, bf16[2,1,16,32,128]{4,3,2,1,0:T(8,128)(2,1)}, u32[]{:S(2)}, u32[]{:S(2)}) %collective-permute-start.10) | collective-permute-done | bytes 262176 | tf_op jit(solution)/shard_map/ppermute | solution.py:504
  94.5 11.8 %all-gather.11.cloned.1.call-done = bf16[24,32,32,128]{3,2,1,0:T(8,128)(2,1)} async-done(((bf16[3,32,32,128]{3,2,1,0:T(8,128)(2,1)}), bf16[24,32,32,128]{3,2,1,0:T(8,128)(2,1)}) %all-gather.11.cloned.1.call-update) | async-done | bytes 6291472 | tf_op jit(solution)/shard_map/all_gather | solution.py:630
  112.5 17.8 %observe.4 = f32[2,2,3,16,128]{4,3,2,1,0:T(8,128)S(1)} custom-call(s32[1]{0:T(128)} %bitcast.core_ref, bf16[8,3,32,32,128]{4,3,2,1,0:T(8,128)(2,1)S(1)} %bitcast.65, bf16[2,128,16,4096]{3,2,1,0:T(8,128)(2,1)} %refs_5_.7, bf16[2,128,16,4096]{3,2,1,0:T(8,128)(2,1)} %collective-permute-done.13.refs_1_.refs_6_.refs_8_, bf16[256,256]{1,0:T(8,128)(2,1)S(1)} %copy.38.refs_2_, ...), custom_call_target="tpu_custom_call" | custom-call | flops 402653184 | bytes 39845888 | tf_op jit(solution)/shard_map/observe/pallas_call | solution.py:363
  141.3 14.6 %pull_back.4 = bf16[4,2,3,16,32,128]{5,4,3,2,1,0:T(8,128)(2,1)S(1)} custom-call(s32[1]{0:T(128)} %bitcast.core_ref, f32[2,2,3,16,128]{4,3,2,1,0:T(8,128)S(1)} %reverse_add_fusion.3.refs_0_, f32[2,2,3,16,128]{4,3,2,1,0:T(8,128)S(1)} %collective-permute-done.17.refs_1_, f32[2,2,3,16,128]{4,3,2,1,0:T(8,128)S(1)} %collective-permute-done.18.refs_2_, ...), custom_call_target="tpu_custom_call" | custom-call | flops 402653184 | bytes 36700160 | tf_op jit(solution)/shard_map/pull_back/pallas_call | solution.py:437
  169.6 17.7 %observe.5 = f32[2,2,3,16,128]{4,3,2,1,0:T(8,128)S(1)} custom-call(s32[1]{0:T(128)} %bitcast.core_ref, bf16[4,2,2,16,32,128]{5,4,3,2,1,0:T(8,128)(2,1)S(1)} %bitcast.74, bf16[2,1,16,32,128]{4,3,2,1,0:T(8,128)(2,1)S(1)} %pad_maximum_fusion.2.refs_0_, bf16[2,1,16,32,128]{4,3,2,1,0:T(8,128)(2,1)S(1)} %collective-permute-done.9.refs_1_, ...), custom_call_target="tpu_custom_call" | custom-call | flops 402653184 | bytes 35651584 | tf_op jit(solution)/shard_map/observe/pallas_call | solution.py:363
  197.7 14.6 %pull_back.5 = bf16[4,2,3,16,32,128]{5,4,3,2,1,0:T(8,128)(2,1)S(1)} custom-call(s32[1]{0:T(128)} %bitcast.core_ref, f32[2,2,3,16,128]{4,3,2,1,0:T(8,128)S(1)} %reverse_add_fusion.2.refs_0_, f32[2,2,3,16,128]{4,3,2,1,0:T(8,128)S(1)} %collective-permute-done.29.refs_1_, f32[2,2,3,16,128]{4,3,2,1,0:T(8,128)S(1)} %collective-permute-done.30.refs_2_, ...), custom_call_target="tpu_custom_call" | custom-call | flops 402653184 | bytes 36700160 | tf_op jit(solution)/shard_map/pull_back/pallas_call | solution.py:437
  214.1 7.3 %reduce-scatter.5.cloned.1.call-done = bf16[1,2,3,16,32,128]{5,4,3,2,1,0:T(8,128)(2,1)} async-done(((bf16[4,2,3,16,32,128]{5,4,3,2,1,0:T(8,128)(2,1)}), bf16[1,2,3,16,32,128]{5,4,3,2,1,0:T(8,128)(2,1)}) %reduce-scatter.5.cloned.1.call-update) | async-done | bytes 786448 | tf_op jit(solution)/shard_map/reduce_scatter | solution.py:666
  230.4 4.6 collective-permute-done.22.cross_ref
  239.0 6.3 %step.2 = (f32[3,32,32,128]{3,2,1,0:T(8,128)S(1)}, bf16[3,32,32,128]{3,2,1,0:T(8,128)(2,1)S(1)}, f32[3,32,32,128]{3,2,1,0:T(8,128)S(1)}, bf16[3,4,32,128]{3,2,1,0:T(8,128)(2,1)S(1)}, bf16[3,4,32,128]{3,2,1,0:T(8,128)(2,1)S(1)}) custom-call(s32[1]{0:T(128)} %bitcast.core_ref, bf16[3,4,32,128]{3,2,1,0:T(8,128)(2,1)S(1)} %collective-permute-done.2.up_ref, ...), custom_call_target="tpu_custom_call" | custom-call | tf_op jit(solution)/shard_map/step/pallas_call | solution.py:203
  254.4 10.4 %collective-permute-done.24.refs_1_ = bf16[2,1,16,32,128]{4,3,2,1,0:T(8,128)(2,1)S(1)} collective-permute-done((bf16[2,1,16,32,128]{4,3,2,1,0:T(8,128)(2,1)S(1)}, bf16[2,1,16,32,128]{4,3,2,1,0:T(8,128)(2,1)S(1)}, u32[]{:S(2)}, u32[]{:S(2)}) %collective-permute-start.24) | collective-permute-done | bytes 262176 | tf_op jit(solution)/shard_map/ppermute | solution.py:503
  266.2 7.4 %collective-permute-done.26.refs_4_ = bf16[2,1,16,32,128]{4,3,2,1,0:T(8,128)(2,1)} collective-permute-done((bf16[2,1,16,32,128]{4,3,2,1,0:T(8,128)(2,1)S(1)}, bf16[2,1,16,32,128]{4,3,2,1,0:T(8,128)(2,1)}, u32[]{:S(2)}, u32[]{:S(2)}) %collective-permute-start.26) | collective-permute-done | bytes 262176 | tf_op jit(solution)/shard_map/ppermute | solution.py:504
  279.3 13.3 %reduce-scatter.7.cloned.1.call-done = bf16[1,2,3,16,32,128]{5,4,3,2,1,0:T(8,128)(2,1)} async-done(((bf16[4,2,3,16,32,128]{5,4,3,2,1,0:T(8,128)(2,1)}), bf16[1,2,3,16,32,128]{5,4,3,2,1,0:T(8,128)(2,1)}) %reduce-scatter.7.cloned.1.call-update) | async-done | bytes 786448 | tf_op jit(solution)/shard_map/reduce_scatter | solution.py:666
  302.5 4.2 collective-permute-done.36.cross_ref
  309.2 7.7 %step.3 = (f32[3,32,32,128]{3,2,1,0:T(8,128)S(1)}, bf16[3,32,32,128]{3,2,1,0:T(8,128)(2,1)S(1)}, f32[3,32,32,128]{3,2,1,0:T(8,128)S(1)}, bf16[3,4,32,128]{3,2,1,0:T(8,128)(2,1)S(1)}, bf16[3,4,32,128]{3,2,1,0:T(8,128)(2,1)}) custom-call(s32[1]{0:T(128)} %bitcast.core_ref, bf16[3,4,32,128]{3,2,1,0:T(8,128)(2,1)} %collective-permute-done.7.up_ref, ...), custom_call_target="tpu_custom_call" | custom-call | tf_op jit(solution)/shard_map/step/pallas_call | solution.py:203
  328.5 8.2 %collective-permute-done.40.refs_1_ = bf16[2,1,16,32,128]{4,3,2,1,0:T(8,128)(2,1)S(1)} collective-permute-done((bf16[2,1,16,32,128]{4,3,2,1,0:T(8,128)(2,1)S(1)}, bf16[2,1,16,32,128]{4,3,2,1,0:T(8,128)(2,1)S(1)}, u32[]{:S(2)}, u32[]{:S(2)}) %collective-permute-start.40) | collective-permute-done | bytes 262176 | tf_op jit(solution)/shard_map/ppermute | solution.py:503
  336.7 8.9 %collective-permute-done.41.refs_4_ = bf16[2,1,16,32,128]{4,3,2,1,0:T(8,128)(2,1)S(1)} collective-permute-done((bf16[2,1,16,32,128]{4,3,2,1,0:T(8,128)(2,1)S(1)}, bf16[2,1,16,32,128]{4,3,2,1,0:T(8,128)(2,1)S(1)}, u32[]{:S(2)}, u32[]{:S(2)}) %collective-permute-start.41) | collective-permute-done | bytes 262176 | tf_op jit(solution)/shard_map/ppermute | solution.py:504
  353.9 17.8 %observe.6 = f32[2,2,3,16,128]{4,3,2,1,0:T(8,128)S(1)} custom-call(s32[1]{0:T(128)} %bitcast.core_ref, bf16[4,2,2,16,32,128]{5,4,3,2,1,0:T(8,128)(2,1)S(1)} %bitcast.75, bf16[2,1,16,32,128]{4,3,2,1,0:T(8,128)(2,1)S(1)} %pad_maximum_fusion.1.refs_0_, bf16[2,1,16,32,128]{4,3,2,1,0:T(8,128)(2,1)S(1)} %collective-permute-done.24.refs_1_, ...), custom_call_target="tpu_custom_call" | custom-call | flops 402653184 | bytes 35651584 | tf_op jit(solution)/shard_map/observe/pallas_call | solution.py:363
  381.9 14.6 %pull_back.6 = bf16[4,2,3,16,32,128]{5,4,3,2,1,0:T(8,128)(2,1)S(1)} custom-call(s32[1]{0:T(128)} %bitcast.core_ref, f32[2,2,3,16,128]{4,3,2,1,0:T(8,128)S(1)} %reverse_add_fusion.1.refs_0_, f32[2,2,3,16,128]{4,3,2,1,0:T(8,128)S(1)} %collective-permute-done.49.refs_1_, f32[2,2,3,16,128]{4,3,2,1,0:T(8,128)S(1)} %collective-permute-done.50.refs_2_, ...), custom_call_target="tpu_custom_call" | custom-call | flops 402653184 | bytes 36700160 | tf_op jit(solution)/shard_map/pull_back/pallas_call | solution.py:437
  409.1 17.6 %observe.7 = f32[2,2,3,16,128]{4,3,2,1,0:T(8,128)S(1)} custom-call(s32[1]{0:T(128)} %bitcast.core_ref, bf16[4,2,2,16,32,128]{5,4,3,2,1,0:T(8,128)(2,1)S(1)} %bitcast.76, bf16[2,1,16,32,128]{4,3,2,1,0:T(8,128)(2,1)S(1)} %pad_maximum_fusion.refs_0_, bf16[2,1,16,32,128]{4,3,2,1,0:T(8,128)(2,1)S(1)} %collective-permute-done.40.refs_1_, ...), custom_call_target="tpu_custom_call" | custom-call | flops 402653184 | bytes 35651584 | tf_op jit(solution)/shard_map/observe/pallas_call | solution.py:363
  437.9 14.6 %pull_back.7 = bf16[4,2,3,16,32,128]{5,4,3,2,1,0:T(8,128)(2,1)S(1)} custom-call(s32[1]{0:T(128)} %bitcast.core_ref, f32[2,2,3,16,128]{4,3,2,1,0:T(8,128)S(1)} %reverse_add_fusion.refs_0_, f32[2,2,3,16,128]{4,3,2,1,0:T(8,128)S(1)} %collective-permute-done.53.refs_1_, f32[2,2,3,16,128]{4,3,2,1,0:T(8,128)S(1)} %collective-permute-done.54.refs_2_, ...), custom_call_target="tpu_custom_call" | custom-call | flops 402653184 | bytes 36700160 | tf_op jit(solution)/shard_map/pull_back/pallas_call | solution.py:437
  454.2 8.7 %reduce-scatter.11.cloned.1.call-done = bf16[1,2,3,16,32,128]{5,4,3,2,1,0:T(8,128)(2,1)} async-done(((bf16[4,2,3,16,32,128]{5,4,3,2,1,0:T(8,128)(2,1)}), bf16[1,2,3,16,32,128]{5,4,3,2,1,0:T(8,128)(2,1)}) %reduce-scatter.11.cloned.1.call-update) | async-done | bytes 786448 | tf_op jit(solution)/shard_map/reduce_scatter | solution.py:666
  471.2 4.5 collective-permute-done.58.cross_ref
  478.3 6.8 %finish.2 = (f32[32,192,128]{2,1,0:T(8,128)}, f32[32,192,128]{2,1,0:T(8,128)}) custom-call(s32[1]{0:T(128)} %bitcast.core_ref, bf16[3,4,32,128]{3,2,1,0:T(8,128)(2,1)S(1)} %collective-permute-done.32.up_ref, f32[3,32,32,128]{3,2,1,0:T(8,128)S(1)} %copy-done.23, bf16[3,4,32,128]{3,2,1,0:T(8,128)(2,1)} %collective-permute-done.33.down_ref, ...), custom_call_target="tpu_custom_call" | custom-call | tf_op jit(solution)/shard_map/finish/pallas_call | solution.py:243
  485.1 40.3 %reduce-scatter.9.cloned.1.call-done = bf16[1,2,3,16,32,128]{5,4,3,2,1,0:T(8,128)(2,1)} async-done(((bf16[4,2,3,16,32,128]{5,4,3,2,1,0:T(8,128)(2,1)}), bf16[1,2,3,16,32,128]{5,4,3,2,1,0:T(8,128)(2,1)}) %reduce-scatter.9.cloned.1.call-update) | async-done | bytes 786448 | tf_op jit(solution)/shard_map/reduce_scatter | solution.py:666
  533.9 4.2 collective-permute-done.61.cross_ref
  542.0 6.0 %finish.3 = (f32[32,192,128]{2,1,0:T(8,128)}, f32[32,192,128]{2,1,0:T(8,128)}) custom-call(s32[1]{0:T(128)} %bitcast.core_ref, bf16[3,4,32,128]{3,2,1,0:T(8,128)(2,1)S(1)} %collective-permute-done.38.up_ref, f32[3,32,32,128]{3,2,1,0:T(8,128)S(1)} %copy-done.27, ...), custom_call_target="tpu_custom_call", output_to_operand_aliasing={{0}: (10, {}), {1}: (11, {})} | custom-call | tf_op jit(solution)/shard_map/finish/pallas_call | solution.py:243
  (276 shorter events, 204.1 us)
Async XLA Ops:
  7.2 99.2 %all-gather.11.cloned.1.call-start = ((), (), s32[]{:S(2)}) async-start(), calls=%async_computation.9 | async-start | bytes 7077888 | tf_op jit(solution)/shard_map/all_gather | solution.py:630
  7.2 102.4 %collective-permute-start.13 = (bf16[2,128,16,4096]{3,2,1,0:T(8,128)(2,1)}, bf16[2,128,16,4096]{3,2,1,0:T(8,128)(2,1)}, u32[]{:S(2)}, u32[]{:S(2)}) collective-permute-start(bf16[2,128,16,4096]{3,2,1,0:T(8,128)(2,1)} %refs_5_.7), channel_id=1, source_target_pairs={{0,1},{1,0},{2,3},{3,2},{4,5},{5,4},{6,7},{7,6},{8,9},{9,8},{10,11... | collective-permute-start | bytes 100663304 | tf_op jit(solution)/shard_map/ppermute | solution.py:479
  34.0 134.0 %all-gather.9.cloned.1.call-start = ((), (), s32[]{:S(2)}) async-start(), calls=%async_computation.8 | async-start | bytes 2621440 | tf_op jit(solution)/shard_map/all_gather | solution.py:630
  68.7 152.7 %reduce-scatter.5.cloned.1.call-start = ((), (), s32[]{:S(2)}) async-start(), calls=%async_computation.4 | async-start | bytes 3932160 | tf_op jit(solution)/shard_map/reduce_scatter | solution.py:666
  70.3 14.5 %collective-permute-start.9 = (bf16[2,1,16,32,128]{4,3,2,1,0:T(8,128)(2,1)S(1)}, bf16[2,1,16,32,128]{4,3,2,1,0:T(8,128)(2,1)S(1)}, u32[]{:S(2)}, u32[]{:S(2)}) collective-permute-start(bf16[2,1,16,32,128]{4,3,2,1,0:T(8,128)(2,1)S(1)} %pad_maximum_fusion.2.refs_0_), channel_id=1, source_target_pairs={{0,2},{1,3},{2,4},{3,5},{4,6},{5,7},{8,10},{9,11},{10,12},{11,13},... | collective-permute-start | bytes 786440 | tf_op jit(solution)/shard_map/ppermute | solution.py:503
  73.5 21.0 %collective-permute-start.10 = (bf16[2,1,16,32,128]{4,3,2,1,0:T(8,128)(2,1)S(1)}, bf16[2,1,16,32,128]{4,3,2,1,0:T(8,128)(2,1)}, u32[]{:S(2)}, u32[]{:S(2)}) collective-permute-start(bf16[2,1,16,32,128]{4,3,2,1,0:T(8,128)(2,1)S(1)} %pad_maximum_fusion.2.refs_0_), channel_id=1, source_target_pairs={{7,5},{6,4},{5,3},{4,2},{3,1},{2,0},{15,13},{14,12},{13,11},{12,10... | collective-permute-start | bytes 786440 | tf_op jit(solution)/shard_map/ppermute | solution.py:504
  106.3 23.9 %collective-permute-start.11 = (bf16[2,1,16,32,128]{4,3,2,1,0:T(8,128)(2,1)S(1)}, bf16[2,1,16,32,128]{4,3,2,1,0:T(8,128)(2,1)}, u32[]{:S(2)}, u32[]{:S(2)}) collective-permute-start(bf16[2,1,16,32,128]{4,3,2,1,0:T(8,128)(2,1)S(1)} %collective-permute-done.9.refs_1_), channel_id=1, source_target_pairs={{2,4},{3,5},{4,6},{5,7},{10,12},{11,13},{12,14},{13,15},{18,20},{1... | collective-permute-start | bytes 786440 | tf_op jit(solution)/shard_map/ppermute | solution.py:503
  107.7 22.6 %collective-permute-start.12 = (bf16[2,1,16,32,128]{4,3,2,1,0:T(8,128)(2,1)}, bf16[2,1,16,32,128]{4,3,2,1,0:T(8,128)(2,1)}, u32[]{:S(2)}, u32[]{:S(2)}) collective-permute-start(bf16[2,1,16,32,128]{4,3,2,1,0:T(8,128)(2,1)} %collective-permute-done.10.refs_4_), channel_id=1, source_target_pairs={{5,3},{4,2},{3,1},{2,0},{13,11},{12,10},{11,9},{10,8},{21,19},{20,... | collective-permute-start | bytes 786440 | tf_op jit(solution)/shard_map/ppermute | solution.py:504
  131.3 26.2 %collective-permute-start.14 = (bf16[2,1,16,32,128]{4,3,2,1,0:T(8,128)(2,1)}, bf16[2,1,16,32,128]{4,3,2,1,0:T(8,128)(2,1)}, u32[]{:S(2)}, u32[]{:S(2)}) collective-permute-start(bf16[2,1,16,32,128]{4,3,2,1,0:T(8,128)(2,1)} %collective-permute-done.11.refs_2_), channel_id=1, source_target_pairs={{4,6},{5,7},{12,14},{13,15},{20,22},{21,23},{28,30},{29,31}} | collective-permute-start | bytes 786440 | tf_op jit(solution)/shard_map/ppermute | solution.py:503
  132.6 25.8 %collective-permute-start.15 = (bf16[2,1,16,32,128]{4,3,2,1,0:T(8,128)(2,1)}, bf16[2,1,16,32,128]{4,3,2,1,0:T(8,128)(2,1)}, u32[]{:S(2)}, u32[]{:S(2)}) collective-permute-start(bf16[2,1,16,32,128]{4,3,2,1,0:T(8,128)(2,1)} %collective-permute-done.12.refs_5_), channel_id=1, source_target_pairs={{3,1},{2,0},{11,9},{10,8},{19,17},{18,16},{27,25},{26,24}} | collective-permute-start | bytes 786440 | tf_op jit(solution)/shard_map/ppermute | solution.py:504
  158.5 134.1 %reduce-scatter.7.cloned.1.call-start = ((), (), s32[]{:S(2)}) async-start(), calls=%async_computation.5 | async-start | bytes 3932160 | tf_op jit(solution)/shard_map/reduce_scatter | solution.py:666
  214.1 134.2 %all-gather.15.cloned.1.call-start = ((), (), s32[]{:S(2)}) async-start(), calls=%async_computation.11 | async-start | bytes 2621440 | tf_op jit(solution)/shard_map/all_gather | solution.py:630
  223.2 11.9 %collective-permute-start.20 = (bf16[1,3,16,32,128]{4,3,2,1,0:T(8,128)(2,1)}, bf16[1,3,16,32,128]{4,3,2,1,0:T(8,128)(2,1)S(1)}, u32[]{:S(2)}, u32[]{:S(2)}) collective-permute-start(bf16[1,3,16,32,128]{4,3,2,1,0:T(8,128)(2,1)} %slice_bitcast_fusion.1), channel_id=1, source_target_pairs={{0,1},{1,0},{2,3},{3,2},{4,5},{5,4},{6,7},{7,6},{8,9},{9,8},{10,11... | collective-permute-start | bytes 1179656 | tf_op jit(solution)/shard_map/ppermute | solution.py:479
  250.4 157.1 %all-gather.13.cloned.1.call-start = ((), (), s32[]{:S(2)}) async-start(), calls=%async_computation.10 | async-start | bytes 2621440 | tf_op jit(solution)/shard_map/all_gather | solution.py:630
  250.5 14.4 %collective-permute-start.24 = (bf16[2,1,16,32,128]{4,3,2,1,0:T(8,128)(2,1)S(1)}, bf16[2,1,16,32,128]{4,3,2,1,0:T(8,128)(2,1)S(1)}, u32[]{:S(2)}, u32[]{:S(2)}) collective-permute-start(bf16[2,1,16,32,128]{4,3,2,1,0:T(8,128)(2,1)S(1)} %pad_maximum_fusion.1.refs_0_), channel_id=1, source_target_pairs={{0,2},{1,3},{2,4},{3,5},{4,6},{5,7},{8,10},{9,11},{10,12},{11,13},... | collective-permute-start | bytes 786440 | tf_op jit(solution)/shard_map/ppermute | solution.py:503
  253.1 20.5 %collective-permute-start.26 = (bf16[2,1,16,32,128]{4,3,2,1,0:T(8,128)(2,1)S(1)}, bf16[2,1,16,32,128]{4,3,2,1,0:T(8,128)(2,1)}, u32[]{:S(2)}, u32[]{:S(2)}) collective-permute-start(bf16[2,1,16,32,128]{4,3,2,1,0:T(8,128)(2,1)S(1)} %pad_maximum_fusion.1.refs_0_), channel_id=1, source_target_pairs={{7,5},{6,4},{5,3},{4,2},{3,1},{2,0},{15,13},{14,12},{13,11},{12,10... | collective-permute-start | bytes 786440 | tf_op jit(solution)/shard_map/ppermute | solution.py:504
  264.9 27.8 %collective-permute-start.25 = (bf16[2,1,16,32,128]{4,3,2,1,0:T(8,128)(2,1)S(1)}, bf16[2,1,16,32,128]{4,3,2,1,0:T(8,128)(2,1)}, u32[]{:S(2)}, u32[]{:S(2)}) collective-permute-start(bf16[2,1,16,32,128]{4,3,2,1,0:T(8,128)(2,1)S(1)} %collective-permute-done.24.refs_1_), channel_id=1, source_target_pairs={{2,4},{3,5},{4,6},{5,7},{10,12},{11,13},{12,14},{13,15},{18,20},{1... | collective-permute-start | bytes 786440 | tf_op jit(solution)/shard_map/ppermute | solution.py:503
  273.6 20.7 %collective-permute-start.27 = (bf16[2,1,16,32,128]{4,3,2,1,0:T(8,128)(2,1)}, bf16[2,1,16,32,128]{4,3,2,1,0:T(8,128)(2,1)}, u32[]{:S(2)}, u32[]{:S(2)}) collective-permute-start(bf16[2,1,16,32,128]{4,3,2,1,0:T(8,128)(2,1)} %collective-permute-done.26.refs_4_), channel_id=1, source_target_pairs={{5,3},{4,2},{3,1},{2,0},{13,11},{12,10},{11,9},{10,8},{21,19},{20,... | collective-permute-start | bytes 786440 | tf_op jit(solution)/shard_map/ppermute | solution.py:504
  274.9 17.7 %collective-permute-start.32 = (bf16[3,4,32,128]{3,2,1,0:T(8,128)(2,1)}, bf16[3,4,32,128]{3,2,1,0:T(8,128)(2,1)S(1)}, u32[]{:S(2)}, u32[]{:S(2)}) collective-permute-start(bf16[3,4,32,128]{3,2,1,0:T(8,128)(2,1)} %copy-done.32), channel_id=1, source_target_pairs={{0,8},{8,16},{16,24},{1,9},{9,17},{17,25},{2,10},{10,18},{18,26},{... | collective-permute-start | bytes 294920 | tf_op jit(solution)/shard_map/ppermute | solution.py:461
  278.0 14.6 %collective-permute-start.33 = (bf16[3,4,32,128]{3,2,1,0:T(8,128)(2,1)}, bf16[3,4,32,128]{3,2,1,0:T(8,128)(2,1)}, u32[]{:S(2)}, u32[]{:S(2)}) collective-permute-start(bf16[3,4,32,128]{3,2,1,0:T(8,128)(2,1)} %copy-done.31), channel_id=1, source_target_pairs={{8,0},{16,8},{24,16},{9,1},{17,9},{25,17},{10,2},{18,10},{26,18},{... | collective-permute-start | bytes 294920 | tf_op jit(solution)/shard_map/ppermute | solution.py:461
  322.0 140.8 %reduce-scatter.11.cloned.1.call-start = ((), (), s32[]{:S(2)}) async-start(), calls=%async_computation.7 | async-start | bytes 3932160 | tf_op jit(solution)/shard_map/reduce_scatter | solution.py:666
  322.1 14.6 %collective-permute-start.40 = (bf16[2,1,16,32,128]{4,3,2,1,0:T(8,128)(2,1)S(1)}, bf16[2,1,16,32,128]{4,3,2,1,0:T(8,128)(2,1)S(1)}, u32[]{:S(2)}, u32[]{:S(2)}) collective-permute-start(bf16[2,1,16,32,128]{4,3,2,1,0:T(8,128)(2,1)S(1)} %pad_maximum_fusion.refs_0_), channel_id=1, source_target_pairs={{0,2},{1,3},{2,4},{3,5},{4,6},{5,7},{8,10},{9,11},{10,12},{11,13},... | collective-permute-start | bytes 786440 | tf_op jit(solution)/shard_map/ppermute | solution.py:503
  325.2 20.4 %collective-permute-start.41 = (bf16[2,1,16,32,128]{4,3,2,1,0:T(8,128)(2,1)S(1)}, bf16[2,1,16,32,128]{4,3,2,1,0:T(8,128)(2,1)S(1)}, u32[]{:S(2)}, u32[]{:S(2)}) collective-permute-start(bf16[2,1,16,32,128]{4,3,2,1,0:T(8,128)(2,1)S(1)} %pad_maximum_fusion.refs_0_), channel_id=1, source_target_pairs={{7,5},{6,4},{5,3},{4,2},{3,1},{2,0},{15,13},{14,12},{13,11},{12,10... | collective-permute-start | bytes 786440 | tf_op jit(solution)/shard_map/ppermute | solution.py:504
  326.5 23.8 %collective-permute-start.44 = (bf16[2,1,16,32,128]{4,3,2,1,0:T(8,128)(2,1)}, bf16[2,1,16,32,128]{4,3,2,1,0:T(8,128)(2,1)S(1)}, u32[]{:S(2)}, u32[]{:S(2)}) collective-permute-start(bf16[2,1,16,32,128]{4,3,2,1,0:T(8,128)(2,1)} %collective-permute-done.25.refs_2_), channel_id=1, source_target_pairs={{4,6},{5,7},{12,14},{13,15},{20,22},{21,23},{28,30},{29,31}} | collective-permute-start | bytes 786440 | tf_op jit(solution)/shard_map/ppermute | solution.py:503
  327.2 25.1 %collective-permute-start.45 = (bf16[2,1,16,32,128]{4,3,2,1,0:T(8,128)(2,1)}, bf16[2,1,16,32,128]{4,3,2,1,0:T(8,128)(2,1)}, u32[]{:S(2)}, u32[]{:S(2)}) collective-permute-start(bf16[2,1,16,32,128]{4,3,2,1,0:T(8,128)(2,1)} %collective-permute-done.27.refs_5_), channel_id=1, source_target_pairs={{3,1},{2,0},{11,9},{10,8},{19,17},{18,16},{27,25},{26,24}} | collective-permute-start | bytes 786440 | tf_op jit(solution)/shard_map/ppermute | solution.py:504
  348.3 23.4 %collective-permute-start.42 = (bf16[2,1,16,32,128]{4,3,2,1,0:T(8,128)(2,1)S(1)}, bf16[2,1,16,32,128]{4,3,2,1,0:T(8,128)(2,1)S(1)}, u32[]{:S(2)}, u32[]{:S(2)}) collective-permute-start(bf16[2,1,16,32,128]{4,3,2,1,0:T(8,128)(2,1)S(1)} %collective-permute-done.40.refs_1_), channel_id=1, source_target_pairs={{2,4},{3,5},{4,6},{5,7},{10,12},{11,13},{12,14},{13,15},{18,20},{1... | collective-permute-start | bytes 786440 | tf_op jit(solution)/shard_map/ppermute | solution.py:503
  349.0 22.7 %collective-permute-start.43 = (bf16[2,1,16,32,128]{4,3,2,1,0:T(8,128)(2,1)S(1)}, bf16[2,1,16,32,128]{4,3,2,1,0:T(8,128)(2,1)S(1)}, u32[]{:S(2)}, u32[]{:S(2)}) collective-permute-start(bf16[2,1,16,32,128]{4,3,2,1,0:T(8,128)(2,1)S(1)} %collective-permute-done.41.refs_4_), channel_id=1, source_target_pairs={{5,3},{4,2},{3,1},{2,0},{13,11},{12,10},{11,9},{10,8},{21,19},{20,... | collective-permute-start | bytes 786440 | tf_op jit(solution)/shard_map/ppermute | solution.py:504
  372.5 25.6 %collective-permute-start.46 = (bf16[2,1,16,32,128]{4,3,2,1,0:T(8,128)(2,1)S(1)}, bf16[2,1,16,32,128]{4,3,2,1,0:T(8,128)(2,1)S(1)}, u32[]{:S(2)}, u32[]{:S(2)}) collective-permute-start(bf16[2,1,16,32,128]{4,3,2,1,0:T(8,128)(2,1)S(1)} %collective-permute-done.42.refs_2_), channel_id=1, source_target_pairs={{4,6},{5,7},{12,14},{13,15},{20,22},{21,23},{28,30},{29,31}} | collective-permute-start | bytes 786440 | tf_op jit(solution)/shard_map/ppermute | solution.py:503
  373.2 25.0 %collective-permute-start.47 = (bf16[2,1,16,32,128]{4,3,2,1,0:T(8,128)(2,1)S(1)}, bf16[2,1,16,32,128]{4,3,2,1,0:T(8,128)(2,1)S(1)}, u32[]{:S(2)}, u32[]{:S(2)}) collective-permute-start(bf16[2,1,16,32,128]{4,3,2,1,0:T(8,128)(2,1)S(1)} %collective-permute-done.43.refs_5_), channel_id=1, source_target_pairs={{3,1},{2,0},{11,9},{10,8},{19,17},{18,16},{27,25},{26,24}} | collective-permute-start | bytes 786440 | tf_op jit(solution)/shard_map/ppermute | solution.py:504
  398.2 127.2 %reduce-scatter.9.cloned.1.call-start = ((), (), s32[]{:S(2)}) async-start(), calls=%async_computation.6 | async-start | bytes 3932160 | tf_op jit(solution)/shard_map/reduce_scatter | solution.py:666
  463.9 11.9 %collective-permute-start.56 = (bf16[1,3,16,32,128]{4,3,2,1,0:T(8,128)(2,1)S(1)}, bf16[1,3,16,32,128]{4,3,2,1,0:T(8,128)(2,1)S(1)}, u32[]{:S(2)}, u32[]{:S(2)}) collective-permute-start(bf16[1,3,16,32,128]{4,3,2,1,0:T(8,128)(2,1)S(1)} %slice_bitcast_fusion), channel_id=1, source_target_pairs={{0,1},{1,0},{2,3},{3,2},{4,5},{5,4},{6,7},{7,6},{8,9},{9,8},{10,11... | collective-permute-start | bytes 1179656 | tf_op jit(solution)/shard_map/ppermute | solution.py:479
  526.5 11.5 %collective-permute-start.59 = (bf16[1,3,16,32,128]{4,3,2,1,0:T(8,128)(2,1)S(1)}, bf16[1,3,16,32,128]{4,3,2,1,0:T(8,128)(2,1)S(1)}, u32[]{:S(2)}, u32[]{:S(2)}) collective-permute-start(bf16[1,3,16,32,128]{4,3,2,1,0:T(8,128)(2,1)S(1)} %slice.160), channel_id=1, source_target_pairs={{0,1},{1,0},{2,3},{3,2},{4,5},{5,4},{6,7},{7,6},{8,9},{9,8},{10,11... | collective-permute-start | bytes 1179656 | tf_op jit(solution)/shard_map/ppermute | solution.py:479
  (73 other events, 310.8 us)
Sparse Core Ops, SparseCore 0:
  34.1 72.2 all-gather.10
  107.9 50.8 all-gather.8
  161.6 59.7 reduce-scatter.4
  224.1 68.4 reduce-scatter.6
  294.1 54.1 all-gather.14
  349.7 50.1 all-gather.12
  402.8 60.0 reduce-scatter.10
  465.1 60.2 reduce-scatter.8

commit v12 on v11

--- a/solution.py
+++ b/solution.py
@@ -32,6 +32,10 @@
 
 def whole_block(array):
     return pl.BlockSpec(array.shape, lambda *_: (0,) * array.ndim)
+
+
+def in_hbm(*arrays):
+    return [pltpu.with_memory_space_constraint(array, pltpu.HBM) for array in arrays]
 
 
 def call(kernel, core, grid, in_specs, out_specs, out_shape, scratch=(), aliases=None, **kwargs):
@@ -114,9 +118,9 @@
 
     specs = [field, field, field, rim, rim]
     shapes = [
-        shape(rows, jnp.float32),
-        shape(rows, jnp.bfloat16),
-        shape(rows, jnp.float32),
+        pltpu.HBM((members, rows, steps, cols), jnp.float32),
+        pltpu.HBM((members, rows, steps, cols), jnp.bfloat16),
+        pltpu.HBM((members, rows, steps, cols), jnp.float32),
         shape(HALO, jnp.bfloat16),
         shape(HALO, jnp.bfloat16),
     ]
@@ -161,7 +165,7 @@
         specs,
         shapes,
         name="start",
-    )(core, flat, up, down, coeff)
+    )(core, *in_hbm(flat), up, down, coeff)
 
 
 def residual_of(core, times, rest_refs, misfit_refs, whole_ref):
@@ -175,6 +179,13 @@
     parts = [jnp.where(first, cross, same), whole_ref[...], jnp.where(first, same, cross)]
     rests = [ref[0, :, times].astype(jnp.float32) for ref in rest_refs]
     return jnp.concatenate([rest - part for rest, part in zip(rests, parts)], axis=0)
+
+
+def held(rests, misfits, iterate):
+    above, rest, below = rests
+    own, other, same, cross = misfits
+    rest, own, iterate = in_hbm(rest, own, iterate)
+    return above, rest, below, own, other, same, cross, iterate
 
 
 def step_kernel(
@@ -209,7 +220,7 @@
         shapes,
         [pltpu.VMEM((rows, SUBLANES, cols), jnp.float32)],
         name="step",
-    )(core, *rests, *misfits, iterate, coeff)
+    )(core, *held(rests, misfits, iterate), coeff)
 
 
 def finish_kernel(
@@ -250,7 +261,7 @@
         [pltpu.VMEM((rows, SUBLANES, cols), jnp.float32)],
         {first + k: k for k in range(len(previous))},
         name="finish",
-    )(core, *rests, *misfits, iterate, coeff, *previous)
+    )(core, *held(rests, misfits, iterate), coeff, *previous)
 
 
 def same_frequency(near, sensors, lanes):
@@ -377,7 +388,7 @@
         ],
         cost_estimate=map_cost(members, own, field.size),
         name="observe",
-    )(core, field, *slots, own, other, table, around, local_cells)
+    )(core, *in_hbm(field), *slots, *in_hbm(own, other), table, around, local_cells)
 
 
 def pull_kernel(core_ref, *refs):
@@ -444,14 +455,14 @@
         pl.BlockSpec(
             (devices, 2, members, CHUNK_ROWS, steps, lanes), lambda c, core: (0, 0, 0, c, 0, 0)
         ),
-        jax.ShapeDtypeStruct(shape, jnp.bfloat16),
+        pltpu.HBM(shape, jnp.bfloat16),
         [
             pltpu.VMEM((2 * members, freqs, 4 * lanes), jnp.float32),
             pltpu.VMEM((2 * members, freqs, width), jnp.float32),
         ],
         cost_estimate=map_cost(members, own, math.prod(shape)),
         name="pull_back",
-    )(core, *small, own, other, back, local_cells)
+    )(core, *small, *in_hbm(own, other), back, local_cells)
 
 
 def rims(top, bottom):

time: 557 us -> 552 us (level)
  local copies, waits for them, and re-layouts: 52.3 us -> 15.3 us
  waiting for transfers between devices: 207 us -> 227 us
  Pallas kernels: 170 us -> 184 us
    unnamed x74 -> x24, local copies, waits for them, and re-layouts: 39.9 us -> 0.1 us
    reduce_scatter x4, waiting for transfers between devices: 69.6 us -> 86 us  [shards(): lax.psum_scatter(misfit, 'sensors', scatter_dimension=0, axis_index_group...]
    ppermute x9, waiting for transfers between devices: 30.6 us -> 36.9 us  [hop(): down = lax.ppermute(self.ends[1], 'sensors', backward)]
  transfers between devices with their start and end apart: 70 -> 70, of which waited for: 44 -> 45; matrix products, arithmetic and copies ran while one was open for 4% -> 4% of each run, Pallas kernels for 30% -> 32%
where the time goes in v12:
time: 552 us; the launch traced here: 550 us
  waiting for transfers between devices  227 us (41%)
  Pallas kernels  184 us (33%)
  starting transfers between devices  100 us (18%)
  local copies, waits for them, and re-layouts  15.3 us (3%)
  between operations  15 us (3%)
  other arithmetic  8.4 us (2%)
    reduce_scatter x4, waiting for transfers between devices, shards(): lax.psum_scatter(misfit, 'sensors', scatter_dimension=0, axis_index_group...  86 us
    pallas_call x4, Pallas kernels, observe(): call(observe_kernel, core, (chunks,), [pl.BlockSpec(block, lambda c, core...  71.5 us
    pallas_call x4, Pallas kernels, pull_back(): call(pull_kernel, core, (rows // CHUNK_ROWS,), [whole_block(array) for ar...  63.6 us
    ppermute x9, waiting for transfers between devices, hop(): down = lax.ppermute(self.ends[1], 'sensors', backward)  36.9 us
    ppermute x9, waiting for transfers between devices, hop(): up = lax.ppermute(self.ends[0], 'sensors', onward)  27.2 us
    ppermute x8, starting transfers between devices, misfit_rims(): return (lax.ppermute(edge, both, same), lax.ppermute(edge, both, cross))  21.9 us
    ppermute x6, starting transfers between devices, rims(): lax.ppermute(bottom, 'cells', onward)  19.2 us
    ppermute x6, waiting for transfers between devices, rims(): lax.ppermute(top, 'cells', backward)  19.1 us
  transfers between devices with their start and end apart: 70, of which 45 were waited for; matrix products, arithmetic and copies ran while one was open for 4% of the time, Pallas kernels for 32%

profile of v12, /device:TPU:1, one launch (start us, length us, event | category | flops | bytes accessed | tf_op | source)
XLA Modules:
  0.0 549.7 jit_solution(4526622778200354391)
XLA Ops:
  10.4 4.6 collective-permute-start
  22.9 8.2 %start.2 = (f32[3,32,32,128]{3,2,1,0:T(8,128)}, bf16[3,32,32,128]{3,2,1,0:T(8,128)(2,1)}, f32[3,32,32,128]{3,2,1,0:T(8,128)}, bf16[3,4,32,128]{3,2,1,0:T(8,128)(2,1)S(1)}, bf16[3,4,32,128]{3,2,1,0:T(8,128)(2,1)S(1)}) custom-call(s32[1]{0:T(128)} %bitcast.core_ref, f32[32,192,128]{2,1,0:T(8,128)} %bitcast.65, bf16[3,4,32,128]{3,2,1,0:T(8,128)(2,1)S(1)} %bitcast.63, ...), custom_call_target="tpu_custom_call" | custom-call | tf_op jit(solution)/shard_map/start/pallas_call | solution.py:155
  31.1 4.0 collective-permute-start.2
  45.2 4.6 collective-permute-done.5.down_ref
  49.7 8.2 %start.3 = (f32[3,32,32,128]{3,2,1,0:T(8,128)}, bf16[3,32,32,128]{3,2,1,0:T(8,128)(2,1)}, f32[3,32,32,128]{3,2,1,0:T(8,128)}, bf16[3,4,32,128]{3,2,1,0:T(8,128)(2,1)}, bf16[3,4,32,128]{3,2,1,0:T(8,128)(2,1)}) custom-call(s32[1]{0:T(128)} %bitcast.core_ref, f32[32,192,128]{2,1,0:T(8,128)} %bitcast.66, ...), custom_call_target="tpu_custom_call" | custom-call | tf_op jit(solution)/shard_map/start/pallas_call | solution.py:155
  71.6 9.3 %collective-permute-done.9.refs_1_ = bf16[2,1,16,32,128]{4,3,2,1,0:T(8,128)(2,1)S(1)} collective-permute-done((bf16[2,1,16,32,128]{4,3,2,1,0:T(8,128)(2,1)S(1)}, bf16[2,1,16,32,128]{4,3,2,1,0:T(8,128)(2,1)S(1)}, u32[]{:S(2)}, u32[]{:S(2)}) %collective-permute-start.9) | collective-permute-done | bytes 262176 | tf_op jit(solution)/shard_map/ppermute | solution.py:514
  80.9 10.8 %collective-permute-done.10.refs_4_ = bf16[2,1,16,32,128]{4,3,2,1,0:T(8,128)(2,1)S(1)} collective-permute-done((bf16[2,1,16,32,128]{4,3,2,1,0:T(8,128)(2,1)S(1)}, bf16[2,1,16,32,128]{4,3,2,1,0:T(8,128)(2,1)S(1)}, u32[]{:S(2)}, u32[]{:S(2)}) %collective-permute-start.10) | collective-permute-done | bytes 262176 | tf_op jit(solution)/shard_map/ppermute | solution.py:515
  91.6 11.8 %all-gather.11.cloned.1.call-done = bf16[24,32,32,128]{3,2,1,0:T(8,128)(2,1)} async-done(((bf16[3,32,32,128]{3,2,1,0:T(8,128)(2,1)}), bf16[24,32,32,128]{3,2,1,0:T(8,128)(2,1)}) %all-gather.11.cloned.1.call-update) | async-done | bytes 6291472 | tf_op jit(solution)/shard_map/all_gather | solution.py:641
  106.1 17.7 %observe.4 = f32[2,2,3,16,128]{4,3,2,1,0:T(8,128)S(1)} custom-call(s32[1]{0:T(128)} %bitcast.core_ref, bf16[8,3,32,32,128]{4,3,2,1,0:T(8,128)(2,1)} %bitcast.67, bf16[2,128,16,4096]{3,2,1,0:T(8,128)(2,1)} %refs_5_.7, bf16[2,128,16,4096]{3,2,1,0:T(8,128)(2,1)} %collective-permute-done.13.refs_1_.refs_6_.refs_8_, bf16[256,256]{1,0:T(8,128)(2,1)S(1)} %copy.38.refs_2_, ...), custom_call_target="tpu_custom_call" | custom-call | flops 402653184 | bytes 39845888 | tf_op jit(solution)/shard_map/observe/pallas_call | solution.py:374
  134.1 15.9 %pull_back.4 = bf16[4,2,3,16,32,128]{5,4,3,2,1,0:T(8,128)(2,1)} custom-call(s32[1]{0:T(128)} %bitcast.core_ref, f32[2,2,3,16,128]{4,3,2,1,0:T(8,128)S(1)} %reverse_add_fusion.3.refs_0_, f32[2,2,3,16,128]{4,3,2,1,0:T(8,128)S(1)} %collective-permute-done.17.refs_1_, f32[2,2,3,16,128]{4,3,2,1,0:T(8,128)S(1)} %collective-permute-done.18.refs_2_, ...), custom_call_target="tpu_custom_call" | custom-call | flops 402653184 | bytes 36700160 | tf_op jit(solution)/shard_map/pull_back/pallas_call | solution.py:448
  161.5 18.2 %observe.5 = f32[2,2,3,16,128]{4,3,2,1,0:T(8,128)S(1)} custom-call(s32[1]{0:T(128)} %bitcast.core_ref, bf16[4,2,2,16,32,128]{5,4,3,2,1,0:T(8,128)(2,1)} %bitcast.78, bf16[2,1,16,32,128]{4,3,2,1,0:T(8,128)(2,1)S(1)} %pad_maximum_fusion.2.refs_0_, bf16[2,1,16,32,128]{4,3,2,1,0:T(8,128)(2,1)S(1)} %collective-permute-done.9.refs_1_, ...), custom_call_target="tpu_custom_call" | custom-call | flops 402653184 | bytes 35651584 | tf_op jit(solution)/shard_map/observe/pallas_call | solution.py:374
  189.7 15.9 %pull_back.5 = bf16[4,2,3,16,32,128]{5,4,3,2,1,0:T(8,128)(2,1)} custom-call(s32[1]{0:T(128)} %bitcast.core_ref, f32[2,2,3,16,128]{4,3,2,1,0:T(8,128)S(1)} %reverse_add_fusion.2.refs_0_, f32[2,2,3,16,128]{4,3,2,1,0:T(8,128)S(1)} %collective-permute-done.29.refs_1_, f32[2,2,3,16,128]{4,3,2,1,0:T(8,128)S(1)} %collective-permute-done.30.refs_2_, ...), custom_call_target="tpu_custom_call" | custom-call | flops 402653184 | bytes 36700160 | tf_op jit(solution)/shard_map/pull_back/pallas_call | solution.py:448
  205.6 11.4 %reduce-scatter.5.cloned.1.call-done = bf16[1,2,3,16,32,128]{5,4,3,2,1,0:T(8,128)(2,1)} async-done(((bf16[4,2,3,16,32,128]{5,4,3,2,1,0:T(8,128)(2,1)}), bf16[1,2,3,16,32,128]{5,4,3,2,1,0:T(8,128)(2,1)}) %reduce-scatter.5.cloned.1.call-update) | async-done | bytes 786448 | tf_op jit(solution)/shard_map/reduce_scatter | solution.py:677
  225.4 4.6 collective-permute-done.22.cross_ref
  230.0 8.7 %step.2 = (f32[3,32,32,128]{3,2,1,0:T(8,128)}, bf16[3,32,32,128]{3,2,1,0:T(8,128)(2,1)}, f32[3,32,32,128]{3,2,1,0:T(8,128)}, bf16[3,4,32,128]{3,2,1,0:T(8,128)(2,1)S(1)}, bf16[3,4,32,128]{3,2,1,0:T(8,128)(2,1)S(1)}) custom-call(s32[1]{0:T(128)} %bitcast.core_ref, bf16[3,4,32,128]{3,2,1,0:T(8,128)(2,1)S(1)} %collective-permute-done.2.up_ref, ...), custom_call_target="tpu_custom_call" | custom-call | tf_op jit(solution)/shard_map/step/pallas_call | solution.py:214
  246.6 10.4 %collective-permute-done.24.refs_1_ = bf16[2,1,16,32,128]{4,3,2,1,0:T(8,128)(2,1)S(1)} collective-permute-done((bf16[2,1,16,32,128]{4,3,2,1,0:T(8,128)(2,1)S(1)}, bf16[2,1,16,32,128]{4,3,2,1,0:T(8,128)(2,1)S(1)}, u32[]{:S(2)}, u32[]{:S(2)}) %collective-permute-start.24) | collective-permute-done | bytes 262176 | tf_op jit(solution)/shard_map/ppermute | solution.py:514
  257.7 10.0 %collective-permute-done.26.refs_4_ = bf16[2,1,16,32,128]{4,3,2,1,0:T(8,128)(2,1)S(1)} collective-permute-done((bf16[2,1,16,32,128]{4,3,2,1,0:T(8,128)(2,1)S(1)}, bf16[2,1,16,32,128]{4,3,2,1,0:T(8,128)(2,1)S(1)}, u32[]{:S(2)}, u32[]{:S(2)}) %collective-permute-start.26) | collective-permute-done | bytes 262176 | tf_op jit(solution)/shard_map/ppermute | solution.py:515
  271.6 18.7 %reduce-scatter.7.cloned.1.call-done = bf16[1,2,3,16,32,128]{5,4,3,2,1,0:T(8,128)(2,1)} async-done(((bf16[4,2,3,16,32,128]{5,4,3,2,1,0:T(8,128)(2,1)}), bf16[1,2,3,16,32,128]{5,4,3,2,1,0:T(8,128)(2,1)}) %reduce-scatter.7.cloned.1.call-update) | async-done | bytes 786448 | tf_op jit(solution)/shard_map/reduce_scatter | solution.py:677
  298.9 4.2 collective-permute-done.36.cross_ref
  303.2 8.7 %step.3 = (f32[3,32,32,128]{3,2,1,0:T(8,128)}, bf16[3,32,32,128]{3,2,1,0:T(8,128)(2,1)}, f32[3,32,32,128]{3,2,1,0:T(8,128)}, bf16[3,4,32,128]{3,2,1,0:T(8,128)(2,1)S(1)}, bf16[3,4,32,128]{3,2,1,0:T(8,128)(2,1)S(1)}) custom-call(s32[1]{0:T(128)} %bitcast.core_ref, bf16[3,4,32,128]{3,2,1,0:T(8,128)(2,1)S(1)} %copy-done.3, ...), custom_call_target="tpu_custom_call" | custom-call | tf_op jit(solution)/shard_map/step/pallas_call | solution.py:214
  323.4 7.5 %collective-permute-done.40.refs_1_ = bf16[2,1,16,32,128]{4,3,2,1,0:T(8,128)(2,1)S(1)} collective-permute-done((bf16[2,1,16,32,128]{4,3,2,1,0:T(8,128)(2,1)S(1)}, bf16[2,1,16,32,128]{4,3,2,1,0:T(8,128)(2,1)S(1)}, u32[]{:S(2)}, u32[]{:S(2)}) %collective-permute-start.40) | collective-permute-done | bytes 262176 | tf_op jit(solution)/shard_map/ppermute | solution.py:514
  330.9 10.1 %collective-permute-done.41.refs_4_ = bf16[2,1,16,32,128]{4,3,2,1,0:T(8,128)(2,1)S(1)} collective-permute-done((bf16[2,1,16,32,128]{4,3,2,1,0:T(8,128)(2,1)S(1)}, bf16[2,1,16,32,128]{4,3,2,1,0:T(8,128)(2,1)S(1)}, u32[]{:S(2)}, u32[]{:S(2)}) %collective-permute-start.41) | collective-permute-done | bytes 262176 | tf_op jit(solution)/shard_map/ppermute | solution.py:515
  348.0 17.8 %observe.6 = f32[2,2,3,16,128]{4,3,2,1,0:T(8,128)S(1)} custom-call(s32[1]{0:T(128)} %bitcast.core_ref, bf16[4,2,2,16,32,128]{5,4,3,2,1,0:T(8,128)(2,1)} %bitcast.79, bf16[2,1,16,32,128]{4,3,2,1,0:T(8,128)(2,1)S(1)} %pad_maximum_fusion.1.refs_0_, bf16[2,1,16,32,128]{4,3,2,1,0:T(8,128)(2,1)S(1)} %collective-permute-done.24.refs_1_, ...), custom_call_target="tpu_custom_call" | custom-call | flops 402653184 | bytes 35651584 | tf_op jit(solution)/shard_map/observe/pallas_call | solution.py:374
  375.9 15.9 %pull_back.6 = bf16[4,2,3,16,32,128]{5,4,3,2,1,0:T(8,128)(2,1)} custom-call(s32[1]{0:T(128)} %bitcast.core_ref, f32[2,2,3,16,128]{4,3,2,1,0:T(8,128)S(1)} %reverse_add_fusion.1.refs_0_, f32[2,2,3,16,128]{4,3,2,1,0:T(8,128)S(1)} %collective-permute-done.49.refs_1_, f32[2,2,3,16,128]{4,3,2,1,0:T(8,128)S(1)} %collective-permute-done.50.refs_2_, ...), custom_call_target="tpu_custom_call" | custom-call | flops 402653184 | bytes 36700160 | tf_op jit(solution)/shard_map/pull_back/pallas_call | solution.py:448
  402.3 17.7 %observe.7 = f32[2,2,3,16,128]{4,3,2,1,0:T(8,128)S(1)} custom-call(s32[1]{0:T(128)} %bitcast.core_ref, bf16[4,2,2,16,32,128]{5,4,3,2,1,0:T(8,128)(2,1)} %bitcast.80, bf16[2,1,16,32,128]{4,3,2,1,0:T(8,128)(2,1)S(1)} %pad_maximum_fusion.refs_0_, bf16[2,1,16,32,128]{4,3,2,1,0:T(8,128)(2,1)S(1)} %collective-permute-done.40.refs_1_, ...), custom_call_target="tpu_custom_call" | custom-call | flops 402653184 | bytes 35651584 | tf_op jit(solution)/shard_map/observe/pallas_call | solution.py:374
  430.8 16.0 %pull_back.7 = bf16[4,2,3,16,32,128]{5,4,3,2,1,0:T(8,128)(2,1)} custom-call(s32[1]{0:T(128)} %bitcast.core_ref, f32[2,2,3,16,128]{4,3,2,1,0:T(8,128)S(1)} %reverse_add_fusion.refs_0_, f32[2,2,3,16,128]{4,3,2,1,0:T(8,128)S(1)} %collective-permute-done.53.refs_1_, f32[2,2,3,16,128]{4,3,2,1,0:T(8,128)S(1)} %collective-permute-done.54.refs_2_, ...), custom_call_target="tpu_custom_call" | custom-call | flops 402653184 | bytes 36700160 | tf_op jit(solution)/shard_map/pull_back/pallas_call | solution.py:448
  446.9 13.5 %reduce-scatter.11.cloned.1.call-done = bf16[1,2,3,16,32,128]{5,4,3,2,1,0:T(8,128)(2,1)} async-done(((bf16[4,2,3,16,32,128]{5,4,3,2,1,0:T(8,128)(2,1)}), bf16[1,2,3,16,32,128]{5,4,3,2,1,0:T(8,128)(2,1)}) %reduce-scatter.11.cloned.1.call-update) | async-done | bytes 786448 | tf_op jit(solution)/shard_map/reduce_scatter | solution.py:677
  468.8 4.6 collective-permute-done.58.cross_ref
  473.3 7.3 %finish.2 = (f32[32,192,128]{2,1,0:T(8,128)}, f32[32,192,128]{2,1,0:T(8,128)}) custom-call(s32[1]{0:T(128)} %bitcast.core_ref, bf16[3,4,32,128]{3,2,1,0:T(8,128)(2,1)S(1)} %collective-permute-done.32.up_ref, f32[3,32,32,128]{3,2,1,0:T(8,128)} %get-tuple-element.130.rest_ref, bf16[3,4,32,128]{3,2,1,0:T(8,128)(2,1)S(1)} %copy-done.1, ...), custom_call_target="tpu_custom_call" | custom-call | tf_op jit(solution)/shard_map/finish/pallas_call | solution.py:254
  480.6 42.4 %reduce-scatter.9.cloned.1.call-done = bf16[1,2,3,16,32,128]{5,4,3,2,1,0:T(8,128)(2,1)} async-done(((bf16[4,2,3,16,32,128]{5,4,3,2,1,0:T(8,128)(2,1)}), bf16[1,2,3,16,32,128]{5,4,3,2,1,0:T(8,128)(2,1)}) %reduce-scatter.9.cloned.1.call-update) | async-done | bytes 786448 | tf_op jit(solution)/shard_map/reduce_scatter | solution.py:677
  531.4 4.2 collective-permute-done.61.cross_ref
  535.6 7.3 %finish.3 = (f32[32,192,128]{2,1,0:T(8,128)}, f32[32,192,128]{2,1,0:T(8,128)}) custom-call(s32[1]{0:T(128)} %bitcast.core_ref, bf16[3,4,32,128]{3,2,1,0:T(8,128)(2,1)S(1)} %collective-permute-done.38.up_ref, f32[3,32,32,128]{3,2,1,0:T(8,128)} %get-tuple-element.114.rest_ref, ...), custom_call_target="tpu_custom_call", output_to_operand_aliasing={{0}: (10, {}), {1}: (11, {})} | custom-call | tf_op jit(solution)/shard_map/finish/pallas_call | solution.py:254
  (226 shorter events, 164.7 us)
Async XLA Ops:
  7.2 96.3 %all-gather.11.cloned.1.call-start = ((), (), s32[]{:S(2)}) async-start(), calls=%async_computation.9 | async-start | bytes 7077888 | tf_op jit(solution)/shard_map/all_gather | solution.py:641
  7.2 98.8 %collective-permute-start.13 = (bf16[2,128,16,4096]{3,2,1,0:T(8,128)(2,1)}, bf16[2,128,16,4096]{3,2,1,0:T(8,128)(2,1)}, u32[]{:S(2)}, u32[]{:S(2)}) collective-permute-start(bf16[2,128,16,4096]{3,2,1,0:T(8,128)(2,1)} %refs_5_.7), channel_id=1, source_target_pairs={{0,1},{1,0},{2,3},{3,2},{4,5},{5,4},{6,7},{7,6},{8,9},{9,8},{10,11... | collective-permute-start | bytes 100663304 | tf_op jit(solution)/shard_map/ppermute | solution.py:490
  31.0 130.4 %all-gather.9.cloned.1.call-start = ((), (), s32[]{:S(2)}) async-start(), calls=%async_computation.8 | async-start | bytes 2621440 | tf_op jit(solution)/shard_map/all_gather | solution.py:641
  64.7 152.3 %reduce-scatter.5.cloned.1.call-start = ((), (), s32[]{:S(2)}) async-start(), calls=%async_computation.4 | async-start | bytes 3932160 | tf_op jit(solution)/shard_map/reduce_scatter | solution.py:677
  66.3 14.5 %collective-permute-start.9 = (bf16[2,1,16,32,128]{4,3,2,1,0:T(8,128)(2,1)S(1)}, bf16[2,1,16,32,128]{4,3,2,1,0:T(8,128)(2,1)S(1)}, u32[]{:S(2)}, u32[]{:S(2)}) collective-permute-start(bf16[2,1,16,32,128]{4,3,2,1,0:T(8,128)(2,1)S(1)} %pad_maximum_fusion.2.refs_0_), channel_id=1, source_target_pairs={{0,2},{1,3},{2,4},{3,5},{4,6},{5,7},{8,10},{9,11},{10,12},{11,13},... | collective-permute-start | bytes 786440 | tf_op jit(solution)/shard_map/ppermute | solution.py:514
  69.5 22.2 %collective-permute-start.10 = (bf16[2,1,16,32,128]{4,3,2,1,0:T(8,128)(2,1)S(1)}, bf16[2,1,16,32,128]{4,3,2,1,0:T(8,128)(2,1)S(1)}, u32[]{:S(2)}, u32[]{:S(2)}) collective-permute-start(bf16[2,1,16,32,128]{4,3,2,1,0:T(8,128)(2,1)S(1)} %pad_maximum_fusion.2.refs_0_), channel_id=1, source_target_pairs={{7,5},{6,4},{5,3},{4,2},{3,1},{2,0},{15,13},{14,12},{13,11},{12,10... | collective-permute-start | bytes 786440 | tf_op jit(solution)/shard_map/ppermute | solution.py:515
  103.5 20.4 %collective-permute-start.11 = (bf16[2,1,16,32,128]{4,3,2,1,0:T(8,128)(2,1)S(1)}, bf16[2,1,16,32,128]{4,3,2,1,0:T(8,128)(2,1)S(1)}, u32[]{:S(2)}, u32[]{:S(2)}) collective-permute-start(bf16[2,1,16,32,128]{4,3,2,1,0:T(8,128)(2,1)S(1)} %collective-permute-done.9.refs_1_), channel_id=1, source_target_pairs={{2,4},{3,5},{4,6},{5,7},{10,12},{11,13},{12,14},{13,15},{18,20},{1... | collective-permute-start | bytes 786440 | tf_op jit(solution)/shard_map/ppermute | solution.py:514
  104.1 19.8 %collective-permute-start.12 = (bf16[2,1,16,32,128]{4,3,2,1,0:T(8,128)(2,1)S(1)}, bf16[2,1,16,32,128]{4,3,2,1,0:T(8,128)(2,1)S(1)}, u32[]{:S(2)}, u32[]{:S(2)}) collective-permute-start(bf16[2,1,16,32,128]{4,3,2,1,0:T(8,128)(2,1)S(1)} %collective-permute-done.10.refs_4_), channel_id=1, source_target_pairs={{5,3},{4,2},{3,1},{2,0},{13,11},{12,10},{11,9},{10,8},{21,19},{20,... | collective-permute-start | bytes 786440 | tf_op jit(solution)/shard_map/ppermute | solution.py:515
  124.9 25.1 %collective-permute-start.14 = (bf16[2,1,16,32,128]{4,3,2,1,0:T(8,128)(2,1)S(1)}, bf16[2,1,16,32,128]{4,3,2,1,0:T(8,128)(2,1)S(1)}, u32[]{:S(2)}, u32[]{:S(2)}) collective-permute-start(bf16[2,1,16,32,128]{4,3,2,1,0:T(8,128)(2,1)S(1)} %collective-permute-done.11.refs_2_), channel_id=1, source_target_pairs={{4,6},{5,7},{12,14},{13,15},{20,22},{21,23},{28,30},{29,31}} | collective-permute-start | bytes 786440 | tf_op jit(solution)/shard_map/ppermute | solution.py:514
  125.6 27.0 %collective-permute-start.15 = (bf16[2,1,16,32,128]{4,3,2,1,0:T(8,128)(2,1)S(1)}, bf16[2,1,16,32,128]{4,3,2,1,0:T(8,128)(2,1)S(1)}, u32[]{:S(2)}, u32[]{:S(2)}) collective-permute-start(bf16[2,1,16,32,128]{4,3,2,1,0:T(8,128)(2,1)S(1)} %collective-permute-done.12.refs_5_), channel_id=1, source_target_pairs={{3,1},{2,0},{11,9},{10,8},{19,17},{18,16},{27,25},{26,24}} | collective-permute-start | bytes 786440 | tf_op jit(solution)/shard_map/ppermute | solution.py:515
  152.6 137.7 %reduce-scatter.7.cloned.1.call-start = ((), (), s32[]{:S(2)}) async-start(), calls=%async_computation.5 | async-start | bytes 3932160 | tf_op jit(solution)/shard_map/reduce_scatter | solution.py:677
  205.6 138.3 %all-gather.15.cloned.1.call-start = ((), (), s32[]{:S(2)}) async-start(), calls=%async_computation.11 | async-start | bytes 2621440 | tf_op jit(solution)/shard_map/all_gather | solution.py:641
  218.0 11.9 %collective-permute-start.20 = (bf16[1,3,16,32,128]{4,3,2,1,0:T(8,128)(2,1)S(1)}, bf16[1,3,16,32,128]{4,3,2,1,0:T(8,128)(2,1)S(1)}, u32[]{:S(2)}, u32[]{:S(2)}) collective-permute-start(bf16[1,3,16,32,128]{4,3,2,1,0:T(8,128)(2,1)S(1)} %slice_bitcast_fusion.1), channel_id=1, source_target_pairs={{0,1},{1,0},{2,3},{3,2},{4,5},{5,4},{6,7},{7,6},{8,9},{9,8},{10,11... | collective-permute-start | bytes 1179656 | tf_op jit(solution)/shard_map/ppermute | solution.py:490
  242.6 159.8 %all-gather.13.cloned.1.call-start = ((), (), s32[]{:S(2)}) async-start(), calls=%async_computation.10 | async-start | bytes 2621440 | tf_op jit(solution)/shard_map/all_gather | solution.py:641
  242.6 14.4 %collective-permute-start.24 = (bf16[2,1,16,32,128]{4,3,2,1,0:T(8,128)(2,1)S(1)}, bf16[2,1,16,32,128]{4,3,2,1,0:T(8,128)(2,1)S(1)}, u32[]{:S(2)}, u32[]{:S(2)}) collective-permute-start(bf16[2,1,16,32,128]{4,3,2,1,0:T(8,128)(2,1)S(1)} %pad_maximum_fusion.1.refs_0_), channel_id=1, source_target_pairs={{0,2},{1,3},{2,4},{3,5},{4,6},{5,7},{8,10},{9,11},{10,12},{11,13},... | collective-permute-start | bytes 786440 | tf_op jit(solution)/shard_map/ppermute | solution.py:514
  245.3 22.4 %collective-permute-start.26 = (bf16[2,1,16,32,128]{4,3,2,1,0:T(8,128)(2,1)S(1)}, bf16[2,1,16,32,128]{4,3,2,1,0:T(8,128)(2,1)S(1)}, u32[]{:S(2)}, u32[]{:S(2)}) collective-permute-start(bf16[2,1,16,32,128]{4,3,2,1,0:T(8,128)(2,1)S(1)} %pad_maximum_fusion.1.refs_0_), channel_id=1, source_target_pairs={{7,5},{6,4},{5,3},{4,2},{3,1},{2,0},{15,13},{14,12},{13,11},{12,10... | collective-permute-start | bytes 786440 | tf_op jit(solution)/shard_map/ppermute | solution.py:515
  257.0 33.4 %collective-permute-start.25 = (bf16[2,1,16,32,128]{4,3,2,1,0:T(8,128)(2,1)S(1)}, bf16[2,1,16,32,128]{4,3,2,1,0:T(8,128)(2,1)S(1)}, u32[]{:S(2)}, u32[]{:S(2)}) collective-permute-start(bf16[2,1,16,32,128]{4,3,2,1,0:T(8,128)(2,1)S(1)} %collective-permute-done.24.refs_1_), channel_id=1, source_target_pairs={{2,4},{3,5},{4,6},{5,7},{10,12},{11,13},{12,14},{13,15},{18,20},{1... | collective-permute-start | bytes 786440 | tf_op jit(solution)/shard_map/ppermute | solution.py:514
  267.7 22.6 %collective-permute-start.27 = (bf16[2,1,16,32,128]{4,3,2,1,0:T(8,128)(2,1)S(1)}, bf16[2,1,16,32,128]{4,3,2,1,0:T(8,128)(2,1)S(1)}, u32[]{:S(2)}, u32[]{:S(2)}) collective-permute-start(bf16[2,1,16,32,128]{4,3,2,1,0:T(8,128)(2,1)S(1)} %collective-permute-done.26.refs_4_), channel_id=1, source_target_pairs={{5,3},{4,2},{3,1},{2,0},{13,11},{12,10},{11,9},{10,8},{21,19},{20,... | collective-permute-start | bytes 786440 | tf_op jit(solution)/shard_map/ppermute | solution.py:515
  269.0 21.3 %collective-permute-start.32 = (bf16[3,4,32,128]{3,2,1,0:T(8,128)(2,1)S(1)}, bf16[3,4,32,128]{3,2,1,0:T(8,128)(2,1)S(1)}, u32[]{:S(2)}, u32[]{:S(2)}) collective-permute-start(bf16[3,4,32,128]{3,2,1,0:T(8,128)(2,1)S(1)} %get-tuple-element.103), channel_id=1, source_target_pairs={{0,8},{8,16},{16,24},{1,9},{9,17},{17,25},{2,10},{10,18},{18,26},{... | collective-permute-start | bytes 294920 | tf_op jit(solution)/shard_map/ppermute | solution.py:472
  270.3 20.0 %collective-permute-start.33 = (bf16[3,4,32,128]{3,2,1,0:T(8,128)(2,1)S(1)}, bf16[3,4,32,128]{3,2,1,0:T(8,128)(2,1)S(1)}, u32[]{:S(2)}, u32[]{:S(2)}) collective-permute-start(bf16[3,4,32,128]{3,2,1,0:T(8,128)(2,1)S(1)} %get-tuple-element.105), channel_id=1, source_target_pairs={{8,0},{16,8},{24,16},{9,1},{17,9},{25,17},{10,2},{18,10},{26,18},{... | collective-permute-start | bytes 294920 | tf_op jit(solution)/shard_map/ppermute | solution.py:472
  291.4 11.7 %collective-permute-start.34 = (bf16[1,3,16,32,128]{4,3,2,1,0:T(8,128)(2,1)S(1)}, bf16[1,3,16,32,128]{4,3,2,1,0:T(8,128)(2,1)S(1)}, u32[]{:S(2)}, u32[]{:S(2)}) collective-permute-start(bf16[1,3,16,32,128]{4,3,2,1,0:T(8,128)(2,1)S(1)} %slice.149), channel_id=1, source_target_pairs={{0,1},{1,0},{2,3},{3,2},{4,5},{5,4},{6,7},{7,6},{8,9},{9,8},{10,11... | collective-permute-start | bytes 1179656 | tf_op jit(solution)/shard_map/ppermute | solution.py:490
  315.8 144.6 %reduce-scatter.11.cloned.1.call-start = ((), (), s32[]{:S(2)}) async-start(), calls=%async_computation.7 | async-start | bytes 3932160 | tf_op jit(solution)/shard_map/reduce_scatter | solution.py:677
  315.9 15.1 %collective-permute-start.40 = (bf16[2,1,16,32,128]{4,3,2,1,0:T(8,128)(2,1)S(1)}, bf16[2,1,16,32,128]{4,3,2,1,0:T(8,128)(2,1)S(1)}, u32[]{:S(2)}, u32[]{:S(2)}) collective-permute-start(bf16[2,1,16,32,128]{4,3,2,1,0:T(8,128)(2,1)S(1)} %pad_maximum_fusion.refs_0_), channel_id=1, source_target_pairs={{0,2},{1,3},{2,4},{3,5},{4,6},{5,7},{8,10},{9,11},{10,12},{11,13},... | collective-permute-start | bytes 786440 | tf_op jit(solution)/shard_map/ppermute | solution.py:514
  319.5 21.5 %collective-permute-start.41 = (bf16[2,1,16,32,128]{4,3,2,1,0:T(8,128)(2,1)S(1)}, bf16[2,1,16,32,128]{4,3,2,1,0:T(8,128)(2,1)S(1)}, u32[]{:S(2)}, u32[]{:S(2)}) collective-permute-start(bf16[2,1,16,32,128]{4,3,2,1,0:T(8,128)(2,1)S(1)} %pad_maximum_fusion.refs_0_), channel_id=1, source_target_pairs={{7,5},{6,4},{5,3},{4,2},{3,1},{2,0},{15,13},{14,12},{13,11},{12,10... | collective-permute-start | bytes 786440 | tf_op jit(solution)/shard_map/ppermute | solution.py:515
  320.8 25.8 %collective-permute-start.44 = (bf16[2,1,16,32,128]{4,3,2,1,0:T(8,128)(2,1)S(1)}, bf16[2,1,16,32,128]{4,3,2,1,0:T(8,128)(2,1)}, u32[]{:S(2)}, u32[]{:S(2)}) collective-permute-start(bf16[2,1,16,32,128]{4,3,2,1,0:T(8,128)(2,1)S(1)} %collective-permute-done.25.refs_2_), channel_id=1, source_target_pairs={{4,6},{5,7},{12,14},{13,15},{20,22},{21,23},{28,30},{29,31}} | collective-permute-start | bytes 786440 | tf_op jit(solution)/shard_map/ppermute | solution.py:514
  322.1 25.9 %collective-permute-start.45 = (bf16[2,1,16,32,128]{4,3,2,1,0:T(8,128)(2,1)S(1)}, bf16[2,1,16,32,128]{4,3,2,1,0:T(8,128)(2,1)}, u32[]{:S(2)}, u32[]{:S(2)}) collective-permute-start(bf16[2,1,16,32,128]{4,3,2,1,0:T(8,128)(2,1)S(1)} %collective-permute-done.27.refs_5_), channel_id=1, source_target_pairs={{3,1},{2,0},{11,9},{10,8},{19,17},{18,16},{27,25},{26,24}} | collective-permute-start | bytes 786440 | tf_op jit(solution)/shard_map/ppermute | solution.py:515
  343.9 22.0 %collective-permute-start.42 = (bf16[2,1,16,32,128]{4,3,2,1,0:T(8,128)(2,1)S(1)}, bf16[2,1,16,32,128]{4,3,2,1,0:T(8,128)(2,1)}, u32[]{:S(2)}, u32[]{:S(2)}) collective-permute-start(bf16[2,1,16,32,128]{4,3,2,1,0:T(8,128)(2,1)S(1)} %collective-permute-done.40.refs_1_), channel_id=1, source_target_pairs={{2,4},{3,5},{4,6},{5,7},{10,12},{11,13},{12,14},{13,15},{18,20},{1... | collective-permute-start | bytes 786440 | tf_op jit(solution)/shard_map/ppermute | solution.py:514
  345.2 20.6 %collective-permute-start.43 = (bf16[2,1,16,32,128]{4,3,2,1,0:T(8,128)(2,1)S(1)}, bf16[2,1,16,32,128]{4,3,2,1,0:T(8,128)(2,1)}, u32[]{:S(2)}, u32[]{:S(2)}) collective-permute-start(bf16[2,1,16,32,128]{4,3,2,1,0:T(8,128)(2,1)S(1)} %collective-permute-done.41.refs_4_), channel_id=1, source_target_pairs={{5,3},{4,2},{3,1},{2,0},{13,11},{12,10},{11,9},{10,8},{21,19},{20,... | collective-permute-start | bytes 786440 | tf_op jit(solution)/shard_map/ppermute | solution.py:515
  366.4 25.4 %collective-permute-start.46 = (bf16[2,1,16,32,128]{4,3,2,1,0:T(8,128)(2,1)}, bf16[2,1,16,32,128]{4,3,2,1,0:T(8,128)(2,1)S(1)}, u32[]{:S(2)}, u32[]{:S(2)}) collective-permute-start(bf16[2,1,16,32,128]{4,3,2,1,0:T(8,128)(2,1)} %collective-permute-done.42.refs_2_), channel_id=1, source_target_pairs={{4,6},{5,7},{12,14},{13,15},{20,22},{21,23},{28,30},{29,31}} | collective-permute-start | bytes 786440 | tf_op jit(solution)/shard_map/ppermute | solution.py:514
  367.1 26.6 %collective-permute-start.47 = (bf16[2,1,16,32,128]{4,3,2,1,0:T(8,128)(2,1)}, bf16[2,1,16,32,128]{4,3,2,1,0:T(8,128)(2,1)S(1)}, u32[]{:S(2)}, u32[]{:S(2)}) collective-permute-start(bf16[2,1,16,32,128]{4,3,2,1,0:T(8,128)(2,1)} %collective-permute-done.43.refs_5_), channel_id=1, source_target_pairs={{3,1},{2,0},{11,9},{10,8},{19,17},{18,16},{27,25},{26,24}} | collective-permute-start | bytes 786440 | tf_op jit(solution)/shard_map/ppermute | solution.py:515
  393.7 129.3 %reduce-scatter.9.cloned.1.call-start = ((), (), s32[]{:S(2)}) async-start(), calls=%async_computation.6 | async-start | bytes 3932160 | tf_op jit(solution)/shard_map/reduce_scatter | solution.py:677
  461.4 11.9 %collective-permute-start.56 = (bf16[1,3,16,32,128]{4,3,2,1,0:T(8,128)(2,1)S(1)}, bf16[1,3,16,32,128]{4,3,2,1,0:T(8,128)(2,1)S(1)}, u32[]{:S(2)}, u32[]{:S(2)}) collective-permute-start(bf16[1,3,16,32,128]{4,3,2,1,0:T(8,128)(2,1)S(1)} %slice_bitcast_fusion), channel_id=1, source_target_pairs={{0,1},{1,0},{2,3},{3,2},{4,5},{5,4},{6,7},{7,6},{8,9},{9,8},{10,11... | collective-permute-start | bytes 1179656 | tf_op jit(solution)/shard_map/ppermute | solution.py:490
  (48 other events, 365.6 us)
Sparse Core Ops, SparseCore 0:
  31.2 72.2 all-gather.10
  105.6 49.2 all-gather.8
  157.8 59.1 reduce-scatter.4
  219.7 70.5 reduce-scatter.6
  291.8 52.0 all-gather.14
  345.9 51.5 all-gather.12
  400.3 60.0 reduce-scatter.10
  462.7 60.2 reduce-scatter.8

commit v13 on v12

--- a/solution.py
+++ b/solution.py
@@ -181,6 +181,34 @@
     return jnp.concatenate([rest - part for rest, part in zip(rests, parts)], axis=0)
 
 
+def inner_kernel(core_ref, rhs_ref, coeff_ref, low_ref, wide_ref):
+    def body(times):
+        update = precondition(jnp.swapaxes(rhs_ref[times], 0, 1), coeff_ref)
+        wide_ref[:, times] = update[1:-1]
+
+    time_chunks(wide_ref.shape[1], body)
+    low_ref[0] = wide_ref[...].astype(low_ref.dtype)
+
+
+def inner(group, members, core, rhs, coeff):
+    steps, _, rows, cols = rhs.shape
+    flat = rhs.reshape(steps, -1, cols)
+    inside = rows - 2 * HALO
+    return call(
+        inner_kernel,
+        core,
+        (members,),
+        [
+            pl.BlockSpec((steps, rows, cols), lambda b, core: (0, b + group * members, 0)),
+            whole_block(coeff),
+        ],
+        pl.BlockSpec((1, inside, steps, cols), lambda b, core: (b, 0, 0, 0)),
+        pltpu.HBM((members, inside, steps, cols), jnp.bfloat16),
+        [pltpu.VMEM((inside, steps, cols), jnp.float32)],
+        name="inner",
+    )(core, *in_hbm(flat), coeff)
+
+
 def held(rests, misfits, iterate):
     above, rest, below = rests
     own, other, same, cross = misfits
@@ -271,8 +299,8 @@
     )
 
 
-def marks_of(cell_ref, width):
-    first = pl.program_id(0) * width
+def marks_of(cell_ref, width, chunk):
+    first = chunk * width
     parts = []
     for start_lane in range(0, width, LANES):
         lane = lax.broadcasted_iota(jnp.int32, cell_ref.shape, 1) + (first + start_lane)
@@ -286,6 +314,11 @@
         ref[part, here].reshape(LANES, width) for part in range(2) for ref in (own_ref, other_ref)
     ]
     return jnp.concatenate(parts, axis=0)
+
+
+def place_of(chunk, core_ref, split):
+    chunks = pl.num_programs(0)
+    return jnp.where(core_ref[0] == 1, chunk, (chunk + 1) % chunks) if split else chunk
 
 
 def observe_kernel(core_ref, field_ref, *refs):
@@ -305,22 +338,42 @@
         acc[...] = jnp.zeros_like(acc)
         picked[...] = jnp.zeros_like(picked)
 
-    marks = marks_of(cell_ref, width)
-
-    def history(b, r):
-        if b < whole:
-            here = field_ref[..., b, r, :, :]
-            return here.reshape(2 * chips * steps, lanes)
-        slots = [slot_refs[0][:, b - whole, r]]
+    split = len(slot_refs) > 0 and len(field_ref.shape) == 5
+    marks = marks_of(cell_ref, width, place_of(chunk, core_ref, split))
+
+    def gathered(b, r):
+        return field_ref[..., b, r, :, :].reshape(2 * chips * steps, lanes)
+
+    def along(b, r):
+        slots = [slot_refs[0][:, b, r]]
         for k in range(1, chips):
-            slots.append(slot_refs[k][:, b - whole, r] + slot_refs[2 * chips - 1 - k][:, b - whole, r])
+            slots.append(slot_refs[k][:, b, r] + slot_refs[2 * chips - 1 - k][:, b, r])
         return jnp.concatenate([slot.reshape(2 * steps, lanes) for slot in slots], axis=0)
 
-    for b in range(members):
-        table = table_ref[...] if b < whole else around_ref[...]
-        spectrum = dot(table, jnp.concatenate([history(b, r) for r in range(rows)], axis=1))
+    def transform(b, table, history, first):
+        times = jnp.concatenate([history(b - first, r) for r in range(rows)], axis=1)
+        spectrum = dot(table[...], times)
         spec[2 * b] = spectrum[:freqs]
         spec[2 * b + 1] = spectrum[freqs:]
+
+    if split:
+
+        @pl.when(chunk < pl.num_programs(0) - 1)
+        def _():
+            for b in range(members):
+                transform(b, table_ref, gathered, 0)
+
+        @pl.when(chunk == pl.num_programs(0) - 1)
+        def _():
+            for b in range(members):
+                transform(b, around_ref, along, 0)
+
+    else:
+        for b in range(members):
+            if b < whole:
+                transform(b, table_ref, gathered, 0)
+            else:
+                transform(b, around_ref, along, whole)
     for m in range(2 * members):
         picked[m] += dot_lanes(spec[m].astype(jnp.bfloat16), marks)
     for q in range(freqs // near):
@@ -360,24 +413,35 @@
 
 def observe(core, field, slots, own, other, table, around, local_cells):
     *sources, whole, rows, steps, lanes = field.shape
-    apart = slots[0].shape[1] if slots else 0
-    members = whole + apart
+    split = len(sources) == 1
+    apart = slots[0].shape[1]
+    members = whole if split else whole + apart
     _, freqs, sensors, cells = own.shape
     width = CHUNK_ROWS * lanes
     near = lanes // sensors
     shape = (2, 2, members, freqs // near, lanes)
     chunks = cells // (2 * width)
-    first = chunks if len(sources) == 1 else 0
     block = (*sources, whole, CHUNK_ROWS, steps, lanes)
     lead = (0,) * len(sources) + (0,)
-    slot = pl.BlockSpec((2, apart, CHUNK_ROWS, steps, lanes), lambda c, core: (0, 0, c, 0, 0))
+
+    def field_place(c, core):
+        return (*lead, core[0] * (chunks - 1) + jnp.minimum(c, chunks - 2) if split else c, 0, 0)
+
+    def map_place(c, core):
+        here = jnp.where(core[0] == 1, c, (c + 1) % chunks) if split else c
+        return (0, 0, 0, core[0] * chunks + here)
+
+    slot = pl.BlockSpec(
+        (2, apart, CHUNK_ROWS, steps, lanes), lambda c, core: (0, 0, 0 if split else c, 0, 0)
+    )
+    map_block = pl.BlockSpec(own.shape[:3] + (width,), map_place)
     return call(
         observe_kernel,
         core,
         (chunks,),
-        [pl.BlockSpec(block, lambda c, core: (*lead, core[0] * first + c, 0, 0))]
+        [pl.BlockSpec(block, field_place)]
         + [slot] * len(slots)
-        + map_specs(own, width)
+        + [map_block] * 2
         + [whole_block(table), whole_block(around), whole_block(local_cells)],
         pl.BlockSpec(shape, lambda c, core: (0, 0, 0, 0, 0)),
         jax.ShapeDtypeStruct(shape, jnp.float32),
@@ -422,7 +486,7 @@
                 weights[2 * b + 1, here, :wide] = w_imag
                 weights[2 * b + 1, here, wide:] = -w_real
 
-    marks = marks_of(cell_ref, width)
+    marks = marks_of(cell_ref, width, pl.program_id(0))
     for m in range(2 * members):
         adjoint[m] = dot(weights[m, :, :wide].astype(jnp.bfloat16), marks)
     for q in range(freqs // near):
@@ -529,6 +593,15 @@
         return [self.value, *self.ups, *self.downs]
 
 
+def coefficients(stiff, diag):
+    inside = diag > 0.0
+    inverse = jnp.where(inside, 1.0 / jnp.where(inside, diag, 1.0), 0.0)
+    unscale = jnp.where(inside, 1.0 / jnp.where(inside, stiff, 1.0), 0.0)
+    scaled = DAMPING * inverse * stiff
+    coeff = jnp.stack([scaled, scaled * stiff, unscale, stiff, diag])
+    return jnp.broadcast_to(coeff[:, :, None, :], (*coeff.shape[:2], SUBLANES, coeff.shape[2]))
+
+
 def shards(rhs, forward_map, stiffness, reaction, noise_weight, sensor_cell):
     steps, samples, rows, cols = rhs.shape
     _, freqs, sensors, cells = forward_map.shape
@@ -581,12 +654,8 @@
         unpacked(value) for value in rims(packed(0), packed(rows - HALO))
     )
     stiff, diag = jnp.concatenate([up, local, down], axis=1)
-    inside = diag > 0.0
-    inverse = jnp.where(inside, 1.0 / jnp.where(inside, diag, 1.0), 0.0)
-    unscale = jnp.where(inside, 1.0 / jnp.where(inside, stiff, 1.0), 0.0)
-    scaled = DAMPING * inverse * stiff
-    coeff = jnp.stack([scaled, scaled * stiff, unscale, stiff, diag])
-    coeff = jnp.broadcast_to(coeff[:, :, None, :], coeff.shape[:2] + (SUBLANES, cols))
+    coeff = coefficients(stiff, diag)
+    local_coeff = coefficients(stiffness, diagonal)
 
     def per_lane(values):
         own = lax.dynamic_slice_in_dim(values, sensor_index * sensors, sensors)
@@ -602,17 +671,16 @@
     lines = [[k for k in range(size) if k % 2 == parity] for parity in range(2)]
     shape = (chips, 2, members, rows // 2, steps, cols)
 
-    def both_cores(low):
-        keep, give = (
-            lax.dynamic_slice_in_dim(low, first * (rows // 2), rows // 2, axis=1)
-            for first in (core[0], 1 - core[0])
-        )
+    def both_cores(low, first, last, count):
+        here = first + (last - first) * core[0]
+        keep = lax.dynamic_slice_in_dim(low, here, count, axis=1)
+        give = lax.dynamic_slice_in_dim(low, first + last - here, count, axis=1)
         return jnp.stack([keep, swap_cores(give)])
 
     def ready(state):
         iterate, low, rest, top, bottom = state
         above, below = rims(top, bottom)
-        pair = both_cores(low)
+        pair = both_cores(low, 0, rows // 2, rows // 2)
         parts = lax.optimization_barrier((pair[:, :whole], pair[:, whole:]))
         return iterate, *parts, (above, rest, below)
 
@@ -623,17 +691,19 @@
         _, cross = misfit_rims(edge[1:])
         return misfit, swap_cores(misfit[1:]), same, cross
 
+    inside = inner(0, members, core, rhs, local_coeff)
     iterate, low, rest, *ends = start(0, members, core, rhs, up_first, down_first, coeff)
     above, below = rims(*ends)
-    states = [(iterate, low, None, (above, rest, below))]
+    states = [(iterate, inside, None, (above, rest, below))]
+    line = Line(both_cores(low, 0, rows - CHUNK_ROWS, CHUNK_ROWS))
+    line.hop()
     for group in range(1, GROUPS):
         ends = tuple(
             rim_rows(groups[group], first).astype(jnp.bfloat16) for first in (0, rows - HALO)
         )
-        _, rests, ends = lax.optimization_barrier((low, states[0][3], ends))
+        rests, ends = line.after((states[0][3], ends))
         states[0] = (*states[0][:3], rests)
         states.append(ready(start(group, members, core, rhs, *rims(*ends), coeff)))
-    line = None
 
     outputs = ()
     for iteration in range(ITERS):
@@ -641,13 +711,12 @@
             lax.all_gather(state[1], "sensors", axis_index_groups=None if state[2] is None else lines)
             for state in states
         ]
-        if line is not None:
-            line.hop(last=True)
+        line.hop(last=True)
         totals = []
         for group in range(GROUPS):
-            iterate, _, _, rests = states[group]
+            iterate, sent, _, rests = states[group]
             field = fields[group]
-            slots, line = (line.slots() if line is not None else []), None
+            slots, line = line.slots(), None
             if group > 0:
                 field, rests = lax.optimization_barrier((field, rests))
             states[group] = iterate, rests
@@ -662,7 +731,7 @@
                 slots,
                 forward_map,
                 other_map,
-                table if slots else in_order,
+                in_order if sent.ndim == 4 else table,
                 around,
                 local_cells,
             )

time: 552 us -> 593 us (1.074)
  starting transfers between devices: 100 us -> 120 us
  waiting for transfers between devices: 227 us -> 243 us
    ppermute x9 -> x12, waiting for transfers between devices: 36.9 us -> 59.9 us  [hop(): down = lax.ppermute(self.ends[1], 'sensors', backward)]
    ppermute x12 -> x13, waiting for transfers between devices: 6.79 us -> 23.3 us  [swap_cores(): return lax.ppermute(value, 'sensors', [(k, k ^ 1) for k in range(size)])]
    all_gather x4, waiting for transfers between devices: 14.7 us -> 2.89 us  [shards(): lax.all_gather(state[1], 'sensors', axis_index_groups=None if state[2] is...]
    ppermute x12 -> x13, starting transfers between devices: 12.5 us -> 22 us  [swap_cores(): return lax.ppermute(value, 'sensors', [(k, k ^ 1) for k in range(size)])]
    ppermute x9 -> x12, waiting for transfers between devices: 27.2 us -> 18 us  [hop(): up = lax.ppermute(self.ends[0], 'sensors', onward)]
    ppermute x9 -> x12, starting transfers between devices: 14.7 us -> 22.3 us  [hop(): up = lax.ppermute(self.ends[0], 'sensors', onward)]
    reduce_scatter x4, waiting for transfers between devices: 86 us -> 79.7 us  [shards(): lax.psum_scatter(misfit, 'sensors', scatter_dimension=0, axis_index_group...]
    pallas_call x4 -> x5, Pallas kernels: 71.5 us -> 77.3 us  [the longest x4 71.5 us: observe(): call(observe_kernel, core, (chunks,), [pl.BlockSpec(block, field_place)]...]
  transfers between devices with their start and end apart: 70 -> 77, of which waited for: 45 -> 43; matrix products, arithmetic and copies ran while one was open for 4% -> 4% of each run, Pallas kernels for 32% -> 31%
where the time goes in v13:
time: 593 us; the launch traced here: 591 us
  waiting for transfers between devices  243 us (41%)
  Pallas kernels  189 us (32%)
  starting transfers between devices  120 us (20%)
  local copies, waits for them, and re-layouts  16.2 us (3%)
  between operations  15.2 us (3%)
  other arithmetic  7.88 us (1%)
    reduce_scatter x4, waiting for transfers between devices, shards(): lax.psum_scatter(misfit, 'sensors', scatter_dimension=0, axis_index_group...  79.7 us
    pallas_call x4, Pallas kernels, observe(): call(observe_kernel, core, (chunks,), [pl.BlockSpec(block, field_place)]...  71.5 us
    pallas_call x4, Pallas kernels, pull_back(): call(pull_kernel, core, (rows // CHUNK_ROWS,), [whole_block(array) for ar...  63.5 us
    ppermute x12, waiting for transfers between devices, hop(): down = lax.ppermute(self.ends[1], 'sensors', backward)  59.9 us
    ppermute x13, waiting for transfers between devices, swap_cores(): return lax.ppermute(value, 'sensors', [(k, k ^ 1) for k in range(size)])  23.3 us
    ppermute x12, starting transfers between devices, hop(): up = lax.ppermute(self.ends[0], 'sensors', onward)  22.3 us
    ppermute x13, starting transfers between devices, swap_cores(): return lax.ppermute(value, 'sensors', [(k, k ^ 1) for k in range(size)])  22 us
    ppermute x8, starting transfers between devices, misfit_rims(): return (lax.ppermute(edge, both, same), lax.ppermute(edge, both, cross))  21.9 us
  transfers between devices with their start and end apart: 77, of which 43 were waited for; matrix products, arithmetic and copies ran while one was open for 4% of the time, Pallas kernels for 31%

profile of v13, /device:TPU:1, one launch (start us, length us, event | category | flops | bytes accessed | tf_op | source)
XLA Modules:
  0.0 590.9 jit_solution(10757964355577488027)
XLA Ops:
  11.1 5.9 inner.1
  18.7 4.6 collective-permute-start
  29.7 8.2 %start.2 = (f32[3,32,32,128]{3,2,1,0:T(8,128)}, bf16[3,32,32,128]{3,2,1,0:T(8,128)(2,1)}, f32[3,32,32,128]{3,2,1,0:T(8,128)}, bf16[3,4,32,128]{3,2,1,0:T(8,128)(2,1)S(1)}, bf16[3,4,32,128]{3,2,1,0:T(8,128)(2,1)S(1)}) custom-call(s32[1]{0:T(128)} %bitcast.core_ref, f32[32,192,128]{2,1,0:T(8,128)} %bitcast.77, bf16[3,4,32,128]{3,2,1,0:T(8,128)(2,1)S(1)} %bitcast.74, ...), custom_call_target="tpu_custom_call" | custom-call | tf_op jit(solution)/shard_map/start/pallas_call | solution.py:155
  40.0 16.7 %collective-permute-done.2 = bf16[3,4,32,128]{3,2,1,0:T(8,128)(2,1)S(1)} collective-permute-done((bf16[3,4,32,128]{3,2,1,0:T(8,128)(2,1)S(1)}, bf16[3,4,32,128]{3,2,1,0:T(8,128)(2,1)S(1)}, u32[]{:S(2)}, u32[]{:S(2)}) %collective-permute-start.2) | collective-permute-done | bytes 98336 | tf_op jit(solution)/shard_map/ppermute | solution.py:554
  56.7 4.3 collective-permute-start.3
  80.8 8.2 %start.3 = (f32[3,32,32,128]{3,2,1,0:T(8,128)}, bf16[3,32,32,128]{3,2,1,0:T(8,128)(2,1)}, f32[3,32,32,128]{3,2,1,0:T(8,128)}, bf16[3,4,32,128]{3,2,1,0:T(8,128)(2,1)}, bf16[3,4,32,128]{3,2,1,0:T(8,128)(2,1)}) custom-call(s32[1]{0:T(128)} %bitcast.core_ref, f32[32,192,128]{2,1,0:T(8,128)} %bitcast.78, ...), custom_call_target="tpu_custom_call" | custom-call | tf_op jit(solution)/shard_map/start/pallas_call | solution.py:155
  106.9 21.3 %collective-permute-done.18.refs_5_ = bf16[2,3,4,32,128]{4,3,2,1,0:T(8,128)(2,1)} collective-permute-done((bf16[2,3,4,32,128]{4,3,2,1,0:T(8,128)(2,1)S(1)}, bf16[2,3,4,32,128]{4,3,2,1,0:T(8,128)(2,1)}, u32[]{:S(2)}, u32[]{:S(2)}) %collective-permute-start.18) | collective-permute-done | bytes 196640 | tf_op jit(solution)/shard_map/ppermute | solution.py:579
  132.2 14.2 %collective-permute-done.19.refs_6_ = bf16[2,3,4,32,128]{4,3,2,1,0:T(8,128)(2,1)} collective-permute-done((bf16[2,3,4,32,128]{4,3,2,1,0:T(8,128)(2,1)}, bf16[2,3,4,32,128]{4,3,2,1,0:T(8,128)(2,1)}, u32[]{:S(2)}, u32[]{:S(2)}) %collective-permute-start.19) | collective-permute-done | bytes 196640 | tf_op jit(solution)/shard_map/ppermute | solution.py:579
  146.5 18.3 %observe.4 = f32[2,2,3,16,128]{4,3,2,1,0:T(8,128)S(1)} custom-call(s32[1]{0:T(128)} %bitcast.core_ref, bf16[8,3,24,32,128]{4,3,2,1,0:T(8,128)(2,1)} %bitcast.79, bf16[2,3,4,32,128]{4,3,2,1,0:T(8,128)(2,1)S(1)} %pad_maximum_fusion.3.refs_0_, bf16[2,3,4,32,128]{4,3,2,1,0:T(8,128)(2,1)S(1)} %collective-permute-done.3.refs_1_, ...), custom_call_target="tpu_custom_call" | custom-call | flops 402653184 | bytes 38273024 | tf_op jit(solution)/shard_map/observe/pallas_call | solution.py:438
  164.8 8.6 %collective-permute-start.23 = (f32[2,2,3,16,128]{4,3,2,1,0:T(8,128)S(1)}, f32[2,2,3,16,128]{4,3,2,1,0:T(8,128)S(1)}, u32[]{:S(2)}, u32[]{:S(2)}) collective-permute-start(f32[2,2,3,16,128]{4,3,2,1,0:T(8,128)S(1)} %observe.4), channel_id=1, source_target_pairs={{0,1},{1,0},{2,3},{3,2},{4,5},{5,4},{6,7},{7,6},{8,9},{9,8},{10,11... | collective-permute-start | bytes 294920 | tf_op jit(solution)/shard_map/ppermute | solution.py:554
  182.9 15.8 %pull_back.4 = bf16[4,2,3,16,32,128]{5,4,3,2,1,0:T(8,128)(2,1)} custom-call(s32[1]{0:T(128)} %bitcast.core_ref, f32[2,2,3,16,128]{4,3,2,1,0:T(8,128)S(1)} %reverse_add_fusion.3.refs_0_, f32[2,2,3,16,128]{4,3,2,1,0:T(8,128)S(1)} %collective-permute-done.24.refs_1_, f32[2,2,3,16,128]{4,3,2,1,0:T(8,128)S(1)} %collective-permute-done.25.refs_2_, ...), custom_call_target="tpu_custom_call" | custom-call | flops 402653184 | bytes 36700160 | tf_op jit(solution)/shard_map/pull_back/pallas_call | solution.py:512
  202.9 4.5 collective-permute-done.11.down_ref
  207.4 17.7 %observe.5 = f32[2,2,3,16,128]{4,3,2,1,0:T(8,128)S(1)} custom-call(s32[1]{0:T(128)} %bitcast.core_ref, bf16[4,2,2,16,32,128]{5,4,3,2,1,0:T(8,128)(2,1)} %bitcast.90, bf16[2,1,16,32,128]{4,3,2,1,0:T(8,128)(2,1)S(1)} %pad_maximum_fusion.2.refs_0_, bf16[2,1,16,32,128]{4,3,2,1,0:T(8,128)(2,1)S(1)} %collective-permute-done.12.refs_1_, ...), custom_call_target="tpu_custom_call" | custom-call | flops 402653184 | bytes 35651584 | tf_op jit(solution)/shard_map/observe/pallas_call | solution.py:438
  236.1 15.9 %pull_back.5 = bf16[4,2,3,16,32,128]{5,4,3,2,1,0:T(8,128)(2,1)} custom-call(s32[1]{0:T(128)} %bitcast.core_ref, f32[2,2,3,16,128]{4,3,2,1,0:T(8,128)S(1)} %reverse_add_fusion.2.refs_0_, f32[2,2,3,16,128]{4,3,2,1,0:T(8,128)S(1)} %collective-permute-done.36.refs_1_, f32[2,2,3,16,128]{4,3,2,1,0:T(8,128)S(1)} %collective-permute-done.37.refs_2_, ...), custom_call_target="tpu_custom_call" | custom-call | flops 402653184 | bytes 36700160 | tf_op jit(solution)/shard_map/pull_back/pallas_call | solution.py:512
  252.1 6.1 %reduce-scatter.5.cloned.1.call-done = bf16[1,2,3,16,32,128]{5,4,3,2,1,0:T(8,128)(2,1)} async-done(((bf16[4,2,3,16,32,128]{5,4,3,2,1,0:T(8,128)(2,1)}), bf16[1,2,3,16,32,128]{5,4,3,2,1,0:T(8,128)(2,1)}) %reduce-scatter.5.cloned.1.call-update) | async-done | bytes 786448 | tf_op jit(solution)/shard_map/reduce_scatter | solution.py:746
  266.6 4.6 collective-permute-done.29.cross_ref
  271.2 8.7 %step.2 = (f32[3,32,32,128]{3,2,1,0:T(8,128)}, bf16[3,32,32,128]{3,2,1,0:T(8,128)(2,1)}, f32[3,32,32,128]{3,2,1,0:T(8,128)}, bf16[3,4,32,128]{3,2,1,0:T(8,128)(2,1)S(1)}, bf16[3,4,32,128]{3,2,1,0:T(8,128)(2,1)S(1)}) custom-call(s32[1]{0:T(128)} %bitcast.core_ref, bf16[3,4,32,128]{3,2,1,0:T(8,128)(2,1)S(1)} %collective-permute-done.5.up_ref, ...), custom_call_target="tpu_custom_call" | custom-call | tf_op jit(solution)/shard_map/step/pallas_call | solution.py:242
  287.8 10.4 %collective-permute-done.31.refs_1_ = bf16[2,1,16,32,128]{4,3,2,1,0:T(8,128)(2,1)S(1)} collective-permute-done((bf16[2,1,16,32,128]{4,3,2,1,0:T(8,128)(2,1)S(1)}, bf16[2,1,16,32,128]{4,3,2,1,0:T(8,128)(2,1)S(1)}, u32[]{:S(2)}, u32[]{:S(2)}) %collective-permute-start.31) | collective-permute-done | bytes 262176 | tf_op jit(solution)/shard_map/ppermute | solution.py:578
  298.8 10.1 %collective-permute-done.33.refs_4_ = bf16[2,1,16,32,128]{4,3,2,1,0:T(8,128)(2,1)S(1)} collective-permute-done((bf16[2,1,16,32,128]{4,3,2,1,0:T(8,128)(2,1)S(1)}, bf16[2,1,16,32,128]{4,3,2,1,0:T(8,128)(2,1)S(1)}, u32[]{:S(2)}, u32[]{:S(2)}) %collective-permute-start.33) | collective-permute-done | bytes 262176 | tf_op jit(solution)/shard_map/ppermute | solution.py:579
  312.8 18.8 %reduce-scatter.7.cloned.1.call-done = bf16[1,2,3,16,32,128]{5,4,3,2,1,0:T(8,128)(2,1)} async-done(((bf16[4,2,3,16,32,128]{5,4,3,2,1,0:T(8,128)(2,1)}), bf16[1,2,3,16,32,128]{5,4,3,2,1,0:T(8,128)(2,1)}) %reduce-scatter.7.cloned.1.call-update) | async-done | bytes 786448 | tf_op jit(solution)/shard_map/reduce_scatter | solution.py:746
  344.4 8.7 %step.3 = (f32[3,32,32,128]{3,2,1,0:T(8,128)}, bf16[3,32,32,128]{3,2,1,0:T(8,128)(2,1)}, f32[3,32,32,128]{3,2,1,0:T(8,128)}, bf16[3,4,32,128]{3,2,1,0:T(8,128)(2,1)S(1)}, bf16[3,4,32,128]{3,2,1,0:T(8,128)(2,1)S(1)}) custom-call(s32[1]{0:T(128)} %bitcast.core_ref, bf16[3,4,32,128]{3,2,1,0:T(8,128)(2,1)S(1)} %copy-done.5, ...), custom_call_target="tpu_custom_call" | custom-call | tf_op jit(solution)/shard_map/step/pallas_call | solution.py:242
  364.7 7.5 %collective-permute-done.47.refs_1_ = bf16[2,1,16,32,128]{4,3,2,1,0:T(8,128)(2,1)S(1)} collective-permute-done((bf16[2,1,16,32,128]{4,3,2,1,0:T(8,128)(2,1)S(1)}, bf16[2,1,16,32,128]{4,3,2,1,0:T(8,128)(2,1)S(1)}, u32[]{:S(2)}, u32[]{:S(2)}) %collective-permute-start.47) | collective-permute-done | bytes 262176 | tf_op jit(solution)/shard_map/ppermute | solution.py:578
  372.2 10.0 %collective-permute-done.48.refs_4_ = bf16[2,1,16,32,128]{4,3,2,1,0:T(8,128)(2,1)S(1)} collective-permute-done((bf16[2,1,16,32,128]{4,3,2,1,0:T(8,128)(2,1)S(1)}, bf16[2,1,16,32,128]{4,3,2,1,0:T(8,128)(2,1)S(1)}, u32[]{:S(2)}, u32[]{:S(2)}) %collective-permute-start.48) | collective-permute-done | bytes 262176 | tf_op jit(solution)/shard_map/ppermute | solution.py:579
  389.2 17.8 %observe.6 = f32[2,2,3,16,128]{4,3,2,1,0:T(8,128)S(1)} custom-call(s32[1]{0:T(128)} %bitcast.core_ref, bf16[4,2,2,16,32,128]{5,4,3,2,1,0:T(8,128)(2,1)} %bitcast.91, bf16[2,1,16,32,128]{4,3,2,1,0:T(8,128)(2,1)S(1)} %pad_maximum_fusion.1.refs_0_, bf16[2,1,16,32,128]{4,3,2,1,0:T(8,128)(2,1)S(1)} %collective-permute-done.31.refs_1_, ...), custom_call_target="tpu_custom_call" | custom-call | flops 402653184 | bytes 35651584 | tf_op jit(solution)/shard_map/observe/pallas_call | solution.py:438
  417.1 15.9 %pull_back.6 = bf16[4,2,3,16,32,128]{5,4,3,2,1,0:T(8,128)(2,1)} custom-call(s32[1]{0:T(128)} %bitcast.core_ref, f32[2,2,3,16,128]{4,3,2,1,0:T(8,128)S(1)} %reverse_add_fusion.1.refs_0_, f32[2,2,3,16,128]{4,3,2,1,0:T(8,128)S(1)} %collective-permute-done.56.refs_1_, f32[2,2,3,16,128]{4,3,2,1,0:T(8,128)S(1)} %collective-permute-done.57.refs_2_, ...), custom_call_target="tpu_custom_call" | custom-call | flops 402653184 | bytes 36700160 | tf_op jit(solution)/shard_map/pull_back/pallas_call | solution.py:512
  443.5 17.7 %observe.7 = f32[2,2,3,16,128]{4,3,2,1,0:T(8,128)S(1)} custom-call(s32[1]{0:T(128)} %bitcast.core_ref, bf16[4,2,2,16,32,128]{5,4,3,2,1,0:T(8,128)(2,1)} %bitcast.92, bf16[2,1,16,32,128]{4,3,2,1,0:T(8,128)(2,1)S(1)} %pad_maximum_fusion.refs_0_, bf16[2,1,16,32,128]{4,3,2,1,0:T(8,128)(2,1)S(1)} %collective-permute-done.47.refs_1_, ...), custom_call_target="tpu_custom_call" | custom-call | flops 402653184 | bytes 35651584 | tf_op jit(solution)/shard_map/observe/pallas_call | solution.py:438
  473.2 16.0 %pull_back.7 = bf16[4,2,3,16,32,128]{5,4,3,2,1,0:T(8,128)(2,1)} custom-call(s32[1]{0:T(128)} %bitcast.core_ref, f32[2,2,3,16,128]{4,3,2,1,0:T(8,128)S(1)} %reverse_add_fusion.refs_0_, f32[2,2,3,16,128]{4,3,2,1,0:T(8,128)S(1)} %collective-permute-done.60.refs_1_, f32[2,2,3,16,128]{4,3,2,1,0:T(8,128)S(1)} %collective-permute-done.61.refs_2_, ...), custom_call_target="tpu_custom_call" | custom-call | flops 402653184 | bytes 36700160 | tf_op jit(solution)/shard_map/pull_back/pallas_call | solution.py:512
  489.2 12.4 %reduce-scatter.11.cloned.1.call-done = bf16[1,2,3,16,32,128]{5,4,3,2,1,0:T(8,128)(2,1)} async-done(((bf16[4,2,3,16,32,128]{5,4,3,2,1,0:T(8,128)(2,1)}), bf16[1,2,3,16,32,128]{5,4,3,2,1,0:T(8,128)(2,1)}) %reduce-scatter.11.cloned.1.call-update) | async-done | bytes 786448 | tf_op jit(solution)/shard_map/reduce_scatter | solution.py:746
  510.0 4.6 collective-permute-done.65.cross_ref
  514.5 7.3 %finish.2 = (f32[32,192,128]{2,1,0:T(8,128)}, f32[32,192,128]{2,1,0:T(8,128)}) custom-call(s32[1]{0:T(128)} %bitcast.core_ref, bf16[3,4,32,128]{3,2,1,0:T(8,128)(2,1)S(1)} %collective-permute-done.39.up_ref, f32[3,32,32,128]{3,2,1,0:T(8,128)} %get-tuple-element.134.rest_ref, bf16[3,4,32,128]{3,2,1,0:T(8,128)(2,1)S(1)} %copy-done.3, ...), custom_call_target="tpu_custom_call" | custom-call | tf_op jit(solution)/shard_map/finish/pallas_call | solution.py:282
  521.8 42.4 %reduce-scatter.9.cloned.1.call-done = bf16[1,2,3,16,32,128]{5,4,3,2,1,0:T(8,128)(2,1)} async-done(((bf16[4,2,3,16,32,128]{5,4,3,2,1,0:T(8,128)(2,1)}), bf16[1,2,3,16,32,128]{5,4,3,2,1,0:T(8,128)(2,1)}) %reduce-scatter.9.cloned.1.call-update) | async-done | bytes 786448 | tf_op jit(solution)/shard_map/reduce_scatter | solution.py:746
  576.8 7.3 %finish.3 = (f32[32,192,128]{2,1,0:T(8,128)}, f32[32,192,128]{2,1,0:T(8,128)}) custom-call(s32[1]{0:T(128)} %bitcast.core_ref, bf16[3,4,32,128]{3,2,1,0:T(8,128)(2,1)S(1)} %collective-permute-done.45.up_ref, f32[3,32,32,128]{3,2,1,0:T(8,128)} %get-tuple-element.118.rest_ref, ...), custom_call_target="tpu_custom_call", output_to_operand_aliasing={{0}: (10, {}), {1}: (11, {})} | custom-call | tf_op jit(solution)/shard_map/finish/pallas_call | solution.py:282
  (254 shorter events, 185.4 us)
Async XLA Ops:
  7.2 122.4 %all-gather.11.cloned.1.call-start = ((), (), s32[]{:S(2)}) async-start(), calls=%async_computation.9 | async-start | bytes 5308416 | tf_op jit(solution)/shard_map/all_gather | solution.py:711
  7.2 139.2 %collective-permute-start.20 = (bf16[2,128,16,4096]{3,2,1,0:T(8,128)(2,1)}, bf16[2,128,16,4096]{3,2,1,0:T(8,128)(2,1)}, u32[]{:S(2)}, u32[]{:S(2)}) collective-permute-start(bf16[2,128,16,4096]{3,2,1,0:T(8,128)(2,1)} %refs_5_.7), channel_id=1, source_target_pairs={{0,1},{1,0},{2,3},{3,2},{4,5},{5,4},{6,7},{7,6},{8,9},{9,8},{10,11... | collective-permute-start | bytes 100663304 | tf_op jit(solution)/shard_map/ppermute | solution.py:554
  17.0 190.4 %all-gather.9.cloned.1.call-start = ((), (), s32[]{:S(2)}) async-start(), calls=%async_computation.8 | async-start | bytes 2621440 | tf_op jit(solution)/shard_map/all_gather | solution.py:711
  38.9 17.8 %collective-permute-start.2 = (bf16[3,4,32,128]{3,2,1,0:T(8,128)(2,1)S(1)}, bf16[3,4,32,128]{3,2,1,0:T(8,128)(2,1)S(1)}, u32[]{:S(2)}, u32[]{:S(2)}) collective-permute-start(bf16[3,4,32,128]{3,2,1,0:T(8,128)(2,1)S(1)} %get-tuple-element.169), channel_id=1, source_target_pairs={{0,1},{1,0},{2,3},{3,2},{4,5},{5,4},{6,7},{7,6},{8,9},{9,8},{10,11... | collective-permute-start | bytes 294920 | tf_op jit(solution)/shard_map/ppermute | solution.py:554
  95.5 162.7 %reduce-scatter.5.cloned.1.call-start = ((), (), s32[]{:S(2)}) async-start(), calls=%async_computation.4 | async-start | bytes 3932160 | tf_op jit(solution)/shard_map/reduce_scatter | solution.py:746
  97.2 32.4 %collective-permute-start.12 = (bf16[2,1,16,32,128]{4,3,2,1,0:T(8,128)(2,1)S(1)}, bf16[2,1,16,32,128]{4,3,2,1,0:T(8,128)(2,1)S(1)}, u32[]{:S(2)}, u32[]{:S(2)}) collective-permute-start(bf16[2,1,16,32,128]{4,3,2,1,0:T(8,128)(2,1)S(1)} %pad_maximum_fusion.2.refs_0_), channel_id=1, source_target_pairs={{0,2},{1,3},{2,4},{3,5},{4,6},{5,7},{8,10},{9,11},{10,12},{11,13},... | collective-permute-start | bytes 786440 | tf_op jit(solution)/shard_map/ppermute | solution.py:578
  101.4 28.1 %collective-permute-start.13 = (bf16[2,1,16,32,128]{4,3,2,1,0:T(8,128)(2,1)S(1)}, bf16[2,1,16,32,128]{4,3,2,1,0:T(8,128)(2,1)S(1)}, u32[]{:S(2)}, u32[]{:S(2)}) collective-permute-start(bf16[2,1,16,32,128]{4,3,2,1,0:T(8,128)(2,1)S(1)} %pad_maximum_fusion.2.refs_0_), channel_id=1, source_target_pairs={{7,5},{6,4},{5,3},{4,2},{3,1},{2,0},{15,13},{14,12},{13,11},{12,10... | collective-permute-start | bytes 786440 | tf_op jit(solution)/shard_map/ppermute | solution.py:579
  103.9 24.4 %collective-permute-start.18 = (bf16[2,3,4,32,128]{4,3,2,1,0:T(8,128)(2,1)S(1)}, bf16[2,3,4,32,128]{4,3,2,1,0:T(8,128)(2,1)}, u32[]{:S(2)}, u32[]{:S(2)}) collective-permute-start(bf16[2,3,4,32,128]{4,3,2,1,0:T(8,128)(2,1)S(1)} %collective-permute-done.4.refs_4_), channel_id=1, source_target_pairs={{5,3},{4,2},{3,1},{2,0},{13,11},{12,10},{11,9},{10,8},{21,19},{20,... | collective-permute-start | bytes 589832 | tf_op jit(solution)/shard_map/ppermute | solution.py:579
  105.6 26.6 %collective-permute-start.17 = (bf16[2,3,4,32,128]{4,3,2,1,0:T(8,128)(2,1)S(1)}, bf16[2,3,4,32,128]{4,3,2,1,0:T(8,128)(2,1)}, u32[]{:S(2)}, u32[]{:S(2)}) collective-permute-start(bf16[2,3,4,32,128]{4,3,2,1,0:T(8,128)(2,1)S(1)} %collective-permute-done.16.refs_2_), channel_id=1, source_target_pairs={{4,6},{5,7},{12,14},{13,15},{20,22},{21,23},{28,30},{29,31}} | collective-permute-start | bytes 589832 | tf_op jit(solution)/shard_map/ppermute | solution.py:578
  128.3 18.2 %collective-permute-start.19 = (bf16[2,3,4,32,128]{4,3,2,1,0:T(8,128)(2,1)}, bf16[2,3,4,32,128]{4,3,2,1,0:T(8,128)(2,1)}, u32[]{:S(2)}, u32[]{:S(2)}) collective-permute-start(bf16[2,3,4,32,128]{4,3,2,1,0:T(8,128)(2,1)} %collective-permute-done.18.refs_5_), channel_id=1, source_target_pairs={{3,1},{2,0},{11,9},{10,8},{19,17},{18,16},{27,25},{26,24}} | collective-permute-start | bytes 589832 | tf_op jit(solution)/shard_map/ppermute | solution.py:579
  129.6 35.2 %collective-permute-start.14 = (bf16[2,1,16,32,128]{4,3,2,1,0:T(8,128)(2,1)S(1)}, bf16[2,1,16,32,128]{4,3,2,1,0:T(8,128)(2,1)S(1)}, u32[]{:S(2)}, u32[]{:S(2)}) collective-permute-start(bf16[2,1,16,32,128]{4,3,2,1,0:T(8,128)(2,1)S(1)} %collective-permute-done.12.refs_1_), channel_id=1, source_target_pairs={{2,4},{3,5},{4,6},{5,7},{10,12},{11,13},{12,14},{13,15},{18,20},{1... | collective-permute-start | bytes 786440 | tf_op jit(solution)/shard_map/ppermute | solution.py:578
  130.3 34.5 %collective-permute-start.15 = (bf16[2,1,16,32,128]{4,3,2,1,0:T(8,128)(2,1)S(1)}, bf16[2,1,16,32,128]{4,3,2,1,0:T(8,128)(2,1)S(1)}, u32[]{:S(2)}, u32[]{:S(2)}) collective-permute-start(bf16[2,1,16,32,128]{4,3,2,1,0:T(8,128)(2,1)S(1)} %collective-permute-done.13.refs_4_), channel_id=1, source_target_pairs={{5,3},{4,2},{3,1},{2,0},{13,11},{12,10},{11,9},{10,8},{21,19},{20,... | collective-permute-start | bytes 786440 | tf_op jit(solution)/shard_map/ppermute | solution.py:579
  173.4 25.3 %collective-permute-start.21 = (bf16[2,1,16,32,128]{4,3,2,1,0:T(8,128)(2,1)S(1)}, bf16[2,1,16,32,128]{4,3,2,1,0:T(8,128)(2,1)S(1)}, u32[]{:S(2)}, u32[]{:S(2)}) collective-permute-start(bf16[2,1,16,32,128]{4,3,2,1,0:T(8,128)(2,1)S(1)} %collective-permute-done.14.refs_2_), channel_id=1, source_target_pairs={{4,6},{5,7},{12,14},{13,15},{20,22},{21,23},{28,30},{29,31}} | collective-permute-start | bytes 786440 | tf_op jit(solution)/shard_map/ppermute | solution.py:578
  174.1 24.7 %collective-permute-start.22 = (bf16[2,1,16,32,128]{4,3,2,1,0:T(8,128)(2,1)S(1)}, bf16[2,1,16,32,128]{4,3,2,1,0:T(8,128)(2,1)S(1)}, u32[]{:S(2)}, u32[]{:S(2)}) collective-permute-start(bf16[2,1,16,32,128]{4,3,2,1,0:T(8,128)(2,1)S(1)} %collective-permute-done.15.refs_5_), channel_id=1, source_target_pairs={{3,1},{2,0},{11,9},{10,8},{19,17},{18,16},{27,25},{26,24}} | collective-permute-start | bytes 786440 | tf_op jit(solution)/shard_map/ppermute | solution.py:579
  198.8 132.8 %reduce-scatter.7.cloned.1.call-start = ((), (), s32[]{:S(2)}) async-start(), calls=%async_computation.5 | async-start | bytes 3932160 | tf_op jit(solution)/shard_map/reduce_scatter | solution.py:746
  252.0 133.0 %all-gather.15.cloned.1.call-start = ((), (), s32[]{:S(2)}) async-start(), calls=%async_computation.11 | async-start | bytes 2621440 | tf_op jit(solution)/shard_map/all_gather | solution.py:711
  283.8 159.8 %all-gather.13.cloned.1.call-start = ((), (), s32[]{:S(2)}) async-start(), calls=%async_computation.10 | async-start | bytes 2621440 | tf_op jit(solution)/shard_map/all_gather | solution.py:711
  286.5 22.5 %collective-permute-start.33 = (bf16[2,1,16,32,128]{4,3,2,1,0:T(8,128)(2,1)S(1)}, bf16[2,1,16,32,128]{4,3,2,1,0:T(8,128)(2,1)S(1)}, u32[]{:S(2)}, u32[]{:S(2)}) collective-permute-start(bf16[2,1,16,32,128]{4,3,2,1,0:T(8,128)(2,1)S(1)} %pad_maximum_fusion.1.refs_0_), channel_id=1, source_target_pairs={{7,5},{6,4},{5,3},{4,2},{3,1},{2,0},{15,13},{14,12},{13,11},{12,10... | collective-permute-start | bytes 786440 | tf_op jit(solution)/shard_map/ppermute | solution.py:579
  298.2 33.4 %collective-permute-start.32 = (bf16[2,1,16,32,128]{4,3,2,1,0:T(8,128)(2,1)S(1)}, bf16[2,1,16,32,128]{4,3,2,1,0:T(8,128)(2,1)S(1)}, u32[]{:S(2)}, u32[]{:S(2)}) collective-permute-start(bf16[2,1,16,32,128]{4,3,2,1,0:T(8,128)(2,1)S(1)} %collective-permute-done.31.refs_1_), channel_id=1, source_target_pairs={{2,4},{3,5},{4,6},{5,7},{10,12},{11,13},{12,14},{13,15},{18,20},{1... | collective-permute-start | bytes 786440 | tf_op jit(solution)/shard_map/ppermute | solution.py:578
  308.9 22.7 %collective-permute-start.34 = (bf16[2,1,16,32,128]{4,3,2,1,0:T(8,128)(2,1)S(1)}, bf16[2,1,16,32,128]{4,3,2,1,0:T(8,128)(2,1)S(1)}, u32[]{:S(2)}, u32[]{:S(2)}) collective-permute-start(bf16[2,1,16,32,128]{4,3,2,1,0:T(8,128)(2,1)S(1)} %collective-permute-done.33.refs_4_), channel_id=1, source_target_pairs={{5,3},{4,2},{3,1},{2,0},{13,11},{12,10},{11,9},{10,8},{21,19},{20,... | collective-permute-start | bytes 786440 | tf_op jit(solution)/shard_map/ppermute | solution.py:579
  310.2 21.4 %collective-permute-start.39 = (bf16[3,4,32,128]{3,2,1,0:T(8,128)(2,1)S(1)}, bf16[3,4,32,128]{3,2,1,0:T(8,128)(2,1)S(1)}, u32[]{:S(2)}, u32[]{:S(2)}) collective-permute-start(bf16[3,4,32,128]{3,2,1,0:T(8,128)(2,1)S(1)} %get-tuple-element.107), channel_id=1, source_target_pairs={{0,8},{8,16},{16,24},{1,9},{9,17},{17,25},{2,10},{10,18},{18,26},{... | collective-permute-start | bytes 294920 | tf_op jit(solution)/shard_map/ppermute | solution.py:536
  311.5 20.1 %collective-permute-start.40 = (bf16[3,4,32,128]{3,2,1,0:T(8,128)(2,1)S(1)}, bf16[3,4,32,128]{3,2,1,0:T(8,128)(2,1)S(1)}, u32[]{:S(2)}, u32[]{:S(2)}) collective-permute-start(bf16[3,4,32,128]{3,2,1,0:T(8,128)(2,1)S(1)} %get-tuple-element.109), channel_id=1, source_target_pairs={{8,0},{16,8},{24,16},{9,1},{17,9},{25,17},{10,2},{18,10},{26,18},{... | collective-permute-start | bytes 294920 | tf_op jit(solution)/shard_map/ppermute | solution.py:536
  357.0 144.5 %reduce-scatter.11.cloned.1.call-start = ((), (), s32[]{:S(2)}) async-start(), calls=%async_computation.7 | async-start | bytes 3932160 | tf_op jit(solution)/shard_map/reduce_scatter | solution.py:746
  357.1 15.1 %collective-permute-start.47 = (bf16[2,1,16,32,128]{4,3,2,1,0:T(8,128)(2,1)S(1)}, bf16[2,1,16,32,128]{4,3,2,1,0:T(8,128)(2,1)S(1)}, u32[]{:S(2)}, u32[]{:S(2)}) collective-permute-start(bf16[2,1,16,32,128]{4,3,2,1,0:T(8,128)(2,1)S(1)} %pad_maximum_fusion.refs_0_), channel_id=1, source_target_pairs={{0,2},{1,3},{2,4},{3,5},{4,6},{5,7},{8,10},{9,11},{10,12},{11,13},... | collective-permute-start | bytes 786440 | tf_op jit(solution)/shard_map/ppermute | solution.py:578
  360.7 21.5 %collective-permute-start.48 = (bf16[2,1,16,32,128]{4,3,2,1,0:T(8,128)(2,1)S(1)}, bf16[2,1,16,32,128]{4,3,2,1,0:T(8,128)(2,1)S(1)}, u32[]{:S(2)}, u32[]{:S(2)}) collective-permute-start(bf16[2,1,16,32,128]{4,3,2,1,0:T(8,128)(2,1)S(1)} %pad_maximum_fusion.refs_0_), channel_id=1, source_target_pairs={{7,5},{6,4},{5,3},{4,2},{3,1},{2,0},{15,13},{14,12},{13,11},{12,10... | collective-permute-start | bytes 786440 | tf_op jit(solution)/shard_map/ppermute | solution.py:579
  362.0 25.7 %collective-permute-start.51 = (bf16[2,1,16,32,128]{4,3,2,1,0:T(8,128)(2,1)S(1)}, bf16[2,1,16,32,128]{4,3,2,1,0:T(8,128)(2,1)}, u32[]{:S(2)}, u32[]{:S(2)}) collective-permute-start(bf16[2,1,16,32,128]{4,3,2,1,0:T(8,128)(2,1)S(1)} %collective-permute-done.32.refs_2_), channel_id=1, source_target_pairs={{4,6},{5,7},{12,14},{13,15},{20,22},{21,23},{28,30},{29,31}} | collective-permute-start | bytes 786440 | tf_op jit(solution)/shard_map/ppermute | solution.py:578
  363.4 25.8 %collective-permute-start.52 = (bf16[2,1,16,32,128]{4,3,2,1,0:T(8,128)(2,1)S(1)}, bf16[2,1,16,32,128]{4,3,2,1,0:T(8,128)(2,1)}, u32[]{:S(2)}, u32[]{:S(2)}) collective-permute-start(bf16[2,1,16,32,128]{4,3,2,1,0:T(8,128)(2,1)S(1)} %collective-permute-done.34.refs_5_), channel_id=1, source_target_pairs={{3,1},{2,0},{11,9},{10,8},{19,17},{18,16},{27,25},{26,24}} | collective-permute-start | bytes 786440 | tf_op jit(solution)/shard_map/ppermute | solution.py:579
  385.1 22.0 %collective-permute-start.49 = (bf16[2,1,16,32,128]{4,3,2,1,0:T(8,128)(2,1)S(1)}, bf16[2,1,16,32,128]{4,3,2,1,0:T(8,128)(2,1)}, u32[]{:S(2)}, u32[]{:S(2)}) collective-permute-start(bf16[2,1,16,32,128]{4,3,2,1,0:T(8,128)(2,1)S(1)} %collective-permute-done.47.refs_1_), channel_id=1, source_target_pairs={{2,4},{3,5},{4,6},{5,7},{10,12},{11,13},{12,14},{13,15},{18,20},{1... | collective-permute-start | bytes 786440 | tf_op jit(solution)/shard_map/ppermute | solution.py:578
  386.5 20.6 %collective-permute-start.50 = (bf16[2,1,16,32,128]{4,3,2,1,0:T(8,128)(2,1)S(1)}, bf16[2,1,16,32,128]{4,3,2,1,0:T(8,128)(2,1)}, u32[]{:S(2)}, u32[]{:S(2)}) collective-permute-start(bf16[2,1,16,32,128]{4,3,2,1,0:T(8,128)(2,1)S(1)} %collective-permute-done.48.refs_4_), channel_id=1, source_target_pairs={{5,3},{4,2},{3,1},{2,0},{13,11},{12,10},{11,9},{10,8},{21,19},{20,... | collective-permute-start | bytes 786440 | tf_op jit(solution)/shard_map/ppermute | solution.py:579
  407.6 25.3 %collective-permute-start.53 = (bf16[2,1,16,32,128]{4,3,2,1,0:T(8,128)(2,1)}, bf16[2,1,16,32,128]{4,3,2,1,0:T(8,128)(2,1)S(1)}, u32[]{:S(2)}, u32[]{:S(2)}) collective-permute-start(bf16[2,1,16,32,128]{4,3,2,1,0:T(8,128)(2,1)} %collective-permute-done.49.refs_2_), channel_id=1, source_target_pairs={{4,6},{5,7},{12,14},{13,15},{20,22},{21,23},{28,30},{29,31}} | collective-permute-start | bytes 786440 | tf_op jit(solution)/shard_map/ppermute | solution.py:578
  408.3 26.6 %collective-permute-start.54 = (bf16[2,1,16,32,128]{4,3,2,1,0:T(8,128)(2,1)}, bf16[2,1,16,32,128]{4,3,2,1,0:T(8,128)(2,1)S(1)}, u32[]{:S(2)}, u32[]{:S(2)}) collective-permute-start(bf16[2,1,16,32,128]{4,3,2,1,0:T(8,128)(2,1)} %collective-permute-done.50.refs_5_), channel_id=1, source_target_pairs={{3,1},{2,0},{11,9},{10,8},{19,17},{18,16},{27,25},{26,24}} | collective-permute-start | bytes 786440 | tf_op jit(solution)/shard_map/ppermute | solution.py:579
  434.9 129.3 %reduce-scatter.9.cloned.1.call-start = ((), (), s32[]{:S(2)}) async-start(), calls=%async_computation.6 | async-start | bytes 3932160 | tf_op jit(solution)/shard_map/reduce_scatter | solution.py:746
  (58 other events, 514.7 us)
Sparse Core Ops, SparseCore 0:
  17.1 55.7 all-gather.10
  95.7 60.0 all-gather.8
  198.9 59.2 reduce-scatter.4
  260.9 70.5 reduce-scatter.6
  333.0 52.0 all-gather.14
  387.1 51.5 all-gather.12
  441.5 60.0 reduce-scatter.10
  503.9 60.2 reduce-scatter.8

commit v14 on v13

--- a/solution.py
+++ b/solution.py
@@ -696,12 +696,11 @@
     above, below = rims(*ends)
     states = [(iterate, inside, None, (above, rest, below))]
     line = Line(both_cores(low, 0, rows - CHUNK_ROWS, CHUNK_ROWS))
-    line.hop()
     for group in range(1, GROUPS):
         ends = tuple(
             rim_rows(groups[group], first).astype(jnp.bfloat16) for first in (0, rows - HALO)
         )
-        rests, ends = line.after((states[0][3], ends))
+        _, rests, ends = lax.optimization_barrier((low, states[0][3], ends))
         states[0] = (*states[0][:3], rests)
         states.append(ready(start(group, members, core, rhs, *rims(*ends), coeff)))
 
@@ -721,10 +720,14 @@
                 field, rests = lax.optimization_barrier((field, rests))
             states[group] = iterate, rests
             if group + 1 < GROUPS:
-                line = Line(states[group + 1][2])
+                value = states[group + 1][2]
+                if iteration == 0:
+                    slots, value = lax.optimization_barrier((slots, value))
+                line = Line(value)
                 line.hop()
-                field = line.after(field)
-                line.hop()
+                if iteration > 0:
+                    field = line.after(field)
+                    line.hop()
             sums = observe(
                 core,
                 field,

time: 593 us -> 580 us (0.978)
  waiting for transfers between devices: 243 us -> 222 us
    ppermute x13, waiting for transfers between devices: 23.3 us -> 6.89 us  [swap_cores(): return lax.ppermute(value, 'sensors', [(k, k ^ 1) for k in range(size)])]
    ppermute x12, waiting for transfers between devices: 18 us -> 3.91 us  [hop(): up = lax.ppermute(self.ends[0], 'sensors', onward)]
    ppermute x12, waiting for transfers between devices: 59.9 us -> 72.5 us  [hop(): down = lax.ppermute(self.ends[1], 'sensors', backward)]
    ppermute x8, waiting for transfers between devices: 17.4 us -> 6.47 us  [misfit_rims(): return (lax.ppermute(edge, both, same), lax.ppermute(edge, both, cross))]
    ppermute x6, starting transfers between devices: 17.4 us -> 23.9 us  [rims(): lax.ppermute(bottom, 'cells', onward)]
  transfers between devices with their start and end apart: 77 -> 77, of which waited for: 43 -> 46; matrix products, arithmetic and copies ran while one was open for 4% -> 4% of each run, Pallas kernels for 31% -> 32%
where the time goes in v14:
time: 580 us; the launch traced here: 577 us
  waiting for transfers between devices  222 us (38%)
  Pallas kernels  189 us (33%)
  starting transfers between devices  124 us (21%)
  local copies, waits for them, and re-layouts  17.6 us (3%)
  between operations  15.2 us (3%)
  other arithmetic  8.53 us (1%)
    reduce_scatter x4, waiting for transfers between devices, shards(): lax.psum_scatter(misfit, 'sensors', scatter_dimension=0, axis_index_group...  83.1 us
    ppermute x12, waiting for transfers between devices, hop(): down = lax.ppermute(self.ends[1], 'sensors', backward)  72.5 us
    pallas_call x4, Pallas kernels, observe(): call(observe_kernel, core, (chunks,), [pl.BlockSpec(block, field_place)]...  71.4 us
    pallas_call x4, Pallas kernels, pull_back(): call(pull_kernel, core, (rows // CHUNK_ROWS,), [whole_block(array) for ar...  63.5 us
    ppermute x8, starting transfers between devices, misfit_rims(): return (lax.ppermute(edge, both, same), lax.ppermute(edge, both, cross))  24.5 us
    ppermute x6, starting transfers between devices, rims(): lax.ppermute(bottom, 'cells', onward)  23.9 us
    ppermute x12, starting transfers between devices, hop(): up = lax.ppermute(self.ends[0], 'sensors', onward)  22.8 us
    ppermute x6, waiting for transfers between devices, rims(): lax.ppermute(top, 'cells', backward)  19.9 us
  transfers between devices with their start and end apart: 77, of which 46 were waited for; matrix products, arithmetic and copies ran while one was open for 4% of the time, Pallas kernels for 32%

profile of v14, /device:TPU:1, one launch (start us, length us, event | category | flops | bytes accessed | tf_op | source)
XLA Modules:
  0.0 576.8 jit_solution(14724778430148502717)
XLA Ops:
  11.1 6.0 %inner.1 = bf16[3,24,32,128]{3,2,1,0:T(8,128)(2,1)} custom-call(s32[1]{0:T(128)} %bitcast.core_ref, f32[32,192,128]{2,1,0:T(8,128)} %bitcast.76, f32[5,32,8,128]{3,2,1,0:T(8,128)S(1)} %broadcast_in_dim.17.coeff_ref), custom_call_target="tpu_custom_call" | custom-call | tf_op jit(solution)/shard_map/inner/pallas_call | solution.py:197
  18.8 4.6 collective-permute-start
  29.9 8.2 %start.2 = (f32[3,32,32,128]{3,2,1,0:T(8,128)}, bf16[3,32,32,128]{3,2,1,0:T(8,128)(2,1)}, f32[3,32,32,128]{3,2,1,0:T(8,128)}, bf16[3,4,32,128]{3,2,1,0:T(8,128)(2,1)S(1)}, bf16[3,4,32,128]{3,2,1,0:T(8,128)(2,1)S(1)}) custom-call(s32[1]{0:T(128)} %bitcast.core_ref, f32[32,192,128]{2,1,0:T(8,128)} %bitcast.77, bf16[3,4,32,128]{3,2,1,0:T(8,128)(2,1)S(1)} %bitcast.74, ...), custom_call_target="tpu_custom_call" | custom-call | tf_op jit(solution)/shard_map/start/pallas_call | solution.py:155
  43.6 4.1 collective-permute-done.3.down_ref
  52.5 4.2 collective-permute-done.5.down_ref
  56.7 8.2 %start.3 = (f32[3,32,32,128]{3,2,1,0:T(8,128)}, bf16[3,32,32,128]{3,2,1,0:T(8,128)(2,1)}, f32[3,32,32,128]{3,2,1,0:T(8,128)}, bf16[3,4,32,128]{3,2,1,0:T(8,128)(2,1)}, bf16[3,4,32,128]{3,2,1,0:T(8,128)(2,1)}) custom-call(s32[1]{0:T(128)} %bitcast.core_ref, f32[32,192,128]{2,1,0:T(8,128)} %bitcast.78, ...), custom_call_target="tpu_custom_call" | custom-call | tf_op jit(solution)/shard_map/start/pallas_call | solution.py:155
  90.1 9.1 %collective-permute-done.14.refs_5_ = bf16[2,3,4,32,128]{4,3,2,1,0:T(8,128)(2,1)S(1)} collective-permute-done((bf16[2,3,4,32,128]{4,3,2,1,0:T(8,128)(2,1)S(1)}, bf16[2,3,4,32,128]{4,3,2,1,0:T(8,128)(2,1)S(1)}, u32[]{:S(2)}, u32[]{:S(2)}) %collective-permute-start.14) | collective-permute-done | bytes 196640 | tf_op jit(solution)/shard_map/ppermute | solution.py:579
  101.9 23.4 %collective-permute-done.15.refs_6_ = bf16[2,3,4,32,128]{4,3,2,1,0:T(8,128)(2,1)S(1)} collective-permute-done((bf16[2,3,4,32,128]{4,3,2,1,0:T(8,128)(2,1)S(1)}, bf16[2,3,4,32,128]{4,3,2,1,0:T(8,128)(2,1)S(1)}, u32[]{:S(2)}, u32[]{:S(2)}) %collective-permute-start.15) | collective-permute-done | bytes 196640 | tf_op jit(solution)/shard_map/ppermute | solution.py:579
  126.5 4.0 collective-permute-start.16
  130.8 18.1 %observe.4 = f32[2,2,3,16,128]{4,3,2,1,0:T(8,128)S(1)} custom-call(s32[1]{0:T(128)} %bitcast.core_ref, bf16[8,3,24,32,128]{4,3,2,1,0:T(8,128)(2,1)} %bitcast.79, bf16[2,3,4,32,128]{4,3,2,1,0:T(8,128)(2,1)S(1)} %pad_maximum_fusion.3.refs_0_, bf16[2,3,4,32,128]{4,3,2,1,0:T(8,128)(2,1)S(1)} %collective-permute-done.10.refs_1_, ...), custom_call_target="tpu_custom_call" | custom-call | flops 402653184 | bytes 38273024 | tf_op jit(solution)/shard_map/observe/pallas_call | solution.py:438
  155.0 7.0 %collective-permute-done.21.refs_5_ = bf16[2,1,16,32,128]{4,3,2,1,0:T(8,128)(2,1)S(1)} collective-permute-done((bf16[2,1,16,32,128]{4,3,2,1,0:T(8,128)(2,1)S(1)}, bf16[2,1,16,32,128]{4,3,2,1,0:T(8,128)(2,1)S(1)}, u32[]{:S(2)}, u32[]{:S(2)}) %collective-permute-start.21) | collective-permute-done | bytes 262176 | tf_op jit(solution)/shard_map/ppermute | solution.py:579
  170.1 15.8 %pull_back.4 = bf16[4,2,3,16,32,128]{5,4,3,2,1,0:T(8,128)(2,1)} custom-call(s32[1]{0:T(128)} %bitcast.core_ref, f32[2,2,3,16,128]{4,3,2,1,0:T(8,128)S(1)} %reverse_add_fusion.3.refs_0_, f32[2,2,3,16,128]{4,3,2,1,0:T(8,128)S(1)} %collective-permute-done.24.refs_1_, f32[2,2,3,16,128]{4,3,2,1,0:T(8,128)S(1)} %collective-permute-done.25.refs_2_, ...), custom_call_target="tpu_custom_call" | custom-call | flops 402653184 | bytes 36700160 | tf_op jit(solution)/shard_map/pull_back/pallas_call | solution.py:512
  194.8 17.6 %observe.5 = f32[2,2,3,16,128]{4,3,2,1,0:T(8,128)S(1)} custom-call(s32[1]{0:T(128)} %bitcast.core_ref, bf16[4,2,2,16,32,128]{5,4,3,2,1,0:T(8,128)(2,1)} %bitcast.90, bf16[2,1,16,32,128]{4,3,2,1,0:T(8,128)(2,1)S(1)} %pad_maximum_fusion.2.refs_0_, bf16[2,1,16,32,128]{4,3,2,1,0:T(8,128)(2,1)S(1)} %collective-permute-done.16.refs_1_, ...), custom_call_target="tpu_custom_call" | custom-call | flops 402653184 | bytes 35651584 | tf_op jit(solution)/shard_map/observe/pallas_call | solution.py:438
  224.9 15.9 %pull_back.5 = bf16[4,2,3,16,32,128]{5,4,3,2,1,0:T(8,128)(2,1)} custom-call(s32[1]{0:T(128)} %bitcast.core_ref, f32[2,2,3,16,128]{4,3,2,1,0:T(8,128)S(1)} %reverse_add_fusion.2.refs_0_, f32[2,2,3,16,128]{4,3,2,1,0:T(8,128)S(1)} %collective-permute-done.36.refs_1_, f32[2,2,3,16,128]{4,3,2,1,0:T(8,128)S(1)} %collective-permute-done.37.refs_2_, ...), custom_call_target="tpu_custom_call" | custom-call | flops 402653184 | bytes 36700160 | tf_op jit(solution)/shard_map/pull_back/pallas_call | solution.py:512
  240.9 6.1 %reduce-scatter.5.cloned.1.call-done = bf16[1,2,3,16,32,128]{5,4,3,2,1,0:T(8,128)(2,1)} async-done(((bf16[4,2,3,16,32,128]{5,4,3,2,1,0:T(8,128)(2,1)}), bf16[1,2,3,16,32,128]{5,4,3,2,1,0:T(8,128)(2,1)}) %reduce-scatter.5.cloned.1.call-update) | async-done | bytes 786448 | tf_op jit(solution)/shard_map/reduce_scatter | solution.py:749
  257.7 8.7 %step.2 = (f32[3,32,32,128]{3,2,1,0:T(8,128)}, bf16[3,32,32,128]{3,2,1,0:T(8,128)(2,1)}, f32[3,32,32,128]{3,2,1,0:T(8,128)}, bf16[3,4,32,128]{3,2,1,0:T(8,128)(2,1)S(1)}, bf16[3,4,32,128]{3,2,1,0:T(8,128)(2,1)S(1)}) custom-call(s32[1]{0:T(128)} %bitcast.core_ref, bf16[3,4,32,128]{3,2,1,0:T(8,128)(2,1)S(1)} %collective-permute-done.2.up_ref, ...), custom_call_target="tpu_custom_call" | custom-call | tf_op jit(solution)/shard_map/step/pallas_call | solution.py:242
  272.2 4.0 collective-permute-start.31
  276.2 14.8 %collective-permute-done.33.refs_4_ = bf16[2,1,16,32,128]{4,3,2,1,0:T(8,128)(2,1)S(1)} collective-permute-done((bf16[2,1,16,32,128]{4,3,2,1,0:T(8,128)(2,1)S(1)}, bf16[2,1,16,32,128]{4,3,2,1,0:T(8,128)(2,1)S(1)}, u32[]{:S(2)}, u32[]{:S(2)}) %collective-permute-start.33) | collective-permute-done | bytes 262176 | tf_op jit(solution)/shard_map/ppermute | solution.py:579
  293.0 6.7 %collective-permute-start.39 = (bf16[3,4,32,128]{3,2,1,0:T(8,128)(2,1)S(1)}, bf16[3,4,32,128]{3,2,1,0:T(8,128)(2,1)S(1)}, u32[]{:S(2)}, u32[]{:S(2)}) collective-permute-start(bf16[3,4,32,128]{3,2,1,0:T(8,128)(2,1)S(1)} %get-tuple-element.113), channel_id=1, source_target_pairs={{0,8},{8,16},{16,24},{1,9},{9,17},{17,25},{2,10},{10,18},{18,26},{... | collective-permute-start | bytes 294920 | tf_op jit(solution)/shard_map/ppermute | solution.py:536
  301.0 20.0 %reduce-scatter.7.cloned.1.call-done = bf16[1,2,3,16,32,128]{5,4,3,2,1,0:T(8,128)(2,1)} async-done(((bf16[4,2,3,16,32,128]{5,4,3,2,1,0:T(8,128)(2,1)}), bf16[1,2,3,16,32,128]{5,4,3,2,1,0:T(8,128)(2,1)}) %reduce-scatter.7.cloned.1.call-update) | async-done | bytes 786448 | tf_op jit(solution)/shard_map/reduce_scatter | solution.py:749
  331.5 8.7 %step.3 = (f32[3,32,32,128]{3,2,1,0:T(8,128)}, bf16[3,32,32,128]{3,2,1,0:T(8,128)(2,1)}, f32[3,32,32,128]{3,2,1,0:T(8,128)}, bf16[3,4,32,128]{3,2,1,0:T(8,128)(2,1)S(1)}, bf16[3,4,32,128]{3,2,1,0:T(8,128)(2,1)S(1)}) custom-call(s32[1]{0:T(128)} %bitcast.core_ref, bf16[3,4,32,128]{3,2,1,0:T(8,128)(2,1)S(1)} %collective-permute-done.7.up_ref, ...), custom_call_target="tpu_custom_call" | custom-call | tf_op jit(solution)/shard_map/step/pallas_call | solution.py:242
  346.1 4.0 collective-permute-start.47
  352.8 13.5 %collective-permute-done.48.refs_4_ = bf16[2,1,16,32,128]{4,3,2,1,0:T(8,128)(2,1)S(1)} collective-permute-done((bf16[2,1,16,32,128]{4,3,2,1,0:T(8,128)(2,1)S(1)}, bf16[2,1,16,32,128]{4,3,2,1,0:T(8,128)(2,1)S(1)}, u32[]{:S(2)}, u32[]{:S(2)}) %collective-permute-start.48) | collective-permute-done | bytes 262176 | tf_op jit(solution)/shard_map/ppermute | solution.py:579
  366.3 8.1 %all-gather.15.cloned.1.call-done = bf16[8,2,16,32,128]{4,3,2,1,0:T(8,128)(2,1)} async-done(((bf16[2,2,16,32,128]{4,3,2,1,0:T(8,128)(2,1)}), bf16[8,2,16,32,128]{4,3,2,1,0:T(8,128)(2,1)}) %all-gather.15.cloned.1.call-update) | async-done | bytes 2097168 | tf_op jit(solution)/shard_map/all_gather | solution.py:710
  377.8 17.7 %observe.6 = f32[2,2,3,16,128]{4,3,2,1,0:T(8,128)S(1)} custom-call(s32[1]{0:T(128)} %bitcast.core_ref, bf16[4,2,2,16,32,128]{5,4,3,2,1,0:T(8,128)(2,1)} %bitcast.91, bf16[2,1,16,32,128]{4,3,2,1,0:T(8,128)(2,1)S(1)} %pad_maximum_fusion.1.refs_0_, bf16[2,1,16,32,128]{4,3,2,1,0:T(8,128)(2,1)S(1)} %collective-permute-done.31.refs_1_, ...), custom_call_target="tpu_custom_call" | custom-call | flops 402653184 | bytes 35651584 | tf_op jit(solution)/shard_map/observe/pallas_call | solution.py:438
  406.4 15.9 %pull_back.6 = bf16[4,2,3,16,32,128]{5,4,3,2,1,0:T(8,128)(2,1)} custom-call(s32[1]{0:T(128)} %bitcast.core_ref, f32[2,2,3,16,128]{4,3,2,1,0:T(8,128)S(1)} %reverse_add_fusion.1.refs_0_, f32[2,2,3,16,128]{4,3,2,1,0:T(8,128)S(1)} %collective-permute-done.56.refs_1_, f32[2,2,3,16,128]{4,3,2,1,0:T(8,128)S(1)} %collective-permute-done.57.refs_2_, ...), custom_call_target="tpu_custom_call" | custom-call | flops 402653184 | bytes 36700160 | tf_op jit(solution)/shard_map/pull_back/pallas_call | solution.py:512
  432.4 18.0 %observe.7 = f32[2,2,3,16,128]{4,3,2,1,0:T(8,128)S(1)} custom-call(s32[1]{0:T(128)} %bitcast.core_ref, bf16[4,2,2,16,32,128]{5,4,3,2,1,0:T(8,128)(2,1)} %bitcast.92, bf16[2,1,16,32,128]{4,3,2,1,0:T(8,128)(2,1)S(1)} %pad_maximum_fusion.refs_0_, bf16[2,1,16,32,128]{4,3,2,1,0:T(8,128)(2,1)S(1)} %collective-permute-done.47.refs_1_, ...), custom_call_target="tpu_custom_call" | custom-call | flops 402653184 | bytes 35651584 | tf_op jit(solution)/shard_map/observe/pallas_call | solution.py:438
  461.1 16.0 %pull_back.7 = bf16[4,2,3,16,32,128]{5,4,3,2,1,0:T(8,128)(2,1)} custom-call(s32[1]{0:T(128)} %bitcast.core_ref, f32[2,2,3,16,128]{4,3,2,1,0:T(8,128)S(1)} %reverse_add_fusion.refs_0_, f32[2,2,3,16,128]{4,3,2,1,0:T(8,128)S(1)} %collective-permute-done.60.refs_1_, f32[2,2,3,16,128]{4,3,2,1,0:T(8,128)S(1)} %collective-permute-done.61.refs_2_, ...), custom_call_target="tpu_custom_call" | custom-call | flops 402653184 | bytes 36700160 | tf_op jit(solution)/shard_map/pull_back/pallas_call | solution.py:512
  477.1 12.3 %reduce-scatter.11.cloned.1.call-done = bf16[1,2,3,16,32,128]{5,4,3,2,1,0:T(8,128)(2,1)} async-done(((bf16[4,2,3,16,32,128]{5,4,3,2,1,0:T(8,128)(2,1)}), bf16[1,2,3,16,32,128]{5,4,3,2,1,0:T(8,128)(2,1)}) %reduce-scatter.11.cloned.1.call-update) | async-done | bytes 786448 | tf_op jit(solution)/shard_map/reduce_scatter | solution.py:749
  500.0 7.3 %finish.2 = (f32[32,192,128]{2,1,0:T(8,128)}, f32[32,192,128]{2,1,0:T(8,128)}) custom-call(s32[1]{0:T(128)} %bitcast.core_ref, bf16[3,4,32,128]{3,2,1,0:T(8,128)(2,1)S(1)} %collective-permute-done.39.up_ref, f32[3,32,32,128]{3,2,1,0:T(8,128)} %get-tuple-element.140.rest_ref, bf16[3,4,32,128]{3,2,1,0:T(8,128)(2,1)S(1)} %copy-done.3, ...), custom_call_target="tpu_custom_call" | custom-call | tf_op jit(solution)/shard_map/finish/pallas_call | solution.py:282
  507.3 44.7 %reduce-scatter.9.cloned.1.call-done = bf16[1,2,3,16,32,128]{5,4,3,2,1,0:T(8,128)(2,1)} async-done(((bf16[4,2,3,16,32,128]{5,4,3,2,1,0:T(8,128)(2,1)}), bf16[1,2,3,16,32,128]{5,4,3,2,1,0:T(8,128)(2,1)}) %reduce-scatter.9.cloned.1.call-update) | async-done | bytes 786448 | tf_op jit(solution)/shard_map/reduce_scatter | solution.py:749
  562.6 7.3 %finish.3 = (f32[32,192,128]{2,1,0:T(8,128)}, f32[32,192,128]{2,1,0:T(8,128)}) custom-call(s32[1]{0:T(128)} %bitcast.core_ref, bf16[3,4,32,128]{3,2,1,0:T(8,128)(2,1)S(1)} %collective-permute-done.45.up_ref, f32[3,32,32,128]{3,2,1,0:T(8,128)} %get-tuple-element.124.rest_ref, ...), custom_call_target="tpu_custom_call", output_to_operand_aliasing={{0}: (10, {}), {1}: (11, {})} | custom-call | tf_op jit(solution)/shard_map/finish/pallas_call | solution.py:282
  (256 shorter events, 181.7 us)
Async XLA Ops:
  7.2 123.5 %all-gather.11.cloned.1.call-start = ((), (), s32[]{:S(2)}) async-start(), calls=%async_computation.9 | async-start | bytes 5308416 | tf_op jit(solution)/shard_map/all_gather | solution.py:710
  7.2 123.5 %collective-permute-start.18 = (bf16[2,128,16,4096]{3,2,1,0:T(8,128)(2,1)}, bf16[2,128,16,4096]{3,2,1,0:T(8,128)(2,1)}, u32[]{:S(2)}, u32[]{:S(2)}) collective-permute-start(bf16[2,128,16,4096]{3,2,1,0:T(8,128)(2,1)} %refs_5_.7), channel_id=1, source_target_pairs={{0,1},{1,0},{2,3},{3,2},{4,5},{5,4},{6,7},{7,6},{8,9},{9,8},{10,11... | collective-permute-start | bytes 100663304 | tf_op jit(solution)/shard_map/ppermute | solution.py:554
  17.1 177.7 %all-gather.9.cloned.1.call-start = ((), (), s32[]{:S(2)}) async-start(), calls=%async_computation.8 | async-start | bytes 2621440 | tf_op jit(solution)/shard_map/all_gather | solution.py:710
  71.6 175.4 %reduce-scatter.5.cloned.1.call-start = ((), (), s32[]{:S(2)}) async-start(), calls=%async_computation.4 | async-start | bytes 3932160 | tf_op jit(solution)/shard_map/reduce_scatter | solution.py:749
  76.6 12.3 %collective-permute-start.10 = (bf16[2,3,4,32,128]{4,3,2,1,0:T(8,128)(2,1)S(1)}, bf16[2,3,4,32,128]{4,3,2,1,0:T(8,128)(2,1)S(1)}, u32[]{:S(2)}, u32[]{:S(2)}) collective-permute-start(bf16[2,3,4,32,128]{4,3,2,1,0:T(8,128)(2,1)S(1)} %pad_maximum_fusion.3.refs_0_), channel_id=1, source_target_pairs={{0,2},{1,3},{2,4},{3,5},{4,6},{5,7},{8,10},{9,11},{10,12},{11,13},... | collective-permute-start | bytes 589832 | tf_op jit(solution)/shard_map/ppermute | solution.py:578
  83.7 15.5 %collective-permute-start.14 = (bf16[2,3,4,32,128]{4,3,2,1,0:T(8,128)(2,1)S(1)}, bf16[2,3,4,32,128]{4,3,2,1,0:T(8,128)(2,1)S(1)}, u32[]{:S(2)}, u32[]{:S(2)}) collective-permute-start(bf16[2,3,4,32,128]{4,3,2,1,0:T(8,128)(2,1)S(1)} %collective-permute-done.13.refs_4_), channel_id=1, source_target_pairs={{5,3},{4,2},{3,1},{2,0},{13,11},{12,10},{11,9},{10,8},{21,19},{20,... | collective-permute-start | bytes 589832 | tf_op jit(solution)/shard_map/ppermute | solution.py:579
  99.2 26.0 %collective-permute-start.15 = (bf16[2,3,4,32,128]{4,3,2,1,0:T(8,128)(2,1)S(1)}, bf16[2,3,4,32,128]{4,3,2,1,0:T(8,128)(2,1)S(1)}, u32[]{:S(2)}, u32[]{:S(2)}) collective-permute-start(bf16[2,3,4,32,128]{4,3,2,1,0:T(8,128)(2,1)S(1)} %collective-permute-done.14.refs_5_), channel_id=1, source_target_pairs={{3,1},{2,0},{11,9},{10,8},{19,17},{18,16},{27,25},{26,24}} | collective-permute-start | bytes 589832 | tf_op jit(solution)/shard_map/ppermute | solution.py:579
  100.5 24.7 %collective-permute-start.12 = (bf16[2,3,4,32,128]{4,3,2,1,0:T(8,128)(2,1)S(1)}, bf16[2,3,4,32,128]{4,3,2,1,0:T(8,128)(2,1)S(1)}, u32[]{:S(2)}, u32[]{:S(2)}) collective-permute-start(bf16[2,3,4,32,128]{4,3,2,1,0:T(8,128)(2,1)S(1)} %collective-permute-done.11.refs_2_), channel_id=1, source_target_pairs={{4,6},{5,7},{12,14},{13,15},{20,22},{21,23},{28,30},{29,31}} | collective-permute-start | bytes 589832 | tf_op jit(solution)/shard_map/ppermute | solution.py:578
  125.2 23.8 %collective-permute-start.17 = (bf16[2,1,16,32,128]{4,3,2,1,0:T(8,128)(2,1)S(1)}, bf16[2,1,16,32,128]{4,3,2,1,0:T(8,128)(2,1)S(1)}, u32[]{:S(2)}, u32[]{:S(2)}) collective-permute-start(bf16[2,1,16,32,128]{4,3,2,1,0:T(8,128)(2,1)S(1)} %pad_maximum_fusion.2.refs_0_), channel_id=1, source_target_pairs={{7,5},{6,4},{5,3},{4,2},{3,1},{2,0},{15,13},{14,12},{13,11},{12,10... | collective-permute-start | bytes 786440 | tf_op jit(solution)/shard_map/ppermute | solution.py:579
  126.5 22.5 %collective-permute-start.16 = (bf16[2,1,16,32,128]{4,3,2,1,0:T(8,128)(2,1)S(1)}, bf16[2,1,16,32,128]{4,3,2,1,0:T(8,128)(2,1)S(1)}, u32[]{:S(2)}, u32[]{:S(2)}) collective-permute-start(bf16[2,1,16,32,128]{4,3,2,1,0:T(8,128)(2,1)S(1)} %pad_maximum_fusion.2.refs_0_), channel_id=1, source_target_pairs={{0,2},{1,3},{2,4},{3,5},{4,6},{5,7},{8,10},{9,11},{10,12},{11,13},... | collective-permute-start | bytes 786440 | tf_op jit(solution)/shard_map/ppermute | solution.py:578
  149.7 12.3 %collective-permute-start.21 = (bf16[2,1,16,32,128]{4,3,2,1,0:T(8,128)(2,1)S(1)}, bf16[2,1,16,32,128]{4,3,2,1,0:T(8,128)(2,1)S(1)}, u32[]{:S(2)}, u32[]{:S(2)}) collective-permute-start(bf16[2,1,16,32,128]{4,3,2,1,0:T(8,128)(2,1)S(1)} %collective-permute-done.17.refs_4_), channel_id=1, source_target_pairs={{5,3},{4,2},{3,1},{2,0},{13,11},{12,10},{11,9},{10,8},{21,19},{20,... | collective-permute-start | bytes 786440 | tf_op jit(solution)/shard_map/ppermute | solution.py:579
  154.3 31.5 %collective-permute-start.20 = (bf16[2,1,16,32,128]{4,3,2,1,0:T(8,128)(2,1)S(1)}, bf16[2,1,16,32,128]{4,3,2,1,0:T(8,128)(2,1)S(1)}, u32[]{:S(2)}, u32[]{:S(2)}) collective-permute-start(bf16[2,1,16,32,128]{4,3,2,1,0:T(8,128)(2,1)S(1)} %collective-permute-done.19.refs_2_), channel_id=1, source_target_pairs={{4,6},{5,7},{12,14},{13,15},{20,22},{21,23},{28,30},{29,31}} | collective-permute-start | bytes 786440 | tf_op jit(solution)/shard_map/ppermute | solution.py:578
  162.0 23.9 %collective-permute-start.22 = (bf16[2,1,16,32,128]{4,3,2,1,0:T(8,128)(2,1)S(1)}, bf16[2,1,16,32,128]{4,3,2,1,0:T(8,128)(2,1)S(1)}, u32[]{:S(2)}, u32[]{:S(2)}) collective-permute-start(bf16[2,1,16,32,128]{4,3,2,1,0:T(8,128)(2,1)S(1)} %collective-permute-done.21.refs_5_), channel_id=1, source_target_pairs={{3,1},{2,0},{11,9},{10,8},{19,17},{18,16},{27,25},{26,24}} | collective-permute-start | bytes 786440 | tf_op jit(solution)/shard_map/ppermute | solution.py:579
  185.9 135.1 %reduce-scatter.7.cloned.1.call-start = ((), (), s32[]{:S(2)}) async-start(), calls=%async_computation.5 | async-start | bytes 3932160 | tf_op jit(solution)/shard_map/reduce_scatter | solution.py:749
  240.8 133.6 %all-gather.15.cloned.1.call-start = ((), (), s32[]{:S(2)}) async-start(), calls=%async_computation.11 | async-start | bytes 2621440 | tf_op jit(solution)/shard_map/all_gather | solution.py:710
  270.9 161.5 %all-gather.13.cloned.1.call-start = ((), (), s32[]{:S(2)}) async-start(), calls=%async_computation.10 | async-start | bytes 2621440 | tf_op jit(solution)/shard_map/all_gather | solution.py:710
  270.9 20.1 %collective-permute-start.33 = (bf16[2,1,16,32,128]{4,3,2,1,0:T(8,128)(2,1)S(1)}, bf16[2,1,16,32,128]{4,3,2,1,0:T(8,128)(2,1)S(1)}, u32[]{:S(2)}, u32[]{:S(2)}) collective-permute-start(bf16[2,1,16,32,128]{4,3,2,1,0:T(8,128)(2,1)S(1)} %pad_maximum_fusion.1.refs_0_), channel_id=1, source_target_pairs={{7,5},{6,4},{5,3},{4,2},{3,1},{2,0},{15,13},{14,12},{13,11},{12,10... | collective-permute-start | bytes 786440 | tf_op jit(solution)/shard_map/ppermute | solution.py:579
  272.2 20.1 %collective-permute-start.31 = (bf16[2,1,16,32,128]{4,3,2,1,0:T(8,128)(2,1)S(1)}, bf16[2,1,16,32,128]{4,3,2,1,0:T(8,128)(2,1)S(1)}, u32[]{:S(2)}, u32[]{:S(2)}) collective-permute-start(bf16[2,1,16,32,128]{4,3,2,1,0:T(8,128)(2,1)S(1)} %pad_maximum_fusion.1.refs_0_), channel_id=1, source_target_pairs={{0,2},{1,3},{2,4},{3,5},{4,6},{5,7},{8,10},{9,11},{10,12},{11,13},... | collective-permute-start | bytes 786440 | tf_op jit(solution)/shard_map/ppermute | solution.py:578
  291.0 30.0 %collective-permute-start.34 = (bf16[2,1,16,32,128]{4,3,2,1,0:T(8,128)(2,1)S(1)}, bf16[2,1,16,32,128]{4,3,2,1,0:T(8,128)(2,1)S(1)}, u32[]{:S(2)}, u32[]{:S(2)}) collective-permute-start(bf16[2,1,16,32,128]{4,3,2,1,0:T(8,128)(2,1)S(1)} %collective-permute-done.33.refs_4_), channel_id=1, source_target_pairs={{5,3},{4,2},{3,1},{2,0},{13,11},{12,10},{11,9},{10,8},{21,19},{20,... | collective-permute-start | bytes 786440 | tf_op jit(solution)/shard_map/ppermute | solution.py:579
  292.3 28.7 %collective-permute-start.32 = (bf16[2,1,16,32,128]{4,3,2,1,0:T(8,128)(2,1)S(1)}, bf16[2,1,16,32,128]{4,3,2,1,0:T(8,128)(2,1)S(1)}, u32[]{:S(2)}, u32[]{:S(2)}) collective-permute-start(bf16[2,1,16,32,128]{4,3,2,1,0:T(8,128)(2,1)S(1)} %collective-permute-done.31.refs_1_), channel_id=1, source_target_pairs={{2,4},{3,5},{4,6},{5,7},{10,12},{11,13},{12,14},{13,15},{18,20},{1... | collective-permute-start | bytes 786440 | tf_op jit(solution)/shard_map/ppermute | solution.py:578
  293.0 28.0 %collective-permute-start.39 = (bf16[3,4,32,128]{3,2,1,0:T(8,128)(2,1)S(1)}, bf16[3,4,32,128]{3,2,1,0:T(8,128)(2,1)S(1)}, u32[]{:S(2)}, u32[]{:S(2)}) collective-permute-start(bf16[3,4,32,128]{3,2,1,0:T(8,128)(2,1)S(1)} %get-tuple-element.113), channel_id=1, source_target_pairs={{0,8},{8,16},{16,24},{1,9},{9,17},{17,25},{2,10},{10,18},{18,26},{... | collective-permute-start | bytes 294920 | tf_op jit(solution)/shard_map/ppermute | solution.py:536
  299.7 21.3 %collective-permute-start.40 = (bf16[3,4,32,128]{3,2,1,0:T(8,128)(2,1)S(1)}, bf16[3,4,32,128]{3,2,1,0:T(8,128)(2,1)S(1)}, u32[]{:S(2)}, u32[]{:S(2)}) collective-permute-start(bf16[3,4,32,128]{3,2,1,0:T(8,128)(2,1)S(1)} %get-tuple-element.115), channel_id=1, source_target_pairs={{8,0},{16,8},{24,16},{9,1},{17,9},{25,17},{10,2},{18,10},{26,18},{... | collective-permute-start | bytes 294920 | tf_op jit(solution)/shard_map/ppermute | solution.py:536
  344.8 144.6 %reduce-scatter.11.cloned.1.call-start = ((), (), s32[]{:S(2)}) async-start(), calls=%async_computation.7 | async-start | bytes 3932160 | tf_op jit(solution)/shard_map/reduce_scatter | solution.py:749
  344.8 21.5 %collective-permute-start.48 = (bf16[2,1,16,32,128]{4,3,2,1,0:T(8,128)(2,1)S(1)}, bf16[2,1,16,32,128]{4,3,2,1,0:T(8,128)(2,1)S(1)}, u32[]{:S(2)}, u32[]{:S(2)}) collective-permute-start(bf16[2,1,16,32,128]{4,3,2,1,0:T(8,128)(2,1)S(1)} %pad_maximum_fusion.refs_0_), channel_id=1, source_target_pairs={{7,5},{6,4},{5,3},{4,2},{3,1},{2,0},{15,13},{14,12},{13,11},{12,10... | collective-permute-start | bytes 786440 | tf_op jit(solution)/shard_map/ppermute | solution.py:579
  346.1 20.2 %collective-permute-start.47 = (bf16[2,1,16,32,128]{4,3,2,1,0:T(8,128)(2,1)S(1)}, bf16[2,1,16,32,128]{4,3,2,1,0:T(8,128)(2,1)S(1)}, u32[]{:S(2)}, u32[]{:S(2)}) collective-permute-start(bf16[2,1,16,32,128]{4,3,2,1,0:T(8,128)(2,1)S(1)} %pad_maximum_fusion.refs_0_), channel_id=1, source_target_pairs={{0,2},{1,3},{2,4},{3,5},{4,6},{5,7},{8,10},{9,11},{10,12},{11,13},... | collective-permute-start | bytes 786440 | tf_op jit(solution)/shard_map/ppermute | solution.py:578
  350.1 26.9 %collective-permute-start.51 = (bf16[2,1,16,32,128]{4,3,2,1,0:T(8,128)(2,1)S(1)}, bf16[2,1,16,32,128]{4,3,2,1,0:T(8,128)(2,1)}, u32[]{:S(2)}, u32[]{:S(2)}) collective-permute-start(bf16[2,1,16,32,128]{4,3,2,1,0:T(8,128)(2,1)S(1)} %collective-permute-done.32.refs_2_), channel_id=1, source_target_pairs={{4,6},{5,7},{12,14},{13,15},{20,22},{21,23},{28,30},{29,31}} | collective-permute-start | bytes 786440 | tf_op jit(solution)/shard_map/ppermute | solution.py:578
  351.5 26.3 %collective-permute-start.52 = (bf16[2,1,16,32,128]{4,3,2,1,0:T(8,128)(2,1)S(1)}, bf16[2,1,16,32,128]{4,3,2,1,0:T(8,128)(2,1)}, u32[]{:S(2)}, u32[]{:S(2)}) collective-permute-start(bf16[2,1,16,32,128]{4,3,2,1,0:T(8,128)(2,1)S(1)} %collective-permute-done.34.refs_5_), channel_id=1, source_target_pairs={{3,1},{2,0},{11,9},{10,8},{19,17},{18,16},{27,25},{26,24}} | collective-permute-start | bytes 786440 | tf_op jit(solution)/shard_map/ppermute | solution.py:579
  374.4 21.1 %collective-permute-start.49 = (bf16[2,1,16,32,128]{4,3,2,1,0:T(8,128)(2,1)S(1)}, bf16[2,1,16,32,128]{4,3,2,1,0:T(8,128)(2,1)}, u32[]{:S(2)}, u32[]{:S(2)}) collective-permute-start(bf16[2,1,16,32,128]{4,3,2,1,0:T(8,128)(2,1)S(1)} %collective-permute-done.47.refs_1_), channel_id=1, source_target_pairs={{2,4},{3,5},{4,6},{5,7},{10,12},{11,13},{12,14},{13,15},{18,20},{1... | collective-permute-start | bytes 786440 | tf_op jit(solution)/shard_map/ppermute | solution.py:578
  375.8 19.8 %collective-permute-start.50 = (bf16[2,1,16,32,128]{4,3,2,1,0:T(8,128)(2,1)S(1)}, bf16[2,1,16,32,128]{4,3,2,1,0:T(8,128)(2,1)}, u32[]{:S(2)}, u32[]{:S(2)}) collective-permute-start(bf16[2,1,16,32,128]{4,3,2,1,0:T(8,128)(2,1)S(1)} %collective-permute-done.48.refs_4_), channel_id=1, source_target_pairs={{5,3},{4,2},{3,1},{2,0},{13,11},{12,10},{11,9},{10,8},{21,19},{20,... | collective-permute-start | bytes 786440 | tf_op jit(solution)/shard_map/ppermute | solution.py:579
  396.3 26.0 %collective-permute-start.53 = (bf16[2,1,16,32,128]{4,3,2,1,0:T(8,128)(2,1)}, bf16[2,1,16,32,128]{4,3,2,1,0:T(8,128)(2,1)S(1)}, u32[]{:S(2)}, u32[]{:S(2)}) collective-permute-start(bf16[2,1,16,32,128]{4,3,2,1,0:T(8,128)(2,1)} %collective-permute-done.49.refs_2_), channel_id=1, source_target_pairs={{4,6},{5,7},{12,14},{13,15},{20,22},{21,23},{28,30},{29,31}} | collective-permute-start | bytes 786440 | tf_op jit(solution)/shard_map/ppermute | solution.py:578
  396.9 26.6 %collective-permute-start.54 = (bf16[2,1,16,32,128]{4,3,2,1,0:T(8,128)(2,1)}, bf16[2,1,16,32,128]{4,3,2,1,0:T(8,128)(2,1)S(1)}, u32[]{:S(2)}, u32[]{:S(2)}) collective-permute-start(bf16[2,1,16,32,128]{4,3,2,1,0:T(8,128)(2,1)} %collective-permute-done.50.refs_5_), channel_id=1, source_target_pairs={{3,1},{2,0},{11,9},{10,8},{19,17},{18,16},{27,25},{26,24}} | collective-permute-start | bytes 786440 | tf_op jit(solution)/shard_map/ppermute | solution.py:579
  423.6 128.4 %reduce-scatter.9.cloned.1.call-start = ((), (), s32[]{:S(2)}) async-start(), calls=%async_computation.6 | async-start | bytes 3932160 | tf_op jit(solution)/shard_map/reduce_scatter | solution.py:749
  (59 other events, 503.0 us)
Sparse Core Ops, SparseCore 0:
  17.2 54.2 all-gather.10
  73.7 52.5 all-gather.8
  186.0 60.9 reduce-scatter.4
  249.7 71.2 reduce-scatter.6
  322.4 51.9 all-gather.14
  376.4 49.9 all-gather.12
  429.3 60.0 reduce-scatter.10
  491.7 60.2 reduce-scatter.8

commit v15 on v12

--- a/solution.py
+++ b/solution.py
@@ -16,6 +16,7 @@
 SUBLANES = 8
 GROUPS = 2
 CHUNK_ROWS = 4
+SPAN = 16
 VMEM_BYTES = 40 * 2**20
 
 
@@ -106,10 +107,11 @@
 
 
 def fields(members, rows, steps, cols):
-    field = pl.BlockSpec((1, rows, steps, cols), lambda b, core: (b, 0, 0, 0))
-    rim = pl.BlockSpec((1, HALO, steps, cols), lambda b, core: (b, 0, 0, 0))
+    span = min(steps, SPAN)
+    field = pl.BlockSpec((1, rows, span, cols), lambda b, t, core: (b, 0, t, 0))
+    rim = pl.BlockSpec((1, HALO, span, cols), lambda b, t, core: (b, 0, t, 0))
     misfits = [
-        pl.BlockSpec((None, 1, count, steps, cols), lambda b, core: (0, b, 0, 0, 0))
+        pl.BlockSpec((None, 1, count, span, cols), lambda b, t, core: (0, b, 0, t, 0))
         for count in (rows // 2, rows // 2, HALO, HALO)
     ]
 
@@ -155,9 +157,11 @@
     return call(
         start_kernel,
         core,
-        (members,),
+        (members, steps // min(steps, SPAN)),
         [
-            pl.BlockSpec((steps, rows, cols), lambda b, core: (0, b + group * members, 0)),
+            pl.BlockSpec(
+        (min(steps, SPAN), rows, cols), lambda b, t, core: (t, b + group * members, 0)
+    ),
             rim,
             rim,
             whole_block(coeff),
@@ -214,7 +218,7 @@
     return call(
         step_kernel,
         core,
-        (members,),
+        (members, steps // min(steps, SPAN)),
         [rim, field, rim, *parts, field, whole_block(coeff)],
         specs,
         shapes,
@@ -247,14 +251,16 @@
 def finish(group, samples, core, rests, misfits, iterate, coeff, previous):
     members, rows, steps, cols = iterate.shape
     field, rim, parts, _, _ = fields(members, rows, steps, cols)
-    result = pl.BlockSpec((steps, rows, cols), lambda b, core: (0, b + group * members, 0))
+    result = pl.BlockSpec(
+        (min(steps, SPAN), rows, cols), lambda b, t, core: (t, b + group * members, 0)
+    )
     shape = jax.ShapeDtypeStruct((steps, samples * rows, cols), jnp.float32)
     in_specs = [rim, field, rim, *parts, field, whole_block(coeff)]
     first = 1 + len(in_specs)
     return call(
         finish_kernel,
         core,
-        (members,),
+        (members, steps // min(steps, SPAN)),
         in_specs + [pl.BlockSpec(memory_space=pl.ANY)] * len(previous),
         [result, result],
         [shape, shape],

time: 552 us -> 553 us (level)
  no operation moved by 1% of the time
where the time goes in v15:
time: 553 us; the launch traced here: 550 us
  waiting for transfers between devices  225 us (41%)
  Pallas kernels  185 us (33%)
  starting transfers between devices  102 us (18%)
  local copies, waits for them, and re-layouts  15.3 us (3%)
  between operations  15 us (3%)
  other arithmetic  8.4 us (2%)
    reduce_scatter x4, waiting for transfers between devices, shards(): lax.psum_scatter(misfit, 'sensors', scatter_dimension=0, axis_index_group...  83.4 us
    pallas_call x4, Pallas kernels, observe(): call(observe_kernel, core, (chunks,), [pl.BlockSpec(block, lambda c, core...  71.5 us
    pallas_call x4, Pallas kernels, pull_back(): call(pull_kernel, core, (rows // CHUNK_ROWS,), [whole_block(array) for ar...  63.6 us
    ppermute x9, waiting for transfers between devices, hop(): down = lax.ppermute(self.ends[1], 'sensors', backward)  37.5 us
    ppermute x9, waiting for transfers between devices, hop(): up = lax.ppermute(self.ends[0], 'sensors', onward)  27.2 us
    ppermute x8, starting transfers between devices, misfit_rims(): return (lax.ppermute(edge, both, same), lax.ppermute(edge, both, cross))  21.9 us
    ppermute x6, starting transfers between devices, rims(): lax.ppermute(bottom, 'cells', onward)  20.9 us
    ppermute x6, waiting for transfers between devices, rims(): lax.ppermute(top, 'cells', backward)  19.2 us
  transfers between devices with their start and end apart: 70, of which 45 were waited for; matrix products, arithmetic and copies ran while one was open for 4% of the time, Pallas kernels for 32%

profile of v15, /device:TPU:1, one launch (start us, length us, event | category | flops | bytes accessed | tf_op | source)
XLA Modules:
  0.0 550.4 jit_solution(9060687670567847454)
XLA Ops:
  10.4 4.6 collective-permute-start
  22.9 8.3 %start.2 = (f32[3,32,32,128]{3,2,1,0:T(8,128)}, bf16[3,32,32,128]{3,2,1,0:T(8,128)(2,1)}, f32[3,32,32,128]{3,2,1,0:T(8,128)}, bf16[3,4,32,128]{3,2,1,0:T(8,128)(2,1)S(1)}, bf16[3,4,32,128]{3,2,1,0:T(8,128)(2,1)S(1)}) custom-call(s32[1]{0:T(128)} %bitcast.core_ref, f32[32,192,128]{2,1,0:T(8,128)} %bitcast.65, bf16[3,4,32,128]{3,2,1,0:T(8,128)(2,1)S(1)} %bitcast.63, ...), custom_call_target="tpu_custom_call" | custom-call | tf_op jit(solution)/shard_map/start/pallas_call | solution.py:157
  31.2 4.0 collective-permute-start.2
  45.3 4.6 collective-permute-done.5.down_ref
  49.9 8.3 %start.3 = (f32[3,32,32,128]{3,2,1,0:T(8,128)}, bf16[3,32,32,128]{3,2,1,0:T(8,128)(2,1)}, f32[3,32,32,128]{3,2,1,0:T(8,128)}, bf16[3,4,32,128]{3,2,1,0:T(8,128)(2,1)}, bf16[3,4,32,128]{3,2,1,0:T(8,128)(2,1)}) custom-call(s32[1]{0:T(128)} %bitcast.core_ref, f32[32,192,128]{2,1,0:T(8,128)} %bitcast.66, ...), custom_call_target="tpu_custom_call" | custom-call | tf_op jit(solution)/shard_map/start/pallas_call | solution.py:157
  71.9 9.3 %collective-permute-done.9.refs_1_ = bf16[2,1,16,32,128]{4,3,2,1,0:T(8,128)(2,1)S(1)} collective-permute-done((bf16[2,1,16,32,128]{4,3,2,1,0:T(8,128)(2,1)S(1)}, bf16[2,1,16,32,128]{4,3,2,1,0:T(8,128)(2,1)S(1)}, u32[]{:S(2)}, u32[]{:S(2)}) %collective-permute-start.9) | collective-permute-done | bytes 262176 | tf_op jit(solution)/shard_map/ppermute | solution.py:520
  81.1 10.7 %collective-permute-done.10.refs_4_ = bf16[2,1,16,32,128]{4,3,2,1,0:T(8,128)(2,1)S(1)} collective-permute-done((bf16[2,1,16,32,128]{4,3,2,1,0:T(8,128)(2,1)S(1)}, bf16[2,1,16,32,128]{4,3,2,1,0:T(8,128)(2,1)S(1)}, u32[]{:S(2)}, u32[]{:S(2)}) %collective-permute-start.10) | collective-permute-done | bytes 262176 | tf_op jit(solution)/shard_map/ppermute | solution.py:521
  91.8 11.8 %all-gather.11.cloned.1.call-done = bf16[24,32,32,128]{3,2,1,0:T(8,128)(2,1)} async-done(((bf16[3,32,32,128]{3,2,1,0:T(8,128)(2,1)}), bf16[24,32,32,128]{3,2,1,0:T(8,128)(2,1)}) %all-gather.11.cloned.1.call-update) | async-done | bytes 6291472 | tf_op jit(solution)/shard_map/all_gather | solution.py:647
  106.3 17.7 %observe.4 = f32[2,2,3,16,128]{4,3,2,1,0:T(8,128)S(1)} custom-call(s32[1]{0:T(128)} %bitcast.core_ref, bf16[8,3,32,32,128]{4,3,2,1,0:T(8,128)(2,1)} %bitcast.67, bf16[2,128,16,4096]{3,2,1,0:T(8,128)(2,1)} %refs_5_.7, bf16[2,128,16,4096]{3,2,1,0:T(8,128)(2,1)} %collective-permute-done.13.refs_1_.refs_6_.refs_8_, bf16[256,256]{1,0:T(8,128)(2,1)S(1)} %copy.38.refs_2_, ...), custom_call_target="tpu_custom_call" | custom-call | flops 402653184 | bytes 39845888 | tf_op jit(solution)/shard_map/observe/pallas_call | solution.py:380
  134.3 15.9 %pull_back.4 = bf16[4,2,3,16,32,128]{5,4,3,2,1,0:T(8,128)(2,1)} custom-call(s32[1]{0:T(128)} %bitcast.core_ref, f32[2,2,3,16,128]{4,3,2,1,0:T(8,128)S(1)} %reverse_add_fusion.3.refs_0_, f32[2,2,3,16,128]{4,3,2,1,0:T(8,128)S(1)} %collective-permute-done.17.refs_1_, f32[2,2,3,16,128]{4,3,2,1,0:T(8,128)S(1)} %collective-permute-done.18.refs_2_, ...), custom_call_target="tpu_custom_call" | custom-call | flops 402653184 | bytes 36700160 | tf_op jit(solution)/shard_map/pull_back/pallas_call | solution.py:454
  161.6 18.3 %observe.5 = f32[2,2,3,16,128]{4,3,2,1,0:T(8,128)S(1)} custom-call(s32[1]{0:T(128)} %bitcast.core_ref, bf16[4,2,2,16,32,128]{5,4,3,2,1,0:T(8,128)(2,1)} %bitcast.78, bf16[2,1,16,32,128]{4,3,2,1,0:T(8,128)(2,1)S(1)} %pad_maximum_fusion.2.refs_0_, bf16[2,1,16,32,128]{4,3,2,1,0:T(8,128)(2,1)S(1)} %collective-permute-done.9.refs_1_, ...), custom_call_target="tpu_custom_call" | custom-call | flops 402653184 | bytes 35651584 | tf_op jit(solution)/shard_map/observe/pallas_call | solution.py:380
  189.8 15.9 %pull_back.5 = bf16[4,2,3,16,32,128]{5,4,3,2,1,0:T(8,128)(2,1)} custom-call(s32[1]{0:T(128)} %bitcast.core_ref, f32[2,2,3,16,128]{4,3,2,1,0:T(8,128)S(1)} %reverse_add_fusion.2.refs_0_, f32[2,2,3,16,128]{4,3,2,1,0:T(8,128)S(1)} %collective-permute-done.29.refs_1_, f32[2,2,3,16,128]{4,3,2,1,0:T(8,128)S(1)} %collective-permute-done.30.refs_2_, ...), custom_call_target="tpu_custom_call" | custom-call | flops 402653184 | bytes 36700160 | tf_op jit(solution)/shard_map/pull_back/pallas_call | solution.py:454
  205.8 11.4 %reduce-scatter.5.cloned.1.call-done = bf16[1,2,3,16,32,128]{5,4,3,2,1,0:T(8,128)(2,1)} async-done(((bf16[4,2,3,16,32,128]{5,4,3,2,1,0:T(8,128)(2,1)}), bf16[1,2,3,16,32,128]{5,4,3,2,1,0:T(8,128)(2,1)}) %reduce-scatter.5.cloned.1.call-update) | async-done | bytes 786448 | tf_op jit(solution)/shard_map/reduce_scatter | solution.py:683
  225.5 4.6 collective-permute-done.22.cross_ref
  230.1 8.9 %step.2 = (f32[3,32,32,128]{3,2,1,0:T(8,128)}, bf16[3,32,32,128]{3,2,1,0:T(8,128)(2,1)}, f32[3,32,32,128]{3,2,1,0:T(8,128)}, bf16[3,4,32,128]{3,2,1,0:T(8,128)(2,1)S(1)}, bf16[3,4,32,128]{3,2,1,0:T(8,128)(2,1)S(1)}) custom-call(s32[1]{0:T(128)} %bitcast.core_ref, bf16[3,4,32,128]{3,2,1,0:T(8,128)(2,1)S(1)} %collective-permute-done.2.up_ref, ...), custom_call_target="tpu_custom_call" | custom-call | tf_op jit(solution)/shard_map/step/pallas_call | solution.py:218
  246.9 10.4 %collective-permute-done.24.refs_1_ = bf16[2,1,16,32,128]{4,3,2,1,0:T(8,128)(2,1)S(1)} collective-permute-done((bf16[2,1,16,32,128]{4,3,2,1,0:T(8,128)(2,1)S(1)}, bf16[2,1,16,32,128]{4,3,2,1,0:T(8,128)(2,1)S(1)}, u32[]{:S(2)}, u32[]{:S(2)}) %collective-permute-start.24) | collective-permute-done | bytes 262176 | tf_op jit(solution)/shard_map/ppermute | solution.py:520
  258.0 10.1 %collective-permute-done.26.refs_4_ = bf16[2,1,16,32,128]{4,3,2,1,0:T(8,128)(2,1)S(1)} collective-permute-done((bf16[2,1,16,32,128]{4,3,2,1,0:T(8,128)(2,1)S(1)}, bf16[2,1,16,32,128]{4,3,2,1,0:T(8,128)(2,1)S(1)}, u32[]{:S(2)}, u32[]{:S(2)}) %collective-permute-start.26) | collective-permute-done | bytes 262176 | tf_op jit(solution)/shard_map/ppermute | solution.py:521
  273.7 16.6 %reduce-scatter.7.cloned.1.call-done = bf16[1,2,3,16,32,128]{5,4,3,2,1,0:T(8,128)(2,1)} async-done(((bf16[4,2,3,16,32,128]{5,4,3,2,1,0:T(8,128)(2,1)}), bf16[1,2,3,16,32,128]{5,4,3,2,1,0:T(8,128)(2,1)}) %reduce-scatter.7.cloned.1.call-update) | async-done | bytes 786448 | tf_op jit(solution)/shard_map/reduce_scatter | solution.py:683
  299.0 4.2 collective-permute-done.36.cross_ref
  303.2 8.9 %step.3 = (f32[3,32,32,128]{3,2,1,0:T(8,128)}, bf16[3,32,32,128]{3,2,1,0:T(8,128)(2,1)}, f32[3,32,32,128]{3,2,1,0:T(8,128)}, bf16[3,4,32,128]{3,2,1,0:T(8,128)(2,1)S(1)}, bf16[3,4,32,128]{3,2,1,0:T(8,128)(2,1)S(1)}) custom-call(s32[1]{0:T(128)} %bitcast.core_ref, bf16[3,4,32,128]{3,2,1,0:T(8,128)(2,1)S(1)} %copy-done.3, ...), custom_call_target="tpu_custom_call" | custom-call | tf_op jit(solution)/shard_map/step/pallas_call | solution.py:218
  323.3 7.5 %collective-permute-done.40.refs_1_ = bf16[2,1,16,32,128]{4,3,2,1,0:T(8,128)(2,1)S(1)} collective-permute-done((bf16[2,1,16,32,128]{4,3,2,1,0:T(8,128)(2,1)S(1)}, bf16[2,1,16,32,128]{4,3,2,1,0:T(8,128)(2,1)S(1)}, u32[]{:S(2)}, u32[]{:S(2)}) %collective-permute-start.40) | collective-permute-done | bytes 262176 | tf_op jit(solution)/shard_map/ppermute | solution.py:520
  330.8 10.5 %collective-permute-done.41.refs_4_ = bf16[2,1,16,32,128]{4,3,2,1,0:T(8,128)(2,1)S(1)} collective-permute-done((bf16[2,1,16,32,128]{4,3,2,1,0:T(8,128)(2,1)S(1)}, bf16[2,1,16,32,128]{4,3,2,1,0:T(8,128)(2,1)S(1)}, u32[]{:S(2)}, u32[]{:S(2)}) %collective-permute-start.41) | collective-permute-done | bytes 262176 | tf_op jit(solution)/shard_map/ppermute | solution.py:521
  348.2 17.8 %observe.6 = f32[2,2,3,16,128]{4,3,2,1,0:T(8,128)S(1)} custom-call(s32[1]{0:T(128)} %bitcast.core_ref, bf16[4,2,2,16,32,128]{5,4,3,2,1,0:T(8,128)(2,1)} %bitcast.79, bf16[2,1,16,32,128]{4,3,2,1,0:T(8,128)(2,1)S(1)} %pad_maximum_fusion.1.refs_0_, bf16[2,1,16,32,128]{4,3,2,1,0:T(8,128)(2,1)S(1)} %collective-permute-done.24.refs_1_, ...), custom_call_target="tpu_custom_call" | custom-call | flops 402653184 | bytes 35651584 | tf_op jit(solution)/shard_map/observe/pallas_call | solution.py:380
  376.0 15.9 %pull_back.6 = bf16[4,2,3,16,32,128]{5,4,3,2,1,0:T(8,128)(2,1)} custom-call(s32[1]{0:T(128)} %bitcast.core_ref, f32[2,2,3,16,128]{4,3,2,1,0:T(8,128)S(1)} %reverse_add_fusion.1.refs_0_, f32[2,2,3,16,128]{4,3,2,1,0:T(8,128)S(1)} %collective-permute-done.49.refs_1_, f32[2,2,3,16,128]{4,3,2,1,0:T(8,128)S(1)} %collective-permute-done.50.refs_2_, ...), custom_call_target="tpu_custom_call" | custom-call | flops 402653184 | bytes 36700160 | tf_op jit(solution)/shard_map/pull_back/pallas_call | solution.py:454
  402.5 17.7 %observe.7 = f32[2,2,3,16,128]{4,3,2,1,0:T(8,128)S(1)} custom-call(s32[1]{0:T(128)} %bitcast.core_ref, bf16[4,2,2,16,32,128]{5,4,3,2,1,0:T(8,128)(2,1)} %bitcast.80, bf16[2,1,16,32,128]{4,3,2,1,0:T(8,128)(2,1)S(1)} %pad_maximum_fusion.refs_0_, bf16[2,1,16,32,128]{4,3,2,1,0:T(8,128)(2,1)S(1)} %collective-permute-done.40.refs_1_, ...), custom_call_target="tpu_custom_call" | custom-call | flops 402653184 | bytes 35651584 | tf_op jit(solution)/shard_map/observe/pallas_call | solution.py:380
  430.9 16.0 %pull_back.7 = bf16[4,2,3,16,32,128]{5,4,3,2,1,0:T(8,128)(2,1)} custom-call(s32[1]{0:T(128)} %bitcast.core_ref, f32[2,2,3,16,128]{4,3,2,1,0:T(8,128)S(1)} %reverse_add_fusion.refs_0_, f32[2,2,3,16,128]{4,3,2,1,0:T(8,128)S(1)} %collective-permute-done.53.refs_1_, f32[2,2,3,16,128]{4,3,2,1,0:T(8,128)S(1)} %collective-permute-done.54.refs_2_, ...), custom_call_target="tpu_custom_call" | custom-call | flops 402653184 | bytes 36700160 | tf_op jit(solution)/shard_map/pull_back/pallas_call | solution.py:454
  447.0 13.5 %reduce-scatter.11.cloned.1.call-done = bf16[1,2,3,16,32,128]{5,4,3,2,1,0:T(8,128)(2,1)} async-done(((bf16[4,2,3,16,32,128]{5,4,3,2,1,0:T(8,128)(2,1)}), bf16[1,2,3,16,32,128]{5,4,3,2,1,0:T(8,128)(2,1)}) %reduce-scatter.11.cloned.1.call-update) | async-done | bytes 786448 | tf_op jit(solution)/shard_map/reduce_scatter | solution.py:683
  468.9 4.5 collective-permute-done.58.cross_ref
  473.5 7.9 %finish.2 = (f32[32,192,128]{2,1,0:T(8,128)}, f32[32,192,128]{2,1,0:T(8,128)}) custom-call(s32[1]{0:T(128)} %bitcast.core_ref, bf16[3,4,32,128]{3,2,1,0:T(8,128)(2,1)S(1)} %collective-permute-done.32.up_ref, f32[3,32,32,128]{3,2,1,0:T(8,128)} %get-tuple-element.130.rest_ref, bf16[3,4,32,128]{3,2,1,0:T(8,128)(2,1)S(1)} %copy-done.1, ...), custom_call_target="tpu_custom_call" | custom-call | tf_op jit(solution)/shard_map/finish/pallas_call | solution.py:260
  481.3 41.8 %reduce-scatter.9.cloned.1.call-done = bf16[1,2,3,16,32,128]{5,4,3,2,1,0:T(8,128)(2,1)} async-done(((bf16[4,2,3,16,32,128]{5,4,3,2,1,0:T(8,128)(2,1)}), bf16[1,2,3,16,32,128]{5,4,3,2,1,0:T(8,128)(2,1)}) %reduce-scatter.9.cloned.1.call-update) | async-done | bytes 786448 | tf_op jit(solution)/shard_map/reduce_scatter | solution.py:683
  531.5 4.1 collective-permute-done.61.cross_ref
  535.7 7.9 %finish.3 = (f32[32,192,128]{2,1,0:T(8,128)}, f32[32,192,128]{2,1,0:T(8,128)}) custom-call(s32[1]{0:T(128)} %bitcast.core_ref, bf16[3,4,32,128]{3,2,1,0:T(8,128)(2,1)S(1)} %collective-permute-done.38.up_ref, f32[3,32,32,128]{3,2,1,0:T(8,128)} %get-tuple-element.114.rest_ref, ...), custom_call_target="tpu_custom_call", output_to_operand_aliasing={{0}: (10, {}), {1}: (11, {})} | custom-call | tf_op jit(solution)/shard_map/finish/pallas_call | solution.py:260
  (226 shorter events, 165.8 us)
Async XLA Ops:
  7.2 96.4 %all-gather.11.cloned.1.call-start = ((), (), s32[]{:S(2)}) async-start(), calls=%async_computation.9 | async-start | bytes 7077888 | tf_op jit(solution)/shard_map/all_gather | solution.py:647
  7.2 99.0 %collective-permute-start.13 = (bf16[2,128,16,4096]{3,2,1,0:T(8,128)(2,1)}, bf16[2,128,16,4096]{3,2,1,0:T(8,128)(2,1)}, u32[]{:S(2)}, u32[]{:S(2)}) collective-permute-start(bf16[2,128,16,4096]{3,2,1,0:T(8,128)(2,1)} %refs_5_.7), channel_id=1, source_target_pairs={{0,1},{1,0},{2,3},{3,2},{4,5},{5,4},{6,7},{7,6},{8,9},{9,8},{10,11... | collective-permute-start | bytes 100663304 | tf_op jit(solution)/shard_map/ppermute | solution.py:496
  31.2 130.4 %all-gather.9.cloned.1.call-start = ((), (), s32[]{:S(2)}) async-start(), calls=%async_computation.8 | async-start | bytes 2621440 | tf_op jit(solution)/shard_map/all_gather | solution.py:647
  64.9 152.3 %reduce-scatter.5.cloned.1.call-start = ((), (), s32[]{:S(2)}) async-start(), calls=%async_computation.4 | async-start | bytes 3932160 | tf_op jit(solution)/shard_map/reduce_scatter | solution.py:683
  66.5 14.6 %collective-permute-start.9 = (bf16[2,1,16,32,128]{4,3,2,1,0:T(8,128)(2,1)S(1)}, bf16[2,1,16,32,128]{4,3,2,1,0:T(8,128)(2,1)S(1)}, u32[]{:S(2)}, u32[]{:S(2)}) collective-permute-start(bf16[2,1,16,32,128]{4,3,2,1,0:T(8,128)(2,1)S(1)} %pad_maximum_fusion.2.refs_0_), channel_id=1, source_target_pairs={{0,2},{1,3},{2,4},{3,5},{4,6},{5,7},{8,10},{9,11},{10,12},{11,13},... | collective-permute-start | bytes 786440 | tf_op jit(solution)/shard_map/ppermute | solution.py:520
  69.7 22.1 %collective-permute-start.10 = (bf16[2,1,16,32,128]{4,3,2,1,0:T(8,128)(2,1)S(1)}, bf16[2,1,16,32,128]{4,3,2,1,0:T(8,128)(2,1)S(1)}, u32[]{:S(2)}, u32[]{:S(2)}) collective-permute-start(bf16[2,1,16,32,128]{4,3,2,1,0:T(8,128)(2,1)S(1)} %pad_maximum_fusion.2.refs_0_), channel_id=1, source_target_pairs={{7,5},{6,4},{5,3},{4,2},{3,1},{2,0},{15,13},{14,12},{13,11},{12,10... | collective-permute-start | bytes 786440 | tf_op jit(solution)/shard_map/ppermute | solution.py:521
  103.6 20.4 %collective-permute-start.11 = (bf16[2,1,16,32,128]{4,3,2,1,0:T(8,128)(2,1)S(1)}, bf16[2,1,16,32,128]{4,3,2,1,0:T(8,128)(2,1)S(1)}, u32[]{:S(2)}, u32[]{:S(2)}) collective-permute-start(bf16[2,1,16,32,128]{4,3,2,1,0:T(8,128)(2,1)S(1)} %collective-permute-done.9.refs_1_), channel_id=1, source_target_pairs={{2,4},{3,5},{4,6},{5,7},{10,12},{11,13},{12,14},{13,15},{18,20},{1... | collective-permute-start | bytes 786440 | tf_op jit(solution)/shard_map/ppermute | solution.py:520
  104.3 19.8 %collective-permute-start.12 = (bf16[2,1,16,32,128]{4,3,2,1,0:T(8,128)(2,1)S(1)}, bf16[2,1,16,32,128]{4,3,2,1,0:T(8,128)(2,1)S(1)}, u32[]{:S(2)}, u32[]{:S(2)}) collective-permute-start(bf16[2,1,16,32,128]{4,3,2,1,0:T(8,128)(2,1)S(1)} %collective-permute-done.10.refs_4_), channel_id=1, source_target_pairs={{5,3},{4,2},{3,1},{2,0},{13,11},{12,10},{11,9},{10,8},{21,19},{20,... | collective-permute-start | bytes 786440 | tf_op jit(solution)/shard_map/ppermute | solution.py:521
  125.0 25.1 %collective-permute-start.14 = (bf16[2,1,16,32,128]{4,3,2,1,0:T(8,128)(2,1)S(1)}, bf16[2,1,16,32,128]{4,3,2,1,0:T(8,128)(2,1)S(1)}, u32[]{:S(2)}, u32[]{:S(2)}) collective-permute-start(bf16[2,1,16,32,128]{4,3,2,1,0:T(8,128)(2,1)S(1)} %collective-permute-done.11.refs_2_), channel_id=1, source_target_pairs={{4,6},{5,7},{12,14},{13,15},{20,22},{21,23},{28,30},{29,31}} | collective-permute-start | bytes 786440 | tf_op jit(solution)/shard_map/ppermute | solution.py:520
  125.7 27.1 %collective-permute-start.15 = (bf16[2,1,16,32,128]{4,3,2,1,0:T(8,128)(2,1)S(1)}, bf16[2,1,16,32,128]{4,3,2,1,0:T(8,128)(2,1)S(1)}, u32[]{:S(2)}, u32[]{:S(2)}) collective-permute-start(bf16[2,1,16,32,128]{4,3,2,1,0:T(8,128)(2,1)S(1)} %collective-permute-done.12.refs_5_), channel_id=1, source_target_pairs={{3,1},{2,0},{11,9},{10,8},{19,17},{18,16},{27,25},{26,24}} | collective-permute-start | bytes 786440 | tf_op jit(solution)/shard_map/ppermute | solution.py:521
  152.8 137.6 %reduce-scatter.7.cloned.1.call-start = ((), (), s32[]{:S(2)}) async-start(), calls=%async_computation.5 | async-start | bytes 3932160 | tf_op jit(solution)/shard_map/reduce_scatter | solution.py:683
  205.7 138.3 %all-gather.15.cloned.1.call-start = ((), (), s32[]{:S(2)}) async-start(), calls=%async_computation.11 | async-start | bytes 2621440 | tf_op jit(solution)/shard_map/all_gather | solution.py:647
  218.2 11.9 %collective-permute-start.20 = (bf16[1,3,16,32,128]{4,3,2,1,0:T(8,128)(2,1)S(1)}, bf16[1,3,16,32,128]{4,3,2,1,0:T(8,128)(2,1)S(1)}, u32[]{:S(2)}, u32[]{:S(2)}) collective-permute-start(bf16[1,3,16,32,128]{4,3,2,1,0:T(8,128)(2,1)S(1)} %slice_bitcast_fusion.1), channel_id=1, source_target_pairs={{0,1},{1,0},{2,3},{3,2},{4,5},{5,4},{6,7},{7,6},{8,9},{9,8},{10,11... | collective-permute-start | bytes 1179656 | tf_op jit(solution)/shard_map/ppermute | solution.py:496
  242.9 159.6 %all-gather.13.cloned.1.call-start = ((), (), s32[]{:S(2)}) async-start(), calls=%async_computation.10 | async-start | bytes 2621440 | tf_op jit(solution)/shard_map/all_gather | solution.py:647
  243.0 14.4 %collective-permute-start.24 = (bf16[2,1,16,32,128]{4,3,2,1,0:T(8,128)(2,1)S(1)}, bf16[2,1,16,32,128]{4,3,2,1,0:T(8,128)(2,1)S(1)}, u32[]{:S(2)}, u32[]{:S(2)}) collective-permute-start(bf16[2,1,16,32,128]{4,3,2,1,0:T(8,128)(2,1)S(1)} %pad_maximum_fusion.1.refs_0_), channel_id=1, source_target_pairs={{0,2},{1,3},{2,4},{3,5},{4,6},{5,7},{8,10},{9,11},{10,12},{11,13},... | collective-permute-start | bytes 786440 | tf_op jit(solution)/shard_map/ppermute | solution.py:520
  245.6 22.5 %collective-permute-start.26 = (bf16[2,1,16,32,128]{4,3,2,1,0:T(8,128)(2,1)S(1)}, bf16[2,1,16,32,128]{4,3,2,1,0:T(8,128)(2,1)S(1)}, u32[]{:S(2)}, u32[]{:S(2)}) collective-permute-start(bf16[2,1,16,32,128]{4,3,2,1,0:T(8,128)(2,1)S(1)} %pad_maximum_fusion.1.refs_0_), channel_id=1, source_target_pairs={{7,5},{6,4},{5,3},{4,2},{3,1},{2,0},{15,13},{14,12},{13,11},{12,10... | collective-permute-start | bytes 786440 | tf_op jit(solution)/shard_map/ppermute | solution.py:521
  257.3 33.0 %collective-permute-start.25 = (bf16[2,1,16,32,128]{4,3,2,1,0:T(8,128)(2,1)S(1)}, bf16[2,1,16,32,128]{4,3,2,1,0:T(8,128)(2,1)S(1)}, u32[]{:S(2)}, u32[]{:S(2)}) collective-permute-start(bf16[2,1,16,32,128]{4,3,2,1,0:T(8,128)(2,1)S(1)} %collective-permute-done.24.refs_1_), channel_id=1, source_target_pairs={{2,4},{3,5},{4,6},{5,7},{10,12},{11,13},{12,14},{13,15},{18,20},{1... | collective-permute-start | bytes 786440 | tf_op jit(solution)/shard_map/ppermute | solution.py:520
  268.1 22.2 %collective-permute-start.27 = (bf16[2,1,16,32,128]{4,3,2,1,0:T(8,128)(2,1)S(1)}, bf16[2,1,16,32,128]{4,3,2,1,0:T(8,128)(2,1)S(1)}, u32[]{:S(2)}, u32[]{:S(2)}) collective-permute-start(bf16[2,1,16,32,128]{4,3,2,1,0:T(8,128)(2,1)S(1)} %collective-permute-done.26.refs_4_), channel_id=1, source_target_pairs={{5,3},{4,2},{3,1},{2,0},{13,11},{12,10},{11,9},{10,8},{21,19},{20,... | collective-permute-start | bytes 786440 | tf_op jit(solution)/shard_map/ppermute | solution.py:521
  269.4 20.9 %collective-permute-start.32 = (bf16[3,4,32,128]{3,2,1,0:T(8,128)(2,1)S(1)}, bf16[3,4,32,128]{3,2,1,0:T(8,128)(2,1)S(1)}, u32[]{:S(2)}, u32[]{:S(2)}) collective-permute-start(bf16[3,4,32,128]{3,2,1,0:T(8,128)(2,1)S(1)} %get-tuple-element.103), channel_id=1, source_target_pairs={{0,8},{8,16},{16,24},{1,9},{9,17},{17,25},{2,10},{10,18},{18,26},{... | collective-permute-start | bytes 294920 | tf_op jit(solution)/shard_map/ppermute | solution.py:478
  272.4 17.9 %collective-permute-start.33 = (bf16[3,4,32,128]{3,2,1,0:T(8,128)(2,1)S(1)}, bf16[3,4,32,128]{3,2,1,0:T(8,128)(2,1)S(1)}, u32[]{:S(2)}, u32[]{:S(2)}) collective-permute-start(bf16[3,4,32,128]{3,2,1,0:T(8,128)(2,1)S(1)} %get-tuple-element.105), channel_id=1, source_target_pairs={{8,0},{16,8},{24,16},{9,1},{17,9},{25,17},{10,2},{18,10},{26,18},{... | collective-permute-start | bytes 294920 | tf_op jit(solution)/shard_map/ppermute | solution.py:478
  291.4 11.8 %collective-permute-start.34 = (bf16[1,3,16,32,128]{4,3,2,1,0:T(8,128)(2,1)S(1)}, bf16[1,3,16,32,128]{4,3,2,1,0:T(8,128)(2,1)S(1)}, u32[]{:S(2)}, u32[]{:S(2)}) collective-permute-start(bf16[1,3,16,32,128]{4,3,2,1,0:T(8,128)(2,1)S(1)} %slice.149), channel_id=1, source_target_pairs={{0,1},{1,0},{2,3},{3,2},{4,5},{5,4},{6,7},{7,6},{8,9},{9,8},{10,11... | collective-permute-start | bytes 1179656 | tf_op jit(solution)/shard_map/ppermute | solution.py:496
  316.1 144.4 %reduce-scatter.11.cloned.1.call-start = ((), (), s32[]{:S(2)}) async-start(), calls=%async_computation.7 | async-start | bytes 3932160 | tf_op jit(solution)/shard_map/reduce_scatter | solution.py:683
  316.1 14.7 %collective-permute-start.40 = (bf16[2,1,16,32,128]{4,3,2,1,0:T(8,128)(2,1)S(1)}, bf16[2,1,16,32,128]{4,3,2,1,0:T(8,128)(2,1)S(1)}, u32[]{:S(2)}, u32[]{:S(2)}) collective-permute-start(bf16[2,1,16,32,128]{4,3,2,1,0:T(8,128)(2,1)S(1)} %pad_maximum_fusion.refs_0_), channel_id=1, source_target_pairs={{0,2},{1,3},{2,4},{3,5},{4,6},{5,7},{8,10},{9,11},{10,12},{11,13},... | collective-permute-start | bytes 786440 | tf_op jit(solution)/shard_map/ppermute | solution.py:520
  319.4 22.0 %collective-permute-start.41 = (bf16[2,1,16,32,128]{4,3,2,1,0:T(8,128)(2,1)S(1)}, bf16[2,1,16,32,128]{4,3,2,1,0:T(8,128)(2,1)S(1)}, u32[]{:S(2)}, u32[]{:S(2)}) collective-permute-start(bf16[2,1,16,32,128]{4,3,2,1,0:T(8,128)(2,1)S(1)} %pad_maximum_fusion.refs_0_), channel_id=1, source_target_pairs={{7,5},{6,4},{5,3},{4,2},{3,1},{2,0},{15,13},{14,12},{13,11},{12,10... | collective-permute-start | bytes 786440 | tf_op jit(solution)/shard_map/ppermute | solution.py:521
  320.7 26.0 %collective-permute-start.44 = (bf16[2,1,16,32,128]{4,3,2,1,0:T(8,128)(2,1)S(1)}, bf16[2,1,16,32,128]{4,3,2,1,0:T(8,128)(2,1)}, u32[]{:S(2)}, u32[]{:S(2)}) collective-permute-start(bf16[2,1,16,32,128]{4,3,2,1,0:T(8,128)(2,1)S(1)} %collective-permute-done.25.refs_2_), channel_id=1, source_target_pairs={{4,6},{5,7},{12,14},{13,15},{20,22},{21,23},{28,30},{29,31}} | collective-permute-start | bytes 786440 | tf_op jit(solution)/shard_map/ppermute | solution.py:520
  322.0 26.2 %collective-permute-start.45 = (bf16[2,1,16,32,128]{4,3,2,1,0:T(8,128)(2,1)S(1)}, bf16[2,1,16,32,128]{4,3,2,1,0:T(8,128)(2,1)}, u32[]{:S(2)}, u32[]{:S(2)}) collective-permute-start(bf16[2,1,16,32,128]{4,3,2,1,0:T(8,128)(2,1)S(1)} %collective-permute-done.27.refs_5_), channel_id=1, source_target_pairs={{3,1},{2,0},{11,9},{10,8},{19,17},{18,16},{27,25},{26,24}} | collective-permute-start | bytes 786440 | tf_op jit(solution)/shard_map/ppermute | solution.py:521
  344.0 22.0 %collective-permute-start.42 = (bf16[2,1,16,32,128]{4,3,2,1,0:T(8,128)(2,1)S(1)}, bf16[2,1,16,32,128]{4,3,2,1,0:T(8,128)(2,1)}, u32[]{:S(2)}, u32[]{:S(2)}) collective-permute-start(bf16[2,1,16,32,128]{4,3,2,1,0:T(8,128)(2,1)S(1)} %collective-permute-done.40.refs_1_), channel_id=1, source_target_pairs={{2,4},{3,5},{4,6},{5,7},{10,12},{11,13},{12,14},{13,15},{18,20},{1... | collective-permute-start | bytes 786440 | tf_op jit(solution)/shard_map/ppermute | solution.py:520
  345.4 20.7 %collective-permute-start.43 = (bf16[2,1,16,32,128]{4,3,2,1,0:T(8,128)(2,1)S(1)}, bf16[2,1,16,32,128]{4,3,2,1,0:T(8,128)(2,1)}, u32[]{:S(2)}, u32[]{:S(2)}) collective-permute-start(bf16[2,1,16,32,128]{4,3,2,1,0:T(8,128)(2,1)S(1)} %collective-permute-done.41.refs_4_), channel_id=1, source_target_pairs={{5,3},{4,2},{3,1},{2,0},{13,11},{12,10},{11,9},{10,8},{21,19},{20,... | collective-permute-start | bytes 786440 | tf_op jit(solution)/shard_map/ppermute | solution.py:521
  366.5 25.4 %collective-permute-start.46 = (bf16[2,1,16,32,128]{4,3,2,1,0:T(8,128)(2,1)}, bf16[2,1,16,32,128]{4,3,2,1,0:T(8,128)(2,1)S(1)}, u32[]{:S(2)}, u32[]{:S(2)}) collective-permute-start(bf16[2,1,16,32,128]{4,3,2,1,0:T(8,128)(2,1)} %collective-permute-done.42.refs_2_), channel_id=1, source_target_pairs={{4,6},{5,7},{12,14},{13,15},{20,22},{21,23},{28,30},{29,31}} | collective-permute-start | bytes 786440 | tf_op jit(solution)/shard_map/ppermute | solution.py:520
  367.2 26.6 %collective-permute-start.47 = (bf16[2,1,16,32,128]{4,3,2,1,0:T(8,128)(2,1)}, bf16[2,1,16,32,128]{4,3,2,1,0:T(8,128)(2,1)S(1)}, u32[]{:S(2)}, u32[]{:S(2)}) collective-permute-start(bf16[2,1,16,32,128]{4,3,2,1,0:T(8,128)(2,1)} %collective-permute-done.43.refs_5_), channel_id=1, source_target_pairs={{3,1},{2,0},{11,9},{10,8},{19,17},{18,16},{27,25},{26,24}} | collective-permute-start | bytes 786440 | tf_op jit(solution)/shard_map/ppermute | solution.py:521
  393.9 129.3 %reduce-scatter.9.cloned.1.call-start = ((), (), s32[]{:S(2)}) async-start(), calls=%async_computation.6 | async-start | bytes 3932160 | tf_op jit(solution)/shard_map/reduce_scatter | solution.py:683
  461.5 11.9 %collective-permute-start.56 = (bf16[1,3,16,32,128]{4,3,2,1,0:T(8,128)(2,1)S(1)}, bf16[1,3,16,32,128]{4,3,2,1,0:T(8,128)(2,1)S(1)}, u32[]{:S(2)}, u32[]{:S(2)}) collective-permute-start(bf16[1,3,16,32,128]{4,3,2,1,0:T(8,128)(2,1)S(1)} %slice_bitcast_fusion), channel_id=1, source_target_pairs={{0,1},{1,0},{2,3},{3,2},{4,5},{5,4},{6,7},{7,6},{8,9},{9,8},{10,11... | collective-permute-start | bytes 1179656 | tf_op jit(solution)/shard_map/ppermute | solution.py:496
  (48 other events, 365.2 us)
Sparse Core Ops, SparseCore 0:
  31.3 72.2 all-gather.10
  105.7 49.2 all-gather.8
  157.9 59.1 reduce-scatter.4
  219.9 70.4 reduce-scatter.6
  291.8 52.2 all-gather.14
  346.0 51.4 all-gather.12
  400.4 60.0 reduce-scatter.10
  462.8 60.2 reduce-scatter.8
